TPU v7x, 32 devices: a whole 2x2x4 slice. The times are simulated.
32 devices in a mesh: dp: 8 (over y, x, core), tensor: 4 (over z).
Axes of the slice: x: 2, y: 2, z: 4, core: 2. Of those that a mesh axis runs over, the one named last changes fastest.
Arguments:
- tokens: bfloat16 [8192, 1536], P(('dp', 'tensor')), may hold values from -6 to 6
- expert_ids: int32 [8192, 4], P('dp'), may hold values from 0 to 31, all different within a row; in each aligned block of 1024 rows (0 to 1023, 1024 to 2047, ...) at most 256 rows name the same one
- route_weights: float32 [8192, 4], P('dp'), may hold values from 0.1 to 0.4
- attn_gain: bfloat16 [1536], P('dp'), may hold values from 0.5 to 1.5
- q_weight: bfloat16 [1536, 1536], P('dp', 'tensor'), may hold values from -0.21875 to 0.21875
- k_weight: bfloat16 [1536, 256], P('dp'), may hold values from -0.21875 to 0.21875
- v_weight: bfloat16 [1536, 256], P('dp'), may hold values from -0.15625 to 0.15625
- o_weight: bfloat16 [1536, 1536], P('dp', 'tensor'), may hold values from -0.875 to 0.875
- moe_gain: bfloat16 [1536], P('dp'), may hold values from 0.5 to 1.5
- gate_weight: bfloat16 [1536, 32, 768], P('dp', None, 'tensor'), may hold values from -0.15625 to 0.15625
- up_weight: bfloat16 [1536, 32, 768], P('dp', None, 'tensor'), may hold values from -0.15625 to 0.15625
- down_weight: bfloat16 [1536, 32, 768], P('dp', None, 'tensor'), may hold values from -0.4375 to 0.4375
- cotangent: float32 [8192, 1536], P(('dp', 'tensor')), may hold values from -6 to 6
Outputs:
- output: bfloat16 [8192, 1536], P(('dp', 'tensor'))
- tokens_grad: float32 [8192, 1536], P(('dp', 'tensor'))
- attn_gain_grad: float32 [1536], P('dp')
- q_grad: float32 [1536, 1536], P('dp', 'tensor')
- k_grad: float32 [1536, 256], P('dp')
- v_grad: float32 [1536, 256], P('dp')
- o_grad: float32 [1536, 1536], P('dp', 'tensor')
- moe_gain_grad: float32 [1536], P('dp')
- gate_grad: float32 [1536, 32, 768], P('dp', None, 'tensor')
- up_grad: float32 [1536, 32, 768], P('dp', None, 'tensor')
- down_grad: float32 [1536, 32, 768], P('dp', None, 'tensor')
Inputs may be any that keep to these rules, and one draw needn't show every extreme that they name: `expert_ids`: each row names 4 different experts. Among the 1024 rows of one index of dp no expert is named more than 256 times, and in some index of dp an expert is named exactly 256 times.
All inputs are finite; a program needn't handle non-finite values.
Results may differ from a plain program's by a relative error of at most 0.023.
Values may be sent and summed in bfloat16 or wider, within the bound.
A program may use at most 192 MiB of HBM per device.

v0:
```python
import jax
import jax.numpy as jnp
from jax import lax
from jax.sharding import PartitionSpec as P

KV = 2
HD = 128
EXPERTS = 32
TOPK = 4
SEQ = 1024
BLOCK = 256
QROWS = 512
GROUP = 2
CAP = 256


eps = 1e-06
rope_base = 1000000.0
negative = -1e30


def plain_dot(left_side, right_side):
    return jnp.dot(left_side, right_side, preferred_element_type=jnp.float32)


def dot_last(left_side, right_side):
    return lax.dot_general(
        left_side, right_side, (((1,), (1,)), ((), ())), preferred_element_type=jnp.float32
    )


def dot_first(left_side, right_side):
    return lax.dot_general(
        left_side, right_side, (((0,), (0,)), ((), ())), preferred_element_type=jnp.float32
    )


def rope_tables(row_count):
    half_size = HD // 2
    positions = (jnp.arange(row_count) % SEQ).astype(jnp.float32)
    frequency = rope_base ** (-(jnp.arange(half_size).astype(jnp.float32) * 2.0 / HD))
    angles = positions[:, None] * frequency[None, :]
    return (jnp.cos(angles), jnp.sin(angles))


def rotate(values, cos_table, sin_table):
    half_size = values.shape[-1] // 2
    first_half = values[..., :half_size]
    second_half = values[..., half_size:]
    return jnp.concatenate(
        [
            first_half * cos_table - second_half * sin_table,
            second_half * cos_table + first_half * sin_table,
        ],
        axis=-1,
    )


def unrotate(incoming_gradient, cos_table, sin_table):
    half_size = incoming_gradient.shape[-1] // 2
    first_half = incoming_gradient[..., :half_size]
    second_half = incoming_gradient[..., half_size:]
    return jnp.concatenate(
        [
            first_half * cos_table + second_half * sin_table,
            second_half * cos_table - first_half * sin_table,
        ],
        axis=-1,
    )


def rmsnorm_pieces(x_rows):
    inverse_rms = lax.rsqrt(jnp.mean(x_rows * x_rows, axis=-1, keepdims=True) + eps)
    return (inverse_rms, x_rows * inverse_rms)


def rmsnorm_backward(normalized_gradient, unit_variance_rows, inverse_rms, norm_weight):
    rescaled_rows = normalized_gradient * norm_weight
    incoming_gradient = inverse_rms * (
        rescaled_rows
        - unit_variance_rows * jnp.mean(rescaled_rows * unit_variance_rows, axis=-1, keepdims=True)
    )
    return (incoming_gradient, jnp.sum(normalized_gradient * unit_variance_rows, axis=0))


def slot_table(id_rows, weight_rows):
    row_count = id_rows.shape[0]
    flattened = id_rows.reshape(-1)
    one_hot = (flattened[:, None] == jnp.arange(EXPERTS, dtype=jnp.int32)[None, :]).astype(
        jnp.int32
    )
    before = jnp.cumsum(one_hot, axis=0) - one_hot
    ranking = jnp.sum(before * one_hot, axis=1)
    slot_index = flattened * CAP + ranking
    owners = jnp.arange(row_count * TOPK, dtype=jnp.int32) // TOPK
    table = jnp.full((EXPERTS * CAP,), row_count, jnp.int32).at[slot_index].set(owners)
    slot_gates = (
        jnp.zeros((EXPERTS * CAP,), jnp.float32).at[slot_index].set(weight_rows.reshape(-1))
    )
    return (table, slot_gates)


def block_inputs(queries, keys_rot, values, block_index):
    seq_blocks = SEQ // QROWS
    q_rows = lax.dynamic_slice_in_dim(queries, block_index * QROWS, QROWS, 0)
    seq_start = block_index // seq_blocks * SEQ
    q_place = block_index % seq_blocks * QROWS + jnp.arange(QROWS, dtype=jnp.int32)
    k_place = jnp.arange(SEQ, dtype=jnp.int32)
    allowed = k_place[None, :] // BLOCK <= q_place[:, None] // BLOCK
    return (q_rows, keys_rot, values, allowed, seq_start)


def attend_forward(queries, keys_rot, values):
    row_count = queries.shape[0]
    head_scale = HD ** (-0.5)

    def one_block(block_index):
        q_rows, k_rows, v_rows, allowed, seq_start = block_inputs(
            queries, keys_rot, values, block_index
        )
        scores = (
            jnp.einsum("qhd,kd->hqk", q_rows, k_rows, preferred_element_type=jnp.float32)
            * head_scale
        )
        scores = jnp.where(allowed[None], scores, negative)
        row_peak = jnp.max(scores, axis=-1, keepdims=True)
        exp_scores = jnp.exp(scores - row_peak)
        row_total = jnp.sum(exp_scores, axis=-1, keepdims=True)
        probs_low = (exp_scores / row_total).astype(jnp.bfloat16)
        mixed_heads = jnp.einsum(
            "hqk,kd->qhd", probs_low, v_rows, preferred_element_type=jnp.float32
        )
        return (mixed_heads.reshape(QROWS, -1), (row_peak + jnp.log(row_total))[..., 0])

    mixed_heads, log_total = lax.map(one_block, jnp.arange(row_count // QROWS, dtype=jnp.int32))
    return (mixed_heads.reshape(row_count, -1), log_total)


def attend_backward(queries, keys_rot, values, grad_heads, log_total):
    row_count = queries.shape[0]
    head_scale = HD ** (-0.5)

    def one_block(carry, block_index):
        grad_keys, grad_values = carry
        q_rows, k_rows, v_rows, allowed, seq_start = block_inputs(
            queries, keys_rot, values, block_index
        )
        grad_rows = lax.dynamic_slice_in_dim(grad_heads, block_index * QROWS, QROWS, 0)
        scores = (
            jnp.einsum("qhd,kd->hqk", q_rows, k_rows, preferred_element_type=jnp.float32)
            * head_scale
        )
        probs = jnp.where(allowed[None], jnp.exp(scores - log_total[block_index][:, :, None]), 0.0)
        grad_probs = jnp.einsum(
            "qhd,kd->hqk", grad_rows, v_rows, preferred_element_type=jnp.float32
        )
        row_inner = jnp.sum(probs * grad_probs, axis=-1, keepdims=True)
        grad_scores = (probs * (grad_probs - row_inner)).astype(jnp.bfloat16)
        block_q = (
            jnp.einsum("hqk,kd->qhd", grad_scores, k_rows, preferred_element_type=jnp.float32)
            * head_scale
        )
        block_k = (
            jnp.einsum("hqk,qhd->kd", grad_scores, q_rows, preferred_element_type=jnp.float32)
            * head_scale
        )
        block_v = jnp.einsum(
            "hqk,qhd->kd", probs.astype(jnp.bfloat16), grad_rows, preferred_element_type=jnp.float32
        )
        grad_keys = grad_keys + block_k
        grad_values = grad_values + block_v
        return ((grad_keys, grad_values), block_q)

    empty = jnp.zeros((row_count, keys_rot.shape[1]), jnp.float32)
    (grad_keys, grad_values), grad_queries = lax.scan(
        one_block, (empty, empty), jnp.arange(row_count // QROWS, dtype=jnp.int32)
    )
    return (grad_queries.reshape(queries.shape), grad_keys, grad_values)


def regroup(stacked):
    return jnp.transpose(stacked, (1, 0, 2, 3)).reshape(stacked.shape[1], EXPERTS, stacked.shape[3])


def body(
    tokens,
    expert_ids,
    route_weights,
    attn_gain,
    q_weight,
    k_weight,
    v_weight,
    o_weight,
    moe_gain,
    gate_weight,
    up_weight,
    down_weight,
    cotangent,
):
    tensor_count = lax.axis_size("tensor")
    member = lax.axis_index("tensor")
    first_norm_weight, q_full, k_full, v_full, o_full, second_norm_weight = (
        lax.all_gather(attn_gain, "dp", axis=0, tiled=True),
        lax.all_gather(q_weight, "dp", axis=0, tiled=True),
        lax.all_gather(k_weight, "dp", axis=0, tiled=True),
        lax.all_gather(v_weight, "dp", axis=0, tiled=True),
        lax.all_gather(o_weight, "dp", axis=0, tiled=True),
        lax.all_gather(moe_gain, "dp", axis=0, tiled=True),
    )
    first_norm_weight = first_norm_weight.astype(jnp.float32)
    second_norm_weight = second_norm_weight.astype(jnp.float32)
    kv_head = member * KV // tensor_count
    k_cols = lax.dynamic_slice_in_dim(k_full, kv_head * HD, HD, 1)
    v_cols = lax.dynamic_slice_in_dim(v_full, kv_head * HD, HD, 1)
    local_input_rows = tokens.astype(jnp.float32)
    first_inverse_rms, first_unit_rows = rmsnorm_pieces(local_input_rows)
    first_normalized = (first_unit_rows * first_norm_weight).astype(jnp.bfloat16)
    rows_all = lax.all_gather(first_normalized, "tensor", axis=0, tiled=True)
    row_count = rows_all.shape[0]
    width = q_full.shape[1]
    heads_dev = width // HD
    cos_table, sin_table = rope_tables(row_count)
    q_pre = plain_dot(rows_all, q_full).reshape(row_count, heads_dev, HD)
    queries = rotate(q_pre, cos_table[:, None, :], sin_table[:, None, :]).astype(jnp.bfloat16)
    keys_rot = rotate(plain_dot(rows_all, k_cols), cos_table, sin_table).astype(jnp.bfloat16)
    values = plain_dot(rows_all, v_cols).astype(jnp.bfloat16)
    mixed_heads, log_total = attend_forward(queries, keys_rot, values)
    mixed_low = mixed_heads.astype(jnp.bfloat16)
    branch = dot_last(mixed_low, o_full)
    branch_own = lax.psum_scatter(
        branch.astype(jnp.bfloat16), "tensor", scatter_dimension=0, tiled=True
    ).astype(jnp.float32)
    residual_state = local_input_rows + branch_own
    second_inverse_rms, second_unit_rows = rmsnorm_pieces(residual_state)
    second_normalized = (second_unit_rows * second_norm_weight).astype(jnp.bfloat16)
    moe_all = lax.all_gather(second_normalized, "tensor", axis=0, tiled=True)
    width_model = moe_all.shape[1]
    padded = jnp.concatenate([moe_all, jnp.zeros((1, width_model), jnp.bfloat16)], axis=0)
    table, slot_gates = slot_table(expert_ids, route_weights)
    group_ids = jnp.arange(EXPERTS // GROUP, dtype=jnp.int32)
    grad_low = cotangent.astype(jnp.bfloat16)
    grad_all = lax.all_gather(grad_low, "tensor", axis=0, tiled=True)
    grad_pad = jnp.concatenate([grad_all, jnp.zeros((1, width_model), jnp.bfloat16)], axis=0)

    def fetch(group_id):
        gate_piece = lax.dynamic_slice_in_dim(gate_weight, group_id * GROUP, GROUP, 1)
        up_piece = lax.dynamic_slice_in_dim(up_weight, group_id * GROUP, GROUP, 1)
        down_piece = lax.dynamic_slice_in_dim(down_weight, group_id * GROUP, GROUP, 1)
        return (
            lax.all_gather(gate_piece, "dp", axis=0, tiled=True),
            lax.all_gather(up_piece, "dp", axis=0, tiled=True),
            lax.all_gather(down_piece, "dp", axis=0, tiled=True),
        )

    def group_rows(group_id):
        token_index = lax.dynamic_slice_in_dim(table, group_id * GROUP * CAP, GROUP * CAP, 0)
        slot_gate = lax.dynamic_slice_in_dim(
            slot_gates, group_id * GROUP * CAP, GROUP * CAP, 0
        ).reshape(GROUP, CAP, 1)
        inputs = jnp.take(padded, token_index, axis=0).reshape(GROUP, CAP, width_model)
        return (token_index, slot_gate, inputs)

    def expert_forward(running, group_id):
        weights_now = fetch(group_id)
        gate_block, up_block, down_block = weights_now
        token_index, slot_gate, inputs = group_rows(group_id)
        gate_value = jnp.einsum(
            "gcd,dgf->gcf", inputs, gate_block, preferred_element_type=jnp.float32
        )
        up_value = jnp.einsum("gcd,dgf->gcf", inputs, up_block, preferred_element_type=jnp.float32)
        activated = (jax.nn.silu(gate_value) * up_value).astype(jnp.bfloat16)
        result = jnp.einsum(
            "gcf,dgf->gcd", activated, down_block, preferred_element_type=jnp.float32
        )
        weighted = (result * slot_gate).reshape(GROUP * CAP, width_model)
        running = running.at[token_index].add(weighted)
        kept_now = None
        return (running, kept_now)

    moe_running, kept_weights = lax.scan(
        expert_forward, jnp.zeros((row_count + 1, width_model), jnp.float32), group_ids
    )

    def expert_backward(running, packed):
        group_id, kept_now = packed
        weights_now = fetch(group_id)
        gate_block, up_block, down_block = weights_now
        token_index, slot_gate, inputs = group_rows(group_id)
        gate_value = jnp.einsum(
            "gcd,dgf->gcf", inputs, gate_block, preferred_element_type=jnp.float32
        )
        up_value = jnp.einsum("gcd,dgf->gcf", inputs, up_block, preferred_element_type=jnp.float32)
        silu_gate = jax.nn.silu(gate_value)
        activated = (silu_gate * up_value).astype(jnp.bfloat16)
        grad_result = (
            jnp.take(grad_pad, token_index, axis=0)
            .reshape(GROUP, CAP, width_model)
            .astype(jnp.float32)
            * slot_gate
        ).astype(jnp.bfloat16)
        grad_hidden = jnp.einsum(
            "gcd,dgf->gcf", grad_result, down_block, preferred_element_type=jnp.float32
        )
        grad_down = jnp.einsum(
            "gcf,gcd->dgf", activated, grad_result, preferred_element_type=jnp.float32
        )
        sigmoid_gate = jax.nn.sigmoid(gate_value)
        grad_gate = (
            grad_hidden * up_value * sigmoid_gate * (1.0 + gate_value * (1.0 - sigmoid_gate))
        ).astype(jnp.bfloat16)
        grad_up = (grad_hidden * silu_gate).astype(jnp.bfloat16)
        grad_inputs = jnp.einsum(
            "gcf,dgf->gcd", grad_gate, gate_block, preferred_element_type=jnp.float32
        ) + jnp.einsum("gcf,dgf->gcd", grad_up, up_block, preferred_element_type=jnp.float32)
        running = running.at[token_index].add(grad_inputs.reshape(GROUP * CAP, width_model))
        grad_gate_w = jnp.einsum(
            "gcd,gcf->dgf", inputs, grad_gate, preferred_element_type=jnp.float32
        )
        grad_up_w = jnp.einsum("gcd,gcf->dgf", inputs, grad_up, preferred_element_type=jnp.float32)
        shards = (
            lax.psum_scatter(grad_gate_w, "dp", scatter_dimension=0, tiled=True),
            lax.psum_scatter(grad_up_w, "dp", scatter_dimension=0, tiled=True),
            lax.psum_scatter(grad_down, "dp", scatter_dimension=0, tiled=True),
        )
        return (running, shards)

    back_running, grad_shards = lax.scan(
        expert_backward,
        jnp.zeros((row_count + 1, width_model), jnp.float32),
        (group_ids, kept_weights),
    )
    gate_shards, up_shards, down_shards = grad_shards
    gate_out = regroup(gate_shards)
    up_out = regroup(up_shards)
    down_out = regroup(down_shards)
    moe_own = lax.psum_scatter(
        moe_running[:row_count].astype(jnp.bfloat16), "tensor", scatter_dimension=0, tiled=True
    ).astype(jnp.float32)
    output = (residual_state + moe_own).astype(jnp.bfloat16)
    second_norm_gradient = lax.psum_scatter(
        back_running[:row_count].astype(jnp.bfloat16), "tensor", scatter_dimension=0, tiled=True
    ).astype(jnp.float32)
    second_input_gradient, second_weight_slice = rmsnorm_backward(
        second_norm_gradient, second_unit_rows, second_inverse_rms, second_norm_weight
    )
    grad_hidden_state = cotangent + second_input_gradient
    grad_hidden_low = grad_hidden_state.astype(jnp.bfloat16)
    grad_rows = lax.all_gather(grad_hidden_low, "tensor", axis=0, tiled=True)
    grad_mixed = plain_dot(grad_rows, o_full).astype(jnp.bfloat16)
    grad_o = dot_first(grad_rows, mixed_low)
    grad_queries, grad_keys, grad_values = attend_backward(
        queries, keys_rot, values, grad_mixed.reshape(row_count, heads_dev, HD), log_total
    )
    grad_q_low = (
        unrotate(grad_queries, cos_table[:, None, :], sin_table[:, None, :])
        .astype(jnp.bfloat16)
        .reshape(row_count, width)
    )
    grad_k_low = unrotate(grad_keys, cos_table, sin_table).astype(jnp.bfloat16)
    grad_v_low = grad_values.astype(jnp.bfloat16)
    normalized_gradient = (
        dot_last(grad_q_low, q_full) + dot_last(grad_k_low, k_cols) + dot_last(grad_v_low, v_cols)
    )
    first_norm_gradient = lax.psum_scatter(
        normalized_gradient.astype(jnp.bfloat16), "tensor", scatter_dimension=0, tiled=True
    ).astype(jnp.float32)
    first_input_gradient, first_weight_slice = rmsnorm_backward(
        first_norm_gradient, first_unit_rows, first_inverse_rms, first_norm_weight
    )
    tokens_grad = grad_hidden_state + first_input_gradient
    grad_q_w = dot_first(rows_all, grad_q_low)
    kv_blank = jnp.zeros((width_model, k_full.shape[1]), jnp.float32)
    grad_k_w = lax.dynamic_update_slice_in_dim(
        kv_blank, dot_first(rows_all, grad_k_low), kv_head * HD, 1
    )
    grad_v_w = lax.dynamic_update_slice_in_dim(
        kv_blank, dot_first(rows_all, grad_v_low), kv_head * HD, 1
    )
    q_share, k_share, v_share, o_share, gain_one_share, gain_two_share = (
        lax.psum_scatter(grad_q_w, "dp", scatter_dimension=0, tiled=True),
        lax.psum_scatter(grad_k_w, "dp", scatter_dimension=0, tiled=True),
        lax.psum_scatter(grad_v_w, "dp", scatter_dimension=0, tiled=True),
        lax.psum_scatter(grad_o, "dp", scatter_dimension=0, tiled=True),
        lax.psum_scatter(first_weight_slice, "dp", scatter_dimension=0, tiled=True),
        lax.psum_scatter(second_weight_slice, "dp", scatter_dimension=0, tiled=True),
    )
    k_total, v_total, gain_one_total, gain_two_total = (
        lax.psum(k_share.astype(jnp.bfloat16), "tensor").astype(jnp.float32),
        lax.psum(v_share.astype(jnp.bfloat16), "tensor").astype(jnp.float32),
        lax.psum(gain_one_share.astype(jnp.bfloat16), "tensor").astype(jnp.float32),
        lax.psum(gain_two_share.astype(jnp.bfloat16), "tensor").astype(jnp.float32),
    )
    return (
        output,
        tokens_grad,
        gain_one_total,
        q_share,
        k_total,
        v_total,
        o_share,
        gain_two_total,
        gate_out,
        up_out,
        down_out,
    )


def solution(mesh):
    placed = (
        P(("dp", "tensor"), None),
        P("dp", None),
        P("dp", None),
        P("dp"),
        P("dp", "tensor"),
        P("dp", None),
        P("dp", None),
        P("dp", "tensor"),
        P("dp"),
        P("dp", None, "tensor"),
        P("dp", None, "tensor"),
        P("dp", None, "tensor"),
        P(("dp", "tensor"), None),
    )
    return jax.shard_map(
        body,
        mesh=mesh,
        in_specs=placed,
        out_specs=(
            P(("dp", "tensor"), None),
            P(("dp", "tensor"), None),
            P("dp"),
            P("dp", "tensor"),
            P("dp", None),
            P("dp", None),
            P("dp", "tensor"),
            P("dp"),
            P("dp", None, "tensor"),
            P("dp", None, "tensor"),
            P("dp", None, "tensor"),
        ),
        check_vma=False,
    )
```

profile of v0, /device:TPU:0, one launch (start us, length us, event | category | flops | bytes accessed | tf_op | source)
XLA Modules:
  0.0 6201.0 jit_solution(3620577795413322107)
XLA Ops:
  157.0 57.7 reduce-scatter.24.cloned.1.call-done
  284.1 60.4 all-gather.19.cloned.1.call-done
  350.1 3637.4 %while.65 = (s32[]{:T(128)}, f32[1025,1536]{1,0:T(8,128)}, f32[16,192,2,192]{1,3,2,0:T(8,128)}, f32[16,192,2,192]{1,3,2,0:T(8,128)}, f32[16,192,2,192]{1,3,2,0:T...) while((s32[]{:T(128)}, f32[1025,1536]{1,0:T(8,128)}, ...), condition=%wide.region_21.23_spmd, body=%wide.region_16.22_spmd.sunk | while | flops 2425655296 | bytes 135788272 | solution.py:327
  481.9 44.0 reduce-scatter.42.cloned.1.call-done
  708.5 43.8 reduce-scatter.42.cloned.1.call-done
  935.3 44.0 reduce-scatter.42.cloned.1.call-done
  1162.1 44.0 reduce-scatter.42.cloned.1.call-done
  1389.0 44.0 reduce-scatter.42.cloned.1.call-done
  1615.8 44.0 reduce-scatter.42.cloned.1.call-done
  1842.7 43.8 reduce-scatter.42.cloned.1.call-done
  2069.4 43.8 reduce-scatter.42.cloned.1.call-done
  2118.7 40.8 reduce-scatter.40.cloned.1.call-done
  2296.3 43.8 reduce-scatter.42.cloned.1.call-done
  2345.6 40.8 reduce-scatter.40.cloned.1.call-done
  2523.1 44.0 reduce-scatter.42.cloned.1.call-done
  2750.0 44.0 reduce-scatter.42.cloned.1.call-done
  2976.7 44.0 reduce-scatter.42.cloned.1.call-done
  3026.1 40.8 reduce-scatter.40.cloned.1.call-done
  3203.7 44.0 reduce-scatter.42.cloned.1.call-done
  3430.3 44.0 reduce-scatter.42.cloned.1.call-done
  3479.7 40.8 reduce-scatter.40.cloned.1.call-done
  3657.2 44.0 reduce-scatter.42.cloned.1.call-done
  3706.6 40.8 reduce-scatter.40.cloned.1.call-done
  3884.0 44.0 reduce-scatter.42.cloned.1.call-done
  3933.4 40.8 reduce-scatter.40.cloned.1.call-done
  3992.4 60.4 reduce-scatter.28.cloned.1.call-done
  4058.9 63.6 %all-gather.23.cloned.1.call-done = bf16[1024,1536]{1,0:T(8,128)(2,1)} async-done(((bf16[256,1536]{1,0:T(8,128)(2,1)}), bf16[1024,1536]{1,0:T(8,128)(2,1)}) %all-gather.23.cloned.1.call-update) | async-done | bytes 3145744 | tf_op jit(solution)/shard_map/all_gather | solution.py:348
  4127.0 62.9 %while.66 = (s32[]{:T(128)}, f32[1024,128]{1,0:T(8,128)}, f32[1024,128]{1,0:T(8,128)}, f32[2,512,3,128]{3,1,0,2:T(8,128)}, s32[2]{0:T(128)S(1)}, /*index=5*/bf16...) while((s32[]{:T(128)}, f32[1024,128]{1,0:T(8,128)}, ...), condition=%wide.region_26.28_spmd.clone, body=%wide.region_24.27_spmd.clone.sunk | while | flops 2038249984 | bytes 93381664 | solution.py:175
  4283.4 1654.0 %while.64 = (s32[]{:T(128)}, f32[1025,1536]{1,0:T(8,128)}, s32[16]{0:T(128)S(1)}, s32[8192]{0:T(1024)S(1)}, bf16[1025,1536]{1,0:T(8,128)(2,1)S(1)}, /*index=5*/b...) while((s32[]{:T(128)}, f32[1025,1536]{1,0:T(8,128)}, ...), condition=%wide.region_14.16_spmd, body=%wide.region_12.15_spmd.sunk | while | flops 908922880 | bytes 40822144 | solution.py:280
  5986.6 51.2 reduce-scatter.30.cloned.1.call-done
  6104.8 42.7 reduce-scatter.38.cloned.1.call-done
  6147.5 46.4 reduce-scatter.32.cloned.1.call-done
  (1623 shorter events, 4804.8 us)
Async XLA Ops:
  31.7 183.1 %reduce-scatter.24.cloned.1.call-start = ((), (), s32[]{:S(2)}) async-start(), calls=%async_computation.14 | async-start | bytes 3932160 | tf_op jit(solution)/shard_map/reduce_scatter | solution.py:230
  154.3 126.0 %all-gather.21.cloned.1.call-start = ((), (), s32[]{:S(2)}) async-start(), calls=%async_computation.17 | async-start | bytes 3932160 | tf_op jit(solution)/shard_map/all_gather | solution.py:242
  156.7 187.8 %all-gather.19.cloned.1.call-start = ((), (), s32[]{:S(2)}) async-start(), calls=%async_computation.15 | async-start | bytes 3932160 | tf_op jit(solution)/shard_map/all_gather | solution.py:236
  442.2 129.8 %reduce-scatter.40.cloned.1.call-start = ((), (), s32[]{:S(2)}) async-start(), calls=%async_computation.32 | async-start | bytes 2654208 | tf_op jit(solution)/shard_map/while
  668.8 129.7 %reduce-scatter.40.cloned.1.call-start = ((), (), s32[]{:S(2)}) async-start(), calls=%async_computation.32 | async-start | bytes 2654208 | tf_op jit(solution)/shard_map/while
  809.6 123.9 %reduce-scatter.44.cloned.1.call-start = ((), (), s32[]{:S(2)}) async-start(), calls=%async_computation.34 | async-start | bytes 2654208 | tf_op jit(solution)/shard_map/while
  895.4 130.0 %reduce-scatter.40.cloned.1.call-start = ((), (), s32[]{:S(2)}) async-start(), calls=%async_computation.32 | async-start | bytes 2654208 | tf_op jit(solution)/shard_map/while
  1122.1 130.0 %reduce-scatter.40.cloned.1.call-start = ((), (), s32[]{:S(2)}) async-start(), calls=%async_computation.32 | async-start | bytes 2654208 | tf_op jit(solution)/shard_map/while
  1263.2 123.9 %reduce-scatter.44.cloned.1.call-start = ((), (), s32[]{:S(2)}) async-start(), calls=%async_computation.34 | async-start | bytes 2654208 | tf_op jit(solution)/shard_map/while
  1349.0 130.0 %reduce-scatter.40.cloned.1.call-start = ((), (), s32[]{:S(2)}) async-start(), calls=%async_computation.32 | async-start | bytes 2654208 | tf_op jit(solution)/shard_map/while
  1490.1 123.8 %reduce-scatter.44.cloned.1.call-start = ((), (), s32[]{:S(2)}) async-start(), calls=%async_computation.34 | async-start | bytes 2654208 | tf_op jit(solution)/shard_map/while
  1575.9 130.1 %reduce-scatter.40.cloned.1.call-start = ((), (), s32[]{:S(2)}) async-start(), calls=%async_computation.32 | async-start | bytes 2654208 | tf_op jit(solution)/shard_map/while
  1802.9 129.7 %reduce-scatter.40.cloned.1.call-start = ((), (), s32[]{:S(2)}) async-start(), calls=%async_computation.32 | async-start | bytes 2654208 | tf_op jit(solution)/shard_map/while
  1943.7 123.8 %reduce-scatter.44.cloned.1.call-start = ((), (), s32[]{:S(2)}) async-start(), calls=%async_computation.34 | async-start | bytes 2654208 | tf_op jit(solution)/shard_map/while
  2029.5 130.0 %reduce-scatter.40.cloned.1.call-start = ((), (), s32[]{:S(2)}) async-start(), calls=%async_computation.32 | async-start | bytes 2654208 | tf_op jit(solution)/shard_map/while
  2170.6 123.9 %reduce-scatter.44.cloned.1.call-start = ((), (), s32[]{:S(2)}) async-start(), calls=%async_computation.34 | async-start | bytes 2654208 | tf_op jit(solution)/shard_map/while
  2256.5 129.8 %reduce-scatter.40.cloned.1.call-start = ((), (), s32[]{:S(2)}) async-start(), calls=%async_computation.32 | async-start | bytes 2654208 | tf_op jit(solution)/shard_map/while
  2397.5 123.7 %reduce-scatter.44.cloned.1.call-start = ((), (), s32[]{:S(2)}) async-start(), calls=%async_computation.34 | async-start | bytes 2654208 | tf_op jit(solution)/shard_map/while
  2483.3 129.8 %reduce-scatter.40.cloned.1.call-start = ((), (), s32[]{:S(2)}) async-start(), calls=%async_computation.32 | async-start | bytes 2654208 | tf_op jit(solution)/shard_map/while
  2624.3 123.8 %reduce-scatter.44.cloned.1.call-start = ((), (), s32[]{:S(2)}) async-start(), calls=%async_computation.34 | async-start | bytes 2654208 | tf_op jit(solution)/shard_map/while
  2710.2 129.8 %reduce-scatter.40.cloned.1.call-start = ((), (), s32[]{:S(2)}) async-start(), calls=%async_computation.32 | async-start | bytes 2654208 | tf_op jit(solution)/shard_map/while
  2936.9 130.0 %reduce-scatter.40.cloned.1.call-start = ((), (), s32[]{:S(2)}) async-start(), calls=%async_computation.32 | async-start | bytes 2654208 | tf_op jit(solution)/shard_map/while
  3078.0 123.9 %reduce-scatter.44.cloned.1.call-start = ((), (), s32[]{:S(2)}) async-start(), calls=%async_computation.34 | async-start | bytes 2654208 | tf_op jit(solution)/shard_map/while
  3164.0 129.8 %reduce-scatter.40.cloned.1.call-start = ((), (), s32[]{:S(2)}) async-start(), calls=%async_computation.32 | async-start | bytes 2654208 | tf_op jit(solution)/shard_map/while
  3390.6 130.0 %reduce-scatter.40.cloned.1.call-start = ((), (), s32[]{:S(2)}) async-start(), calls=%async_computation.32 | async-start | bytes 2654208 | tf_op jit(solution)/shard_map/while
  3617.3 130.1 %reduce-scatter.40.cloned.1.call-start = ((), (), s32[]{:S(2)}) async-start(), calls=%async_computation.32 | async-start | bytes 2654208 | tf_op jit(solution)/shard_map/while
  3844.2 130.0 %reduce-scatter.40.cloned.1.call-start = ((), (), s32[]{:S(2)}) async-start(), calls=%async_computation.32 | async-start | bytes 2654208 | tf_op jit(solution)/shard_map/while
  3992.3 130.1 %all-gather.23.cloned.1.call-start = ((), (), s32[]{:S(2)}) async-start(), calls=%async_computation.19 | async-start | bytes 3932160 | tf_op jit(solution)/shard_map/all_gather | solution.py:348
  4058.8 177.8 %reduce-scatter.34.cloned.1.call-start = ((), (), s32[]{:S(2)}) async-start(), calls=%async_computation.22 | async-start | bytes 1769472 | tf_op jit(solution)/shard_map/reduce_scatter | solution.py:381
  5945.6 155.0 %reduce-scatter.26.cloned.1.call-start = ((), (), s32[]{:S(2)}) async-start(), calls=%async_computation.16 | async-start | bytes 3932160 | tf_op jit(solution)/shard_map/reduce_scatter | solution.py:336
  5950.6 197.0 %reduce-scatter.38.cloned.1.call-start = ((), (), s32[]{:S(2)}) async-start(), calls=%async_computation.24 | async-start | bytes 2654208 | tf_op jit(solution)/shard_map/reduce_scatter | solution.py:383
  5956.1 237.8 %reduce-scatter.32.cloned.1.call-start = ((), (), s32[]{:S(2)}) async-start(), calls=%async_computation.21 | async-start | bytes 2654208 | tf_op jit(solution)/shard_map/reduce_scatter | solution.py:380
  (296 other events, 10521.2 us)
Sparse Core Ops, SparseCore 0:
  30.3 62.8 all-gather.12
  154.4 60.2 reduce-scatter.23
  216.7 63.5 all-gather.20
  282.3 62.1 all-gather.18
  437.6 42.4 reduce-scatter.43
  529.5 42.4 reduce-scatter.39
  664.2 42.4 reduce-scatter.43
  755.9 42.4 reduce-scatter.39
  890.9 42.4 reduce-scatter.43
  982.8 42.4 reduce-scatter.39
  1117.7 42.4 reduce-scatter.43
  1209.6 42.4 reduce-scatter.39
  1344.6 42.4 reduce-scatter.43
  1436.5 42.4 reduce-scatter.39
  1571.4 42.4 reduce-scatter.43
  1663.5 42.4 reduce-scatter.39
  1798.3 42.4 reduce-scatter.43
  1890.1 42.4 reduce-scatter.39
  2025.0 42.4 reduce-scatter.43
  2117.0 42.4 reduce-scatter.39
  2343.9 42.4 reduce-scatter.39
  2478.7 42.4 reduce-scatter.43
  2705.6 42.4 reduce-scatter.43
  2797.5 42.4 reduce-scatter.39
  3024.4 42.4 reduce-scatter.39
  3251.3 42.4 reduce-scatter.39
  3478.0 42.4 reduce-scatter.39
  3992.5 60.2 reduce-scatter.27
  4058.9 63.5 all-gather.22
  5977.8 59.9 reduce-scatter.29
  6040.2 60.3 reduce-scatter.25
  6104.9 42.5 reduce-scatter.37
  (127 shorter events, 3718.8 us)
where the time goes:
time: 6220 us; the launch traced here: 6200 us
  waiting for transfers between devices  4040 us (65%)
  local copies, waits for them, and re-layouts  846 us (14%)
  matrix products  587 us (9%)
  other arithmetic  559 us (9%)
  blocking collectives  73.5 us (1%)
  loops' own time  68.9 us (1%)
    while x192, waiting for transfers between devices  1590 us
    all_gather x32, waiting for transfers between devices, fetch(): lax.all_gather(down_piece, 'dp', axis=0, tiled=True)  712 us
    all_gather x32, waiting for transfers between devices, fetch(): lax.all_gather(gate_piece, 'dp', axis=0, tiled=True)  640 us
    all_gather x32, waiting for transfers between devices, fetch(): lax.all_gather(up_piece, 'dp', axis=0, tiled=True)  565 us
    while x344, local copies, waits for them, and re-layouts  245 us
    scatter-add x16, other arithmetic, expert_backward(): running.at[token_index].add(grad_inputs.reshape(GROUP * CAP, width_model))  195 us
    scatter-add x16, other arithmetic, expert_forward(): running = running.at[token_index].add(weighted)  195 us
  transfers between devices with their start and end apart: 159, of which 157 were waited for; matrix products, arithmetic and copies ran while one was open for 24% of the time, Pallas kernels for 0%

commit v1 on v0

v1 whole, which is shorter than its diff:
```python
import jax
import jax.numpy as jnp
from jax import lax
from jax.experimental import pallas as pl
from jax.experimental.pallas import tpu as pltpu
from jax.sharding import PartitionSpec as P

KV = 2
HD = 128
EXPERTS = 32
TOPK = 4
SEQ = 1024
BLOCK = 256
CAP = 256
TAIL = 64
CALL_PAIRS = 4

eps = 1e-06
rope_base = 1000000.0
negative = -1e30
bf16 = jnp.bfloat16
f32 = jnp.float32


def nn(a, b):
    return jnp.dot(a, b, preferred_element_type=f32)


def nt(a, b):
    return lax.dot_general(a, b, (((1,), (1,)), ((), ())), preferred_element_type=f32)


def tn(a, b):
    return lax.dot_general(a, b, (((0,), (0,)), ((), ())), preferred_element_type=f32)


def rope_tables(positions):
    half = HD // 2
    frequency = rope_base ** (-(jnp.arange(half).astype(f32) * 2.0 / HD))
    angles = positions.astype(f32)[:, None] * frequency[None, :]
    return jnp.cos(angles), jnp.sin(angles)


def rotate(values, cos_table, sin_table):
    rows = values.shape[0]
    heads = values.reshape(rows, -1, 2, HD // 2)
    a, b = heads[:, :, 0], heads[:, :, 1]
    cos_table, sin_table = cos_table[:, None], sin_table[:, None]
    turned = jnp.stack([a * cos_table - b * sin_table, b * cos_table + a * sin_table], axis=2)
    return turned.reshape(rows, -1)


def rms_pieces(x):
    inverse = lax.rsqrt(jnp.mean(x * x, axis=-1, keepdims=True) + eps)
    return inverse, x * inverse


def rms_backward(grad, unit, inverse, gain):
    u = grad * gain
    back = inverse * (u - unit * jnp.mean(u * unit, axis=-1, keepdims=True))
    return back, jnp.sum(grad * unit, axis=0)


def probabilities(q, k, first_row):
    rows, keys = q.shape[0], k.shape[0]
    scores = nt(q, k) * (HD**-0.5)
    q_block = (first_row + lax.broadcasted_iota(jnp.int32, (rows, keys), 0)) // BLOCK
    k_block = lax.broadcasted_iota(jnp.int32, (rows, keys), 1) // BLOCK
    scores = jnp.where(k_block <= q_block, scores, negative)
    raised = jnp.exp(scores - jnp.max(scores, axis=-1, keepdims=True))
    return raised / jnp.sum(raised, axis=-1, keepdims=True)


def attend_forward(first_row, q, k, v):
    rows, width = q.shape
    heads = width // HD
    shared = heads // KV

    def kernel(first_ref, q_ref, k_ref, v_ref, o_ref):
        p = probabilities(q_ref[...], k_ref[...], first_ref[0]).astype(bf16)
        o_ref[...] = nn(p, v_ref[...]).astype(bf16)

    per_head = pl.BlockSpec((rows, HD), lambda h, f: (0, h))
    per_kv = pl.BlockSpec((k.shape[0], HD), lambda h, f: (0, h // shared))
    return pl.pallas_call(
        kernel,
        grid_spec=pltpu.PrefetchScalarGridSpec(
            num_scalar_prefetch=1,
            grid=(heads,),
            in_specs=[per_head, per_kv, per_kv],
            out_specs=per_head,
        ),
        out_shape=jax.ShapeDtypeStruct((rows, width), bf16),
        compiler_params=pltpu.CompilerParams(vmem_limit_bytes=32 * 2**20),
        cost_estimate=pl.CostEstimate(
            flops=4 * rows * width * k.shape[0],
            bytes_accessed=4 * rows * width,
            transcendentals=rows * heads * k.shape[0],
        ),
        name="attend",
    )(first_row, q, k, v)


def attend_backward(first_row, q, k, v, do):
    rows, width = q.shape
    keys = k.shape[0]
    heads = width // HD
    shared = heads // KV

    def kernel(first_ref, q_ref, k_ref, v_ref, do_ref, dq_ref, dk_ref, dv_ref):
        q_now, k_now, v_now, do_now = q_ref[...], k_ref[...], v_ref[...], do_ref[...]
        p = probabilities(q_now, k_now, first_ref[0])
        dp = nt(do_now, v_now)
        ds = (p * (dp - jnp.sum(p * dp, axis=-1, keepdims=True))).astype(bf16)
        dq_ref[...] = nn(ds, k_now) * (HD**-0.5)
        dk = tn(ds, q_now) * (HD**-0.5)
        dv = tn(p.astype(bf16), do_now)
        head = pl.program_id(0)

        @pl.when(lax.rem(head, shared) == 0)
        def _():
            dk_ref[...] = dk
            dv_ref[...] = dv

        @pl.when(lax.rem(head, shared) != 0)
        def _():
            dk_ref[...] += dk
            dv_ref[...] += dv

    per_head = pl.BlockSpec((rows, HD), lambda h, f: (0, h))
    per_kv = pl.BlockSpec((keys, HD), lambda h, f: (0, h // shared))
    return pl.pallas_call(
        kernel,
        grid_spec=pltpu.PrefetchScalarGridSpec(
            num_scalar_prefetch=1,
            grid=(heads,),
            in_specs=[per_head, per_kv, per_kv, per_head],
            out_specs=[per_head, per_kv, per_kv],
        ),
        out_shape=[
            jax.ShapeDtypeStruct((rows, width), f32),
            jax.ShapeDtypeStruct((keys, KV * HD), f32),
            jax.ShapeDtypeStruct((keys, KV * HD), f32),
        ],
        compiler_params=pltpu.CompilerParams(vmem_limit_bytes=32 * 2**20),
        cost_estimate=pl.CostEstimate(
            flops=10 * rows * width * keys,
            bytes_accessed=8 * rows * width,
            transcendentals=rows * heads * keys,
        ),
        name="attend_back",
    )(first_row, q, k, v, do)


def expert_call(first, rank_cols, rank_rows, weight_rows, x, gy, pieces, sums, out_count):
    rows, width = x.shape
    subs, per_sub = len(pieces), len(pieces[0])
    sub_pairs, height, lanes = pieces[0][0].shape
    pairs = subs * sub_pairs
    blocks = 6
    tile = 2 * width // blocks
    per_out = per_sub // out_count
    flat = [piece for sub in pieces for piece in sub]
    half = lanes // 3

    def kernel(first_ref, rank_c, rank_r, weight_r, x_ref, gy_ref, *rest):
        w_hbm = rest[: len(flat)]
        sums_in = rest[len(flat)]
        grads = rest[len(flat) + 1 : len(flat) + 1 + out_count]
        sums_out = rest[len(flat) + 1 + out_count]
        w_buf, y_buf, pick_buf, sems = rest[len(flat) + 2 + out_count :]
        step = pl.program_id(0)

        def copies(pair, slot, sub):
            return [
                pltpu.make_async_copy(
                    w_hbm[sub * per_sub + k].at[pair - sub * sub_pairs],
                    w_buf.at[slot, pl.ds(k * height, height)],
                    sems.at[slot, k],
                )
                for k in range(per_sub)
            ]

        def start(pair):
            slot = lax.rem(pair, 2)
            for sub in range(subs):

                @pl.when((pair >= sub * sub_pairs) & (pair < (sub + 1) * sub_pairs))
                def _():
                    for copy in copies(pair, slot, sub):
                        copy.start()

        def put(at, value):
            for n in range(out_count):
                for m in range(per_out):
                    row = (m * out_count + n) * height
                    grads[n][m, 0, :, at : at + value.shape[1]] = value[row : row + height]

        @pl.when(step == 0)
        def _():
            start(step)

        @pl.when(step + 1 < pairs)
        def _():
            start(step + 1)

        @pl.when(step < pairs)
        def _():
            slot = lax.rem(step, 2)
            for copy in copies(0, slot, 0):
                copy.wait()
            w = w_buf.at[slot]
            low_half = lax.broadcasted_iota(jnp.int32, (CAP, HD), 1) < TAIL
            tails = []
            for q in range(2):
                e = 2 * step + q
                column = (lax.broadcasted_iota(jnp.int32, (HD, CAP), 0) == first_ref[0] + e).astype(bf16)
                rank = nn(rank_c[...], column)
                slot_of = lax.broadcasted_iota(jnp.int32, (rows, CAP), 1).astype(f32)
                at = pl.ds(pl.multiple_of(e * CAP, CAP), CAP)
                pick_buf[:, at] = (rank == slot_of).astype(bf16)
                hit = lax.broadcasted_iota(jnp.int32, (CAP, rows), 0) == rank_r[q]
                pick = hit.astype(bf16)
                weight = jnp.sum(jnp.where(hit, weight_r[q], 0.0), axis=1, keepdims=True)
                xe = nn(pick, x_ref[...]).astype(bf16)
                deo = (nn(pick, gy_ref[...]) * weight).astype(bf16)
                gate_up = slice(q * half, (q + 1) * half)
                down = slice(2 * half + q * HD, 2 * half + (q + 1) * HD)
                down_tail = slice(2 * half + 2 * HD, lanes)
                gu = nn(xe, w[:, gate_up])
                d0 = nn(deo, w[:, down])
                d1 = nn(deo, w[:, down_tail])
                if q == 1:
                    d1 = pltpu.roll(d1, TAIL, 1)
                tail = gu[:, 2 * HD :]

                def unit(gate, up, dact):
                    sig = jax.nn.sigmoid(gate)
                    silu = gate * sig
                    return silu * up, dact * up * sig * (1.0 + gate * (1.0 - sig)), dact * silu

                a0, dg0, du0 = unit(gu[:, :HD], gu[:, HD : 2 * HD], d0)
                a1, dg1, du1 = unit(tail, pltpu.roll(tail, TAIL, 1), d1)
                a1 = jnp.where(low_half, a1, 0.0)
                if q == 1:
                    a1 = pltpu.roll(a1, TAIL, 1)
                dgu1 = jnp.where(low_half, dg1, pltpu.roll(du1, TAIL, 1))
                a0, a1 = a0.astype(bf16), a1.astype(bf16)
                dgu = jnp.concatenate([dg0.astype(bf16), du0.astype(bf16), dgu1.astype(bf16)], axis=1)
                eo = nt(a0, w[:, down]) + nt(a1, w[:, down_tail])
                y_buf[at, :width] = (eo * weight).astype(bf16)
                y_buf[at, width:] = nt(dgu, w[:, gate_up]).astype(bf16)
                put(q * half, tn(xe, dgu).astype(bf16))
                put(2 * half + q * HD, tn(deo, a0).astype(bf16))
                tails.append((deo, a1))
            put(2 * half + 2 * HD, (tn(*tails[0]) + tn(*tails[1])).astype(bf16))

        @pl.when(step >= pairs)
        def _():
            at = pl.ds(pl.multiple_of((step - pairs) * tile, tile), tile)
            sums_out[...] = sums_in[...] + nn(pick_buf[...], y_buf[:, at])

    def held(step):
        return jnp.minimum(step, pairs - 1)

    def block(step, _):
        return (0, jnp.maximum(step - pairs, 0))

    once = pl.Buffered(1)
    whole = pl.BlockSpec((rows, width), lambda s, f: (0, 0), pipeline_mode=once)
    routes = pl.BlockSpec((2, 1, rows), lambda s, f: (f[0] // 2 + held(s), 0, 0))
    grad_shape = (per_out, pairs, height, lanes)
    return pl.pallas_call(
        kernel,
        grid_spec=pltpu.PrefetchScalarGridSpec(
            num_scalar_prefetch=1,
            grid=(pairs + blocks,),
            in_specs=[
                pl.BlockSpec((rows, HD), lambda s, f: (0, 0), pipeline_mode=once),
                routes,
                routes,
                whole,
                whole,
            ]
            + [pl.BlockSpec(memory_space=pl.ANY)] * len(flat)
            + [pl.BlockSpec((rows, tile), block)],
            out_specs=[
                pl.BlockSpec((per_out, 1, height, lanes), lambda s, f: (0, held(s), 0, 0))
            ]
            * out_count
            + [pl.BlockSpec((rows, tile), block)],
            scratch_shapes=[
                pltpu.VMEM((2, width, lanes), bf16),
                pltpu.VMEM((2 * pairs * CAP, 2 * width), bf16),
                pltpu.VMEM((rows, 2 * pairs * CAP), bf16),
                pltpu.SemaphoreType.DMA((2, per_sub)),
            ],
        ),
        out_shape=[jax.ShapeDtypeStruct(grad_shape, bf16)] * out_count
        + [jax.ShapeDtypeStruct((rows, 2 * width), f32)],
        compiler_params=pltpu.CompilerParams(vmem_limit_bytes=60 * 2**20),
        cost_estimate=pl.CostEstimate(
            flops=pairs * 2 * CAP * width * (4 * rows * 2 + 18 * lanes // 6),
            bytes_accessed=8 * rows * width * 3,
            transcendentals=0,
        ),
        name="experts",
    )(first, rank_cols, rank_rows, weight_rows, x, gy, *flat, sums)


def pack(gate, up, down):
    def pair(a, b):
        return jnp.concatenate([a[..., :HD], b[..., :HD], a[..., HD:], b[..., HD:]], axis=-1)

    gate, up, down = (jnp.transpose(w, (1, 0, 2)) for w in (gate, up, down))
    gate_up = pair(gate, up)
    return jnp.concatenate([gate_up[0::2], gate_up[1::2], pair(down[0::2], down[1::2])], axis=-1)


def unpack(packed):
    n, height, lanes = packed.shape
    third = lanes // 3

    def halves(both):
        tail = third // 2 - HD
        a = jnp.concatenate([both[..., :HD], both[..., 2 * HD : 2 * HD + tail]], axis=-1)
        b = jnp.concatenate([both[..., HD : 2 * HD], both[..., 2 * HD + tail :]], axis=-1)
        return a, b

    def experts(even, odd):
        both = jnp.stack([even, odd], axis=1).reshape(2 * n, height, third // 2)
        return jnp.transpose(both, (1, 0, 2))

    gate0, up0 = halves(packed[..., :third])
    gate1, up1 = halves(packed[..., third : 2 * third])
    down0, down1 = halves(packed[..., 2 * third :])
    return experts(gate0, gate1), experts(up0, up1), experts(down0, down1)


def flip(value, bit):
    count = lax.axis_size("dp")
    return lax.ppermute(value, "dp", [(i, i ^ bit) for i in range(count)])


def relative(values, me):
    rows, width = values.shape
    blocks = values.reshape(rows, 2, 2, 2 * (width // 8))
    for axis, bit in ((1, 4), (2, 2)):
        blocks = jnp.where((me & bit) != 0, jnp.flip(blocks, axis), blocks)
    cut = width // 8
    swapped = jnp.concatenate([blocks[..., cut:], blocks[..., :cut]], axis=-1)
    blocks = jnp.where((me & 1) != 0, swapped, blocks)
    return blocks.reshape(rows, width)


def gather_pieces(own, turn):
    from_x, from_y = flip(own, 2), flip(own, 4)
    diagonal = flip(from_x, 4) if turn % 2 == 0 else flip(from_y, 2)
    even = [own, from_x, from_y, diagonal]
    odd = [flip(piece, 1) for piece in even]
    return [piece for both in zip(even, odd) for piece in both]


def scatter_pieces(even, odd):
    other = flip(odd, 1)
    cut = even.shape[1] // 2
    first, second = slice(0, cut), slice(cut, None)

    def both(m, part):
        return even[m, part].astype(f32) + other[m, part].astype(f32)

    via_x = flip(both(3, first).astype(bf16), 2)
    via_y = flip(both(3, second).astype(bf16), 4)
    x_parts = [flip(both(1, first).astype(bf16), 2), flip((both(1, second) + via_y.astype(f32)).astype(bf16), 2)]
    y_parts = [flip((both(2, first) + via_x.astype(f32)).astype(bf16), 4), flip(both(2, second).astype(bf16), 4)]
    return jnp.concatenate(
        [
            both(0, part) + x_parts[i].astype(f32) + y_parts[i].astype(f32)
            for i, part in enumerate((first, second))
        ],
        axis=0,
    )


def body(
    tokens,
    expert_ids,
    route_weights,
    attn_gain,
    q_weight,
    k_weight,
    v_weight,
    o_weight,
    moe_gain,
    gate_weight,
    up_weight,
    down_weight,
    cotangent,
):
    members = lax.axis_size("tensor")
    member = lax.axis_index("tensor")
    devices = lax.axis_size("dp")
    me = lax.axis_index("dp")
    own_rows, width = tokens.shape
    rows = own_rows * members
    by_bits = devices == 8
    pairs = EXPERTS // 2
    calls = pairs // CALL_PAIRS
    sub_pairs = CALL_PAIRS // 2

    packed = [
        pack(*(w[:, 2 * sub_pairs * i : 2 * sub_pairs * (i + 1)] for w in (gate_weight, up_weight, down_weight)))
        for i in range(2 * calls)
    ]
    if by_bits:
        gathered = [gather_pieces(own, i) for i, own in enumerate(packed)]
    else:
        gathered = [[lax.all_gather(own, "dp", axis=1, tiled=True)] for own in packed]

    gain_one = lax.all_gather(attn_gain, "dp", axis=0, tiled=True).astype(f32)
    gain_two = lax.all_gather(moe_gain, "dp", axis=0, tiled=True).astype(f32)
    kv_full = lax.all_gather(jnp.concatenate([k_weight, v_weight], axis=1), "dp", axis=0, tiled=True)
    q_full = lax.all_gather(lax.all_gather(q_weight, "dp", axis=0, tiled=True), "tensor", axis=0)
    o_full = lax.all_gather(lax.all_gather(o_weight, "dp", axis=0, tiled=True), "tensor", axis=0)
    kv_width = k_weight.shape[1]

    lanes = jnp.arange(EXPERTS, dtype=jnp.int32)
    named = expert_ids[:, :, None] == lanes
    member_of = jnp.any(named, axis=1)
    weight_of = jnp.sum(jnp.where(named, route_weights[:, :, None], 0.0), axis=1)
    earlier = jnp.arange(rows)[:, None] > jnp.arange(rows)[None, :]
    rank = jnp.where(member_of, nn(earlier.astype(bf16), member_of.astype(bf16)), -1.0)
    rank_cols = jnp.pad(rank, ((0, 0), (0, HD - EXPERTS)), constant_values=-1.0).astype(bf16)
    rank_rows = rank.T.astype(jnp.int32).reshape(EXPERTS, 1, rows)
    weight_rows = weight_of.T.reshape(EXPERTS, 1, rows)

    grad_low = cotangent.astype(bf16)
    if by_bits:
        grad_low = relative(grad_low, me)
    grad_all = lax.all_gather(grad_low, "tensor", axis=0, tiled=True)

    x = tokens.astype(f32)
    inverse_one, unit_one = rms_pieces(x)
    normed_one = (unit_one * gain_one).astype(bf16)
    first_row = (member * own_rows).reshape(1)
    cos_table, sin_table = rope_tables(member * own_rows + jnp.arange(own_rows, dtype=jnp.int32))
    kv_own = nn(normed_one, kv_full)
    kv_own = jnp.concatenate(
        [rotate(kv_own[:, :kv_width], cos_table, sin_table), kv_own[:, kv_width:]], axis=1
    ).astype(bf16)
    kv_all = lax.all_gather(kv_own, "tensor", axis=0, tiled=True)
    keys, values = kv_all[:, :kv_width], kv_all[:, kv_width:]
    queries = jnp.concatenate([nn(normed_one, q_full[t]) for t in range(members)], axis=1)
    queries = rotate(queries, cos_table, sin_table).astype(bf16)
    mixed = attend_forward(first_row, queries, keys, values)
    part = width // members
    branch = sum(nt(mixed[:, t * part : (t + 1) * part], o_full[t]) for t in range(members))
    hidden = x + branch
    inverse_two, unit_two = rms_pieces(hidden)
    normed_two = (unit_two * gain_two).astype(bf16)
    if by_bits:
        normed_two = relative(normed_two, me)
    rows_all = lax.all_gather(normed_two, "tensor", axis=0, tiled=True)

    sums = jnp.zeros((rows, 2 * width), f32)
    shares = []
    for call in range(calls):
        *grads, sums = expert_call(
            jnp.full((1,), 2 * CALL_PAIRS * call, jnp.int32),
            rank_cols,
            rank_rows,
            weight_rows,
            rows_all,
            grad_all,
            gathered[2 * call : 2 * call + 2],
            sums,
            2 if by_bits else 1,
        )
        if by_bits:
            shares.append(unpack(scatter_pieces(*grads)))
        else:
            shares.append(
                unpack(lax.psum_scatter(grads[0][0], "dp", scatter_dimension=1, tiled=True).astype(f32))
            )
    gate_out, up_out, down_out = (jnp.concatenate(parts, axis=1) for parts in zip(*shares))

    low_sums = sums.astype(bf16)
    normed_grad = lax.psum_scatter(low_sums[:, width:], "tensor", scatter_dimension=0, tiled=True).astype(f32)
    moe_own = lax.psum_scatter(low_sums[:, :width], "tensor", scatter_dimension=0, tiled=True).astype(f32)
    if by_bits:
        normed_grad, moe_own = relative(normed_grad, me), relative(moe_own, me)
    output = (hidden + moe_own).astype(bf16)

    back_two, gain_two_part = rms_backward(normed_grad, unit_two, inverse_two, gain_two)
    hidden_grad = cotangent + back_two
    hidden_low = hidden_grad.astype(bf16)
    mixed_grad = jnp.concatenate([nn(hidden_low, o_full[t]) for t in range(members)], axis=1).astype(bf16)
    o_part = jnp.stack([tn(hidden_low, mixed[:, t * part : (t + 1) * part]) for t in range(members)])
    dq, dk, dv = attend_backward(first_row, queries, keys, values, mixed_grad)
    kv_grad = lax.psum_scatter(
        jnp.concatenate([dk, dv], axis=1).astype(bf16), "tensor", scatter_dimension=0, tiled=True
    ).astype(f32)
    dq_low = rotate(dq, cos_table, -sin_table).astype(bf16)
    kv_low = jnp.concatenate(
        [rotate(kv_grad[:, :kv_width], cos_table, -sin_table), kv_grad[:, kv_width:]], axis=1
    ).astype(bf16)
    normed_one_grad = nt(kv_low, kv_full) + sum(
        nt(dq_low[:, t * part : (t + 1) * part], q_full[t]) for t in range(members)
    )
    back_one, gain_one_part = rms_backward(normed_one_grad, unit_one, inverse_one, gain_one)
    tokens_grad = hidden_grad + back_one
    q_part = jnp.stack([tn(normed_one, dq_low[:, t * part : (t + 1) * part]) for t in range(members)])
    kv_part = tn(normed_one, kv_low)

    def shared(values):
        summed = lax.psum_scatter(values.astype(bf16), "tensor", scatter_dimension=0, tiled=False)
        return lax.psum_scatter(summed, "dp", scatter_dimension=0, tiled=True).astype(f32)

    q_grad, o_grad = shared(q_part), shared(o_part)
    small = jnp.concatenate([kv_part, gain_one_part[:, None], gain_two_part[:, None]], axis=1)
    small = lax.psum_scatter(small, "dp", scatter_dimension=0, tiled=True)
    small = lax.psum(small.astype(bf16), "tensor").astype(f32)
    return (
        output,
        tokens_grad,
        small[:, 2 * kv_width],
        q_grad,
        small[:, :kv_width],
        small[:, kv_width : 2 * kv_width],
        o_grad,
        small[:, 2 * kv_width + 1],
        gate_out,
        up_out,
        down_out,
    )


def solution(mesh):
    rows = P(("dp", "tensor"), None)
    experts = P("dp", None, "tensor")
    square = P("dp", "tensor")
    tall = P("dp", None)
    return jax.shard_map(
        body,
        mesh=mesh,
        in_specs=(
            rows, tall, tall, P("dp"), square, tall, tall, square, P("dp"), experts, experts, experts, rows
        ),
        out_specs=(rows, rows, P("dp"), square, tall, tall, square, P("dp"), experts, experts, experts),
        check_vma=False,
    )
```

time: 6220 us -> 1510 us (0.24)
  waiting for transfers between devices: 4040 us -> 751 us
  local copies, waits for them, and re-layouts: 846 us -> 215 us
  matrix products: 587 us -> 37.1 us
  other arithmetic: 559 us -> 135 us
  Pallas kernels: 0 us -> 267 us
  loops' own time: 68.9 us -> 0 us
    all_gather x99 -> x5, waiting for transfers between devices: 2080 us -> 148 us  [the longest x1 71.6 us: body(): lax.all_gather(lax.all_gather(q_weight, 'dp', axis=0, tiled=True), 'tenso...]
    while x192 -> x0, waiting for transfers between devices: 1590 us -> none
    dot_general x186 -> x28, matrix products: 587 us -> 37.1 us  [the longest x9 16.1 us: nt(): lax.dot_general(a, b, (((1,), (1,)), ((), ())), preferred_element_type=f32)]
    scatter-add x32 -> x0, other arithmetic: 391 us -> none  [the longest x16 195 us: expert_backward(): running.at[token_index].add(grad_inputs.reshape(GROUP * CAP, width_model))]
    ppermute x0 -> x84, waiting for transfers between devices: none -> 379 us  [flip(): return lax.ppermute(value, 'dp', [(i, i ^ bit) for i in range(count)])]
    pallas_call x0 -> x6, Pallas kernels: none -> 267 us  [the longest x4 239 us: expert_call(): pl.pallas_call(kernel, grid_spec=pltpu.PrefetchScalarGridSpec(num_scalar_...]
    while x347 -> x0, local copies, waits for them, and re-layouts: 247 us -> none
    dynamic_slice x180 -> x0, local copies, waits for them, and re-layouts: 218 us -> none  [the longest x48 65 us: fetch(): lax.dynamic_slice_in_dim(down_weight, group_id * GROUP, GROUP, 1)]
  transfers between devices with their start and end apart: 159 -> 101, of which waited for: 157 -> 43; matrix products, arithmetic and copies ran while one was open for 24% -> 20% of each run, Pallas kernels for 0% -> 13%
where the time goes in v1:
time: 1510 us; the launch traced here: 1500 us
  waiting for transfers between devices  751 us (50%)
  Pallas kernels  267 us (18%)
  local copies, waits for them, and re-layouts  215 us (14%)
  other arithmetic  135 us (9%)
  starting transfers between devices  65.9 us (4%)
  matrix products  37.1 us (2%)
  between operations  17.2 us (1%)
  blocking collectives  15.5 us (1%)
    ppermute x84, waiting for transfers between devices, flip(): return lax.ppermute(value, 'dp', [(i, i ^ bit) for i in range(count)])  379 us
    pallas_call x4, Pallas kernels, expert_call(): pl.pallas_call(kernel, grid_spec=pltpu.PrefetchScalarGridSpec(num_scalar_...  239 us
    all_gather x1, waiting for transfers between devices, body(): lax.all_gather(lax.all_gather(q_weight, 'dp', axis=0, tiled=True), 'tenso...  71.6 us
    all_gather x1, waiting for transfers between devices, body(): lax.all_gather(lax.all_gather(o_weight, 'dp', axis=0, tiled=True), 'tenso...  69.6 us
    ppermute x84, starting transfers between devices, flip(): return lax.ppermute(value, 'dp', [(i, i ^ bit) for i in range(count)])  64.6 us
    reduce_scatter x1, waiting for transfers between devices, body(): lax.psum_scatter(low_sums[:, :width], 'tensor', scatter_dimension=0, tile...  57.3 us
    unnamed x285, local copies, waits for them, and re-layouts  56.2 us
    reduce_scatter x2, waiting for transfers between devices, shared(): lax.psum_scatter(summed, 'dp', scatter_dimension=0, tiled=True).astype(f32)  54.4 us
  transfers between devices with their start and end apart: 101, of which 43 were waited for; matrix products, arithmetic and copies ran while one was open for 20% of the time, Pallas kernels for 13%

profile of v1, /device:TPU:0, one launch (start us, length us, event | category | flops | bytes accessed | tf_op | source)
XLA Modules:
  0.0 1503.5 jit_solution(17470447693675959398)
XLA Ops:
  14.1 15.5 %all-reduce.3 = (bf16[1536]{0:T(1024)(128)(2,1)S(1)}, bf16[1536]{0:T(1024)(128)(2,1)S(1)}) all-reduce(bf16[1536]{0:T(1024)(128)(2,1)S(1)} %dynamic-update-slice, bf16[1536]{0:T(1024)(128)(2,1)S(1)} %dynamic-update-slice.1), channel_id=1, replica_groups=mesh['dp'=8,'tensor'=4] {'dp'}, use_global_device_ids=true, to_apply=%add.1 | all-reduce | flops 3072 | bytes 12288
  42.4 22.8 %all-gather.11.cloned.1.call-done = bf16[1536,384]{1,0:T(8,128)(2,1)} async-done(((bf16[192,384]{1,0:T(8,128)(2,1)}), bf16[1536,384]{1,0:T(8,128)(2,1)}) %all-gather.11.cloned.1.call-update) | async-done | bytes 1179664 | tf_op jit(solution)/shard_map/all_gather | solution.py:423
  65.2 25.9 %all-gather.17.cloned.1.call-done = bf16[1536,384]{1,0:T(8,128)(2,1)} async-done(((bf16[192,384]{1,0:T(8,128)(2,1)}), bf16[1536,384]{1,0:T(8,128)(2,1)}) %all-gather.17.cloned.1.call-update) | async-done | bytes 1179664 | tf_op jit(solution)/shard_map/all_gather | solution.py:424
  139.3 71.6 %all-gather.23.cloned.1.call-done = bf16[6144,384]{1,0:T(8,128)(2,1)} async-done(((bf16[1536,384]{1,0:T(8,128)(2,1)}), bf16[6144,384]{1,0:T(8,128)(2,1)}) %all-gather.23.cloned.1.call-update) | async-done | bytes 4718608 | tf_op jit(solution)/shard_map/all_gather | solution.py:423
  230.6 69.6 %all-gather.25.cloned.1.call-done = bf16[6144,384]{1,0:T(8,128)(2,1)} async-done(((bf16[1536,384]{1,0:T(8,128)(2,1)}), bf16[6144,384]{1,0:T(8,128)(2,1)}) %all-gather.25.cloned.1.call-update) | async-done | bytes 4718608 | tf_op jit(solution)/shard_map/all_gather | solution.py:424
  311.0 16.7 %rev.31 = bf16[256,2,2,384]{3,2,1,0:T(2,128)(2,1)S(1)} reverse(bf16[256,2,2,384]{3,2,1,0:T(2,128)(2,1)S(1)} %get-tuple-element.276), dimensions={2} | reverse | bytes 1572864 | tf_op jit(solution)/shard_map/jit(_flip)/rev | solution.py:349
  388.3 19.5 %collective-permute-done.29.rest_2_ = bf16[2,192,1152]{2,1,0:T(8,128)(2,1)} collective-permute-done((bf16[2,192,1152]{2,1,0:T(8,128)(2,1)}, bf16[2,192,1152]{2,1,0:T(8,128)(2,1)}, u32[]{:S(2)}, u32[]{:S(2)}) %collective-permute-start.29) | collective-permute-done | bytes 884768 | tf_op jit(solution)/shard_map/ppermute | solution.py:342
  430.7 17.2 %collective-permute-done.15.rest_2_ = bf16[2,192,1152]{2,1,0:T(8,128)(2,1)} collective-permute-done((bf16[2,192,1152]{2,1,0:T(8,128)(2,1)}, bf16[2,192,1152]{2,1,0:T(8,128)(2,1)}, u32[]{:S(2)}, u32[]{:S(2)}) %collective-permute-start.15) | collective-permute-done | bytes 884768 | tf_op jit(solution)/shard_map/ppermute | solution.py:342
  452.0 18.5 %collective-permute-done.10.rest_12_ = bf16[2,192,1152]{2,1,0:T(8,128)(2,1)S(1)} collective-permute-done((bf16[2,192,1152]{2,1,0:T(8,128)(2,1)S(1)}, bf16[2,192,1152]{2,1,0:T(8,128)(2,1)S(1)}, u32[]{:S(2)}, u32[]{:S(2)}) %collective-permute-start.10) | collective-permute-done | bytes 884768 | tf_op jit(solution)/shard_map/ppermute | solution.py:342
  472.8 15.5 %collective-permute-done.8.rest_10_ = bf16[2,192,1152]{2,1,0:T(8,128)(2,1)S(1)} collective-permute-done((bf16[2,192,1152]{2,1,0:T(8,128)(2,1)S(1)}, bf16[2,192,1152]{2,1,0:T(8,128)(2,1)S(1)}, u32[]{:S(2)}, u32[]{:S(2)}) %collective-permute-start.8) | collective-permute-done | bytes 884768 | tf_op jit(solution)/shard_map/ppermute | solution.py:342
  490.3 15.1 %collective-permute-done.47.rest_6_ = bf16[2,192,1152]{2,1,0:T(8,128)(2,1)} collective-permute-done((bf16[2,192,1152]{2,1,0:T(8,128)(2,1)}, bf16[2,192,1152]{2,1,0:T(8,128)(2,1)}, u32[]{:S(2)}, u32[]{:S(2)}) %collective-permute-start.47) | collective-permute-done | bytes 884768 | tf_op jit(solution)/shard_map/ppermute | solution.py:342
  509.5 18.2 %collective-permute-done.40.rest_14_ = bf16[2,192,1152]{2,1,0:T(8,128)(2,1)S(1)} collective-permute-done((bf16[2,192,1152]{2,1,0:T(8,128)(2,1)}, bf16[2,192,1152]{2,1,0:T(8,128)(2,1)S(1)}, u32[]{:S(2)}, u32[]{:S(2)}) %collective-permute-start.40) | collective-permute-done | bytes 884768 | tf_op jit(solution)/shard_map/ppermute | solution.py:342
  558.5 59.8 %experts.4 = (bf16[4,4,192,1152]{3,2,1,0:T(8,128)(2,1)}, bf16[4,4,192,1152]{3,2,1,0:T(8,128)(2,1)}, f32[1024,3072]{1,0:T(8,128)}) custom-call(s32[1]{0:T(128)} %constant.50.clone.1.first_ref, bf16[1024,128]{1,0:T(8,128)(2,1)} %pad.5.clone.rank_c, s32[32,1,1024]{2,1,0:T(1,128)} %reshape.350.rank_r, f32[32,1,1024]{2,1,0:T(1,128)} %reshape.351.weight_r, ...), custom_call_target="tpu_custom_call" | custom-call | flops 36641439744 | bytes 37748736 | tf_op jit(solution)/shard_map/experts/pallas_call | solution.py:273
  621.1 59.5 %experts.5 = (bf16[4,4,192,1152]{3,2,1,0:T(8,128)(2,1)}, bf16[4,4,192,1152]{3,2,1,0:T(8,128)(2,1)}, f32[1024,3072]{1,0:T(8,128)}) custom-call(s32[1]{0:T(128)} %constant.49.clone.1.first_ref, bf16[1024,128]{1,0:T(8,128)(2,1)} %pad.5.clone.rank_c, s32[32,1,1024]{2,1,0:T(1,128)} %reshape.350.rank_r, f32[32,1,1024]{2,1,0:T(1,128)} %reshape.351.weight_r, ...), custom_call_target="tpu_custom_call" | custom-call | flops 36641439744 | bytes 37748736 | tf_op jit(solution)/shard_map/experts/pallas_call | solution.py:273
  681.8 59.5 %experts.6 = (bf16[4,4,192,1152]{3,2,1,0:T(8,128)(2,1)}, bf16[4,4,192,1152]{3,2,1,0:T(8,128)(2,1)}, f32[1024,3072]{1,0:T(8,128)}) custom-call(s32[1]{0:T(128)} %constant.48.clone.1.first_ref, bf16[1024,128]{1,0:T(8,128)(2,1)} %pad.5.clone.rank_c, s32[32,1,1024]{2,1,0:T(1,128)} %reshape.350.rank_r, f32[32,1,1024]{2,1,0:T(1,128)} %reshape.351.weight_r, ...), custom_call_target="tpu_custom_call" | custom-call | flops 36641439744 | bytes 37748736 | tf_op jit(solution)/shard_map/experts/pallas_call | solution.py:273
  742.3 59.7 %experts.7 = (bf16[4,4,192,1152]{3,2,1,0:T(8,128)(2,1)}, bf16[4,4,192,1152]{3,2,1,0:T(8,128)(2,1)}, f32[1024,3072]{1,0:T(8,128)}) custom-call(s32[1]{0:T(128)} %constant.44.clone.1.first_ref, bf16[1024,128]{1,0:T(8,128)(2,1)} %pad.5.clone.rank_c, s32[32,1,1024]{2,1,0:T(1,128)} %reshape.350.rank_r, f32[32,1,1024]{2,1,0:T(1,128)} %reshape.351.weight_r, ...), custom_call_target="tpu_custom_call" | custom-call | flops 36641439744 | bytes 37748736 | tf_op jit(solution)/shard_map/experts/pallas_call | solution.py:273
  816.9 57.3 %reduce-scatter.11.cloned.1.call-done = bf16[256,1536]{1,0:T(8,128)(2,1)} async-done(((bf16[1024,1536]{1,0:T(8,128)(2,1)}), bf16[256,1536]{1,0:T(8,128)(2,1)}) %reduce-scatter.11.cloned.1.call-update) | async-done | bytes 786448 | tf_op jit(solution)/shard_map/reduce_scatter | solution.py:489
  893.5 43.8 %reduce-scatter.13.cloned.1.call-done = bf16[256,1536]{1,0:T(8,128)(2,1)} async-done(((bf16[1024,1536]{1,0:T(8,128)(2,1)}), bf16[256,1536]{1,0:T(8,128)(2,1)}) %reduce-scatter.13.cloned.1.call-update) | async-done | bytes 786448 | tf_op jit(solution)/shard_map/reduce_scatter | solution.py:488
  972.0 17.8 %attend_back.1 = (f32[256,1536]{1,0:T(8,128)S(1)}, f32[1024,256]{1,0:T(8,128)S(1)}, f32[1024,256]{1,0:T(8,128)S(1)}) custom-call(s32[1]{0:T(128)} %bitcast.first_ref, bf16[256,1536]{1,0:T(8,128)(2,1)S(1)} %copy-done.3, bf16[1024,256]{1,0:T(8,128)(2,1)S(1)} %get-tuple-element.197.k_ref, bf16[1024,256]{1,0:T(8,128)(2,1)S(1)} %get-tuple-element.196.v_ref, ...), custom_call_target="tpu_custom_call" | custom-call | flops 4026531840 | bytes 3145728 | tf_op jit(solution)/shard_map/attend_back/pallas_call | solution.py:132
  1001.6 18.1 %reduce-scatter.15.cloned.1.call-done = bf16[256,512]{1,0:T(8,128)(2,1)} async-done(((bf16[1024,512]{1,0:T(8,128)(2,1)}), bf16[256,512]{1,0:T(8,128)(2,1)}) %reduce-scatter.15.cloned.1.call-update) | async-done | bytes 262160 | tf_op jit(solution)/shard_map/reduce_scatter | solution.py:500
  1094.3 40.6 %collective-permute-done.67 = bf16[2,192,1152]{2,1,0:T(8,128)(2,1)S(1)} collective-permute-done((bf16[2,192,1152]{2,1,0:T(8,128)(2,1)S(1)}, bf16[2,192,1152]{2,1,0:T(8,128)(2,1)S(1)}, u32[]{:S(2)}, u32[]{:S(2)}) %collective-permute-start.67) | collective-permute-done | bytes 884768 | tf_op jit(solution)/shard_map/ppermute | solution.py:342
  1138.1 15.7 %collective-permute-done.74 = bf16[2,192,1152]{2,1,0:T(8,128)(2,1)S(1)} collective-permute-done((bf16[2,192,1152]{2,1,0:T(8,128)(2,1)S(1)}, bf16[2,192,1152]{2,1,0:T(8,128)(2,1)S(1)}, u32[]{:S(2)}, u32[]{:S(2)}) %collective-permute-start.74) | collective-permute-done | bytes 884768 | tf_op jit(solution)/shard_map/ppermute | solution.py:342
  1158.0 14.8 collective-permute-done.81
  1199.6 14.7 collective-permute-done.72
  1216.1 17.2 %collective-permute-done.68 = bf16[2,192,1152]{2,1,0:T(8,128)(2,1)S(1)} collective-permute-done((bf16[2,192,1152]{2,1,0:T(8,128)(2,1)S(1)}, bf16[2,192,1152]{2,1,0:T(8,128)(2,1)S(1)}, u32[]{:S(2)}, u32[]{:S(2)}) %collective-permute-start.68) | collective-permute-done | bytes 884768 | tf_op jit(solution)/shard_map/ppermute | solution.py:342
  1237.6 14.7 collective-permute-done.75
  1257.4 13.8 collective-permute-done.79
  1273.3 16.9 %collective-permute-done.82 = bf16[2,192,1152]{2,1,0:T(8,128)(2,1)S(1)} collective-permute-done((bf16[2,192,1152]{2,1,0:T(8,128)(2,1)}, bf16[2,192,1152]{2,1,0:T(8,128)(2,1)S(1)}, u32[]{:S(2)}, u32[]{:S(2)}) %collective-permute-start.82) | collective-permute-done | bytes 884768 | tf_op jit(solution)/shard_map/ppermute | solution.py:342
  1294.6 14.6 collective-permute-done.57
  1314.7 13.4 collective-permute-done.64
  1438.8 15.8 %reduce-scatter.23.cloned.1.call-done = bf16[192,384]{1,0:T(8,128)(2,1)} async-done(((bf16[1536,384]{1,0:T(8,128)(2,1)}), bf16[192,384]{1,0:T(8,128)(2,1)}) %reduce-scatter.23.cloned.1.call-update) | async-done | bytes 147472 | tf_op jit(solution)/shard_map/reduce_scatter | solution.py:517
  1456.3 38.6 %reduce-scatter.19.cloned.1.call-done = bf16[192,384]{1,0:T(8,128)(2,1)} async-done(((bf16[1536,384]{1,0:T(8,128)(2,1)}), bf16[192,384]{1,0:T(8,128)(2,1)}) %reduce-scatter.19.cloned.1.call-update) | async-done | bytes 147472 | tf_op jit(solution)/shard_map/reduce_scatter | solution.py:517
  (782 shorter events, 553.9 us)
Async XLA Ops:
  9.7 81.4 %all-gather.17.cloned.1.call-start = ((), (), s32[]{:S(2)}) async-start(), calls=%async_computation.11 | async-start | bytes 1327104 | tf_op jit(solution)/shard_map/all_gather | solution.py:424
  10.4 127.6 %all-gather.15.cloned.1.call-start = ((), (), s32[]{:S(2)}) async-start(), calls=%async_computation.10 | async-start | bytes 1310720 | tf_op jit(solution)/shard_map/all_gather | solution.py:451
  42.3 168.5 %all-gather.23.cloned.1.call-start = ((), (), s32[]{:S(2)}) async-start(), calls=%async_computation.22 | async-start | bytes 5898240 | tf_op jit(solution)/shard_map/all_gather | solution.py:423
  65.2 235.0 %all-gather.25.cloned.1.call-start = ((), (), s32[]{:S(2)}) async-start(), calls=%async_computation.23 | async-start | bytes 5898240 | tf_op jit(solution)/shard_map/all_gather | solution.py:424
  91.2 461.2 %all-gather.21.cloned.1.call-start = ((), (), s32[]{:S(2)}) async-start(), calls=%async_computation.13 | async-start | bytes 3932160 | tf_op jit(solution)/shard_map/all_gather | solution.py:440
  109.7 227.4 %collective-permute-start.43 = (bf16[2,192,1152]{2,1,0:T(8,128)(2,1)}, bf16[2,192,1152]{2,1,0:T(8,128)(2,1)}, u32[]{:S(2)}, u32[]{:S(2)}) collective-permute-start(bf16[2,192,1152]{2,1,0:T(8,128)(2,1)} %concatenate.196.rest_0_), channel_id=1, source_target_pairs={{0,8},{4,12},{8,0},{12,4},{16,24},{20,28},{24,16},{28,20},{1,9},{5... | collective-permute-start | bytes 2654216 | tf_op jit(solution)/shard_map/ppermute | solution.py:342
  111.2 255.9 %collective-permute-start.45 = (bf16[2,192,1152]{2,1,0:T(8,128)(2,1)}, bf16[2,192,1152]{2,1,0:T(8,128)(2,1)}, u32[]{:S(2)}, u32[]{:S(2)}) collective-permute-start(bf16[2,192,1152]{2,1,0:T(8,128)(2,1)} %concatenate.196.rest_0_), channel_id=1, source_target_pairs={{0,16},{4,20},{8,24},{12,28},{16,0},{20,4},{24,8},{28,12},{1,17},{... | collective-permute-start | bytes 2654216 | tf_op jit(solution)/shard_map/ppermute | solution.py:342
  121.2 244.3 %collective-permute-start.52 = (bf16[2,192,1152]{2,1,0:T(8,128)(2,1)}, bf16[2,192,1152]{2,1,0:T(8,128)(2,1)}, u32[]{:S(2)}, u32[]{:S(2)}) collective-permute-start(bf16[2,192,1152]{2,1,0:T(8,128)(2,1)} %concatenate.198.rest_8_), channel_id=1, source_target_pairs={{0,16},{4,20},{8,24},{12,28},{16,0},{20,4},{24,8},{28,12},{1,17},{... | collective-permute-start | bytes 2654216 | tf_op jit(solution)/shard_map/ppermute | solution.py:342
  122.7 245.8 %collective-permute-start.50 = (bf16[2,192,1152]{2,1,0:T(8,128)(2,1)}, bf16[2,192,1152]{2,1,0:T(8,128)(2,1)}, u32[]{:S(2)}, u32[]{:S(2)}) collective-permute-start(bf16[2,192,1152]{2,1,0:T(8,128)(2,1)} %concatenate.198.rest_8_), channel_id=1, source_target_pairs={{0,8},{4,12},{8,0},{12,4},{16,24},{20,28},{24,16},{28,20},{1,9},{5... | collective-permute-start | bytes 2654216 | tf_op jit(solution)/shard_map/ppermute | solution.py:342
  123.3 245.8 %collective-permute-start.42 = (bf16[2,192,1152]{2,1,0:T(8,128)(2,1)}, bf16[2,192,1152]{2,1,0:T(8,128)(2,1)}, u32[]{:S(2)}, u32[]{:S(2)}) collective-permute-start(bf16[2,192,1152]{2,1,0:T(8,128)(2,1)} %concatenate.196.rest_0_), channel_id=1, source_target_pairs={{0,4},{4,0},{8,12},{12,8},{16,20},{20,16},{24,28},{28,24},{1,5},{5... | collective-permute-start | bytes 2654216 | tf_op jit(solution)/shard_map/ppermute | solution.py:342
  332.9 219.5 %all-gather.19.cloned.1.call-start = ((), (), s32[]{:S(2)}) async-start(), calls=%async_computation.12 | async-start | bytes 3932160 | tf_op jit(solution)/shard_map/all_gather | solution.py:463
  416.1 458.1 %reduce-scatter.11.cloned.1.call-start = ((), (), s32[]{:S(2)}) async-start(), calls=%async_computation.14 | async-start | bytes 3932160 | tf_op jit(solution)/shard_map/reduce_scatter | solution.py:489
  550.0 68.3 %collective-permute-start.16 = (bf16[2,192,1152]{2,1,0:T(8,128)(2,1)}, bf16[2,192,1152]{2,1,0:T(8,128)(2,1)}, u32[]{:S(2)}, u32[]{:S(2)}) collective-permute-start(bf16[2,192,1152]{2,1,0:T(8,128)(2,1)} %collective-permute-done.15.rest_2_), channel_id=1, source_target_pairs={{0,4},{4,0},{8,12},{12,8},{16,20},{20,16},{24,28},{28,24},{1,5},{5... | collective-permute-start | bytes 2654216 | tf_op jit(solution)/shard_map/ppermute | solution.py:342
  551.4 67.6 %collective-permute-start.23 = (bf16[2,192,1152]{2,1,0:T(8,128)(2,1)}, bf16[2,192,1152]{2,1,0:T(8,128)(2,1)}, u32[]{:S(2)}, u32[]{:S(2)}) collective-permute-start(bf16[2,192,1152]{2,1,0:T(8,128)(2,1)} %collective-permute-done.22.rest_10_), channel_id=1, source_target_pairs={{0,4},{4,0},{8,12},{12,8},{16,20},{20,16},{24,28},{28,24},{1,5},{5... | collective-permute-start | bytes 2654216 | tf_op jit(solution)/shard_map/ppermute | solution.py:342
  551.4 67.6 %collective-permute-start.18 = (bf16[2,192,1152]{2,1,0:T(8,128)(2,1)}, bf16[2,192,1152]{2,1,0:T(8,128)(2,1)}, u32[]{:S(2)}, u32[]{:S(2)}) collective-permute-start(bf16[2,192,1152]{2,1,0:T(8,128)(2,1)} %collective-permute-done.17.rest_4_), channel_id=1, source_target_pairs={{0,4},{4,0},{8,12},{12,8},{16,20},{20,16},{24,28},{28,24},{1,5},{5... | collective-permute-start | bytes 2654216 | tf_op jit(solution)/shard_map/ppermute | solution.py:342
  551.9 68.7 %collective-permute-start.41 = (bf16[2,192,1152]{2,1,0:T(8,128)(2,1)}, bf16[2,192,1152]{2,1,0:T(8,128)(2,1)}, u32[]{:S(2)}, u32[]{:S(2)}) collective-permute-start(bf16[2,192,1152]{2,1,0:T(8,128)(2,1)} %copy-done.121), channel_id=1, source_target_pairs={{0,4},{4,0},{8,12},{12,8},{16,20},{20,16},{24,28},{28,24},{1,5},{5... | collective-permute-start | bytes 2654216 | tf_op jit(solution)/shard_map/ppermute | solution.py:342
  552.0 68.8 %collective-permute-start.34 = (bf16[2,192,1152]{2,1,0:T(8,128)(2,1)}, bf16[2,192,1152]{2,1,0:T(8,128)(2,1)}, u32[]{:S(2)}, u32[]{:S(2)}) collective-permute-start(bf16[2,192,1152]{2,1,0:T(8,128)(2,1)} %copy-done.122), channel_id=1, source_target_pairs={{0,4},{4,0},{8,12},{12,8},{16,20},{20,16},{24,28},{28,24},{1,5},{5... | collective-permute-start | bytes 2654216 | tf_op jit(solution)/shard_map/ppermute | solution.py:342
  816.3 121.0 %reduce-scatter.13.cloned.1.call-start = ((), (), s32[]{:S(2)}) async-start(), calls=%async_computation.15 | async-start | bytes 3932160 | tf_op jit(solution)/shard_map/reduce_scatter | solution.py:488
  816.9 202.9 %reduce-scatter.15.cloned.1.call-start = ((), (), s32[]{:S(2)}) async-start(), calls=%async_computation.16 | async-start | bytes 1310720 | tf_op jit(solution)/shard_map/reduce_scatter | solution.py:500
  991.0 389.1 %reduce-scatter.25.cloned.1.call-start = ((), (), s32[]{:S(2)}) async-start(), calls=%async_computation.24 | async-start | bytes 4423680
  1034.3 358.4 %reduce-scatter.21.cloned.1.call-start = ((), (), s32[]{:S(2)}) async-start(), calls=%async_computation.20 | async-start | bytes 5898240 | tf_op jit(solution)/shard_map/reduce_scatter | solution.py:516
  1040.4 366.9 %reduce-scatter.17.cloned.1.call-start = ((), (), s32[]{:S(2)}) async-start(), calls=%async_computation.18 | async-start | bytes 5898240 | tf_op jit(solution)/shard_map/reduce_scatter | solution.py:516
  1046.9 388.0 %all-reduce.6.cloned.1.call-start = ((), (), s32[]{:S(2)}) async-start(), calls=%async_computation.17 | async-start | bytes 532480 | tf_op jit(solution)/shard_map/psum | solution.py:522
  1060.4 116.8 %collective-permute-start.58 = (bf16[2,192,1152]{2,1,0:T(8,128)(2,1)}, bf16[2,192,1152]{2,1,0:T(8,128)(2,1)S(1)}, u32[]{:S(2)}, u32[]{:S(2)}) collective-permute-start(bf16[2,192,1152]{2,1,0:T(8,128)(2,1)} %get-tuple-element.97), channel_id=1, source_target_pairs={{0,8},{4,12},{8,0},{12,4},{16,24},{20,28},{24,16},{28,20},{1,9},{5... | collective-permute-start | bytes 2654216 | tf_op jit(solution)/shard_map/ppermute | solution.py:342
  1063.7 113.9 %collective-permute-start.62 = (bf16[2,192,1152]{2,1,0:T(8,128)(2,1)S(1)}, bf16[2,192,1152]{2,1,0:T(8,128)(2,1)S(1)}, u32[]{:S(2)}, u32[]{:S(2)}) collective-permute-start(bf16[2,192,1152]{2,1,0:T(8,128)(2,1)S(1)} %get-tuple-element.96), channel_id=1, source_target_pairs={{0,16},{4,20},{8,24},{12,28},{16,0},{20,4},{24,8},{28,12},{1,17},{... | collective-permute-start | bytes 2654216 | tf_op jit(solution)/shard_map/ppermute | solution.py:342
  1084.1 96.7 %collective-permute-start.65 = (bf16[2,192,1152]{2,1,0:T(8,128)(2,1)}, bf16[2,192,1152]{2,1,0:T(8,128)(2,1)S(1)}, u32[]{:S(2)}, u32[]{:S(2)}) collective-permute-start(bf16[2,192,1152]{2,1,0:T(8,128)(2,1)} %get-tuple-element.103), channel_id=1, source_target_pairs={{0,8},{4,12},{8,0},{12,4},{16,24},{20,28},{24,16},{28,20},{1,9},{5... | collective-permute-start | bytes 2654216 | tf_op jit(solution)/shard_map/ppermute | solution.py:342
  1199.3 71.9 %collective-permute-start.79 = (bf16[2,192,1152]{2,1,0:T(8,128)(2,1)}, bf16[2,192,1152]{2,1,0:T(8,128)(2,1)S(1)}, u32[]{:S(2)}, u32[]{:S(2)}) collective-permute-start(bf16[2,192,1152]{2,1,0:T(8,128)(2,1)} %get-tuple-element.115), channel_id=1, source_target_pairs={{0,8},{4,12},{8,0},{12,4},{16,24},{20,28},{24,16},{28,20},{1,9},{5... | collective-permute-start | bytes 2654216 | tf_op jit(solution)/shard_map/ppermute | solution.py:342
  1237.2 72.0 %collective-permute-start.57 = (bf16[2,192,1152]{2,1,0:T(8,128)(2,1)}, bf16[2,192,1152]{2,1,0:T(8,128)(2,1)}, u32[]{:S(2)}, u32[]{:S(2)}) collective-permute-start(bf16[2,192,1152]{2,1,0:T(8,128)(2,1)} %get-tuple-element.98), channel_id=1, source_target_pairs={{0,8},{4,12},{8,0},{12,4},{16,24},{20,28},{24,16},{28,20},{1,9},{5... | collective-permute-start | bytes 2654216 | tf_op jit(solution)/shard_map/ppermute | solution.py:342
  1273.0 74.2 %collective-permute-start.71 = (bf16[2,192,1152]{2,1,0:T(8,128)(2,1)}, bf16[2,192,1152]{2,1,0:T(8,128)(2,1)}, u32[]{:S(2)}, u32[]{:S(2)}) collective-permute-start(bf16[2,192,1152]{2,1,0:T(8,128)(2,1)} %get-tuple-element.110), channel_id=1, source_target_pairs={{0,8},{4,12},{8,0},{12,4},{16,24},{20,28},{24,16},{28,20},{1,9},{5... | collective-permute-start | bytes 2654216 | tf_op jit(solution)/shard_map/ppermute | solution.py:342
  1290.2 74.2 %collective-permute-start.78 = (bf16[2,192,1152]{2,1,0:T(8,128)(2,1)}, bf16[2,192,1152]{2,1,0:T(8,128)(2,1)S(1)}, u32[]{:S(2)}, u32[]{:S(2)}) collective-permute-start(bf16[2,192,1152]{2,1,0:T(8,128)(2,1)} %get-tuple-element.116), channel_id=1, source_target_pairs={{0,8},{4,12},{8,0},{12,4},{16,24},{20,28},{24,16},{28,20},{1,9},{5... | collective-permute-start | bytes 2654216 | tf_op jit(solution)/shard_map/ppermute | solution.py:342
  1382.0 72.7 %reduce-scatter.23.cloned.1.call-start = ((), (), s32[]{:S(2)}) async-start(), calls=%async_computation.21 | async-start | bytes 1327104 | tf_op jit(solution)/shard_map/reduce_scatter | solution.py:517
  1392.7 102.2 %reduce-scatter.19.cloned.1.call-start = ((), (), s32[]{:S(2)}) async-start(), calls=%async_computation.19 | async-start | bytes 1327104 | tf_op jit(solution)/shard_map/reduce_scatter | solution.py:517
  (205 other events, 4558.5 us)
Sparse Core Ops, SparseCore 0:
  10.5 28.6 all-gather.12
  41.1 24.0 all-gather.10
  67.0 24.0 all-gather.16
  92.6 27.9 all-gather.14
  121.9 88.8 all-gather.22
  212.3 87.8 all-gather.24
  333.0 61.9 all-gather.20
  416.3 60.9 all-gather.18
  816.4 57.7 reduce-scatter.10
  876.9 60.2 reduce-scatter.12
  991.1 28.5 reduce-scatter.14
  1034.4 91.0 reduce-scatter.24
  1128.4 85.2 reduce-scatter.20
  1216.4 85.7 reduce-scatter.16
  1382.1 32.6 all-reduce.5
  1417.9 36.7 reduce-scatter.22
  1458.1 36.7 reduce-scatter.18

commit v2 on v1

--- a/solution.py
+++ b/solution.py
@@ -152,34 +152,79 @@
     )(first_row, q, k, v, do)
 
 
-def expert_call(first, rank_cols, rank_rows, weight_rows, x, gy, pieces, sums, out_count):
+def after(value, waits):
+    if not waits:
+        return value
+
+    def kernel(*refs):
+        del refs
+
+    anywhere = pl.BlockSpec(memory_space=pl.ANY)
+    return pl.pallas_call(
+        kernel,
+        in_specs=[anywhere] * (1 + len(waits)),
+        out_specs=anywhere,
+        out_shape=jax.ShapeDtypeStruct(value.shape, value.dtype),
+        input_output_aliases={0: 0},
+        name="after",
+    )(value, *waits)
+
+
+def sibling():
+    me = lax.axis_index("dp")
+    return me + 1 - 2 * lax.rem(me, 2)
+
+
+def expert_call(rank_cols, rank_rows, weight_rows, x, gy, pieces, sums, exchange):
     rows, width = x.shape
-    subs, per_sub = len(pieces), len(pieces[0])
-    sub_pairs, height, lanes = pieces[0][0].shape
-    pairs = subs * sub_pairs
-    blocks = 6
+    subs, count = len(pieces), len(pieces[0])
+    height, lanes = pieces[0][0][0].shape[1:]
+    pairs = rank_rows.shape[0] // 2
+    sub_pairs = pairs // subs
+    blocks = 12
     tile = 2 * width // blocks
-    per_out = per_sub // out_count
-    flat = [piece for sub in pieces for piece in sub]
-    half = lanes // 3
-
-    def kernel(first_ref, rank_c, rank_r, weight_r, x_ref, gy_ref, *rest):
+    flat = []
+    place = []
+    for sub in pieces:
+        place.append([])
+        for array, begin in sub:
+            known = [i for i, other in enumerate(flat) if other is array]
+            if not known:
+                flat.append(array)
+            place[-1].append((known[0] if known else len(flat) - 1, begin))
+    third = lanes // 3
+    stride = 2 if exchange else 1
+
+    def kernel(rank_c, rank_r, weight_r, x_ref, gy_ref, *rest):
         w_hbm = rest[: len(flat)]
-        sums_in = rest[len(flat)]
-        grads = rest[len(flat) + 1 : len(flat) + 1 + out_count]
-        sums_out = rest[len(flat) + 1 + out_count]
-        w_buf, y_buf, pick_buf, sems = rest[len(flat) + 2 + out_count :]
+        rest = rest[len(flat) :]
+        sums_in, rest = rest[0], rest[1:]
+        grad_out, sums_out, w_buf, y_buf, pick_buf, local_sem = rest[:6]
         step = pl.program_id(0)
-
-        def copies(pair, slot, sub):
-            return [
-                pltpu.make_async_copy(
-                    w_hbm[sub * per_sub + k].at[pair - sub * sub_pairs],
-                    w_buf.at[slot, pl.ds(k * height, height)],
-                    sems.at[slot, k],
-                )
-                for k in range(per_sub)
-            ]
+        if exchange:
+            kept, leaving, arriving, push_sem, pull_sem, send_sem, recv_sem, w_free, g_free = rest[6:]
+            other = {"dp": sibling()}
+
+        def weights(pair, slot, sub):
+            found = []
+            for k in range(count):
+                array, begin = place[sub][k]
+                source = w_hbm[array].at[pair - sub * sub_pairs + begin]
+                target = w_buf.at[slot, pl.ds(stride * k * height, height)]
+                found.append(pltpu.make_async_copy(source, target, local_sem.at[slot, k]))
+                if exchange:
+                    target = w_buf.at[slot, pl.ds((stride * k + 1) * height, height)]
+                    found.append(
+                        pltpu.make_async_remote_copy(
+                            src_ref=source,
+                            dst_ref=target,
+                            send_sem=push_sem.at[slot, k],
+                            recv_sem=pull_sem.at[slot, k],
+                            device_id=other,
+                            device_id_type=pl.DeviceIdType.MESH,
+                        )
+                    )
+            return found
 
         def start(pair):
             slot = lax.rem(pair, 2)
@@ -187,18 +232,56 @@
 
                 @pl.when((pair >= sub * sub_pairs) & (pair < (sub + 1) * sub_pairs))
                 def _():
-                    for copy in copies(pair, slot, sub):
+                    for copy in weights(pair, slot, sub):
                         copy.start()
 
-        def put(at, value):
-            for n in range(out_count):
-                for m in range(per_out):
-                    row = (m * out_count + n) * height
-                    grads[n][m, 0, :, at : at + value.shape[1]] = value[row : row + height]
+        def leave(slot):
+            return pltpu.make_async_remote_copy(
+                src_ref=leaving.at[slot],
+                dst_ref=arriving.at[slot],
+                send_sem=send_sem.at[slot],
+                recv_sem=recv_sem.at[slot],
+                device_id=other,
+                device_id_type=pl.DeviceIdType.MESH,
+            )
+
+        def put(at, value, slot):
+            for k in range(count):
+                for parity in range(stride):
+                    row = (stride * k + parity) * height
+                    part = value[row : row + height].astype(bf16)
+                    span = slice(at, at + value.shape[1])
+                    if not exchange:
+                        grad_out[k, 0, :, span] = part
+                    elif parity == 0:
+                        kept[slot, k, :, span] = part
+                    else:
+                        leaving[slot, k, :, span] = part
+
+        def signal(sem):
+            pl.semaphore_signal(sem, inc=1, device_id=other, device_id_type=pl.DeviceIdType.MESH)
+
+        def finish(pair):
+            slot = lax.rem(pair, 2)
+            leave(slot).wait()
+            for k in range(count):
+                both = kept[slot, k].astype(f32) + arriving[slot, k].astype(f32)
+                grad_out[k, 0] = both.astype(bf16)
 
         @pl.when(step == 0)
         def _():
+            if exchange:
+                barrier = pltpu.get_barrier_semaphore()
+                signal(barrier)
+                pl.semaphore_wait(barrier, 1)
             start(step)
+
+        if exchange:
+
+            @pl.when((step >= 1) & (step + 1 < pairs))
+            def _():
+                signal(w_free)
+                pl.semaphore_wait(w_free, 1)
 
         @pl.when(step + 1 < pairs)
         def _():
@@ -207,14 +290,14 @@
         @pl.when(step < pairs)
         def _():
             slot = lax.rem(step, 2)
-            for copy in copies(0, slot, 0):
+            for copy in weights(0, slot, 0):
                 copy.wait()
             w = w_buf.at[slot]
             low_half = lax.broadcasted_iota(jnp.int32, (CAP, HD), 1) < TAIL
             tails = []
             for q in range(2):
                 e = 2 * step + q
-                column = (lax.broadcasted_iota(jnp.int32, (HD, CAP), 0) == first_ref[0] + e).astype(bf16)
+                column = (lax.broadcasted_iota(jnp.int32, (HD, CAP), 0) == e).astype(bf16)
                 rank = nn(rank_c[...], column)
                 slot_of = lax.broadcasted_iota(jnp.int32, (rows, CAP), 1).astype(f32)
                 at = pl.ds(pl.multiple_of(e * CAP, CAP), CAP)
@@ -224,9 +307,9 @@
                 weight = jnp.sum(jnp.where(hit, weight_r[q], 0.0), axis=1, keepdims=True)
                 xe = nn(pick, x_ref[...]).astype(bf16)
                 deo = (nn(pick, gy_ref[...]) * weight).astype(bf16)
-                gate_up = slice(q * half, (q + 1) * half)
-                down = slice(2 * half + q * HD, 2 * half + (q + 1) * HD)
-                down_tail = slice(2 * half + 2 * HD, lanes)
+                gate_up = slice(q * third, (q + 1) * third)
+                down = slice(2 * third + q * HD, 2 * third + (q + 1) * HD)
+                down_tail = slice(2 * third + 2 * HD, lanes)
                 gu = nn(xe, w[:, gate_up])
                 d0 = nn(deo, w[:, down])
                 d1 = nn(deo, w[:, down_tail])
@@ -250,10 +333,28 @@
                 eo = nt(a0, w[:, down]) + nt(a1, w[:, down_tail])
                 y_buf[at, :width] = (eo * weight).astype(bf16)
                 y_buf[at, width:] = nt(dgu, w[:, gate_up]).astype(bf16)
-                put(q * half, tn(xe, dgu).astype(bf16))
-                put(2 * half + q * HD, tn(deo, a0).astype(bf16))
+                put(q * third, tn(xe, dgu), slot)
+                put(2 * third + q * HD, tn(deo, a0), slot)
                 tails.append((deo, a1))
-            put(2 * half + 2 * HD, (tn(*tails[0]) + tn(*tails[1])).astype(bf16))
+            put(2 * third + 2 * HD, tn(*tails[0]) + tn(*tails[1]), slot)
+
+        if exchange:
+
+            @pl.when((step >= 1) & (step <= pairs))
+            def _():
+                finish(step - 1)
+
+            @pl.when((step >= 1) & (step + 1 < pairs))
+            def _():
+                signal(g_free)
+
+            @pl.when((step >= 2) & (step < pairs))
+            def _():
+                pl.semaphore_wait(g_free, 1)
+
+            @pl.when(step < pairs)
+            def _():
+                leave(lax.rem(step, 2)).start()
 
         @pl.when(step >= pairs)
         def _():
@@ -263,49 +364,58 @@
     def held(step):
         return jnp.minimum(step, pairs - 1)
 
-    def block(step, _):
+    def behind(step):
+        return jnp.clip(step - 1, 0, pairs - 1) if exchange else held(step)
+
+    def block(step):
         return (0, jnp.maximum(step - pairs, 0))
 
     once = pl.Buffered(1)
-    whole = pl.BlockSpec((rows, width), lambda s, f: (0, 0), pipeline_mode=once)
-    routes = pl.BlockSpec((2, 1, rows), lambda s, f: (f[0] // 2 + held(s), 0, 0))
-    grad_shape = (per_out, pairs, height, lanes)
+    whole = pl.BlockSpec((rows, width), lambda s: (0, 0), pipeline_mode=once)
+    routes = pl.BlockSpec((2, 1, rows), lambda s: (held(s), 0, 0))
+    anywhere = pl.BlockSpec(memory_space=pl.ANY)
+    dma = pltpu.SemaphoreType.DMA
+    traded = [
+        pltpu.VMEM((2, count, height, lanes), bf16),
+        pltpu.VMEM((2, count, height, lanes), bf16),
+        pltpu.VMEM((2, count, height, lanes), bf16),
+        dma((2, count)),
+        dma((2, count)),
+        dma((2,)),
+        dma((2,)),
+        pltpu.SemaphoreType.REGULAR,
+        pltpu.SemaphoreType.REGULAR,
+    ]
+    remote = dict(collective_id=1, has_side_effects=True) if exchange else {}
     return pl.pallas_call(
         kernel,
-        grid_spec=pltpu.PrefetchScalarGridSpec(
-            num_scalar_prefetch=1,
-            grid=(pairs + blocks,),
-            in_specs=[
-                pl.BlockSpec((rows, HD), lambda s, f: (0, 0), pipeline_mode=once),
-                routes,
-                routes,
-                whole,
-                whole,
-            ]
-            + [pl.BlockSpec(memory_space=pl.ANY)] * len(flat)
-            + [pl.BlockSpec((rows, tile), block)],
-            out_specs=[
-                pl.BlockSpec((per_out, 1, height, lanes), lambda s, f: (0, held(s), 0, 0))
-            ]
-            * out_count
-            + [pl.BlockSpec((rows, tile), block)],
-            scratch_shapes=[
-                pltpu.VMEM((2, width, lanes), bf16),
-                pltpu.VMEM((2 * pairs * CAP, 2 * width), bf16),
-                pltpu.VMEM((rows, 2 * pairs * CAP), bf16),
-                pltpu.SemaphoreType.DMA((2, per_sub)),
-            ],
-        ),
-        out_shape=[jax.ShapeDtypeStruct(grad_shape, bf16)] * out_count
-        + [jax.ShapeDtypeStruct((rows, 2 * width), f32)],
-        compiler_params=pltpu.CompilerParams(vmem_limit_bytes=60 * 2**20),
+        grid=(pairs + blocks,),
+        in_specs=[pl.BlockSpec((rows, HD), lambda s: (0, 0), pipeline_mode=once), routes, routes, whole, whole]
+        + [anywhere] * len(flat)
+        + [pl.BlockSpec((rows, tile), block)],
+        out_specs=[
+            pl.BlockSpec((count, 1, height, lanes), lambda s: (0, behind(s), 0, 0)),
+            pl.BlockSpec((rows, tile), block),
+        ],
+        scratch_shapes=[
+            pltpu.VMEM((2, width, lanes), bf16),
+            pltpu.VMEM((2 * pairs * CAP, 2 * width), bf16),
+            pltpu.VMEM((rows, 2 * pairs * CAP), bf16),
+            dma((2, count)),
+        ]
+        + (traded if exchange else []),
+        out_shape=[
+            jax.ShapeDtypeStruct((count, pairs, height, lanes), bf16),
+            jax.ShapeDtypeStruct((rows, 2 * width), f32),
+        ],
+        compiler_params=pltpu.CompilerParams(vmem_limit_bytes=62 * 10**6, **remote),
         cost_estimate=pl.CostEstimate(
-            flops=pairs * 2 * CAP * width * (4 * rows * 2 + 18 * lanes // 6),
+            flops=pairs * 4 * CAP * width * (4 * rows * 2 + 18 * lanes // 6),
             bytes_accessed=8 * rows * width * 3,
             transcendentals=0,
         ),
         name="experts",
-    )(first, rank_cols, rank_rows, weight_rows, x, gy, *flat, sums)
+    )(rank_cols, rank_rows, weight_rows, x, gy, *flat, sums)
 
 
 def pack(gate, up, down):
@@ -353,33 +463,40 @@
     return blocks.reshape(rows, width)
 
 
-def gather_pieces(own, turn):
-    from_x, from_y = flip(own, 2), flip(own, 4)
-    diagonal = flip(from_x, 4) if turn % 2 == 0 else flip(from_y, 2)
-    even = [own, from_x, from_y, diagonal]
-    odd = [flip(piece, 1) for piece in even]
-    return [piece for both in zip(even, odd) for piece in both]
-
-
-def scatter_pieces(even, odd):
-    other = flip(odd, 1)
-    cut = even.shape[1] // 2
-    first, second = slice(0, cut), slice(cut, None)
-
-    def both(m, part):
-        return even[m, part].astype(f32) + other[m, part].astype(f32)
-
-    via_x = flip(both(3, first).astype(bf16), 2)
-    via_y = flip(both(3, second).astype(bf16), 4)
-    x_parts = [flip(both(1, first).astype(bf16), 2), flip((both(1, second) + via_y.astype(f32)).astype(bf16), 2)]
-    y_parts = [flip((both(2, first) + via_x.astype(f32)).astype(bf16), 4), flip(both(2, second).astype(bf16), 4)]
-    return jnp.concatenate(
-        [
-            both(0, part) + x_parts[i].astype(f32) + y_parts[i].astype(f32)
-            for i, part in enumerate((first, second))
-        ],
-        axis=0,
-    )
+def gather_step(waiting, arrived):
+    to_x = ([arrived[1][half_of(arrived[1])[1]]] if arrived else []) + ([waiting] if waiting is not None else [])
+    to_y = ([arrived[0][half_of(arrived[0])[0]]] if arrived else []) + ([waiting] if waiting is not None else [])
+    return flip(jnp.concatenate(to_x), 2), flip(jnp.concatenate(to_y), 4)
+
+
+def half_of(chunk):
+    cut = chunk.shape[0] // 2
+    return slice(0, cut), slice(cut, None)
+
+
+def scatter_step(chunk, before):
+    to_x, to_y = [], []
+    if before is not None:
+        blocks, via_x, via_y = before
+        first, second = half_of(blocks[0])
+        to_x += [blocks[1, first], add(blocks[1, second], via_y)]
+        to_y += [add(blocks[2, first], via_x), blocks[2, second]]
+    if chunk is not None:
+        first, second = half_of(chunk[0])
+        to_x.append(chunk[3, first])
+        to_y.append(chunk[3, second])
+    return flip(jnp.concatenate(to_x), 2), flip(jnp.concatenate(to_y), 4)
+
+
+def before_of(chunks, moved, call):
+    if call == 0:
+        return None
+    cut = CALL_PAIRS // 2
+    return chunks[call - 1], moved[call - 1][0][-cut:], moved[call - 1][1][-cut:]
+
+
+def add(a, b):
+    return (a.astype(f32) + b.astype(f32)).astype(bf16)
 
 
 def body(
@@ -409,13 +526,26 @@
     sub_pairs = CALL_PAIRS // 2
 
     packed = [
-        pack(*(w[:, 2 * sub_pairs * i : 2 * sub_pairs * (i + 1)] for w in (gate_weight, up_weight, down_weight)))
-        for i in range(2 * calls)
+        pack(*(w[:, 2 * CALL_PAIRS * i : 2 * CALL_PAIRS * (i + 1)] for w in (gate_weight, up_weight, down_weight)))
+        for i in range(calls)
     ]
     if by_bits:
-        gathered = [gather_pieces(own, i) for i, own in enumerate(packed)]
+        steps = [gather_step(packed[0], None)]
+        for i in range(calls):
+            arrived = tuple(got[-CALL_PAIRS:] for got in steps[i])
+            steps.append(gather_step(packed[i + 1] if i + 1 < calls else None, arrived))
+        gathered = []
+        for i in range(calls):
+            from_x, from_y = (got[-CALL_PAIRS:] for got in steps[i])
+            second, first = (got[:sub_pairs] for got in steps[i + 1])
+            gathered.append(
+                [
+                    [(packed[i], 0), (from_x, 0), (from_y, 0), (first, 0)],
+                    [(packed[i], sub_pairs), (from_x, sub_pairs), (from_y, sub_pairs), (second, 0)],
+                ]
+            )
     else:
-        gathered = [[lax.all_gather(own, "dp", axis=1, tiled=True)] for own in packed]
+        gathered = [[[(lax.all_gather(own, "dp", axis=1, tiled=True), 0)]] for own in packed]
 
     gain_one = lax.all_gather(attn_gain, "dp", axis=0, tiled=True).astype(f32)
     gain_two = lax.all_gather(moe_gain, "dp", axis=0, tiled=True).astype(f32)
@@ -430,7 +560,7 @@
     weight_of = jnp.sum(jnp.where(named, route_weights[:, :, None], 0.0), axis=1)
     earlier = jnp.arange(rows)[:, None] > jnp.arange(rows)[None, :]
     rank = jnp.where(member_of, nn(earlier.astype(bf16), member_of.astype(bf16)), -1.0)
-    rank_cols = jnp.pad(rank, ((0, 0), (0, HD - EXPERTS)), constant_values=-1.0).astype(bf16)
+    rank_cols = jnp.pad(rank, ((0, 0), (0, HD)), constant_values=-1.0).astype(bf16)
     rank_rows = rank.T.astype(jnp.int32).reshape(EXPERTS, 1, rows)
     weight_rows = weight_of.T.reshape(EXPERTS, 1, rows)
 
@@ -452,7 +582,7 @@
     keys, values = kv_all[:, :kv_width], kv_all[:, kv_width:]
     queries = jnp.concatenate([nn(normed_one, q_full[t]) for t in range(members)], axis=1)
     queries = rotate(queries, cos_table, sin_table).astype(bf16)
-    mixed = attend_forward(first_row, queries, keys, values)
+    mixed = attend_forward(after(first_row, steps[0] if by_bits else ()), queries, keys, values)
     part = width // members
     branch = sum(nt(mixed[:, t * part : (t + 1) * part], o_full[t]) for t in range(members))
     hidden = x + branch
@@ -463,25 +593,34 @@
     rows_all = lax.all_gather(normed_two, "tensor", axis=0, tiled=True)
 
     sums = jnp.zeros((rows, 2 * width), f32)
-    shares = []
+    chunks, moved = [], []
     for call in range(calls):
-        *grads, sums = expert_call(
-            jnp.full((1,), 2 * CALL_PAIRS * call, jnp.int32),
-            rank_cols,
-            rank_rows,
-            weight_rows,
+        some = slice(2 * CALL_PAIRS * call, 2 * CALL_PAIRS * (call + 1))
+        columns = slice(2 * CALL_PAIRS * call, 2 * CALL_PAIRS * call + HD)
+        grads, sums = expert_call(
+            rank_cols[:, columns],
+            after(rank_rows[some], moved[call - 2] if by_bits and call >= 2 else ()),
+            weight_rows[some],
             rows_all,
             grad_all,
-            gathered[2 * call : 2 * call + 2],
+            gathered[call],
             sums,
-            2 if by_bits else 1,
+            by_bits,
         )
+        chunks.append(grads)
         if by_bits:
-            shares.append(unpack(scatter_pieces(*grads)))
-        else:
-            shares.append(
-                unpack(lax.psum_scatter(grads[0][0], "dp", scatter_dimension=1, tiled=True).astype(f32))
-            )
+            moved.append(scatter_step(grads, before_of(chunks, moved, call)))
+    if by_bits:
+        moved.append(scatter_step(None, before_of(chunks, moved, calls)))
+        shares = []
+        for call in range(calls):
+            from_x, from_y = (got[:CALL_PAIRS].astype(f32) for got in moved[call + 1])
+            shares.append(unpack(chunks[call][0].astype(f32) + from_x + from_y))
+    else:
+        shares = [
+            unpack(lax.psum_scatter(grads[0], "dp", scatter_dimension=1, tiled=True).astype(f32))
+            for grads in chunks
+        ]
     gate_out, up_out, down_out = (jnp.concatenate(parts, axis=1) for parts in zip(*shares))
 
     low_sums = sums.astype(bf16)
@@ -496,7 +635,9 @@
     hidden_low = hidden_grad.astype(bf16)
     mixed_grad = jnp.concatenate([nn(hidden_low, o_full[t]) for t in range(members)], axis=1).astype(bf16)
     o_part = jnp.stack([tn(hidden_low, mixed[:, t * part : (t + 1) * part]) for t in range(members)])
-    dq, dk, dv = attend_backward(first_row, queries, keys, values, mixed_grad)
+    dq, dk, dv = attend_backward(
+        after(first_row, moved[calls - 2] if by_bits else ()), queries, keys, values, mixed_grad
+    )
     kv_grad = lax.psum_scatter(
         jnp.concatenate([dk, dv], axis=1).astype(bf16), "tensor", scatter_dimension=0, tiled=True
     ).astype(f32)

time: 1510 us -> 1350 us (0.89)
  waiting for transfers between devices: 751 us -> 614 us
  starting transfers between devices: 65.9 us -> 26.2 us
  Pallas kernels: 267 us -> 304 us
  other arithmetic: 135 us -> 105 us
    ppermute x84 -> x20, waiting for transfers between devices: 379 us -> 293 us  [flip(): return lax.ppermute(value, 'dp', [(i, i ^ bit) for i in range(count)])]
    reduce_scatter x2, waiting for transfers between devices: 0.01 us -> 78.1 us  [shared(): lax.psum_scatter(values.astype(bf16), 'tensor', scatter_dimension=0, tile...]
    all_gather x1, waiting for transfers between devices: 71.6 us -> 0.01 us  [body(): lax.all_gather(lax.all_gather(q_weight, 'dp', axis=0, tiled=True), 'tenso...]
    all_gather x1, waiting for transfers between devices: 69.6 us -> 22.2 us  [body(): lax.all_gather(lax.all_gather(o_weight, 'dp', axis=0, tiled=True), 'tenso...]
    slice x3 -> x36, local copies, waits for them, and re-layouts: 9.71 us -> 55.5 us  [the longest x4 11.4 us: body(): from_x, from_y = (got[-CALL_PAIRS:] for got in steps[i])]
    reduce_scatter x1, waiting for transfers between devices: 43.8 us -> 0.02 us  [body(): lax.psum_scatter(low_sums[:, width:], 'tensor', scatter_dimension=0, tile...]
    ppermute x84 -> x20, starting transfers between devices: 64.6 us -> 24.2 us  [flip(): return lax.ppermute(value, 'dp', [(i, i ^ bit) for i in range(count)])]
    pallas_call x4 -> x8, Pallas kernels: 239 us -> 275 us  [the longest x4 274 us: expert_call(): pl.pallas_call(kernel, grid=(pairs + blocks,), in_specs=[pl.BlockSpec((ro...]
  transfers between devices with their start and end apart: 101 -> 37, of which waited for: 43 -> 21; matrix products, arithmetic and copies ran while one was open for 20% -> 20% of each run, Pallas kernels for 13% -> 16%
where the time goes in v2:
time: 1350 us; the launch traced here: 1340 us
  waiting for transfers between devices  614 us (45%)
  Pallas kernels  304 us (23%)
  local copies, waits for them, and re-layouts  227 us (17%)
  other arithmetic  105 us (8%)
  matrix products  31.1 us (2%)
  starting transfers between devices  26.2 us (2%)
  between operations  17.1 us (1%)
  blocking collectives  15.5 us (1%)
    ppermute x20, waiting for transfers between devices, flip(): return lax.ppermute(value, 'dp', [(i, i ^ bit) for i in range(count)])  293 us
    pallas_call x4, Pallas kernels, expert_call(): pl.pallas_call(kernel, grid=(pairs + blocks,), in_specs=[pl.BlockSpec((ro...  274 us
    reduce_scatter x2, waiting for transfers between devices, shared(): lax.psum_scatter(values.astype(bf16), 'tensor', scatter_dimension=0, tile...  78.1 us
    reduce_scatter x2, waiting for transfers between devices, shared(): lax.psum_scatter(summed, 'dp', scatter_dimension=0, tiled=True).astype(f32)  74.5 us
    unnamed x158, local copies, waits for them, and re-layouts  43.4 us
    reduce_scatter x1, waiting for transfers between devices, body(): lax.psum_scatter(low_sums[:, :width], 'tensor', scatter_dimension=0, tile...  36.7 us
    all_gather x1, waiting for transfers between devices, body(): rows_all = lax.all_gather(normed_two, 'tensor', axis=0, tiled=True)  30.6 us
    rev x4, local copies, waits for them, and re-layouts, relative(): blocks = jnp.where(me & bit != 0, jnp.flip(blocks, axis), blocks)  27.3 us
  transfers between devices with their start and end apart: 37, of which 21 were waited for; matrix products, arithmetic and copies ran while one was open for 20% of the time, Pallas kernels for 16%

profile of v2, /device:TPU:0, one launch (start us, length us, event | category | flops | bytes accessed | tf_op | source)
XLA Modules:
  0.0 1339.8 jit_solution(12986127169415019171)
XLA Ops:
  14.1 15.5 %all-reduce.3 = (bf16[1536]{0:T(1024)(128)(2,1)S(1)}, bf16[1536]{0:T(1024)(128)(2,1)S(1)}) all-reduce(bf16[1536]{0:T(1024)(128)(2,1)S(1)} %dynamic-update-slice, bf16[1536]{0:T(1024)(128)(2,1)S(1)} %dynamic-update-slice.1), channel_id=1, replica_groups=mesh['dp'=8,'tensor'=4] {'dp'}, use_global_device_ids=true, to_apply=%add.1 | all-reduce | flops 3072 | bytes 12288
  32.0 7.2 all-gather.13.cloned.1.call-done
  42.4 22.8 %all-gather.11.cloned.1.call-done = bf16[1536,384]{1,0:T(8,128)(2,1)} async-done(((bf16[192,384]{1,0:T(8,128)(2,1)}), bf16[1536,384]{1,0:T(8,128)(2,1)}) %all-gather.11.cloned.1.call-update) | async-done | bytes 1179664 | tf_op jit(solution)/shard_map/all_gather | solution.py:553
  88.3 6.0 all-gather.17.cloned.1.call-done
  101.6 25.7 %collective-permute-done.1.refs_2_.rest_2_ = bf16[4,192,1152]{2,1,0:T(8,128)(2,1)} collective-permute-done((bf16[4,192,1152]{2,1,0:T(8,128)(2,1)}, bf16[4,192,1152]{2,1,0:T(8,128)(2,1)}, u32[]{:S(2)}, u32[]{:S(2)}) %collective-permute-start.1) | collective-permute-done | bytes 1769504 | tf_op jit(solution)/shard_map/ppermute | solution.py:452
  147.1 45.1 %collective-permute-done.2 = bf16[6,192,1152]{2,1,0:T(8,128)(2,1)} collective-permute-done((bf16[6,192,1152]{2,1,0:T(8,128)(2,1)}, bf16[6,192,1152]{2,1,0:T(8,128)(2,1)}, u32[]{:S(2)}, u32[]{:S(2)}) %collective-permute-start.2) | collective-permute-done | bytes 2654240 | tf_op jit(solution)/shard_map/ppermute | solution.py:452
  221.9 36.8 %collective-permute-done.6 = bf16[6,192,1152]{2,1,0:T(8,128)(2,1)} collective-permute-done((bf16[6,192,1152]{2,1,0:T(8,128)(2,1)}, bf16[6,192,1152]{2,1,0:T(8,128)(2,1)}, u32[]{:S(2)}, u32[]{:S(2)}) %collective-permute-start.6) | collective-permute-done | bytes 2654240 | tf_op jit(solution)/shard_map/ppermute | solution.py:452
  270.6 11.1 attend.1
  281.7 22.2 %all-gather.25.cloned.1.call-done = bf16[6144,384]{1,0:T(8,128)(2,1)} async-done(((bf16[1536,384]{1,0:T(8,128)(2,1)}), bf16[6144,384]{1,0:T(8,128)(2,1)}) %all-gather.25.cloned.1.call-update) | async-done | bytes 4718608 | tf_op jit(solution)/shard_map/all_gather | solution.py:554
  350.2 36.9 %collective-permute-done.11 = bf16[6,192,1152]{2,1,0:T(8,128)(2,1)} collective-permute-done((bf16[6,192,1152]{2,1,0:T(8,128)(2,1)}, bf16[6,192,1152]{2,1,0:T(8,128)(2,1)}, u32[]{:S(2)}, u32[]{:S(2)}) %collective-permute-start.11) | collective-permute-done | bytes 2654240 | tf_op jit(solution)/shard_map/ppermute | solution.py:452
  401.3 30.6 %all-gather.19.cloned.1.call-done.x_ref = bf16[1024,1536]{1,0:T(8,128)(2,1)} async-done(((bf16[256,1536]{1,0:T(8,128)(2,1)}), bf16[1024,1536]{1,0:T(8,128)(2,1)}) %all-gather.19.cloned.1.call-update) | async-done | bytes 3145744 | tf_op jit(solution)/shard_map/all_gather | solution.py:593
  431.8 6.2 broadcast_in_dim.25.rest_5_
  438.0 68.4 %experts.4 = (bf16[4,4,192,1152]{3,2,1,0:T(8,128)(2,1)}, f32[1024,3072]{1,0:T(8,128)}) custom-call(bf16[1024,128]{1,0:T(8,128)(2,1)} %get-tuple-element.237.rank_c, s32[8,1,1024]{2,1,0:T(1,128)} %copy.159.rank_r, f32[8,1,1024]{2,1,0:T(1,128)} %copy.160.weight_r, bf16[1024,1536]{1,0:T(8,128)(2,1)} %all-gather.19.cloned.1.call-done.x_ref, ...), custom_call_target="tpu_custom_call" | custom-call | flops 73282879488 | bytes 37748736 | tf_op jit(solution)/shard_map/experts/pallas_call | solution.py:390
  512.9 68.4 %experts.5 = (bf16[4,4,192,1152]{3,2,1,0:T(8,128)(2,1)}, f32[1024,3072]{1,0:T(8,128)}) custom-call(bf16[1024,128]{1,0:T(8,128)(2,1)} %get-tuple-element.238.rank_c, s32[8,1,1024]{2,1,0:T(1,128)} %copy.164.rank_r, f32[8,1,1024]{2,1,0:T(1,128)} %copy.165.weight_r, bf16[1024,1536]{1,0:T(8,128)(2,1)} %all-gather.19.cloned.1.call-done.x_ref, ...), custom_call_target="tpu_custom_call" | custom-call | flops 73282879488 | bytes 37748736 | tf_op jit(solution)/shard_map/experts/pallas_call | solution.py:390
  592.2 68.6 %experts.6 = (bf16[4,4,192,1152]{3,2,1,0:T(8,128)(2,1)}, f32[1024,3072]{1,0:T(8,128)}) custom-call(bf16[1024,128]{1,0:T(8,128)(2,1)} %get-tuple-element.236.rank_c, s32[8,1,1024]{2,1,0:T(1,128)} %after.6.rank_r, f32[8,1,1024]{2,1,0:T(1,128)} %copy.170.weight_r, bf16[1024,1536]{1,0:T(8,128)(2,1)} %all-gather.19.cloned.1.call-done.x_ref, ...), custom_call_target="tpu_custom_call" | custom-call | flops 73282879488 | bytes 37748736 | tf_op jit(solution)/shard_map/experts/pallas_call | solution.py:390
  660.8 68.6 %experts.7 = (bf16[4,4,192,1152]{3,2,1,0:T(8,128)(2,1)}, f32[1024,3072]{1,0:T(8,128)}) custom-call(bf16[1024,128]{1,0:T(8,128)(2,1)} %get-tuple-element.239.rank_c, s32[8,1,1024]{2,1,0:T(1,128)} %after.5.rank_r, f32[8,1,1024]{2,1,0:T(1,128)} %slice.888.weight_r, bf16[1024,1536]{1,0:T(8,128)(2,1)} %all-gather.19.cloned.1.call-done.x_ref, ...), custom_call_target="tpu_custom_call" | custom-call | flops 73282879488 | bytes 37748736 | tf_op jit(solution)/shard_map/experts/pallas_call | solution.py:390
  729.5 8.2 convert_element_type.241
  754.9 56.2 %collective-permute-done.14.refs_1_ = bf16[6,192,1152]{2,1,0:T(8,128)(2,1)} collective-permute-done((bf16[6,192,1152]{2,1,0:T(8,128)(2,1)S(1)}, bf16[6,192,1152]{2,1,0:T(8,128)(2,1)}, u32[]{:S(2)}, u32[]{:S(2)}) %collective-permute-start.14) | collective-permute-done | bytes 2654240 | tf_op jit(solution)/shard_map/ppermute | solution.py:452
  817.6 8.4 rev.35
  829.1 36.7 %reduce-scatter.11.cloned.1.call-done = bf16[256,1536]{1,0:T(8,128)(2,1)} async-done(((bf16[1024,1536]{1,0:T(8,128)(2,1)}), bf16[256,1536]{1,0:T(8,128)(2,1)}) %reduce-scatter.11.cloned.1.call-update) | async-done | bytes 786448 | tf_op jit(solution)/shard_map/reduce_scatter | solution.py:628
  872.7 8.4 rev.33
  908.3 18.3 %attend_back.1 = (f32[256,1536]{1,0:T(8,128)S(1)}, f32[1024,256]{1,0:T(8,128)S(1)}, f32[1024,256]{1,0:T(8,128)S(1)}) custom-call(s32[1]{0:T(128)} %after.7.first_ref, bf16[256,1536]{1,0:T(8,128)(2,1)S(1)} %copy-done.3, bf16[1024,256]{1,0:T(8,128)(2,1)S(1)} %get-tuple-element.207.k_ref, bf16[1024,256]{1,0:T(8,128)(2,1)S(1)} %get-tuple-element.206.v_ref, ...), custom_call_target="tpu_custom_call" | custom-call | flops 4026531840 | bytes 3145728 | tf_op jit(solution)/shard_map/attend_back/pallas_call | solution.py:132
  935.7 19.9 %reduce-scatter.15.cloned.1.call-done = bf16[256,512]{1,0:T(8,128)(2,1)} async-done(((bf16[1024,512]{1,0:T(8,128)(2,1)}), bf16[256,512]{1,0:T(8,128)(2,1)}) %reduce-scatter.15.cloned.1.call-update) | async-done | bytes 262160 | tf_op jit(solution)/shard_map/reduce_scatter | solution.py:641
  1010.1 58.3 %collective-permute-done.16 = bf16[6,192,1152]{2,1,0:T(8,128)(2,1)S(1)} collective-permute-done((bf16[6,192,1152]{2,1,0:T(8,128)(2,1)S(1)}, bf16[6,192,1152]{2,1,0:T(8,128)(2,1)S(1)}, u32[]{:S(2)}, u32[]{:S(2)}) %collective-permute-start.16) | collective-permute-done | bytes 2654240 | tf_op jit(solution)/shard_map/ppermute | solution.py:452
  1078.8 30.4 %collective-permute-done.19 = bf16[4,192,1152]{2,1,0:T(8,128)(2,1)S(1)} collective-permute-done((bf16[4,192,1152]{2,1,0:T(8,128)(2,1)S(1)}, bf16[4,192,1152]{2,1,0:T(8,128)(2,1)S(1)}, u32[]{:S(2)}, u32[]{:S(2)}) %collective-permute-start.19) | collective-permute-done | bytes 1769504 | tf_op jit(solution)/shard_map/ppermute | solution.py:452
  1133.4 6.3 copy.191
  1139.7 72.6 %reduce-scatter.17.cloned.1.call-done = bf16[1,1536,384]{2,1,0:T(8,128)(2,1)} async-done(((bf16[4,1536,384]{2,1,0:T(8,128)(2,1)}), bf16[1,1536,384]{2,1,0:T(8,128)(2,1)}) %reduce-scatter.17.cloned.1.call-update) | async-done | bytes 1179664 | tf_op jit(solution)/shard_map/reduce_scatter | solution.py:657
  1215.1 6.3 copy.190
  1222.4 6.3 copy.189
  1230.4 20.7 %all-reduce.6.cloned.1.call-done = bf16[192,514]{0,1:T(8,128)(2,1)} async-done(((bf16[192,514]{0,1:T(8,128)(2,1)}), bf16[192,514]{0,1:T(8,128)(2,1)}) %all-reduce.6.cloned.1.call-update) | async-done | bytes 197392 | tf_op jit(solution)/shard_map/psum | solution.py:663
  1255.0 36.0 %reduce-scatter.23.cloned.1.call-done = bf16[192,384]{1,0:T(8,128)(2,1)} async-done(((bf16[1536,384]{1,0:T(8,128)(2,1)}), bf16[192,384]{1,0:T(8,128)(2,1)}) %reduce-scatter.23.cloned.1.call-update) | async-done | bytes 147472 | tf_op jit(solution)/shard_map/reduce_scatter | solution.py:658
  1292.6 38.6 %reduce-scatter.19.cloned.1.call-done = bf16[192,384]{1,0:T(8,128)(2,1)} async-done(((bf16[1536,384]{1,0:T(8,128)(2,1)}), bf16[192,384]{1,0:T(8,128)(2,1)}) %reduce-scatter.19.cloned.1.call-update) | async-done | bytes 147472 | tf_op jit(solution)/shard_map/reduce_scatter | solution.py:658
  (506 shorter events, 350.8 us)
Async XLA Ops:
  9.0 56.2 %all-gather.11.cloned.1.call-start = ((), (), s32[]{:S(2)}) async-start(), calls=%async_computation.8 | async-start | bytes 1327104 | tf_op jit(solution)/shard_map/all_gather | solution.py:553
  9.7 84.6 %all-gather.17.cloned.1.call-start = ((), (), s32[]{:S(2)}) async-start(), calls=%async_computation.11 | async-start | bytes 1327104 | tf_op jit(solution)/shard_map/all_gather | solution.py:554
  10.4 209.6 %all-gather.15.cloned.1.call-start = ((), (), s32[]{:S(2)}) async-start(), calls=%async_computation.10 | async-start | bytes 1310720 | tf_op jit(solution)/shard_map/all_gather | solution.py:581
  42.3 219.2 %all-gather.23.cloned.1.call-start = ((), (), s32[]{:S(2)}) async-start(), calls=%async_computation.22 | async-start | bytes 5898240 | tf_op jit(solution)/shard_map/all_gather | solution.py:553
  65.2 238.8 %all-gather.25.cloned.1.call-start = ((), (), s32[]{:S(2)}) async-start(), calls=%async_computation.23 | async-start | bytes 5898240 | tf_op jit(solution)/shard_map/all_gather | solution.py:554
  94.3 306.9 %all-gather.21.cloned.1.call-start = ((), (), s32[]{:S(2)}) async-start(), calls=%async_computation.13 | async-start | bytes 3932160 | tf_op jit(solution)/shard_map/all_gather | solution.py:570
  132.6 59.6 %collective-permute-start.2 = (bf16[6,192,1152]{2,1,0:T(8,128)(2,1)}, bf16[6,192,1152]{2,1,0:T(8,128)(2,1)}, u32[]{:S(2)}, u32[]{:S(2)}) collective-permute-start(bf16[6,192,1152]{2,1,0:T(8,128)(2,1)} %get-tuple-element.187), channel_id=1, source_target_pairs={{0,16},{4,20},{8,24},{12,28},{16,0},{20,4},{24,8},{28,12},{1,17},{... | collective-permute-start | bytes 7962632 | tf_op jit(solution)/shard_map/ppermute | solution.py:452
  133.2 61.4 %collective-permute-start.3 = (bf16[6,192,1152]{2,1,0:T(8,128)(2,1)}, bf16[6,192,1152]{2,1,0:T(8,128)(2,1)}, u32[]{:S(2)}, u32[]{:S(2)}) collective-permute-start(bf16[6,192,1152]{2,1,0:T(8,128)(2,1)} %get-tuple-element.188), channel_id=1, source_target_pairs={{0,8},{4,12},{8,0},{12,4},{16,24},{20,28},{24,16},{28,20},{1,9},{5... | collective-permute-start | bytes 7962632 | tf_op jit(solution)/shard_map/ppermute | solution.py:452
  200.0 58.7 %collective-permute-start.6 = (bf16[6,192,1152]{2,1,0:T(8,128)(2,1)}, bf16[6,192,1152]{2,1,0:T(8,128)(2,1)}, u32[]{:S(2)}, u32[]{:S(2)}) collective-permute-start(bf16[6,192,1152]{2,1,0:T(8,128)(2,1)} %get-tuple-element.185), channel_id=1, source_target_pairs={{0,8},{4,12},{8,0},{12,4},{16,24},{20,28},{24,16},{28,20},{1,9},{5... | collective-permute-start | bytes 7962632 | tf_op jit(solution)/shard_map/ppermute | solution.py:452
  215.3 216.6 %all-gather.19.cloned.1.call-start = ((), (), s32[]{:S(2)}) async-start(), calls=%async_computation.12 | async-start | bytes 3932160 | tf_op jit(solution)/shard_map/all_gather | solution.py:593
  221.4 100.5 %collective-permute-start.5 = (bf16[6,192,1152]{2,1,0:T(8,128)(2,1)}, bf16[6,192,1152]{2,1,0:T(8,128)(2,1)}, u32[]{:S(2)}, u32[]{:S(2)}) collective-permute-start(bf16[6,192,1152]{2,1,0:T(8,128)(2,1)} %get-tuple-element.186), channel_id=1, source_target_pairs={{0,16},{4,20},{8,24},{12,28},{16,0},{20,4},{24,8},{28,12},{1,17},{... | collective-permute-start | bytes 7962632 | tf_op jit(solution)/shard_map/ppermute | solution.py:452
  321.8 491.6 %reduce-scatter.13.cloned.1.call-start = ((), (), s32[]{:S(2)}) async-start(), calls=%async_computation.15 | async-start | bytes 3932160 | tf_op jit(solution)/shard_map/reduce_scatter | solution.py:627
  327.3 59.7 %collective-permute-start.11 = (bf16[6,192,1152]{2,1,0:T(8,128)(2,1)}, bf16[6,192,1152]{2,1,0:T(8,128)(2,1)}, u32[]{:S(2)}, u32[]{:S(2)}) collective-permute-start(bf16[6,192,1152]{2,1,0:T(8,128)(2,1)} %get-tuple-element.183), channel_id=1, source_target_pairs={{0,16},{4,20},{8,24},{12,28},{16,0},{20,4},{24,8},{28,12},{1,17},{... | collective-permute-start | bytes 7962632 | tf_op jit(solution)/shard_map/ppermute | solution.py:452
  328.9 62.5 %collective-permute-start.10 = (bf16[6,192,1152]{2,1,0:T(8,128)(2,1)}, bf16[6,192,1152]{2,1,0:T(8,128)(2,1)}, u32[]{:S(2)}, u32[]{:S(2)}) collective-permute-start(bf16[6,192,1152]{2,1,0:T(8,128)(2,1)} %get-tuple-element.184), channel_id=1, source_target_pairs={{0,8},{4,12},{8,0},{12,4},{16,24},{20,28},{24,16},{28,20},{1,9},{5... | collective-permute-start | bytes 7962632 | tf_op jit(solution)/shard_map/ppermute | solution.py:452
  389.8 271.0 %collective-permute-start.13 = (bf16[2,192,1152]{2,1,0:T(8,128)(2,1)}, bf16[2,192,1152]{2,1,0:T(8,128)(2,1)}, u32[]{:S(2)}, u32[]{:S(2)}) collective-permute-start(bf16[2,192,1152]{2,1,0:T(8,128)(2,1)} %get-tuple-element.174), channel_id=1, source_target_pairs={{0,8},{4,12},{8,0},{12,4},{16,24},{20,28},{24,16},{28,20},{1,9},{5... | collective-permute-start | bytes 2654216 | tf_op jit(solution)/shard_map/ppermute | solution.py:452
  394.1 266.7 %collective-permute-start.12 = (bf16[2,192,1152]{2,1,0:T(8,128)(2,1)}, bf16[2,192,1152]{2,1,0:T(8,128)(2,1)}, u32[]{:S(2)}, u32[]{:S(2)}) collective-permute-start(bf16[2,192,1152]{2,1,0:T(8,128)(2,1)} %get-tuple-element.172), channel_id=1, source_target_pairs={{0,16},{4,20},{8,24},{12,28},{16,0},{20,4},{24,8},{28,12},{1,17},{... | collective-permute-start | bytes 2654216 | tf_op jit(solution)/shard_map/ppermute | solution.py:452
  509.9 74.8 %collective-permute-start.8 = (bf16[2,192,1152]{2,1,0:T(8,128)(2,1)}, bf16[2,192,1152]{2,1,0:T(8,128)(2,1)S(1)}, u32[]{:S(2)}, u32[]{:S(2)}) collective-permute-start(bf16[2,192,1152]{2,1,0:T(8,128)(2,1)} %get-tuple-element.105), channel_id=1, source_target_pairs={{0,8},{4,12},{8,0},{12,4},{16,24},{20,28},{24,16},{28,20},{1,9},{5... | collective-permute-start | bytes 2654216 | tf_op jit(solution)/shard_map/ppermute | solution.py:452
  511.4 73.3 %collective-permute-start.4 = (bf16[2,192,1152]{2,1,0:T(8,128)(2,1)}, bf16[2,192,1152]{2,1,0:T(8,128)(2,1)S(1)}, u32[]{:S(2)}, u32[]{:S(2)}) collective-permute-start(bf16[2,192,1152]{2,1,0:T(8,128)(2,1)} %get-tuple-element.107), channel_id=1, source_target_pairs={{0,16},{4,20},{8,24},{12,28},{16,0},{20,4},{24,8},{28,12},{1,17},{... | collective-permute-start | bytes 2654216 | tf_op jit(solution)/shard_map/ppermute | solution.py:452
  589.2 71.6 %collective-permute-start.7 = (bf16[6,192,1152]{2,1,0:T(8,128)(2,1)}, bf16[6,192,1152]{2,1,0:T(8,128)(2,1)}, u32[]{:S(2)}, u32[]{:S(2)}) collective-permute-start(bf16[6,192,1152]{2,1,0:T(8,128)(2,1)} %pad_maximum_fusion.12), channel_id=1, source_target_pairs={{0,8},{4,12},{8,0},{12,4},{16,24},{20,28},{24,16},{28,20},{1,9},{5... | collective-permute-start | bytes 7962632 | tf_op jit(solution)/shard_map/ppermute | solution.py:452
  591.6 69.2 %collective-permute-start.9 = (bf16[6,192,1152]{2,1,0:T(8,128)(2,1)}, bf16[6,192,1152]{2,1,0:T(8,128)(2,1)}, u32[]{:S(2)}, u32[]{:S(2)}) collective-permute-start(bf16[6,192,1152]{2,1,0:T(8,128)(2,1)} %pad_maximum_fusion.13), channel_id=1, source_target_pairs={{0,16},{4,20},{8,24},{12,28},{16,0},{20,4},{24,8},{28,12},{1,17},{... | collective-permute-start | bytes 7962632 | tf_op jit(solution)/shard_map/ppermute | solution.py:452
  743.7 122.1 %reduce-scatter.11.cloned.1.call-start = ((), (), s32[]{:S(2)}) async-start(), calls=%async_computation.14 | async-start | bytes 3932160 | tf_op jit(solution)/shard_map/reduce_scatter | solution.py:628
  744.3 211.3 %reduce-scatter.15.cloned.1.call-start = ((), (), s32[]{:S(2)}) async-start(), calls=%async_computation.16 | async-start | bytes 1310720 | tf_op jit(solution)/shard_map/reduce_scatter | solution.py:641
  751.2 59.9 %collective-permute-start.14 = (bf16[6,192,1152]{2,1,0:T(8,128)(2,1)S(1)}, bf16[6,192,1152]{2,1,0:T(8,128)(2,1)}, u32[]{:S(2)}, u32[]{:S(2)}) collective-permute-start(bf16[6,192,1152]{2,1,0:T(8,128)(2,1)S(1)} %pad_maximum_fusion.14), channel_id=1, source_target_pairs={{0,8},{4,12},{8,0},{12,4},{16,24},{20,28},{24,16},{28,20},{1,9},{5... | collective-permute-start | bytes 7962632 | tf_op jit(solution)/shard_map/ppermute | solution.py:452
  753.3 59.5 %collective-permute-start.15 = (bf16[6,192,1152]{2,1,0:T(8,128)(2,1)S(1)}, bf16[6,192,1152]{2,1,0:T(8,128)(2,1)}, u32[]{:S(2)}, u32[]{:S(2)}) collective-permute-start(bf16[6,192,1152]{2,1,0:T(8,128)(2,1)S(1)} %pad_maximum_fusion.15), channel_id=1, source_target_pairs={{0,16},{4,20},{8,24},{12,28},{16,0},{20,4},{24,8},{28,12},{1,17},{... | collective-permute-start | bytes 7962632 | tf_op jit(solution)/shard_map/ppermute | solution.py:452
  927.9 185.2 %reduce-scatter.25.cloned.1.call-start = ((), (), s32[]{:S(2)}) async-start(), calls=%async_computation.24 | async-start | bytes 4423680
  972.7 151.1 %reduce-scatter.21.cloned.1.call-start = ((), (), s32[]{:S(2)}) async-start(), calls=%async_computation.20 | async-start | bytes 5898240 | tf_op jit(solution)/shard_map/reduce_scatter | solution.py:657
  979.1 233.2 %reduce-scatter.17.cloned.1.call-start = ((), (), s32[]{:S(2)}) async-start(), calls=%async_computation.18 | async-start | bytes 5898240 | tf_op jit(solution)/shard_map/reduce_scatter | solution.py:657
  992.2 258.8 %all-reduce.6.cloned.1.call-start = ((), (), s32[]{:S(2)}) async-start(), calls=%async_computation.17 | async-start | bytes 532480 | tf_op jit(solution)/shard_map/psum | solution.py:663
  998.2 70.1 %collective-permute-start.16 = (bf16[6,192,1152]{2,1,0:T(8,128)(2,1)S(1)}, bf16[6,192,1152]{2,1,0:T(8,128)(2,1)S(1)}, u32[]{:S(2)}, u32[]{:S(2)}) collective-permute-start(bf16[6,192,1152]{2,1,0:T(8,128)(2,1)S(1)} %pad_maximum_fusion.16), channel_id=1, source_target_pairs={{0,8},{4,12},{8,0},{12,4},{16,24},{20,28},{24,16},{28,20},{1,9},{5... | collective-permute-start | bytes 7962632 | tf_op jit(solution)/shard_map/ppermute | solution.py:452
  999.9 68.5 %collective-permute-start.17 = (bf16[6,192,1152]{2,1,0:T(8,128)(2,1)S(1)}, bf16[6,192,1152]{2,1,0:T(8,128)(2,1)S(1)}, u32[]{:S(2)}, u32[]{:S(2)}) collective-permute-start(bf16[6,192,1152]{2,1,0:T(8,128)(2,1)S(1)} %pad_maximum_fusion.17), channel_id=1, source_target_pairs={{0,16},{4,20},{8,24},{12,28},{16,0},{20,4},{24,8},{28,12},{1,17},{... | collective-permute-start | bytes 7962632 | tf_op jit(solution)/shard_map/ppermute | solution.py:452
  1115.0 175.9 %reduce-scatter.23.cloned.1.call-start = ((), (), s32[]{:S(2)}) async-start(), calls=%async_computation.21 | async-start | bytes 1327104 | tf_op jit(solution)/shard_map/reduce_scatter | solution.py:658
  1123.8 207.4 %reduce-scatter.19.cloned.1.call-start = ((), (), s32[]{:S(2)}) async-start(), calls=%async_computation.19 | async-start | bytes 1327104 | tf_op jit(solution)/shard_map/reduce_scatter | solution.py:658
  (78 other events, 1526.0 us)
Sparse Core Ops, SparseCore 0:
  10.5 28.6 all-gather.12
  41.1 24.0 all-gather.10
  67.0 27.2 all-gather.16
  96.3 27.9 all-gather.14
  125.7 88.8 all-gather.22
  216.0 87.8 all-gather.24
  305.5 61.9 all-gather.20
  369.7 62.1 all-gather.18
  743.8 58.8 reduce-scatter.12
  805.5 60.2 reduce-scatter.10
  928.0 27.5 reduce-scatter.14
  972.8 62.7 reduce-scatter.24
  1038.5 85.2 reduce-scatter.20
  1126.5 85.7 reduce-scatter.16
  1215.0 35.9 all-reduce.5
  1254.1 36.7 reduce-scatter.22
  1294.4 36.7 reduce-scatter.18

commit v3 on v2

--- a/solution.py
+++ b/solution.py
@@ -418,6 +418,628 @@
     )(rank_cols, rank_rows, weight_rows, x, gy, *flat, sums)
 
 
+def remote(source, target, send_sem, recv_sem, device):
+    return pltpu.make_async_remote_copy(
+        src_ref=source,
+        dst_ref=target,
+        send_sem=send_sem,
+        recv_sem=recv_sem,
+        device_id=device,
+        device_id_type=pl.DeviceIdType.MESH,
+    )
+
+
+def chip_neighbours():
+    me = lax.axis_index("dp")
+    return me + 2 - 4 * lax.rem(me // 2, 2), me + 4 - 8 * lax.rem(me // 4, 2)
+
+
+def meet(members, chips):
+    barrier = pltpu.get_barrier_semaphore()
+    z = lax.axis_index("tensor")
+
+    def signal(device):
+        pl.semaphore_signal(barrier, inc=1, device_id=device, device_id_type=pl.DeviceIdType.MESH)
+
+    @pl.when(z > 0)
+    def _():
+        signal({"tensor": z - 1})
+
+    @pl.when(z < members - 1)
+    def _():
+        signal({"tensor": z + 1})
+
+    if chips:
+        for other in (*chip_neighbours(), sibling()):
+            signal({"dp": other})
+    inner = jnp.where((z > 0) & (z < members - 1), 1, 0)
+    pl.semaphore_wait(barrier, 1 + inner + (3 if chips else 0))
+
+
+class LineGather:
+    def __init__(self, members, at, send, recv):
+        self.members, self.at, self.send, self.recv = members, at, send, recv
+
+    def copies(self, hop):
+        z, last = lax.axis_index("tensor"), self.members - 1
+        up, down = z - hop + 1, z + hop - 1
+
+        def copy(block, way, device):
+            return lambda: remote(
+                self.at(block), self.at(block), self.send.at[way, hop - 1], self.recv.at[way, hop - 1], {"tensor": device}
+            )
+
+        return (
+            ((up >= 0) & (z < last), copy(up, 0, z + 1)),
+            ((down <= last) & (z > 0), copy(down, 1, z - 1)),
+        ), (
+            (z - hop >= 0, copy(z - hop, 0, z)),
+            (z + hop <= last, copy(z + hop, 1, z)),
+        )
+
+    def start(self, hop):
+        for present, copy in self.copies(hop)[0]:
+
+            @pl.when(present)
+            def _():
+                copy().start()
+
+    def arrive(self, hop):
+        for present, copy in self.copies(hop)[1]:
+
+            @pl.when(present)
+            def _():
+                copy().wait_recv()
+
+    def close(self):
+        for hop in range(1, self.members):
+            for present, copy in self.copies(hop)[0]:
+
+                @pl.when(present)
+                def _():
+                    copy().wait_send()
+
+
+class LineSum:
+    def __init__(self, members, part, leaving, arriving, send, recv):
+        self.members, self.part, self.leaving, self.arriving = members, part, leaving, arriving
+        self.send, self.recv = send, recv
+
+    def copy(self, way, hop, device):
+        return remote(
+            self.leaving.at[way],
+            self.arriving.at[way, hop - 1],
+            self.send.at[way, hop - 1],
+            self.recv.at[way, hop - 1],
+            {"tensor": device},
+        )
+
+    def ways(self, hop):
+        z, last = lax.axis_index("tensor"), self.members - 1
+        return (
+            (0, z - hop >= 0, z - hop, z < last, z - 1, (z < last) & (z + 1 - hop >= 0)),
+            (1, z + hop <= last, z + hop, z > 0, z + 1, (z > 0) & (z - 1 + hop <= last)),
+        )
+
+    def start(self, hop):
+        if hop + 1 < self.members:
+            self.leave(hop + 1)
+        for way, present, block, behind, device, _ in self.ways(hop):
+
+            @pl.when(present)
+            def _():
+                self.leaving[way] = self.part(block).astype(bf16)
+
+            if hop + 1 < self.members:
+
+                @pl.when(present & behind)
+                def _():
+                    both = self.part(block).astype(f32) + self.arriving[way, hop].astype(f32)
+                    self.leaving[way] = both.astype(bf16)
+
+            @pl.when(present)
+            def _():
+                self.copy(way, hop, device).start()
+
+    def arrive(self, hop):
+        for way, _, _, _, device, present in self.ways(hop):
+
+            @pl.when(present)
+            def _():
+                self.copy(way, hop, device).wait_recv()
+
+    def total(self, out):
+        z, last = lax.axis_index("tensor"), self.members - 1
+        out[...] = self.part(z).astype(f32)
+        for way, present in ((0, z < last), (1, z > 0)):
+
+            @pl.when(present)
+            def _():
+                out[...] += self.arriving[way, 0].astype(f32)
+
+    def leave(self, hop):
+        for way, present, _, _, device, _ in self.ways(hop):
+
+            @pl.when(present)
+            def _():
+                self.copy(way, hop, device).wait_send()
+
+    def close(self):
+        self.leave(1)
+
+
+def swap_blocks(values):
+    me = lax.axis_index("dp")
+    chip = values.shape[1] // 4
+    four = [values[:, i * chip : (i + 1) * chip] for i in range(4)]
+    y_side, x_side, core_side = lax.rem(me // 4, 2) == 1, lax.rem(me // 2, 2) == 1, lax.rem(me, 2) == 1
+    four = [jnp.where(y_side, four[i ^ 2], four[i]) for i in range(4)]
+    four = [jnp.where(x_side, four[i ^ 1], four[i]) for i in range(4)]
+    four = [jnp.where(core_side, pltpu.roll(part, chip // 2, 1), part) for part in four]
+    return jnp.concatenate(four, axis=1)
+
+
+def in_vmem(count):
+    return [pl.BlockSpec(memory_space=pltpu.VMEM)] * count
+
+
+def gather_small(square, tall, cotangent, members, devices):
+    height = square.shape[0]
+    own_rows, width = cotangent.shape
+    dma = pltpu.SemaphoreType.DMA
+    cut = square.shape[1] // 2
+
+    def kernel(square_ref, tall_ref, cot_ref, square_all, tall_all, grad_all, *sems):
+        line_send, line_recv, grad_send, grad_recv, chip_send, chip_recv, core_send, core_recv = sems
+        me, z = lax.axis_index("dp"), lax.axis_index("tensor")
+        x_side, y_side = chip_neighbours()
+        core = sibling()
+        meet(members, True)
+
+        def rows(device):
+            return pl.ds(pl.multiple_of(device * height, 16), height)
+
+        square_all[z, rows(me), :] = square_ref[...]
+        tall_all[rows(me), :] = tall_ref[...]
+        line = LineGather(members, lambda block: square_all.at[block, rows(me)], line_send, line_recv)
+        group = LineGather(
+            members,
+            lambda block: grad_all.at[pl.ds(pl.multiple_of(block * own_rows, 16), own_rows)],
+            grad_send,
+            grad_recv,
+        )
+
+        def chip(index, source, device):
+            return remote(source, source, chip_send.at[index], chip_recv.at[index], {"dp": device})
+
+        def across(index, source):
+            return remote(source, source, core_send.at[index], core_recv.at[index], {"dp": core})
+
+        def tall_at(device):
+            return tall_all.at[rows(device)]
+
+        def square_at(device, half=None):
+            lanes = slice(None) if half is None else slice(half * cut, (half + 1) * cut)
+            return square_all.at[:, rows(device), lanes]
+
+        line.start(1)
+        near = [chip(0, tall_at(me), x_side), chip(1, tall_at(me), y_side)]
+        for copy in near:
+            copy.start()
+        grad_all[pl.ds(pl.multiple_of(z * own_rows, 16), own_rows), :] = swap_blocks(cot_ref[...]).astype(bf16)
+        for hop in range(1, members):
+            line.arrive(hop)
+            if hop + 1 < members:
+                line.start(hop + 1)
+        near += [chip(2, square_at(me), x_side), chip(3, square_at(me), y_side)]
+        for copy in near[2:]:
+            copy.start()
+        group.start(1)
+        trades = [across(0, tall_at(me)), across(1, square_at(me))]
+        for copy in trades:
+            copy.start()
+        chip(0, tall_at(x_side), x_side).wait_recv()
+        chip(1, tall_at(y_side), y_side).wait_recv()
+        diagonal = x_side + y_side - me
+        far = [chip(4, tall_at(x_side), y_side)]
+        far[0].start()
+        trades += [across(2, tall_at(x_side)), across(3, tall_at(y_side))]
+        for copy in trades[2:]:
+            copy.start()
+        group.arrive(1)
+        if members > 2:
+            group.start(2)
+        chip(2, square_at(x_side), x_side).wait_recv()
+        chip(3, square_at(y_side), y_side).wait_recv()
+        far += [chip(5, square_at(x_side, 0), y_side), chip(6, square_at(y_side, 1), x_side)]
+        for copy in far[1:]:
+            copy.start()
+        trades += [across(4, square_at(x_side)), across(5, square_at(y_side))]
+        for copy in trades[4:]:
+            copy.start()
+        chip(4, tall_at(diagonal), y_side).wait_recv()
+        trades.append(across(6, tall_at(diagonal)))
+        trades[-1].start()
+        for hop in range(2, members - 1):
+            group.arrive(hop)
+            group.start(hop + 1)
+        chip(5, square_at(diagonal, 0), y_side).wait_recv()
+        chip(6, square_at(diagonal, 1), x_side).wait_recv()
+        trades.append(across(7, square_at(diagonal)))
+        trades[-1].start()
+        theirs = [core, core, x_side, y_side, x_side, y_side, diagonal, diagonal]
+        for index, device in enumerate(theirs):
+            there = device if index < 2 else device + core - me
+            source = square_at(there) if index in (1, 4, 5, 7) else tall_at(there)
+            across(index, source).wait_recv()
+        if members > 2:
+            group.arrive(members - 1)
+        for copy in near + far + trades:
+            copy.wait_send()
+        line.close()
+        group.close()
+
+    return pl.pallas_call(
+        kernel,
+        in_specs=in_vmem(3),
+        out_specs=in_vmem(3),
+        out_shape=[
+            jax.ShapeDtypeStruct((members, devices * height, square.shape[1]), bf16),
+            jax.ShapeDtypeStruct((devices * height, tall.shape[1]), bf16),
+            jax.ShapeDtypeStruct((members * own_rows, width), bf16),
+        ],
+        scratch_shapes=[dma((2, members - 1))] * 4 + [dma((7,))] * 2 + [dma((8,))] * 2,
+        compiler_params=pltpu.CompilerParams(collective_id=2, has_side_effects=True, vmem_limit_bytes=40 * 2**20),
+        cost_estimate=pl.CostEstimate(flops=8 * 10**10, bytes_accessed=10**7, transcendentals=0),
+        name="gather_small",
+    )(square, tall, cotangent)
+
+
+def turn(values, cosine, sine):
+    return values * cosine + pltpu.roll(values, HD // 2, 1) * sine
+
+
+def gain_rows(tall_ref, kv):
+    return jnp.transpose(tall_ref[:, kv:].astype(f32))
+
+
+def attention_front(tokens, square, tall, cosine, sine, members):
+    own_rows, width = tokens.shape
+    rows = own_rows * members
+    kv = 2 * KV * HD
+    heads = width // HD
+    per_kv = heads // KV
+    part = width // members
+    dma = pltpu.SemaphoreType.DMA
+
+    def kernel(x_ref, square_ref, tall_ref, cos_ref, sin_ref, *rest):
+        normed_ref, q_ref, kv_all, mixed_ref, hidden_ref, rows_all = rest[:6]
+        kv_send, kv_recv, row_send, row_recv = rest[6:]
+        z = lax.axis_index("tensor")
+
+        def block_of(ref):
+            return lambda block: ref.at[pl.ds(pl.multiple_of(block * own_rows, 16), own_rows)]
+
+        own = pl.ds(pl.multiple_of(z * own_rows, 16), own_rows)
+        kv_line = LineGather(members, block_of(kv_all), kv_send, kv_recv)
+        row_line = LineGather(members, block_of(rows_all), row_send, row_recv)
+        gains = gain_rows(tall_ref, kv)
+        x = x_ref[...].astype(f32)
+        normed_ref[...] = (rms_pieces(x)[1] * gains[0:1]).astype(bf16)
+        cosine, sine = cos_ref[...], sin_ref[...]
+        made = nn(normed_ref[...], tall_ref[:, :kv])
+        for head in range(KV):
+            span = slice(head * HD, (head + 1) * HD)
+            kv_all[own, span] = turn(made[:, span], cosine, sine).astype(bf16)
+        kv_all[own, KV * HD :] = made[:, KV * HD :].astype(bf16)
+        meet(members, False)
+        kv_line.start(1)
+        for t in range(members):
+            made = nn(normed_ref[...], square_ref[t, :, :part])
+            for head in range(part // HD):
+                span = slice(head * HD, (head + 1) * HD)
+                q_ref[:, t * part + head * HD : t * part + (head + 1) * HD] = turn(
+                    made[:, span], cosine, sine
+                ).astype(bf16)
+            if 1 <= t + 1 < members:
+                kv_line.arrive(t + 1)
+                if t + 2 < members:
+                    kv_line.start(t + 2)
+        first = z * own_rows
+
+        @pl.loop(0, heads)
+        def _(head):
+            span = pl.ds(pl.multiple_of(head * HD, HD), HD)
+            key_span = pl.ds(pl.multiple_of(head // per_kv * HD, HD), HD)
+            value_span = pl.ds(pl.multiple_of((KV + head // per_kv) * HD, HD), HD)
+            p = probabilities(q_ref[:, span], kv_all[:, key_span], first).astype(bf16)
+            mixed_ref[:, span] = nn(p, kv_all[:, value_span]).astype(bf16)
+
+        hidden = x_ref[...].astype(f32)
+        for t in range(members):
+            hidden += nt(mixed_ref[:, t * part : (t + 1) * part], square_ref[t, :, part:])
+        hidden_ref[...] = hidden
+        normed = rms_pieces(hidden)[1] * gains[1:2]
+        rows_all[own, :] = swap_blocks(normed).astype(bf16)
+        for hop in range(1, members):
+            row_line.start(hop)
+            row_line.arrive(hop)
+        kv_line.close()
+        row_line.close()
+
+    return pl.pallas_call(
+        kernel,
+        in_specs=in_vmem(5),
+        out_specs=in_vmem(6),
+        out_shape=[
+            jax.ShapeDtypeStruct((own_rows, width), bf16),
+            jax.ShapeDtypeStruct((own_rows, width), bf16),
+            jax.ShapeDtypeStruct((rows, kv), bf16),
+            jax.ShapeDtypeStruct((own_rows, width), bf16),
+            jax.ShapeDtypeStruct((own_rows, width), f32),
+            jax.ShapeDtypeStruct((rows, width), bf16),
+        ],
+        scratch_shapes=[dma((2, members - 1))] * 4,
+        compiler_params=pltpu.CompilerParams(collective_id=3, has_side_effects=True, vmem_limit_bytes=56 * 2**20),
+        cost_estimate=pl.CostEstimate(flops=10**11, bytes_accessed=10**7, transcendentals=0),
+        name="attention_front",
+    )(tokens, square, tall, cosine, sine)
+
+
+def attention_back(sums, cotangent, hidden, tokens, normed, q, kv_all, mixed, square, tall, cosine, sine, members):
+    own_rows, width = tokens.shape
+    rows = own_rows * members
+    kv = 2 * KV * HD
+    heads = width // HD
+    per_kv = heads // KV
+    part = width // members
+    dma = pltpu.SemaphoreType.DMA
+
+    def kernel(sums_ref, cot_ref, hidden_ref, x_ref, normed_ref, q_ref, kv_ref, mixed_ref, square_ref, tall_ref, *rest):
+        cos_ref, sin_ref = rest[:2]
+        out_ref, grad_ref, parts = rest[2:5]
+        do_ref, dq_ref, dkv_ref, total, kv_total, stage, tall_part = rest[5:12]
+        back_leave, back_arrive, moe_leave, moe_arrive, kv_leave, kv_arrive = rest[12:18]
+        back_send, back_recv, moe_send, moe_recv, kv_send, kv_recv, stage_sem = rest[18:]
+        z = lax.axis_index("tensor")
+
+        def block(ref, span):
+            return lambda b: ref[pl.ds(pl.multiple_of(b * own_rows, 16), own_rows), span]
+
+        back = LineSum(members, block(sums_ref, slice(width, 2 * width)), back_leave, back_arrive, back_send, back_recv)
+        moe = LineSum(members, block(sums_ref, slice(0, width)), moe_leave, moe_arrive, moe_send, moe_recv)
+        pairs = LineSum(members, block(dkv_ref, slice(None)), kv_leave, kv_arrive, kv_send, kv_recv)
+        meet(members, False)
+        gains = gain_rows(tall_ref, kv)
+        cosine, sine = cos_ref[...], sin_ref[...]
+        last = members - 1
+        stored = []
+
+        def store(value, at):
+            slot = len(stored) % 2
+            if len(stored) >= 2:
+                stored[-2].wait()
+            stage[slot] = value.astype(bf16)
+            copy = pltpu.make_async_copy(stage.at[slot], parts.at[:, at : at + part], stage_sem.at[slot])
+            copy.start()
+            stored.append(copy)
+
+        for hop in range(last, 0, -1):
+            back.start(hop)
+            back.arrive(hop)
+        moe.start(last)
+        back.total(total)
+        normed_grad = swap_blocks(total[...])
+        inverse, unit = rms_pieces(hidden_ref[...])
+        by_hidden, gain_two = rms_backward(normed_grad, unit, inverse, gains[1:2])
+        grad_ref[...] = cot_ref[...] + by_hidden
+        low = grad_ref[...].astype(bf16)
+        for t in range(members):
+            span = slice(t * part, (t + 1) * part)
+            do_ref[:, span] = nn(low, square_ref[t, :, part:]).astype(bf16)
+            store(tn(low, mixed_ref[:, span]), width + t * part)
+        moe.arrive(last)
+        if last > 1:
+            moe.start(last - 1)
+        dkv_ref[...] = jnp.zeros_like(dkv_ref)
+        first = z * own_rows
+
+        @pl.loop(0, heads)
+        def _(head):
+            span = pl.ds(pl.multiple_of(head * HD, HD), HD)
+            key_span = pl.ds(pl.multiple_of(head // per_kv * HD, HD), HD)
+            value_span = pl.ds(pl.multiple_of((KV + head // per_kv) * HD, HD), HD)
+            q_now, k_now, do_now = q_ref[:, span], kv_ref[:, key_span], do_ref[:, span]
+            p = probabilities(q_now, k_now, first)
+            dp = nt(do_now, kv_ref[:, value_span])
+            ds = (p * (dp - jnp.sum(p * dp, axis=-1, keepdims=True))).astype(bf16)
+            dq_ref[:, span] = turn(nn(ds, k_now) * (HD**-0.5), cosine, -sine).astype(bf16)
+            dkv_ref[:, key_span] += tn(ds, q_now) * (HD**-0.5)
+            dkv_ref[:, value_span] += tn(p.astype(bf16), do_now)
+
+        pairs.start(last)
+        for t in range(members):
+            span = slice(t * part, (t + 1) * part)
+            store(tn(normed_ref[...], dq_ref[:, span]), t * part)
+        for hop in range(last, 0, -1):
+            if hop < last:
+                pairs.start(hop)
+            pairs.arrive(hop)
+        for hop in range(last - 1, 0, -1):
+            moe.arrive(hop)
+            if hop > 1:
+                moe.start(hop - 1)
+        pairs.total(kv_total)
+        low_kv = [
+            turn(kv_total[:, head * HD : (head + 1) * HD], cosine, -sine).astype(bf16) for head in range(KV)
+        ] + [kv_total[:, KV * HD :].astype(bf16)]
+        low_kv = jnp.concatenate(low_kv, axis=1)
+        normed_grad = nt(low_kv, tall_ref[:, :kv])
+        for t in range(members):
+            normed_grad += nt(dq_ref[:, t * part : (t + 1) * part], square_ref[t, :, :part])
+        inverse, unit = rms_pieces(x_ref[...].astype(f32))
+        by_tokens, gain_one = rms_backward(normed_grad, unit, inverse, gains[0:1])
+        grad_ref[...] += by_tokens
+        tall_part[:, :kv] = tn(normed_ref[...], low_kv).astype(bf16)
+        row = lax.broadcasted_iota(jnp.int32, (HD, width), 0)
+        both = jnp.where(row == 0, gain_one[None], jnp.where(row == 1, gain_two[None], 0.0))
+        tall_part[:, kv:] = jnp.transpose(both).astype(bf16)
+        tall_copy = pltpu.make_async_copy(tall_part, parts.at[:, 2 * width :], stage_sem.at[2])
+        tall_copy.start()
+        moe.total(total)
+        out_ref[...] = (hidden_ref[...] + swap_blocks(total[...])).astype(bf16)
+        for line in (back, moe, pairs):
+            line.close()
+        for copy in (*stored[-2:], tall_copy):
+            copy.wait()
+
+    hops = (2, members - 1)
+    return pl.pallas_call(
+        kernel,
+        in_specs=in_vmem(12),
+        out_specs=in_vmem(2) + [pl.BlockSpec(memory_space=pl.ANY)],
+        out_shape=[
+            jax.ShapeDtypeStruct((own_rows, width), bf16),
+            jax.ShapeDtypeStruct((own_rows, width), f32),
+            jax.ShapeDtypeStruct((width, 2 * width + tall.shape[1]), bf16),
+        ],
+        scratch_shapes=[
+            pltpu.VMEM((own_rows, width), bf16),
+            pltpu.VMEM((own_rows, width), bf16),
+            pltpu.VMEM((rows, kv), f32),
+            pltpu.VMEM((own_rows, width), f32),
+            pltpu.VMEM((own_rows, kv), f32),
+            pltpu.VMEM((2, width, part), bf16),
+            pltpu.VMEM(tall.shape, bf16),
+        ]
+        + [pltpu.VMEM((2, own_rows, width), bf16), pltpu.VMEM((*hops, own_rows, width), bf16)] * 2
+        + [pltpu.VMEM((2, own_rows, kv), bf16), pltpu.VMEM((*hops, own_rows, kv), bf16)]
+        + [dma(hops)] * 6
+        + [dma((3,))],
+        compiler_params=pltpu.CompilerParams(collective_id=4, has_side_effects=True, vmem_limit_bytes=62 * 10**6),
+        cost_estimate=pl.CostEstimate(flops=10**11, bytes_accessed=10**7, transcendentals=0),
+        name="attention_back",
+    )(sums, cotangent, hidden, tokens, normed, q, kv_all, mixed, square, tall, cosine, sine)
+
+
+def reduce_small(parts, members, devices):
+    width = parts.shape[0]
+    height = width // devices
+    lanes = parts.shape[1]
+    tall = lanes - 2 * width
+    part = width // members
+    half = height // 2
+    dma = pltpu.SemaphoreType.DMA
+
+    def kernel(parts_ref, square_out, tall_out, own, theirs, leave, arrive, blocks, line_leave, line_arrive, tall_all, *sems):
+        own_sem, core_send, core_recv, chip_send, chip_recv, line_send, line_recv, tall_send, tall_recv = sems
+        me, z = lax.axis_index("dp"), lax.axis_index("tensor")
+        x_side, y_side = chip_neighbours()
+        core = sibling()
+        chips = [me, x_side, y_side, x_side + y_side - me]
+        meet(members, True)
+
+        def rows(device):
+            return parts_ref.at[pl.ds(pl.multiple_of(device * height, 16), height)]
+
+        def trade(m):
+            return remote(rows(chips[m] + core - me), theirs.at[m], core_send.at[m], core_recv.at[m], {"dp": core})
+
+        def keep(m):
+            return pltpu.make_async_copy(rows(chips[m]), own.at[m], own_sem.at[m])
+
+        for m in (3, 2, 1, 0):
+            trade(m).start()
+            keep(m).start()
+
+        def both(m, span):
+            return own[m, span].astype(f32) + theirs[m, span].astype(f32)
+
+        def chip(index, source, target, device):
+            return remote(source, target, chip_send.at[index], chip_recv.at[index], {"dp": device})
+
+        first, second = slice(0, half), slice(half, height)
+        far = [
+            chip(0, leave.at[0, first], arrive.at[0, first], x_side),
+            chip(1, leave.at[0, second], arrive.at[0, second], y_side),
+        ]
+        near = [chip(2, leave.at[1], arrive.at[1], x_side), chip(3, leave.at[2], arrive.at[2], y_side)]
+        for m in (3, 2, 1, 0):
+            trade(m).wait()
+            keep(m).wait()
+            if m == 3:
+                for copy, span in zip(far, (first, second)):
+                    leave[0, span] = both(3, span).astype(bf16)
+                    copy.start()
+        for copy in far:
+            copy.wait()
+        leave[1, first] = both(1, first).astype(bf16)
+        leave[1, second] = (both(1, second) + arrive[0, second].astype(f32)).astype(bf16)
+        near[0].start()
+        leave[2, first] = (both(2, first) + arrive[0, first].astype(f32)).astype(bf16)
+        leave[2, second] = both(2, second).astype(bf16)
+        near[1].start()
+        for copy in near:
+            copy.wait()
+
+        def total(span):
+            return (
+                own[0, :, span].astype(f32)
+                + theirs[0, :, span].astype(f32)
+                + arrive[1, :, span].astype(f32)
+                + arrive[2, :, span].astype(f32)
+            )
+
+        tall_all[z] = total(slice(2 * width, lanes)).astype(bf16)
+        for t in range(members):
+            blocks[t, :, :part] = total(slice(t * part, (t + 1) * part))
+            blocks[t, :, part:] = total(slice(width + t * part, width + (t + 1) * part))
+        line = LineSum(members, lambda b: blocks[b], line_leave, line_arrive, line_send, line_recv)
+        group = LineGather(members, lambda b: tall_all.at[b], tall_send, tall_recv)
+        for hop in range(1, members):
+            line.start(members - hop)
+            group.start(hop)
+            line.arrive(members - hop)
+            group.arrive(hop)
+        line.total(square_out)
+        summed = tall_all[0].astype(f32)
+        for t in range(1, members):
+            summed += tall_all[t].astype(f32)
+        tall_out[...] = summed
+        line.close()
+        group.close()
+
+    hops = (2, members - 1)
+    return pl.pallas_call(
+        kernel,
+        in_specs=[pl.BlockSpec(memory_space=pl.ANY)],
+        out_specs=in_vmem(2),
+        out_shape=[
+            jax.ShapeDtypeStruct((height, 2 * part), f32),
+            jax.ShapeDtypeStruct((height, tall), f32),
+        ],
+        scratch_shapes=[
+            pltpu.VMEM((4, height, lanes), bf16),
+            pltpu.VMEM((4, height, lanes), bf16),
+            pltpu.VMEM((3, height, lanes), bf16),
+            pltpu.VMEM((3, height, lanes), bf16),
+            pltpu.VMEM((members, height, 2 * part), f32),
+            pltpu.VMEM((2, height, 2 * part), bf16),
+            pltpu.VMEM((*hops, height, 2 * part), bf16),
+            pltpu.VMEM((members, height, tall), bf16),
+            dma((4,)),
+            dma((4,)),
+            dma((4,)),
+            dma((4,)),
+            dma((4,)),
+        ]
+        + [dma(hops)] * 4,
+        compiler_params=pltpu.CompilerParams(collective_id=5, has_side_effects=True, vmem_limit_bytes=48 * 2**20),
+        cost_estimate=pl.CostEstimate(flops=8 * 10**10, bytes_accessed=10**7, transcendentals=0),
+        name="reduce_small",
+    )(parts)
+
+
 def pack(gate, up, down):
     def pair(a, b):
         return jnp.concatenate([a[..., :HD], b[..., :HD], a[..., HD:], b[..., HD:]], axis=-1)
@@ -452,21 +1074,36 @@
     return lax.ppermute(value, "dp", [(i, i ^ bit) for i in range(count)])
 
 
-def relative(values, me):
-    rows, width = values.shape
-    blocks = values.reshape(rows, 2, 2, 2 * (width // 8))
-    for axis, bit in ((1, 4), (2, 2)):
-        blocks = jnp.where((me & bit) != 0, jnp.flip(blocks, axis), blocks)
-    cut = width // 8
-    swapped = jnp.concatenate([blocks[..., cut:], blocks[..., :cut]], axis=-1)
-    blocks = jnp.where((me & 1) != 0, swapped, blocks)
-    return blocks.reshape(rows, width)
-
-
-def gather_step(waiting, arrived):
-    to_x = ([arrived[1][half_of(arrived[1])[1]]] if arrived else []) + ([waiting] if waiting is not None else [])
-    to_y = ([arrived[0][half_of(arrived[0])[0]]] if arrived else []) + ([waiting] if waiting is not None else [])
+def gather_step(fresh, arrived):
+    to_x = [from_y[half_of(from_y)[1]] for _, from_y in arrived] + fresh
+    to_y = [from_x[half_of(from_x)[0]] for from_x, _ in arrived] + fresh
     return flip(jnp.concatenate(to_x), 2), flip(jnp.concatenate(to_y), 4)
+
+
+def gather_chunks(packed):
+    size = packed[0].shape[0]
+    cut = size // 2
+    fresh, steps, near, far = [[packed[0], packed[1]], *([p] for p in packed[2:]), []], [], [], []
+    arrived = []
+    for chunks in fresh:
+        got = gather_step(chunks, arrived)
+        steps.append(got)
+        for i in range(len(arrived)):
+            far.append(tuple(side[cut * i : cut * (i + 1)] for side in got))
+        begin = cut * len(arrived)
+        arrived = [
+            tuple(side[begin + size * i : begin + size * (i + 1)] for side in got) for i in range(len(chunks))
+        ]
+        near += arrived
+    gathered = []
+    for own, (from_x, from_y), (second, first) in zip(packed, near, far):
+        gathered.append(
+            [
+                [(own, 0), (from_x, 0), (from_y, 0), (first, 0)],
+                [(own, cut), (from_x, cut), (from_y, cut), (second, 0)],
+            ]
+        )
+    return gathered, steps
 
 
 def half_of(chunk):
@@ -499,7 +1136,151 @@
     return (a.astype(f32) + b.astype(f32)).astype(bf16)
 
 
-def body(
+def routes_of(expert_ids, route_weights):
+    rows = expert_ids.shape[0]
+    lanes = jnp.arange(EXPERTS, dtype=jnp.int32)
+    named = expert_ids[:, :, None] == lanes
+    member_of = jnp.any(named, axis=1)
+    weight_of = jnp.sum(jnp.where(named, route_weights[:, :, None], 0.0), axis=1)
+    earlier = jnp.arange(rows)[:, None] > jnp.arange(rows)[None, :]
+    rank = jnp.where(member_of, nn(earlier.astype(bf16), member_of.astype(bf16)), -1.0)
+    rank_cols = jnp.pad(rank, ((0, 0), (0, HD)), constant_values=-1.0).astype(bf16)
+    rank_rows = rank.T.astype(jnp.int32).reshape(EXPERTS, 1, rows)
+    weight_rows = weight_of.T.reshape(EXPERTS, 1, rows)
+    return rank_cols, rank_rows, weight_rows
+
+
+def body_anywhere(
+    tokens,
+    expert_ids,
+    route_weights,
+    attn_gain,
+    q_weight,
+    k_weight,
+    v_weight,
+    o_weight,
+    moe_gain,
+    gate_weight,
+    up_weight,
+    down_weight,
+    cotangent,
+):
+    members = lax.axis_size("tensor")
+    member = lax.axis_index("tensor")
+    own_rows, width = tokens.shape
+    rows = own_rows * members
+    pairs = EXPERTS // 2
+    calls = pairs // CALL_PAIRS
+
+    packed = [
+        pack(*(w[:, 2 * CALL_PAIRS * i : 2 * CALL_PAIRS * (i + 1)] for w in (gate_weight, up_weight, down_weight)))
+        for i in range(calls)
+    ]
+    gathered = [[[(lax.all_gather(own, "dp", axis=1, tiled=True), 0)]] for own in packed]
+
+    gain_one = lax.all_gather(attn_gain, "dp", axis=0, tiled=True).astype(f32)
+    gain_two = lax.all_gather(moe_gain, "dp", axis=0, tiled=True).astype(f32)
+    kv_full = lax.all_gather(jnp.concatenate([k_weight, v_weight], axis=1), "dp", axis=0, tiled=True)
+    q_full = lax.all_gather(lax.all_gather(q_weight, "dp", axis=0, tiled=True), "tensor", axis=0)
+    o_full = lax.all_gather(lax.all_gather(o_weight, "dp", axis=0, tiled=True), "tensor", axis=0)
+    kv_width = k_weight.shape[1]
+
+    rank_cols, rank_rows, weight_rows = routes_of(expert_ids, route_weights)
+
+    grad_low = cotangent.astype(bf16)
+    grad_all = lax.all_gather(grad_low, "tensor", axis=0, tiled=True)
+
+    x = tokens.astype(f32)
+    inverse_one, unit_one = rms_pieces(x)
+    normed_one = (unit_one * gain_one).astype(bf16)
+    first_row = (member * own_rows).reshape(1)
+    cos_table, sin_table = rope_tables(member * own_rows + jnp.arange(own_rows, dtype=jnp.int32))
+    kv_own = nn(normed_one, kv_full)
+    kv_own = jnp.concatenate(
+        [rotate(kv_own[:, :kv_width], cos_table, sin_table), kv_own[:, kv_width:]], axis=1
+    ).astype(bf16)
+    kv_all = lax.all_gather(kv_own, "tensor", axis=0, tiled=True)
+    keys, values = kv_all[:, :kv_width], kv_all[:, kv_width:]
+    queries = jnp.concatenate([nn(normed_one, q_full[t]) for t in range(members)], axis=1)
+    queries = rotate(queries, cos_table, sin_table).astype(bf16)
+    mixed = attend_forward(first_row, queries, keys, values)
+    part = width // members
+    branch = sum(nt(mixed[:, t * part : (t + 1) * part], o_full[t]) for t in range(members))
+    hidden = x + branch
+    inverse_two, unit_two = rms_pieces(hidden)
+    normed_two = (unit_two * gain_two).astype(bf16)
+    rows_all = lax.all_gather(normed_two, "tensor", axis=0, tiled=True)
+
+    sums = jnp.zeros((rows, 2 * width), f32)
+    chunks = []
+    for call in range(calls):
+        some = slice(2 * CALL_PAIRS * call, 2 * CALL_PAIRS * (call + 1))
+        columns = slice(2 * CALL_PAIRS * call, 2 * CALL_PAIRS * call + HD)
+        grads, sums = expert_call(
+            rank_cols[:, columns],
+            rank_rows[some],
+            weight_rows[some],
+            rows_all,
+            grad_all,
+            gathered[call],
+            sums,
+            False,
+        )
+        chunks.append(grads)
+    shares = [
+        unpack(lax.psum_scatter(grads[0], "dp", scatter_dimension=1, tiled=True).astype(f32)) for grads in chunks
+    ]
+    gate_out, up_out, down_out = (jnp.concatenate(parts, axis=1) for parts in zip(*shares))
+
+    low_sums = sums.astype(bf16)
+    normed_grad = lax.psum_scatter(low_sums[:, width:], "tensor", scatter_dimension=0, tiled=True).astype(f32)
+    moe_own = lax.psum_scatter(low_sums[:, :width], "tensor", scatter_dimension=0, tiled=True).astype(f32)
+    output = (hidden + moe_own).astype(bf16)
+
+    back_two, gain_two_part = rms_backward(normed_grad, unit_two, inverse_two, gain_two)
+    hidden_grad = cotangent + back_two
+    hidden_low = hidden_grad.astype(bf16)
+    mixed_grad = jnp.concatenate([nn(hidden_low, o_full[t]) for t in range(members)], axis=1).astype(bf16)
+    o_part = jnp.stack([tn(hidden_low, mixed[:, t * part : (t + 1) * part]) for t in range(members)])
+    dq, dk, dv = attend_backward(first_row, queries, keys, values, mixed_grad)
+    kv_grad = lax.psum_scatter(
+        jnp.concatenate([dk, dv], axis=1).astype(bf16), "tensor", scatter_dimension=0, tiled=True
+    ).astype(f32)
+    dq_low = rotate(dq, cos_table, -sin_table).astype(bf16)
+    kv_low = jnp.concatenate(
+        [rotate(kv_grad[:, :kv_width], cos_table, -sin_table), kv_grad[:, kv_width:]], axis=1
+    ).astype(bf16)
+    normed_one_grad = nt(kv_low, kv_full) + sum(
+        nt(dq_low[:, t * part : (t + 1) * part], q_full[t]) for t in range(members)
+    )
+    back_one, gain_one_part = rms_backward(normed_one_grad, unit_one, inverse_one, gain_one)
+    tokens_grad = hidden_grad + back_one
+    q_part = jnp.stack([tn(normed_one, dq_low[:, t * part : (t + 1) * part]) for t in range(members)])
+    kv_part = tn(normed_one, kv_low)
+
+    def shared(values):
+        summed = lax.psum_scatter(values.astype(bf16), "tensor", scatter_dimension=0, tiled=False)
+        return lax.psum_scatter(summed, "dp", scatter_dimension=0, tiled=True).astype(f32)
+
+    q_grad, o_grad = shared(q_part), shared(o_part)
+    small = jnp.concatenate([kv_part, gain_one_part[:, None], gain_two_part[:, None]], axis=1)
+    small = lax.psum_scatter(small, "dp", scatter_dimension=0, tiled=True)
+    small = lax.psum(small.astype(bf16), "tensor").astype(f32)
+    return (
+        output,
+        tokens_grad,
+        small[:, 2 * kv_width],
+        q_grad,
+        small[:, :kv_width],
+        small[:, kv_width : 2 * kv_width],
+        o_grad,
+        small[:, 2 * kv_width + 1],
+        gate_out,
+        up_out,
+        down_out,
+    )
+
+def body_by_chips(
     tokens,
     expert_ids,
     route_weights,
@@ -517,80 +1298,29 @@
     members = lax.axis_size("tensor")
     member = lax.axis_index("tensor")
     devices = lax.axis_size("dp")
-    me = lax.axis_index("dp")
     own_rows, width = tokens.shape
     rows = own_rows * members
-    by_bits = devices == 8
-    pairs = EXPERTS // 2
-    calls = pairs // CALL_PAIRS
-    sub_pairs = CALL_PAIRS // 2
+    calls = EXPERTS // 2 // CALL_PAIRS
+    kv_width = k_weight.shape[1]
 
     packed = [
         pack(*(w[:, 2 * CALL_PAIRS * i : 2 * CALL_PAIRS * (i + 1)] for w in (gate_weight, up_weight, down_weight)))
         for i in range(calls)
     ]
-    if by_bits:
-        steps = [gather_step(packed[0], None)]
-        for i in range(calls):
-            arrived = tuple(got[-CALL_PAIRS:] for got in steps[i])
-            steps.append(gather_step(packed[i + 1] if i + 1 < calls else None, arrived))
-        gathered = []
-        for i in range(calls):
-            from_x, from_y = (got[-CALL_PAIRS:] for got in steps[i])
-            second, first = (got[:sub_pairs] for got in steps[i + 1])
-            gathered.append(
-                [
-                    [(packed[i], 0), (from_x, 0), (from_y, 0), (first, 0)],
-                    [(packed[i], sub_pairs), (from_x, sub_pairs), (from_y, sub_pairs), (second, 0)],
-                ]
-            )
-    else:
-        gathered = [[[(lax.all_gather(own, "dp", axis=1, tiled=True), 0)]] for own in packed]
-
-    gain_one = lax.all_gather(attn_gain, "dp", axis=0, tiled=True).astype(f32)
-    gain_two = lax.all_gather(moe_gain, "dp", axis=0, tiled=True).astype(f32)
-    kv_full = lax.all_gather(jnp.concatenate([k_weight, v_weight], axis=1), "dp", axis=0, tiled=True)
-    q_full = lax.all_gather(lax.all_gather(q_weight, "dp", axis=0, tiled=True), "tensor", axis=0)
-    o_full = lax.all_gather(lax.all_gather(o_weight, "dp", axis=0, tiled=True), "tensor", axis=0)
-    kv_width = k_weight.shape[1]
-
-    lanes = jnp.arange(EXPERTS, dtype=jnp.int32)
-    named = expert_ids[:, :, None] == lanes
-    member_of = jnp.any(named, axis=1)
-    weight_of = jnp.sum(jnp.where(named, route_weights[:, :, None], 0.0), axis=1)
-    earlier = jnp.arange(rows)[:, None] > jnp.arange(rows)[None, :]
-    rank = jnp.where(member_of, nn(earlier.astype(bf16), member_of.astype(bf16)), -1.0)
-    rank_cols = jnp.pad(rank, ((0, 0), (0, HD)), constant_values=-1.0).astype(bf16)
-    rank_rows = rank.T.astype(jnp.int32).reshape(EXPERTS, 1, rows)
-    weight_rows = weight_of.T.reshape(EXPERTS, 1, rows)
-
-    grad_low = cotangent.astype(bf16)
-    if by_bits:
-        grad_low = relative(grad_low, me)
-    grad_all = lax.all_gather(grad_low, "tensor", axis=0, tiled=True)
-
-    x = tokens.astype(f32)
-    inverse_one, unit_one = rms_pieces(x)
-    normed_one = (unit_one * gain_one).astype(bf16)
-    first_row = (member * own_rows).reshape(1)
+    gathered, steps = gather_chunks(packed)
+    square = jnp.concatenate([q_weight, o_weight], axis=1)
+    gains = jnp.stack([attn_gain, moe_gain], axis=1)
+    tall = jnp.concatenate([k_weight, v_weight, jnp.pad(gains, ((0, 0), (0, HD - 2)))], axis=1)
+    tall = after(tall, packed[:2])
+    square_all, tall_all, grad_all = gather_small(square, tall, cotangent, members, devices)
+
+    rank_cols, rank_rows, weight_rows = routes_of(expert_ids, route_weights)
     cos_table, sin_table = rope_tables(member * own_rows + jnp.arange(own_rows, dtype=jnp.int32))
-    kv_own = nn(normed_one, kv_full)
-    kv_own = jnp.concatenate(
-        [rotate(kv_own[:, :kv_width], cos_table, sin_table), kv_own[:, kv_width:]], axis=1
-    ).astype(bf16)
-    kv_all = lax.all_gather(kv_own, "tensor", axis=0, tiled=True)
-    keys, values = kv_all[:, :kv_width], kv_all[:, kv_width:]
-    queries = jnp.concatenate([nn(normed_one, q_full[t]) for t in range(members)], axis=1)
-    queries = rotate(queries, cos_table, sin_table).astype(bf16)
-    mixed = attend_forward(after(first_row, steps[0] if by_bits else ()), queries, keys, values)
-    part = width // members
-    branch = sum(nt(mixed[:, t * part : (t + 1) * part], o_full[t]) for t in range(members))
-    hidden = x + branch
-    inverse_two, unit_two = rms_pieces(hidden)
-    normed_two = (unit_two * gain_two).astype(bf16)
-    if by_bits:
-        normed_two = relative(normed_two, me)
-    rows_all = lax.all_gather(normed_two, "tensor", axis=0, tiled=True)
+    cosine = jnp.concatenate([cos_table, cos_table], axis=1)
+    sine = after(jnp.concatenate([-sin_table, sin_table], axis=1), steps[0])
+    normed_one, queries, kv_all, mixed, hidden, rows_all = attention_front(
+        tokens, square_all, tall_all, cosine, sine, members
+    )
 
     sums = jnp.zeros((rows, 2 * width), f32)
     chunks, moved = [], []
@@ -599,77 +1329,49 @@
         columns = slice(2 * CALL_PAIRS * call, 2 * CALL_PAIRS * call + HD)
         grads, sums = expert_call(
             rank_cols[:, columns],
-            after(rank_rows[some], moved[call - 2] if by_bits and call >= 2 else ()),
+            after(rank_rows[some], moved[call - 2] if call >= 2 else ()),
             weight_rows[some],
             rows_all,
             grad_all,
             gathered[call],
             sums,
-            by_bits,
+            True,
         )
         chunks.append(grads)
-        if by_bits:
-            moved.append(scatter_step(grads, before_of(chunks, moved, call)))
-    if by_bits:
-        moved.append(scatter_step(None, before_of(chunks, moved, calls)))
-        shares = []
-        for call in range(calls):
-            from_x, from_y = (got[:CALL_PAIRS].astype(f32) for got in moved[call + 1])
-            shares.append(unpack(chunks[call][0].astype(f32) + from_x + from_y))
-    else:
-        shares = [
-            unpack(lax.psum_scatter(grads[0], "dp", scatter_dimension=1, tiled=True).astype(f32))
-            for grads in chunks
-        ]
-    gate_out, up_out, down_out = (jnp.concatenate(parts, axis=1) for parts in zip(*shares))
-
-    low_sums = sums.astype(bf16)
-    normed_grad = lax.psum_scatter(low_sums[:, width:], "tensor", scatter_dimension=0, tiled=True).astype(f32)
-    moe_own = lax.psum_scatter(low_sums[:, :width], "tensor", scatter_dimension=0, tiled=True).astype(f32)
-    if by_bits:
-        normed_grad, moe_own = relative(normed_grad, me), relative(moe_own, me)
-    output = (hidden + moe_own).astype(bf16)
-
-    back_two, gain_two_part = rms_backward(normed_grad, unit_two, inverse_two, gain_two)
-    hidden_grad = cotangent + back_two
-    hidden_low = hidden_grad.astype(bf16)
-    mixed_grad = jnp.concatenate([nn(hidden_low, o_full[t]) for t in range(members)], axis=1).astype(bf16)
-    o_part = jnp.stack([tn(hidden_low, mixed[:, t * part : (t + 1) * part]) for t in range(members)])
-    dq, dk, dv = attend_backward(
-        after(first_row, moved[calls - 2] if by_bits else ()), queries, keys, values, mixed_grad
+        moved.append(scatter_step(grads, before_of(chunks, moved, call)))
+    moved.append(scatter_step(None, before_of(chunks, moved, calls)))
+
+    output, tokens_grad, parts = attention_back(
+        sums.astype(bf16),
+        cotangent,
+        hidden,
+        tokens,
+        normed_one,
+        queries,
+        kv_all,
+        mixed,
+        square_all,
+        tall_all,
+        cosine,
+        after(sine, moved[calls - 2]),
+        members,
     )
-    kv_grad = lax.psum_scatter(
-        jnp.concatenate([dk, dv], axis=1).astype(bf16), "tensor", scatter_dimension=0, tiled=True
-    ).astype(f32)
-    dq_low = rotate(dq, cos_table, -sin_table).astype(bf16)
-    kv_low = jnp.concatenate(
-        [rotate(kv_grad[:, :kv_width], cos_table, -sin_table), kv_grad[:, kv_width:]], axis=1
-    ).astype(bf16)
-    normed_one_grad = nt(kv_low, kv_full) + sum(
-        nt(dq_low[:, t * part : (t + 1) * part], q_full[t]) for t in range(members)
-    )
-    back_one, gain_one_part = rms_backward(normed_one_grad, unit_one, inverse_one, gain_one)
-    tokens_grad = hidden_grad + back_one
-    q_part = jnp.stack([tn(normed_one, dq_low[:, t * part : (t + 1) * part]) for t in range(members)])
-    kv_part = tn(normed_one, kv_low)
-
-    def shared(values):
-        summed = lax.psum_scatter(values.astype(bf16), "tensor", scatter_dimension=0, tiled=False)
-        return lax.psum_scatter(summed, "dp", scatter_dimension=0, tiled=True).astype(f32)
-
-    q_grad, o_grad = shared(q_part), shared(o_part)
-    small = jnp.concatenate([kv_part, gain_one_part[:, None], gain_two_part[:, None]], axis=1)
-    small = lax.psum_scatter(small, "dp", scatter_dimension=0, tiled=True)
-    small = lax.psum(small.astype(bf16), "tensor").astype(f32)
+    square_grad, tall_grad = reduce_small(parts, members, devices)
+    shares = []
+    for call in range(calls):
+        from_x, from_y = (got[:CALL_PAIRS].astype(f32) for got in moved[call + 1])
+        shares.append(unpack(chunks[call][0].astype(f32) + from_x + from_y))
+    gate_out, up_out, down_out = (jnp.concatenate(blocks, axis=1) for blocks in zip(*shares))
+    part = width // members
     return (
         output,
         tokens_grad,
-        small[:, 2 * kv_width],
-        q_grad,
-        small[:, :kv_width],
-        small[:, kv_width : 2 * kv_width],
-        o_grad,
-        small[:, 2 * kv_width + 1],
+        tall_grad[:, 2 * kv_width],
+        square_grad[:, :part],
+        tall_grad[:, :kv_width],
+        tall_grad[:, kv_width : 2 * kv_width],
+        square_grad[:, part:],
+        tall_grad[:, 2 * kv_width + 1],
         gate_out,
         up_out,
         down_out,
@@ -682,7 +1384,7 @@
     square = P("dp", "tensor")
     tall = P("dp", None)
     return jax.shard_map(
-        body,
+        body_by_chips if mesh.shape["dp"] == 8 else body_anywhere,
         mesh=mesh,
         in_specs=(
             rows, tall, tall, P("dp"), square, tall, tall, square, P("dp"), experts, experts, experts, rows

time: 1350 us -> 1030 us (0.76)
  waiting for transfers between devices: 614 us -> 74.2 us
  Pallas kernels: 304 us -> 730 us
  local copies, waits for them, and re-layouts: 227 us -> 138 us
  other arithmetic: 105 us -> 56.2 us
  matrix products: 31.1 us -> 1.4 us
  blocking collectives: 15.5 us -> 0 us
  between operations: 17.1 us -> 2.54 us
    pallas_call x2 -> x4, Pallas kernels: 29.5 us -> 456 us  [the longest x1 143 us: attention_back(): pl.pallas_call(kernel, in_specs=in_vmem(12), out_specs=in_vmem(2) + [pl.B...]
    ppermute x20 -> x18, waiting for transfers between devices: 293 us -> 74.2 us  [flip(): return lax.ppermute(value, 'dp', [(i, i ^ bit) for i in range(count)])]
    reduce_scatter x7 -> x0, waiting for transfers between devices: 209 us -> none  [the longest x2 78.1 us: shared(): lax.psum_scatter(values.astype(bf16), 'tensor', scatter_dimension=0, tile...]
    all_gather x8 -> x0, waiting for transfers between devices: 88.8 us -> none  [the longest x1 30.6 us: body(): rows_all = lax.all_gather(normed_two, 'tensor', axis=0, tiled=True)]
    rev x4 -> x0, local copies, waits for them, and re-layouts: 27.3 us -> none  [relative(): blocks = jnp.where(me & bit != 0, jnp.flip(blocks, axis), blocks)]
    select_n x12 -> x0, other arithmetic: 24.8 us -> none  [the longest x8 15.9 us: relative(): blocks = jnp.where(me & bit != 0, jnp.flip(blocks, axis), blocks)]
    dot_general x18 -> x0, matrix products: 20.9 us -> none  [the longest x9 15 us: nt(): lax.dot_general(a, b, (((1,), (1,)), ((), ())), preferred_element_type=f32)]
    psum x1 -> x0, waiting for transfers between devices: 20.7 us -> none  [body(): small = lax.psum(small.astype(bf16), 'tensor').astype(f32)]
  transfers between devices with their start and end apart: 37 -> 18, of which waited for: 21 -> 3; matrix products, arithmetic and copies ran while one was open for 20% -> 12% of each run, Pallas kernels for 16% -> 48%
where the time goes in v3:
time: 1030 us; the launch traced here: 1020 us
  Pallas kernels  730 us (71%)
  local copies, waits for them, and re-layouts  138 us (13%)
  waiting for transfers between devices  74.2 us (7%)
  other arithmetic  56.2 us (5%)
  starting transfers between devices  20.8 us (2%)
    pallas_call x4, Pallas kernels, expert_call(): pl.pallas_call(kernel, grid=(pairs + blocks,), in_specs=[pl.BlockSpec((ro...  274 us
    pallas_call x1, Pallas kernels, attention_back(): pl.pallas_call(kernel, in_specs=in_vmem(12), out_specs=in_vmem(2) + [pl.B...  143 us
    pallas_call x1, Pallas kernels, gather_small(): pl.pallas_call(kernel, in_specs=in_vmem(3), out_specs=in_vmem(3), out_sha...  128 us
    pallas_call x1, Pallas kernels, reduce_small(): pl.pallas_call(kernel, in_specs=[pl.BlockSpec(memory_space=pl.ANY)], out_...  92.9 us
    pallas_call x1, Pallas kernels, attention_front(): pl.pallas_call(kernel, in_specs=in_vmem(5), out_specs=in_vmem(6), out_sha...  91.8 us
    ppermute x18, waiting for transfers between devices, flip(): return lax.ppermute(value, 'dp', [(i, i ^ bit) for i in range(count)])  74.2 us
    unnamed x109, local copies, waits for them, and re-layouts  34.7 us
    ppermute x18, starting transfers between devices, flip(): return lax.ppermute(value, 'dp', [(i, i ^ bit) for i in range(count)])  20.8 us
  transfers between devices with their start and end apart: 18, of which 3 were waited for; matrix products, arithmetic and copies ran while one was open for 12% of the time, Pallas kernels for 48%

profile of v3, /device:TPU:0, one launch (start us, length us, event | category | flops | bytes accessed | tf_op | source)
XLA Modules:
  0.0 1023.5 jit_solution(14705485913667832086)
XLA Ops:
  0.6 3.2 fusion.33
  19.2 3.2 concatenate.160.refs_1_.rest_0_
  24.8 3.0 collective-permute-start.1
  34.8 128.1 %gather_small.1 = (bf16[4,1536,768]{2,1,0:T(8,128)(2,1)}, bf16[1536,640]{1,0:T(8,128)(2,1)S(1)}, bf16[1024,1536]{1,0:T(8,128)(2,1)S(1)}) custom-call(bf16[192,768]{1,0:T(8,128)(2,1)S(1)} %pad_maximum_fusion.32.square_ref, bf16[192,640]{1,0:T(8,128)(2,1)S(1)} %copy-done, f32[256,1536]{1,0:T(8,128)S(1)} %copy-done.1), custom_call_target="tpu_custom_call" | custom-call | flops 80000000000 | bytes 10000000 | tf_op jit(solution)/shard_map/gather_small/pallas_call | solution.py:682
  198.6 3.4 pad_maximum_fusion.3
  205.0 91.8 %attention_front.1 = (bf16[256,1536]{1,0:T(8,128)(2,1)}, bf16[256,1536]{1,0:T(8,128)(2,1)}, bf16[1024,512]{1,0:T(8,128)(2,1)}, bf16[256,1536]{1,0:T(8,128)(2,1)}...) custom-call(bf16[256,1536]{1,0:T(8,128)(2,1)} %x_ref.3, bf16[4,1536,768]{2,1,0:T(8,128)(2,1)} %get-tuple-element.33.square_ref, ...), custom_call_target="tpu_custom_call" | custom-call | flops 99999997952 | bytes 10000000 | tf_op jit(solution)/shard_map/attention_front/pallas_call | solution.py:770
  296.7 4.1 fusion.28
  300.8 4.0 fusion.29
  304.8 3.1 fusion.26
  308.0 3.1 fusion.27
  311.1 2.9 pad_maximum_fusion.6
  315.0 6.1 broadcast_in_dim.29.rest_5_
  321.1 68.4 %experts.4 = (bf16[4,4,192,1152]{3,2,1,0:T(8,128)(2,1)}, f32[1024,3072]{1,0:T(8,128)}) custom-call(bf16[1024,128]{1,0:T(8,128)(2,1)} %get-tuple-element.223.rank_c, s32[8,1,1024]{2,1,0:T(1,128)} %copy.141.rank_r, f32[8,1,1024]{2,1,0:T(1,128)} %copy.142.weight_r, bf16[1024,1536]{1,0:T(8,128)(2,1)} %get-tuple-element.35.x_ref, bf16[1024,1536]{1,0:T(8,128)(2,1)} %copy-done.2, ...), custom_call_target="tpu_custom_call" | custom-call | flops 73282879488 | bytes 37748736 | tf_op jit(solution)/shard_map/experts/pallas_call | solution.py:390
  389.6 3.4 slice_bitcast_fusion.12
  396.0 68.6 %experts.5 = (bf16[4,4,192,1152]{3,2,1,0:T(8,128)(2,1)}, f32[1024,3072]{1,0:T(8,128)}) custom-call(bf16[1024,128]{1,0:T(8,128)(2,1)} %get-tuple-element.224.rank_c, s32[8,1,1024]{2,1,0:T(1,128)} %copy.143.rank_r, f32[8,1,1024]{2,1,0:T(1,128)} %copy.144.weight_r, bf16[1024,1536]{1,0:T(8,128)(2,1)} %get-tuple-element.35.x_ref, bf16[1024,1536]{1,0:T(8,128)(2,1)} %copy-done.2, ...), custom_call_target="tpu_custom_call" | custom-call | flops 73282879488 | bytes 37748736 | tf_op jit(solution)/shard_map/experts/pallas_call | solution.py:390
  464.6 3.0 slice.910.rest_1_
  467.6 3.0 slice.911.rest_2_
  488.1 68.3 %experts.6 = (bf16[4,4,192,1152]{3,2,1,0:T(8,128)(2,1)}, f32[1024,3072]{1,0:T(8,128)}) custom-call(bf16[1024,128]{1,0:T(8,128)(2,1)} %get-tuple-element.222.rank_c, s32[8,1,1024]{2,1,0:T(1,128)} %after.8.rank_r, f32[8,1,1024]{2,1,0:T(1,128)} %copy.149.weight_r, bf16[1024,1536]{1,0:T(8,128)(2,1)} %get-tuple-element.35.x_ref, bf16[1024,1536]{1,0:T(8,128)(2,1)} %copy-done.2, ...), custom_call_target="tpu_custom_call" | custom-call | flops 73282879488 | bytes 37748736 | tf_op jit(solution)/shard_map/experts/pallas_call | solution.py:390
  556.5 3.0 slice.905.rest_2_
  559.5 3.0 slice.903.rest_1_
  564.0 3.1 fusion.9
  572.0 68.8 %experts.7 = (bf16[4,4,192,1152]{3,2,1,0:T(8,128)(2,1)}, f32[1024,3072]{1,0:T(8,128)}) custom-call(bf16[1024,128]{1,0:T(8,128)(2,1)} %get-tuple-element.225.rank_c, s32[8,1,1024]{2,1,0:T(1,128)} %after.7.rank_r, f32[8,1,1024]{2,1,0:T(1,128)} %slice.735.weight_r, bf16[1024,1536]{1,0:T(8,128)(2,1)} %get-tuple-element.35.x_ref, bf16[1024,1536]{1,0:T(8,128)(2,1)} %copy-done.2, ...), custom_call_target="tpu_custom_call" | custom-call | flops 73282879488 | bytes 37748736 | tf_op jit(solution)/shard_map/experts/pallas_call | solution.py:390
  640.8 3.1 fusion.4
  643.9 8.2 convert_element_type.184.sums_ref
  662.3 143.1 %attention_back.1 = (bf16[256,1536]{1,0:T(8,128)(2,1)}, f32[256,1536]{1,0:T(8,128)}, bf16[1536,3712]{1,0:T(8,128)(2,1)}) custom-call(bf16[1024,3072]{1,0:T(8,128)(2,1)} %convert_element_type.184.sums_ref, f32[256,1536]{1,0:T(8,128)} %cot_ref.3, f32[256,1536]{1,0:T(8,128)} %get-tuple-element.43.hidden_ref, bf16[256,1536]{1,0:T(8,128)(2,1)} %x_ref.3, ...), custom_call_target="tpu_custom_call" | custom-call | flops 99999997952 | bytes 10000000 | tf_op jit(solution)/shard_map/attention_back/pallas_call | solution.py:897
  805.5 92.9 %reduce_small.1 = (f32[192,768]{1,0:T(8,128)S(1)}, f32[192,640]{1,0:T(8,128)S(1)}) custom-call(bf16[1536,3712]{1,0:T(8,128)(2,1)} %get-tuple-element.51.parts_ref), custom_call_target="tpu_custom_call" | custom-call | flops 80000000000 | bytes 10000000 | tf_op jit(solution)/shard_map/reduce_small/pallas_call | solution.py:1013
  910.4 43.5 %collective-permute-done.14 = bf16[6,192,1152]{2,1,0:T(8,128)(2,1)S(1)} collective-permute-done((bf16[6,192,1152]{2,1,0:T(8,128)(2,1)S(1)}, bf16[6,192,1152]{2,1,0:T(8,128)(2,1)S(1)}, u32[]{:S(2)}, u32[]{:S(2)}) %collective-permute-start.14) | collective-permute-done | bytes 2654240 | tf_op jit(solution)/shard_map/ppermute | solution.py:1074
  953.9 4.1 collective-permute-done.15
  966.4 26.6 %collective-permute-done.17 = bf16[4,192,1152]{2,1,0:T(8,128)(2,1)} collective-permute-done((bf16[4,192,1152]{2,1,0:T(8,128)(2,1)S(1)}, bf16[4,192,1152]{2,1,0:T(8,128)(2,1)}, u32[]{:S(2)}, u32[]{:S(2)}) %collective-permute-start.17) | collective-permute-done | bytes 1769504 | tf_op jit(solution)/shard_map/ppermute | solution.py:1074
  999.4 6.3 copy.164
  1006.4 6.3 copy.163
  1013.8 6.3 copy.162
  (309 shorter events, 131.8 us)
Async XLA Ops:
  22.3 6.9 copy-start.34
  22.4 6.9 copy-start.35
  24.8 170.6 %collective-permute-start.1 = (bf16[8,192,1152]{2,1,0:T(8,128)(2,1)}, bf16[8,192,1152]{2,1,0:T(8,128)(2,1)}, u32[]{:S(2)}, u32[]{:S(2)}) collective-permute-start(bf16[8,192,1152]{2,1,0:T(8,128)(2,1)} %pad_maximum_fusion.5), channel_id=1, source_target_pairs={{0,16},{4,20},{8,24},{12,28},{16,0},{20,4},{24,8},{28,12},{1,17},{... | collective-permute-start | bytes 10616840 | tf_op jit(solution)/shard_map/ppermute | solution.py:1074
  27.7 169.2 %collective-permute-start = (bf16[8,192,1152]{2,1,0:T(8,128)(2,1)}, bf16[8,192,1152]{2,1,0:T(8,128)(2,1)}, u32[]{:S(2)}, u32[]{:S(2)}) collective-permute-start(bf16[8,192,1152]{2,1,0:T(8,128)(2,1)} %pad_maximum_fusion.5), channel_id=1, source_target_pairs={{0,8},{4,12},{8,0},{12,4},{16,24},{20,28},{24,16},{28,20},{1,9},{5... | collective-permute-start | bytes 10616840 | tf_op jit(solution)/shard_map/ppermute | solution.py:1074
  34.8 129.4 %copy-start.30 = (bf16[192,8,192]{2,1,0:T(8,128)(2,1)S(1)}, bf16[192,8,192]{2,1,0:T(8,128)(2,1)}, u32[]{:S(2)}) copy-start(bf16[192,8,192]{2,1,0:T(8,128)(2,1)} %get-tuple-element.184) | copy-start | bytes 1769476
  34.8 129.4 %copy-start.31 = (bf16[192,8,192]{2,1,0:T(8,128)(2,1)S(1)}, bf16[192,8,192]{2,1,0:T(8,128)(2,1)}, u32[]{:S(2)}) copy-start(bf16[192,8,192]{2,1,0:T(8,128)(2,1)} %get-tuple-element.185) | copy-start | bytes 1769476
  185.4 125.7 %copy-start.13 = (bf16[4,192,1152]{2,1,0:T(8,128)(2,1)}, bf16[4,192,1152]{2,1,0:T(8,128)(2,1)S(1)}, u32[]{:S(2)}) copy-start(bf16[4,192,1152]{2,1,0:T(8,128)(2,1)S(1)} %concatenate.173.rest_0_) | copy-start | bytes 5308420
  191.2 7.3 copy-start.9
  201.9 102.9 %collective-permute-start.3 = (bf16[8,192,1152]{2,1,0:T(8,128)(2,1)}, bf16[8,192,1152]{2,1,0:T(8,128)(2,1)}, u32[]{:S(2)}, u32[]{:S(2)}) collective-permute-start(bf16[8,192,1152]{2,1,0:T(8,128)(2,1)} %get-tuple-element.194), channel_id=1, source_target_pairs={{0,8},{4,12},{8,0},{12,4},{16,24},{20,28},{24,16},{28,20},{1,9},{5... | collective-permute-start | bytes 10616840 | tf_op jit(solution)/shard_map/ppermute | solution.py:1074
  203.4 104.5 %collective-permute-start.2 = (bf16[8,192,1152]{2,1,0:T(8,128)(2,1)}, bf16[8,192,1152]{2,1,0:T(8,128)(2,1)}, u32[]{:S(2)}, u32[]{:S(2)}) collective-permute-start(bf16[8,192,1152]{2,1,0:T(8,128)(2,1)} %get-tuple-element.195), channel_id=1, source_target_pairs={{0,16},{4,20},{8,24},{12,28},{16,0},{20,4},{24,8},{28,12},{1,17},{... | collective-permute-start | bytes 10616840 | tf_op jit(solution)/shard_map/ppermute | solution.py:1074
  313.9 165.6 %collective-permute-start.9 = (bf16[6,192,1152]{2,1,0:T(8,128)(2,1)}, bf16[6,192,1152]{2,1,0:T(8,128)(2,1)}, u32[]{:S(2)}, u32[]{:S(2)}) collective-permute-start(bf16[6,192,1152]{2,1,0:T(8,128)(2,1)} %get-tuple-element.192), channel_id=1, source_target_pairs={{0,16},{4,20},{8,24},{12,28},{16,0},{20,4},{24,8},{28,12},{1,17},{... | collective-permute-start | bytes 7962632 | tf_op jit(solution)/shard_map/ppermute | solution.py:1074
  314.5 169.4 %collective-permute-start.8 = (bf16[6,192,1152]{2,1,0:T(8,128)(2,1)}, bf16[6,192,1152]{2,1,0:T(8,128)(2,1)}, u32[]{:S(2)}, u32[]{:S(2)}) collective-permute-start(bf16[6,192,1152]{2,1,0:T(8,128)(2,1)} %get-tuple-element.193), channel_id=1, source_target_pairs={{0,8},{4,12},{8,0},{12,4},{16,24},{20,28},{24,16},{28,20},{1,9},{5... | collective-permute-start | bytes 7962632 | tf_op jit(solution)/shard_map/ppermute | solution.py:1074
  393.0 79.1 %collective-permute-start.6 = (bf16[2,192,1152]{2,1,0:T(8,128)(2,1)}, bf16[2,192,1152]{2,1,0:T(8,128)(2,1)S(1)}, u32[]{:S(2)}, u32[]{:S(2)}) collective-permute-start(bf16[2,192,1152]{2,1,0:T(8,128)(2,1)} %get-tuple-element.110), channel_id=1, source_target_pairs={{0,8},{4,12},{8,0},{12,4},{16,24},{20,28},{24,16},{28,20},{1,9},{5... | collective-permute-start | bytes 2654216 | tf_op jit(solution)/shard_map/ppermute | solution.py:1074
  394.5 77.7 %collective-permute-start.4 = (bf16[2,192,1152]{2,1,0:T(8,128)(2,1)S(1)}, bf16[2,192,1152]{2,1,0:T(8,128)(2,1)S(1)}, u32[]{:S(2)}, u32[]{:S(2)}) collective-permute-start(bf16[2,192,1152]{2,1,0:T(8,128)(2,1)S(1)} %get-tuple-element.112), channel_id=1, source_target_pairs={{0,16},{4,20},{8,24},{12,28},{16,0},{20,4},{24,8},{28,12},{1,17},{... | collective-permute-start | bytes 2654216 | tf_op jit(solution)/shard_map/ppermute | solution.py:1074
  476.6 87.4 %collective-permute-start.5 = (bf16[6,192,1152]{2,1,0:T(8,128)(2,1)}, bf16[6,192,1152]{2,1,0:T(8,128)(2,1)S(1)}, u32[]{:S(2)}, u32[]{:S(2)}) collective-permute-start(bf16[6,192,1152]{2,1,0:T(8,128)(2,1)} %pad_maximum_fusion.8), channel_id=1, source_target_pairs={{0,8},{4,12},{8,0},{12,4},{16,24},{20,28},{24,16},{28,20},{1,9},{5... | collective-permute-start | bytes 7962632 | tf_op jit(solution)/shard_map/ppermute | solution.py:1074
  479.0 85.0 %collective-permute-start.7 = (bf16[6,192,1152]{2,1,0:T(8,128)(2,1)}, bf16[6,192,1152]{2,1,0:T(8,128)(2,1)}, u32[]{:S(2)}, u32[]{:S(2)}) collective-permute-start(bf16[6,192,1152]{2,1,0:T(8,128)(2,1)} %pad_maximum_fusion.9), channel_id=1, source_target_pairs={{0,16},{4,20},{8,24},{12,28},{16,0},{20,4},{24,8},{28,12},{1,17},{... | collective-permute-start | bytes 7962632 | tf_op jit(solution)/shard_map/ppermute | solution.py:1074
  482.3 89.7 %collective-permute-start.11 = (bf16[2,192,1152]{2,1,0:T(8,128)(2,1)}, bf16[2,192,1152]{2,1,0:T(8,128)(2,1)}, u32[]{:S(2)}, u32[]{:S(2)}) collective-permute-start(bf16[2,192,1152]{2,1,0:T(8,128)(2,1)} %get-tuple-element.191), channel_id=1, source_target_pairs={{0,8},{4,12},{8,0},{12,4},{16,24},{20,28},{24,16},{28,20},{1,9},{5... | collective-permute-start | bytes 2654216 | tf_op jit(solution)/shard_map/ppermute | solution.py:1074
  486.6 85.4 %collective-permute-start.10 = (bf16[2,192,1152]{2,1,0:T(8,128)(2,1)}, bf16[2,192,1152]{2,1,0:T(8,128)(2,1)}, u32[]{:S(2)}, u32[]{:S(2)}) collective-permute-start(bf16[2,192,1152]{2,1,0:T(8,128)(2,1)} %get-tuple-element.189), channel_id=1, source_target_pairs={{0,16},{4,20},{8,24},{12,28},{16,0},{20,4},{24,8},{28,12},{1,17},{... | collective-permute-start | bytes 2654216 | tf_op jit(solution)/shard_map/ppermute | solution.py:1074
  569.0 91.8 %collective-permute-start.12 = (bf16[6,192,1152]{2,1,0:T(8,128)(2,1)}, bf16[6,192,1152]{2,1,0:T(8,128)(2,1)S(1)}, u32[]{:S(2)}, u32[]{:S(2)}) collective-permute-start(bf16[6,192,1152]{2,1,0:T(8,128)(2,1)} %pad_maximum_fusion.10), channel_id=1, source_target_pairs={{0,8},{4,12},{8,0},{12,4},{16,24},{20,28},{24,16},{28,20},{1,9},{5... | collective-permute-start | bytes 7962632 | tf_op jit(solution)/shard_map/ppermute | solution.py:1074
  571.5 89.3 %collective-permute-start.13 = (bf16[6,192,1152]{2,1,0:T(8,128)(2,1)}, bf16[6,192,1152]{2,1,0:T(8,128)(2,1)}, u32[]{:S(2)}, u32[]{:S(2)}) collective-permute-start(bf16[6,192,1152]{2,1,0:T(8,128)(2,1)} %pad_maximum_fusion.11), channel_id=1, source_target_pairs={{0,16},{4,20},{8,24},{12,28},{16,0},{20,4},{24,8},{28,12},{1,17},{... | collective-permute-start | bytes 7962632 | tf_op jit(solution)/shard_map/ppermute | solution.py:1074
  805.5 92.9 %copy-start.7 = (bf16[6,192,1152]{2,1,0:T(8,128)(2,1)S(1)}, bf16[6,192,1152]{2,1,0:T(8,128)(2,1)}, u32[]{:S(2)}) copy-start(bf16[6,192,1152]{2,1,0:T(8,128)(2,1)} %copy-done.6) | copy-start | bytes 7962628
  805.5 92.9 %copy-start.11 = (bf16[4,4,192,1152]{3,2,1,0:T(8,128)(2,1)S(1)}, bf16[4,4,192,1152]{3,2,1,0:T(8,128)(2,1)}, u32[]{:S(2)}) copy-start(bf16[4,4,192,1152]{3,2,1,0:T(8,128)(2,1)} %get-tuple-element.48) | copy-start | bytes 21233668
  900.6 53.3 %collective-permute-start.14 = (bf16[6,192,1152]{2,1,0:T(8,128)(2,1)S(1)}, bf16[6,192,1152]{2,1,0:T(8,128)(2,1)S(1)}, u32[]{:S(2)}, u32[]{:S(2)}) collective-permute-start(bf16[6,192,1152]{2,1,0:T(8,128)(2,1)S(1)} %pad_maximum_fusion.12), channel_id=1, source_target_pairs={{0,8},{4,12},{8,0},{12,4},{16,24},{20,28},{24,16},{28,20},{1,9},{5... | collective-permute-start | bytes 7962632 | tf_op jit(solution)/shard_map/ppermute | solution.py:1074
  902.0 55.9 %collective-permute-start.15 = (bf16[6,192,1152]{2,1,0:T(8,128)(2,1)S(1)}, bf16[6,192,1152]{2,1,0:T(8,128)(2,1)}, u32[]{:S(2)}, u32[]{:S(2)}) collective-permute-start(bf16[6,192,1152]{2,1,0:T(8,128)(2,1)S(1)} %pad_maximum_fusion.13), channel_id=1, source_target_pairs={{0,16},{4,20},{8,24},{12,28},{16,0},{20,4},{24,8},{28,12},{1,17},{... | collective-permute-start | bytes 7962632 | tf_op jit(solution)/shard_map/ppermute | solution.py:1074
  907.3 50.6 %slice-start.2 = ((s8[7077888]{0:T(1024)(128)(4,1)}), s8[4194304]{0:T(1024)(128)(4,1)S(1)}, s32[]{:S(2)}) async-start(s8[7077888]{0:T(1024)(128)(4,1)} %bitcast.196), calls=%async_computation.2 | async-start | bytes 8388608
  907.6 50.3 %slice-start.3 = ((s8[7077888]{0:T(1024)(128)(4,1)}), s8[2883584]{0:T(1024)(128)(4,1)S(1)}, s32[]{:S(2)}) async-start(s8[7077888]{0:T(1024)(128)(4,1)} %bitcast.196), calls=%async_computation.3 | async-start | bytes 5767168
  910.4 49.1 %copy-start.18 = (bf16[2,192,1152]{2,1,0:T(8,128)(2,1)S(1)}, bf16[2,192,1152]{2,1,0:T(8,128)(2,1)}, u32[]{:S(2)}) copy-start(bf16[2,192,1152]{2,1,0:T(8,128)(2,1)} %get-tuple-element.91) | copy-start | bytes 2654212
  959.7 33.3 %collective-permute-start.17 = (bf16[4,192,1152]{2,1,0:T(8,128)(2,1)S(1)}, bf16[4,192,1152]{2,1,0:T(8,128)(2,1)}, u32[]{:S(2)}, u32[]{:S(2)}) collective-permute-start(bf16[4,192,1152]{2,1,0:T(8,128)(2,1)S(1)} %pad_maximum_fusion.15), channel_id=1, source_target_pairs={{0,16},{4,20},{8,24},{12,28},{16,0},{20,4},{24,8},{28,12},{1,17},{... | collective-permute-start | bytes 5308424 | tf_op jit(solution)/shard_map/ppermute | solution.py:1074
  961.4 31.7 %collective-permute-start.16 = (bf16[4,192,1152]{2,1,0:T(8,128)(2,1)S(1)}, bf16[4,192,1152]{2,1,0:T(8,128)(2,1)}, u32[]{:S(2)}, u32[]{:S(2)}) collective-permute-start(bf16[4,192,1152]{2,1,0:T(8,128)(2,1)S(1)} %pad_maximum_fusion.14), channel_id=1, source_target_pairs={{0,8},{4,12},{8,0},{12,4},{16,24},{20,28},{24,16},{28,20},{1,9},{5... | collective-permute-start | bytes 5308424 | tf_op jit(solution)/shard_map/ppermute | solution.py:1074
  999.4 6.4 copy-start.15
  1006.4 6.4 copy-start.16
  1013.8 6.4 copy-start.39
  (38 other events, 94.4 us)

commit v4 on v3

--- a/solution.py
+++ b/solution.py
@@ -1,5 +1,6 @@
 import jax
 import jax.numpy as jnp
+import numpy as np
 from jax import lax
 from jax.experimental import pallas as pl
 from jax.experimental.pallas import tpu as pltpu
@@ -175,11 +176,11 @@
     return me + 1 - 2 * lax.rem(me, 2)
 
 
-def expert_call(rank_cols, rank_rows, weight_rows, x, gy, pieces, sums, exchange):
+def expert_call(rank_cols, routes, x, gy, pieces, sums, exchange):
     rows, width = x.shape
     subs, count = len(pieces), len(pieces[0])
     height, lanes = pieces[0][0][0].shape[1:]
-    pairs = rank_rows.shape[0] // 2
+    pairs = routes.shape[0] // 2
     sub_pairs = pairs // subs
     blocks = 12
     tile = 2 * width // blocks
@@ -195,7 +196,7 @@
     third = lanes // 3
     stride = 2 if exchange else 1
 
-    def kernel(rank_c, rank_r, weight_r, x_ref, gy_ref, *rest):
+    def kernel(rank_c, routes_ref, x_ref, gy_ref, *rest):
         w_hbm = rest[: len(flat)]
         rest = rest[len(flat) :]
         sums_in, rest = rest[0], rest[1:]
@@ -302,9 +303,9 @@
                 slot_of = lax.broadcasted_iota(jnp.int32, (rows, CAP), 1).astype(f32)
                 at = pl.ds(pl.multiple_of(e * CAP, CAP), CAP)
                 pick_buf[:, at] = (rank == slot_of).astype(bf16)
-                hit = lax.broadcasted_iota(jnp.int32, (CAP, rows), 0) == rank_r[q]
+                hit = lax.broadcasted_iota(jnp.int32, (CAP, rows), 0).astype(f32) == routes_ref[q, 0:1]
                 pick = hit.astype(bf16)
-                weight = jnp.sum(jnp.where(hit, weight_r[q], 0.0), axis=1, keepdims=True)
+                weight = jnp.sum(jnp.where(hit, routes_ref[q, 1:2], 0.0), axis=1, keepdims=True)
                 xe = nn(pick, x_ref[...]).astype(bf16)
                 deo = (nn(pick, gy_ref[...]) * weight).astype(bf16)
                 gate_up = slice(q * third, (q + 1) * third)
@@ -372,7 +373,7 @@
 
     once = pl.Buffered(1)
     whole = pl.BlockSpec((rows, width), lambda s: (0, 0), pipeline_mode=once)
-    routes = pl.BlockSpec((2, 1, rows), lambda s: (held(s), 0, 0))
+    of_pair = pl.BlockSpec((2, 2, rows), lambda s: (held(s), 0, 0))
     anywhere = pl.BlockSpec(memory_space=pl.ANY)
     dma = pltpu.SemaphoreType.DMA
     traded = [
@@ -390,7 +391,7 @@
     return pl.pallas_call(
         kernel,
         grid=(pairs + blocks,),
-        in_specs=[pl.BlockSpec((rows, HD), lambda s: (0, 0), pipeline_mode=once), routes, routes, whole, whole]
+        in_specs=[pl.BlockSpec((rows, HD), lambda s: (0, 0), pipeline_mode=once), of_pair, whole, whole]
         + [anywhere] * len(flat)
         + [pl.BlockSpec((rows, tile), block)],
         out_specs=[
@@ -415,7 +416,7 @@
             transcendentals=0,
         ),
         name="experts",
-    )(rank_cols, rank_rows, weight_rows, x, gy, *flat, sums)
+    )(rank_cols, routes, x, gy, *flat, sums)
 
 
 def remote(source, target, send_sem, recv_sem, device):
@@ -434,7 +435,7 @@
     return me + 2 - 4 * lax.rem(me // 2, 2), me + 4 - 8 * lax.rem(me // 4, 2)
 
 
-def meet(members, chips):
+def meet(members, core):
     barrier = pltpu.get_barrier_semaphore()
     z = lax.axis_index("tensor")
 
@@ -449,11 +450,10 @@
     def _():
         signal({"tensor": z + 1})
 
-    if chips:
-        for other in (*chip_neighbours(), sibling()):
-            signal({"dp": other})
+    for other in (*chip_neighbours(), *([sibling()] if core else [])):
+        signal({"dp": other})
     inner = jnp.where((z > 0) & (z < members - 1), 1, 0)
-    pl.semaphore_wait(barrier, 1 + inner + (3 if chips else 0))
+    pl.semaphore_wait(barrier, 3 + inner + (1 if core else 0))
 
 
 class LineGather:
@@ -583,48 +583,88 @@
     return [pl.BlockSpec(memory_space=pltpu.VMEM)] * count
 
 
-def gather_small(square, tall, cotangent, members, devices):
-    height = square.shape[0]
+def pack_chunk(gate, up, down, begin):
+    gate, up, down = (
+        jnp.swapaxes(w[:, begin : begin + 2 * CALL_PAIRS, :], 0, 1) for w in (gate, up, down)
+    )
+
+    def pair(a, b):
+        return [a[:, :HD], b[:, :HD], jnp.concatenate([a[:, HD:], b[:, HD:]], axis=1)]
+
+    return [
+        jnp.concatenate(
+            pair(gate[e], up[e]) + pair(gate[e + 1], up[e + 1]) + pair(down[e], down[e + 1]), axis=1
+        )
+        for e in range(0, 2 * CALL_PAIRS, 2)
+    ]
+
+
+def gather_small(
+    q_weight, o_weight, k_weight, v_weight, gains, cotangent, ids, route_weights, gate, up, down, members, devices
+):
+    height, part = q_weight.shape
     own_rows, width = cotangent.shape
+    rows = own_rows * members
+    kv = k_weight.shape[1]
+    tall = 2 * kv + HD
+    lanes = 9 * HD
+    calls = EXPERTS // 2 // CALL_PAIRS
     dma = pltpu.SemaphoreType.DMA
-    cut = square.shape[1] // 2
-
-    def kernel(square_ref, tall_ref, cot_ref, square_all, tall_all, grad_all, *sems):
+    cut = part
+
+    def kernel(*refs):
+        q_ref, o_ref, k_ref, v_ref, gains_ref, cot_ref, ids_ref, weights_ref, gate_ref, up_ref, down_ref = refs[:11]
+        square_all, tall_all, grad_all = refs[11:14]
+        rank_cols, routes, packed = (refs[14 + calls * i : 14 + calls * (i + 1)] for i in range(3))
+        from_x, from_y = refs[14 + 3 * calls : 16 + 3 * calls]
+        sems = refs[16 + 3 * calls :]
         line_send, line_recv, grad_send, grad_recv, chip_send, chip_recv, core_send, core_recv = sems
         me, z = lax.axis_index("dp"), lax.axis_index("tensor")
         x_side, y_side = chip_neighbours()
         core = sibling()
-        meet(members, True)
-
-        def rows(device):
+
+        def rows_of(device):
             return pl.ds(pl.multiple_of(device * height, 16), height)
 
-        square_all[z, rows(me), :] = square_ref[...]
-        tall_all[rows(me), :] = tall_ref[...]
-        line = LineGather(members, lambda block: square_all.at[block, rows(me)], line_send, line_recv)
+        def pack(call):
+            chunk = pack_chunk(gate_ref, up_ref, down_ref, 2 * CALL_PAIRS * call)
+            for pair, value in enumerate(chunk):
+                packed[call][pair] = value
+
+        def chip(index, source, device, target=None):
+            target = source if target is None else target
+            return remote(source, target, chip_send.at[index], chip_recv.at[index], {"dp": device})
+
+        def across(index, source):
+            return remote(source, source, core_send.at[index], core_recv.at[index], {"dp": core})
+
+        def tall_at(device):
+            return tall_all.at[rows_of(device)]
+
+        def square_at(device, half=None):
+            span = slice(None) if half is None else slice(half * cut, (half + 1) * cut)
+            return square_all.at[:, rows_of(device), span]
+
+        square_all[z, rows_of(me), :part] = q_ref[...]
+        square_all[z, rows_of(me), part:] = o_ref[...]
+        tall_all[rows_of(me), :kv] = k_ref[...]
+        tall_all[rows_of(me), kv : 2 * kv] = v_ref[...]
+        tall_all[rows_of(me), 2 * kv :] = gains_ref[...]
+        line = LineGather(members, lambda block: square_all.at[block, rows_of(me)], line_send, line_recv)
         group = LineGather(
             members,
             lambda block: grad_all.at[pl.ds(pl.multiple_of(block * own_rows, 16), own_rows)],
             grad_send,
             grad_recv,
         )
-
-        def chip(index, source, device):
-            return remote(source, source, chip_send.at[index], chip_recv.at[index], {"dp": device})
-
-        def across(index, source):
-            return remote(source, source, core_send.at[index], core_recv.at[index], {"dp": core})
-
-        def tall_at(device):
-            return tall_all.at[rows(device)]
-
-        def square_at(device, half=None):
-            lanes = slice(None) if half is None else slice(half * cut, (half + 1) * cut)
-            return square_all.at[:, rows(device), lanes]
-
+        meet(members, True)
         line.start(1)
         near = [chip(0, tall_at(me), x_side), chip(1, tall_at(me), y_side)]
         for copy in near:
+            copy.start()
+        pack(0)
+        chunk = [chip(7, packed[0], x_side, from_x), chip(8, packed[0], y_side, from_y)]
+        for copy in chunk:
             copy.start()
         grad_all[pl.ds(pl.multiple_of(z * own_rows, 16), own_rows), :] = swap_blocks(cot_ref[...]).astype(bf16)
         for hop in range(1, members):
@@ -646,6 +686,28 @@
         trades += [across(2, tall_at(x_side)), across(3, tall_at(y_side))]
         for copy in trades[2:]:
             copy.start()
+
+        lane = lax.broadcasted_iota(jnp.int32, (rows, HD), 1)
+        weight = jnp.zeros((rows, HD), f32)
+        named = jnp.zeros((rows, HD), f32)
+        for route in range(ids_ref.shape[1]):
+            here = ids_ref[:, route : route + 1] == lane
+            named = jnp.where(here, 1.0, named)
+            weight = jnp.where(here, weights_ref[:, route : route + 1], weight)
+        row = lax.broadcasted_iota(jnp.int32, (rows, rows), 0)
+        earlier = (row > lax.broadcasted_iota(jnp.int32, (rows, rows), 1)).astype(bf16)
+        rank = jnp.where(named > 0.0, nn(earlier, named.astype(bf16)), -1.0)
+        by_rank, by_weight = jnp.transpose(rank), jnp.transpose(weight)
+        for call in range(calls):
+            turned = rank if call == 0 else pltpu.roll(rank, HD - 2 * CALL_PAIRS * call, 1)
+            rank_cols[call][...] = turned.astype(bf16)
+            for e in range(2 * CALL_PAIRS):
+                at = 2 * CALL_PAIRS * call + e
+                routes[call][e, 0:1, :] = by_rank[at : at + 1]
+                routes[call][e, 1:2, :] = by_weight[at : at + 1]
+        for call in range(1, calls):
+            pack(call)
+
         group.arrive(1)
         if members > 2:
             group.start(2)
@@ -674,25 +736,31 @@
             across(index, source).wait_recv()
         if members > 2:
             group.arrive(members - 1)
+        for copy in chunk:
+            copy.wait()
         for copy in near + far + trades:
             copy.wait_send()
         line.close()
         group.close()
 
+    chunk_shape = jax.ShapeDtypeStruct((CALL_PAIRS, height, lanes), bf16)
     return pl.pallas_call(
         kernel,
-        in_specs=in_vmem(3),
-        out_specs=in_vmem(3),
+        in_specs=in_vmem(11),
+        out_specs=in_vmem(3 + 3 * calls) + [pl.BlockSpec(memory_space=pl.ANY)] * 2,
         out_shape=[
-            jax.ShapeDtypeStruct((members, devices * height, square.shape[1]), bf16),
-            jax.ShapeDtypeStruct((devices * height, tall.shape[1]), bf16),
-            jax.ShapeDtypeStruct((members * own_rows, width), bf16),
-        ],
-        scratch_shapes=[dma((2, members - 1))] * 4 + [dma((7,))] * 2 + [dma((8,))] * 2,
-        compiler_params=pltpu.CompilerParams(collective_id=2, has_side_effects=True, vmem_limit_bytes=40 * 2**20),
+            jax.ShapeDtypeStruct((members, devices * height, 2 * part), bf16),
+            jax.ShapeDtypeStruct((devices * height, tall), bf16),
+            jax.ShapeDtypeStruct((rows, width), bf16),
+        ]
+        + [jax.ShapeDtypeStruct((rows, HD), bf16)] * calls
+        + [jax.ShapeDtypeStruct((2 * CALL_PAIRS, 2, rows), f32)] * calls
+        + [chunk_shape] * (calls + 2),
+        scratch_shapes=[dma((2, members - 1))] * 4 + [dma((9,))] * 2 + [dma((8,))] * 2,
+        compiler_params=pltpu.CompilerParams(collective_id=2, has_side_effects=True, vmem_limit_bytes=56 * 2**20),
         cost_estimate=pl.CostEstimate(flops=8 * 10**10, bytes_accessed=10**7, transcendentals=0),
         name="gather_small",
-    )(square, tall, cotangent)
+    )(q_weight, o_weight, k_weight, v_weight, gains, cotangent, ids, route_weights, gate, up, down)
 
 
 def turn(values, cosine, sine):
@@ -703,7 +771,7 @@
     return jnp.transpose(tall_ref[:, kv:].astype(f32))
 
 
-def attention_front(tokens, square, tall, cosine, sine, members):
+def attention_front(tokens, square, tall, cosine, sine, packed, near, members):
     own_rows, width = tokens.shape
     rows = own_rows * members
     kv = 2 * KV * HD
@@ -713,9 +781,32 @@
     dma = pltpu.SemaphoreType.DMA
 
     def kernel(x_ref, square_ref, tall_ref, cos_ref, sin_ref, *rest):
-        normed_ref, q_ref, kv_all, mixed_ref, hidden_ref, rows_all = rest[:6]
-        kv_send, kv_recv, row_send, row_recv = rest[6:]
+        chunks, rest = rest[:count], rest[count:]
+        normed_ref, q_ref, kv_all, mixed_ref, hidden_ref, rows_all, sums_ref = rest[:7]
+        landed, rest = rest[7 : 5 + 2 * count], rest[5 + 2 * count :]
+        blank, kv_send, kv_recv, row_send, row_recv, chip_send, chip_recv, blank_sem = rest
         z = lax.axis_index("tensor")
+        x_side, y_side = chip_neighbours()
+        meet(members, False)
+        pairs = chunks[0].shape[0]
+        first, second = slice(0, pairs // 2), slice(pairs // 2, pairs)
+        moves = [(chunks[0].at[first], y_side), (chunks[1].at[second], x_side)]
+        for chunk in chunks[2:]:
+            moves += [(chunk, x_side), (chunk, y_side)]
+        moves = [
+            remote(source, landed[i], chip_send.at[i], chip_recv.at[i], {"dp": device})
+            for i, (source, device) in enumerate(moves)
+        ]
+        for copy in moves:
+            copy.start()
+        blank[...] = jnp.zeros_like(blank)
+        fills = [
+            pltpu.make_async_copy(blank, sums_ref.at[b * own_rows : (b + 1) * own_rows, s * width : (s + 1) * width], blank_sem.at[b, s])
+            for b in range(members)
+            for s in range(2)
+        ]
+        for copy in fills:
+            copy.start()
 
         def block_of(ref):
             return lambda block: ref.at[pl.ds(pl.multiple_of(block * own_rows, 16), own_rows)]
@@ -726,13 +817,12 @@
         gains = gain_rows(tall_ref, kv)
         x = x_ref[...].astype(f32)
         normed_ref[...] = (rms_pieces(x)[1] * gains[0:1]).astype(bf16)
-        cosine, sine = cos_ref[...], sin_ref[...]
+        cosine, sine = cos_ref[own], sin_ref[own]
         made = nn(normed_ref[...], tall_ref[:, :kv])
         for head in range(KV):
             span = slice(head * HD, (head + 1) * HD)
             kv_all[own, span] = turn(made[:, span], cosine, sine).astype(bf16)
         kv_all[own, KV * HD :] = made[:, KV * HD :].astype(bf16)
-        meet(members, False)
         kv_line.start(1)
         for t in range(members):
             made = nn(normed_ref[...], square_ref[t, :, :part])
@@ -745,14 +835,14 @@
                 kv_line.arrive(t + 1)
                 if t + 2 < members:
                     kv_line.start(t + 2)
-        first = z * own_rows
+        first_row = z * own_rows
 
         @pl.loop(0, heads)
         def _(head):
             span = pl.ds(pl.multiple_of(head * HD, HD), HD)
             key_span = pl.ds(pl.multiple_of(head // per_kv * HD, HD), HD)
             value_span = pl.ds(pl.multiple_of((KV + head // per_kv) * HD, HD), HD)
-            p = probabilities(q_ref[:, span], kv_all[:, key_span], first).astype(bf16)
+            p = probabilities(q_ref[:, span], kv_all[:, key_span], first_row).astype(bf16)
             mixed_ref[:, span] = nn(p, kv_all[:, value_span]).astype(bf16)
 
         hidden = x_ref[...].astype(f32)
@@ -766,11 +856,18 @@
             row_line.arrive(hop)
         kv_line.close()
         row_line.close()
-
+        for copy in moves:
+            copy.wait()
+        for copy in fills:
+            copy.wait()
+
+    count = 2 + len(packed)
+    anywhere = pl.BlockSpec(memory_space=pl.ANY)
+    size, height, lanes = near[0].shape
     return pl.pallas_call(
         kernel,
-        in_specs=in_vmem(5),
-        out_specs=in_vmem(6),
+        in_specs=in_vmem(5) + [anywhere] * count,
+        out_specs=in_vmem(6) + [anywhere] * (1 + 2 + 2 * len(packed)),
         out_shape=[
             jax.ShapeDtypeStruct((own_rows, width), bf16),
             jax.ShapeDtypeStruct((own_rows, width), bf16),
@@ -778,15 +875,23 @@
             jax.ShapeDtypeStruct((own_rows, width), bf16),
             jax.ShapeDtypeStruct((own_rows, width), f32),
             jax.ShapeDtypeStruct((rows, width), bf16),
-        ],
-        scratch_shapes=[dma((2, members - 1))] * 4,
+            jax.ShapeDtypeStruct((rows, 2 * width), f32),
+        ]
+        + [jax.ShapeDtypeStruct((size // 2, height, lanes), bf16)] * 2
+        + [jax.ShapeDtypeStruct((size, height, lanes), bf16)] * (2 * len(packed)),
+        scratch_shapes=[pltpu.VMEM((own_rows, width), f32)]
+        + [dma((2, members - 1))] * 4
+        + [dma((2 + 2 * len(packed),))] * 2
+        + [dma((members, 2))],
         compiler_params=pltpu.CompilerParams(collective_id=3, has_side_effects=True, vmem_limit_bytes=56 * 2**20),
         cost_estimate=pl.CostEstimate(flops=10**11, bytes_accessed=10**7, transcendentals=0),
         name="attention_front",
-    )(tokens, square, tall, cosine, sine)
-
-
-def attention_back(sums, cotangent, hidden, tokens, normed, q, kv_all, mixed, square, tall, cosine, sine, members):
+    )(tokens, square, tall, cosine, sine, *near, *packed)
+
+
+def attention_back(
+    sums, cotangent, hidden, tokens, normed, q, kv_all, mixed, square, tall, cosine, sine, last_chunk, to_x, to_y, members
+):
     own_rows, width = tokens.shape
     rows = own_rows * members
     kv = 2 * KV * HD
@@ -796,22 +901,54 @@
     dma = pltpu.SemaphoreType.DMA
 
     def kernel(sums_ref, cot_ref, hidden_ref, x_ref, normed_ref, q_ref, kv_ref, mixed_ref, square_ref, tall_ref, *rest):
-        cos_ref, sin_ref = rest[:2]
-        out_ref, grad_ref, parts = rest[2:5]
-        do_ref, dq_ref, dkv_ref, total, kv_total, stage, tall_part = rest[5:12]
-        back_leave, back_arrive, moe_leave, moe_arrive, kv_leave, kv_arrive = rest[12:18]
-        back_send, back_recv, moe_send, moe_recv, kv_send, kv_recv, stage_sem = rest[18:]
+        cos_ref, sin_ref, chunk, to_x_ref, to_y_ref = rest[:5]
+        grad_ref, parts, x_before, y_before, x_last, y_last = rest[5:11]
+        do_ref, dq_ref, dkv_ref, total, kv_total, stage, tall_part, back_part = rest[11:19]
+        back_leave, back_arrive, kv_leave, kv_arrive = rest[19:23]
+        back_send, back_recv, kv_send, kv_recv, stage_sem, part_sem = rest[23:29]
+        through, added, added_sem, chip_send, chip_recv = rest[29:]
         z = lax.axis_index("tensor")
+        x_side, y_side = chip_neighbours()
+        first, second = slice(0, size // 2), slice(size // 2, size)
+
+        def chip(index, source, target, device):
+            return remote(source, target, chip_send.at[index], chip_recv.at[index], {"dp": device})
+
+        loads = [
+            pltpu.make_async_copy(
+                sums_ref.at[b * own_rows : (b + 1) * own_rows, width:], back_part.at[b], part_sem.at[b]
+            )
+            for b in range(members)
+        ] + [
+            pltpu.make_async_copy(chunk.at[1, second], added.at[0], added_sem.at[0]),
+            pltpu.make_async_copy(chunk.at[2, first], added.at[1], added_sem.at[1]),
+        ]
+        for copy in loads:
+            copy.start()
+        meet(members, False)
+        moves = [
+            chip(0, chunk.at[3, first], through.at[0], x_side),
+            chip(1, chunk.at[3, second], through.at[1], y_side),
+            chip(2, to_x_ref, x_before, x_side),
+            chip(3, to_y_ref, y_before, y_side),
+            chip(4, chunk.at[1, first], x_last.at[first], x_side),
+            chip(5, chunk.at[2, second], y_last.at[second], y_side),
+            chip(6, added.at[0], x_last.at[second], x_side),
+            chip(7, added.at[1], y_last.at[first], y_side),
+        ]
+        for copy in moves[:6]:
+            copy.start()
+        own = pl.ds(pl.multiple_of(z * own_rows, 16), own_rows)
+        for copy in loads:
+            copy.wait()
 
         def block(ref, span):
             return lambda b: ref[pl.ds(pl.multiple_of(b * own_rows, 16), own_rows), span]
 
-        back = LineSum(members, block(sums_ref, slice(width, 2 * width)), back_leave, back_arrive, back_send, back_recv)
-        moe = LineSum(members, block(sums_ref, slice(0, width)), moe_leave, moe_arrive, moe_send, moe_recv)
+        back = LineSum(members, lambda b: back_part[b], back_leave, back_arrive, back_send, back_recv)
         pairs = LineSum(members, block(dkv_ref, slice(None)), kv_leave, kv_arrive, kv_send, kv_recv)
-        meet(members, False)
         gains = gain_rows(tall_ref, kv)
-        cosine, sine = cos_ref[...], sin_ref[...]
+        cosine, sine = cos_ref[own], sin_ref[own]
         last = members - 1
         stored = []
 
@@ -827,7 +964,6 @@
         for hop in range(last, 0, -1):
             back.start(hop)
             back.arrive(hop)
-        moe.start(last)
         back.total(total)
         normed_grad = swap_blocks(total[...])
         inverse, unit = rms_pieces(hidden_ref[...])
@@ -838,11 +974,8 @@
             span = slice(t * part, (t + 1) * part)
             do_ref[:, span] = nn(low, square_ref[t, :, part:]).astype(bf16)
             store(tn(low, mixed_ref[:, span]), width + t * part)
-        moe.arrive(last)
-        if last > 1:
-            moe.start(last - 1)
         dkv_ref[...] = jnp.zeros_like(dkv_ref)
-        first = z * own_rows
+        first_row = z * own_rows
 
         @pl.loop(0, heads)
         def _(head):
@@ -850,7 +983,7 @@
             key_span = pl.ds(pl.multiple_of(head // per_kv * HD, HD), HD)
             value_span = pl.ds(pl.multiple_of((KV + head // per_kv) * HD, HD), HD)
             q_now, k_now, do_now = q_ref[:, span], kv_ref[:, key_span], do_ref[:, span]
-            p = probabilities(q_now, k_now, first)
+            p = probabilities(q_now, k_now, first_row)
             dp = nt(do_now, kv_ref[:, value_span])
             ds = (p * (dp - jnp.sum(p * dp, axis=-1, keepdims=True))).astype(bf16)
             dq_ref[:, span] = turn(nn(ds, k_now) * (HD**-0.5), cosine, -sine).astype(bf16)
@@ -858,6 +991,10 @@
             dkv_ref[:, value_span] += tn(p.astype(bf16), do_now)
 
         pairs.start(last)
+        for i, copy in enumerate(moves[:2]):
+            copy.wait()
+            added[1 - i] = (added[1 - i].astype(f32) + through[i].astype(f32)).astype(bf16)
+            moves[7 - i].start()
         for t in range(members):
             span = slice(t * part, (t + 1) * part)
             store(tn(normed_ref[...], dq_ref[:, span]), t * part)
@@ -865,10 +1002,6 @@
             if hop < last:
                 pairs.start(hop)
             pairs.arrive(hop)
-        for hop in range(last - 1, 0, -1):
-            moe.arrive(hop)
-            if hop > 1:
-                moe.start(hop - 1)
         pairs.total(kv_total)
         low_kv = [
             turn(kv_total[:, head * HD : (head + 1) * HD], cosine, -sine).astype(bf16) for head in range(KV)
@@ -886,23 +1019,24 @@
         tall_part[:, kv:] = jnp.transpose(both).astype(bf16)
         tall_copy = pltpu.make_async_copy(tall_part, parts.at[:, 2 * width :], stage_sem.at[2])
         tall_copy.start()
-        moe.total(total)
-        out_ref[...] = (hidden_ref[...] + swap_blocks(total[...])).astype(bf16)
-        for line in (back, moe, pairs):
+        for line in (back, pairs):
             line.close()
-        for copy in (*stored[-2:], tall_copy):
+        for copy in (*stored[-2:], tall_copy, *moves[2:]):
             copy.wait()
 
     hops = (2, members - 1)
+    anywhere = pl.BlockSpec(memory_space=pl.ANY)
+    size, height, lanes = to_x.shape
+    halves = (2, size // 2, height, lanes)
     return pl.pallas_call(
         kernel,
-        in_specs=in_vmem(12),
-        out_specs=in_vmem(2) + [pl.BlockSpec(memory_space=pl.ANY)],
+        in_specs=[anywhere] + in_vmem(11) + [anywhere] * 3,
+        out_specs=in_vmem(1) + [anywhere] * 5,
         out_shape=[
-            jax.ShapeDtypeStruct((own_rows, width), bf16),
             jax.ShapeDtypeStruct((own_rows, width), f32),
             jax.ShapeDtypeStruct((width, 2 * width + tall.shape[1]), bf16),
-        ],
+        ]
+        + [jax.ShapeDtypeStruct((size, height, lanes), bf16)] * 4,
         scratch_shapes=[
             pltpu.VMEM((own_rows, width), bf16),
             pltpu.VMEM((own_rows, width), bf16),
@@ -911,18 +1045,24 @@
             pltpu.VMEM((own_rows, kv), f32),
             pltpu.VMEM((2, width, part), bf16),
             pltpu.VMEM(tall.shape, bf16),
+            pltpu.VMEM((members, own_rows, width), f32),
+            pltpu.VMEM((2, own_rows, width), bf16),
+            pltpu.VMEM((*hops, own_rows, width), bf16),
+            pltpu.VMEM((2, own_rows, kv), bf16),
+            pltpu.VMEM((*hops, own_rows, kv), bf16),
         ]
-        + [pltpu.VMEM((2, own_rows, width), bf16), pltpu.VMEM((*hops, own_rows, width), bf16)] * 2
-        + [pltpu.VMEM((2, own_rows, kv), bf16), pltpu.VMEM((*hops, own_rows, kv), bf16)]
-        + [dma(hops)] * 6
-        + [dma((3,))],
+        + [dma(hops)] * 4
+        + [dma((3,)), dma((members,)), pltpu.VMEM(halves, bf16), pltpu.VMEM(halves, bf16), dma((2,)), dma((8,)), dma((8,))],
         compiler_params=pltpu.CompilerParams(collective_id=4, has_side_effects=True, vmem_limit_bytes=62 * 10**6),
         cost_estimate=pl.CostEstimate(flops=10**11, bytes_accessed=10**7, transcendentals=0),
         name="attention_back",
-    )(sums, cotangent, hidden, tokens, normed, q, kv_all, mixed, square, tall, cosine, sine)
-
-
-def reduce_small(parts, members, devices):
+    )(
+        sums, cotangent, hidden, tokens, normed, q, kv_all, mixed, square, tall, cosine, sine, last_chunk, to_x, to_y
+    )
+
+
+def reduce_small(parts, sums, hidden, members, devices):
+    own_rows = hidden.shape[0]
     width = parts.shape[0]
     height = width // devices
     lanes = parts.shape[1]
@@ -931,13 +1071,26 @@
     half = height // 2
     dma = pltpu.SemaphoreType.DMA
 
-    def kernel(parts_ref, square_out, tall_out, own, theirs, leave, arrive, blocks, line_leave, line_arrive, tall_all, *sems):
-        own_sem, core_send, core_recv, chip_send, chip_recv, line_send, line_recv, tall_send, tall_recv = sems
+    def kernel(parts_ref, sums_ref, hidden_ref, out_ref, square_out, tall_out, *rest):
+        own, theirs, leave, arrive, blocks, line_leave, line_arrive, tall_all = rest[:8]
+        moe_part, moe_leave, moe_arrive, total_ref = rest[8:12]
+        own_sem, core_send, core_recv, chip_send, chip_recv, line_send, line_recv, tall_send, tall_recv = rest[12:21]
+        moe_send, moe_recv, part_sem = rest[21:]
         me, z = lax.axis_index("dp"), lax.axis_index("tensor")
         x_side, y_side = chip_neighbours()
         core = sibling()
         chips = [me, x_side, y_side, x_side + y_side - me]
+        loads = [
+            pltpu.make_async_copy(
+                sums_ref.at[b * own_rows : (b + 1) * own_rows, :width], moe_part.at[b], part_sem.at[b]
+            )
+            for b in range(members)
+        ]
+        for copy in loads:
+            copy.start()
         meet(members, True)
+        moe = LineSum(members, lambda b: moe_part[b], moe_leave, moe_arrive, moe_send, moe_recv)
+        last = members - 1
 
         def rows(device):
             return parts_ref.at[pl.ds(pl.multiple_of(device * height, 16), height)]
@@ -951,6 +1104,9 @@
         for m in (3, 2, 1, 0):
             trade(m).start()
             keep(m).start()
+        for copy in loads:
+            copy.wait()
+        moe.start(last)
 
         def both(m, span):
             return own[m, span].astype(f32) + theirs[m, span].astype(f32)
@@ -973,12 +1129,21 @@
                     copy.start()
         for copy in far:
             copy.wait()
+        moe.arrive(last)
+        if last > 1:
+            moe.start(last - 1)
         leave[1, first] = both(1, first).astype(bf16)
         leave[1, second] = (both(1, second) + arrive[0, second].astype(f32)).astype(bf16)
         near[0].start()
         leave[2, first] = (both(2, first) + arrive[0, first].astype(f32)).astype(bf16)
         leave[2, second] = both(2, second).astype(bf16)
         near[1].start()
+        for hop in range(last - 1, 0, -1):
+            moe.arrive(hop)
+            if hop > 1:
+                moe.start(hop - 1)
+        moe.total(total_ref)
+        out_ref[...] = (hidden_ref[...] + swap_blocks(total_ref[...])).astype(bf16)
         for copy in near:
             copy.wait()
 
@@ -1008,13 +1173,15 @@
         tall_out[...] = summed
         line.close()
         group.close()
+        moe.close()
 
     hops = (2, members - 1)
     return pl.pallas_call(
         kernel,
-        in_specs=[pl.BlockSpec(memory_space=pl.ANY)],
-        out_specs=in_vmem(2),
+        in_specs=[pl.BlockSpec(memory_space=pl.ANY)] * 2 + in_vmem(1),
+        out_specs=in_vmem(3),
         out_shape=[
+            jax.ShapeDtypeStruct((own_rows, width), bf16),
             jax.ShapeDtypeStruct((height, 2 * part), f32),
             jax.ShapeDtypeStruct((height, tall), f32),
         ],
@@ -1027,17 +1194,63 @@
             pltpu.VMEM((2, height, 2 * part), bf16),
             pltpu.VMEM((*hops, height, 2 * part), bf16),
             pltpu.VMEM((members, height, tall), bf16),
+            pltpu.VMEM((members, own_rows, width), f32),
+            pltpu.VMEM((2, own_rows, width), bf16),
+            pltpu.VMEM((*hops, own_rows, width), bf16),
+            pltpu.VMEM((own_rows, width), f32),
             dma((4,)),
             dma((4,)),
             dma((4,)),
             dma((4,)),
             dma((4,)),
         ]
-        + [dma(hops)] * 4,
-        compiler_params=pltpu.CompilerParams(collective_id=5, has_side_effects=True, vmem_limit_bytes=48 * 2**20),
+        + [dma(hops)] * 6
+        + [dma((members,))],
+        compiler_params=pltpu.CompilerParams(collective_id=5, has_side_effects=True, vmem_limit_bytes=60 * 2**20),
         cost_estimate=pl.CostEstimate(flops=8 * 10**10, bytes_accessed=10**7, transcendentals=0),
         name="reduce_small",
-    )(parts)
+    )(parts, sums, hidden)
+
+
+def unpack_all(chunks, from_x, from_y):
+    calls = len(chunks)
+    _, pairs, height, lanes = chunks[0].shape
+    units = lanes // 6
+    tail = units - HD
+    step = 48 if height % 48 == 0 else height
+
+    def kernel(*refs):
+        gate, up, down = refs[3 * calls :]
+        for call in range(calls):
+            own, by_x, by_y = refs[3 * call : 3 * call + 3]
+            found = [[], [], []]
+            for pair in range(pairs):
+                value = own[0, pair].astype(f32) + by_x[pair].astype(f32) + by_y[pair].astype(f32)
+                tiles = [value[:, i * HD : (i + 1) * HD] for i in range(9)]
+                for i, (a, b) in enumerate(((0, 1), (3, 4), (6, 7))):
+                    ends = tiles[a - a % 3 + 2]
+                    left = jnp.concatenate([tiles[a], ends[:, :tail]], axis=1)
+                    right = jnp.concatenate([tiles[b], ends[:, tail:]], axis=1)
+                    if i < 2:
+                        found[0].append(left)
+                        found[1].append(right)
+                    else:
+                        found[2] += [left, right]
+            for out, values in zip((gate, up, down), found):
+                out[:, 2 * pairs * call : 2 * pairs * (call + 1), :] = jnp.swapaxes(jnp.stack(values), 0, 1)
+
+    chunk = pl.BlockSpec((1, pairs, step, lanes), lambda i: (0, 0, i, 0))
+    other = pl.BlockSpec((pairs, step, lanes), lambda i: (0, i, 0))
+    shape = (height, 2 * pairs * calls, units)
+    return pl.pallas_call(
+        kernel,
+        grid=(height // step,),
+        in_specs=[chunk, other, other] * calls,
+        out_specs=[pl.BlockSpec((step, *shape[1:]), lambda i: (i, 0, 0))] * 3,
+        out_shape=[jax.ShapeDtypeStruct(shape, f32)] * 3,
+        compiler_params=pltpu.CompilerParams(vmem_limit_bytes=48 * 2**20),
+        name="unpack",
+    )(*(array for call in zip(chunks, from_x, from_y) for array in call))
 
 
 def pack(gate, up, down):
@@ -1072,38 +1285,6 @@
 def flip(value, bit):
     count = lax.axis_size("dp")
     return lax.ppermute(value, "dp", [(i, i ^ bit) for i in range(count)])
-
-
-def gather_step(fresh, arrived):
-    to_x = [from_y[half_of(from_y)[1]] for _, from_y in arrived] + fresh
-    to_y = [from_x[half_of(from_x)[0]] for from_x, _ in arrived] + fresh
-    return flip(jnp.concatenate(to_x), 2), flip(jnp.concatenate(to_y), 4)
-
-
-def gather_chunks(packed):
-    size = packed[0].shape[0]
-    cut = size // 2
-    fresh, steps, near, far = [[packed[0], packed[1]], *([p] for p in packed[2:]), []], [], [], []
-    arrived = []
-    for chunks in fresh:
-        got = gather_step(chunks, arrived)
-        steps.append(got)
-        for i in range(len(arrived)):
-            far.append(tuple(side[cut * i : cut * (i + 1)] for side in got))
-        begin = cut * len(arrived)
-        arrived = [
-            tuple(side[begin + size * i : begin + size * (i + 1)] for side in got) for i in range(len(chunks))
-        ]
-        near += arrived
-    gathered = []
-    for own, (from_x, from_y), (second, first) in zip(packed, near, far):
-        gathered.append(
-            [
-                [(own, 0), (from_x, 0), (from_y, 0), (first, 0)],
-                [(own, cut), (from_x, cut), (from_y, cut), (second, 0)],
-            ]
-        )
-    return gathered, steps
 
 
 def half_of(chunk):
@@ -1145,9 +1326,7 @@
     earlier = jnp.arange(rows)[:, None] > jnp.arange(rows)[None, :]
     rank = jnp.where(member_of, nn(earlier.astype(bf16), member_of.astype(bf16)), -1.0)
     rank_cols = jnp.pad(rank, ((0, 0), (0, HD)), constant_values=-1.0).astype(bf16)
-    rank_rows = rank.T.astype(jnp.int32).reshape(EXPERTS, 1, rows)
-    weight_rows = weight_of.T.reshape(EXPERTS, 1, rows)
-    return rank_cols, rank_rows, weight_rows
+    return rank_cols, jnp.stack([rank.T, weight_of.T], axis=1)
 
 
 def body_anywhere(
@@ -1185,7 +1364,7 @@
     o_full = lax.all_gather(lax.all_gather(o_weight, "dp", axis=0, tiled=True), "tensor", axis=0)
     kv_width = k_weight.shape[1]
 
-    rank_cols, rank_rows, weight_rows = routes_of(expert_ids, route_weights)
+    rank_cols, routes = routes_of(expert_ids, route_weights)
 
     grad_low = cotangent.astype(bf16)
     grad_all = lax.all_gather(grad_low, "tensor", axis=0, tiled=True)
@@ -1218,8 +1397,7 @@
         columns = slice(2 * CALL_PAIRS * call, 2 * CALL_PAIRS * call + HD)
         grads, sums = expert_call(
             rank_cols[:, columns],
-            rank_rows[some],
-            weight_rows[some],
+            routes[some],
             rows_all,
             grad_all,
             gathered[call],
@@ -1303,46 +1481,65 @@
     calls = EXPERTS // 2 // CALL_PAIRS
     kv_width = k_weight.shape[1]
 
-    packed = [
-        pack(*(w[:, 2 * CALL_PAIRS * i : 2 * CALL_PAIRS * (i + 1)] for w in (gate_weight, up_weight, down_weight)))
-        for i in range(calls)
-    ]
-    gathered, steps = gather_chunks(packed)
-    square = jnp.concatenate([q_weight, o_weight], axis=1)
-    gains = jnp.stack([attn_gain, moe_gain], axis=1)
-    tall = jnp.concatenate([k_weight, v_weight, jnp.pad(gains, ((0, 0), (0, HD - 2)))], axis=1)
-    tall = after(tall, packed[:2])
-    square_all, tall_all, grad_all = gather_small(square, tall, cotangent, members, devices)
-
-    rank_cols, rank_rows, weight_rows = routes_of(expert_ids, route_weights)
-    cos_table, sin_table = rope_tables(member * own_rows + jnp.arange(own_rows, dtype=jnp.int32))
-    cosine = jnp.concatenate([cos_table, cos_table], axis=1)
-    sine = after(jnp.concatenate([-sin_table, sin_table], axis=1), steps[0])
-    normed_one, queries, kv_all, mixed, hidden, rows_all = attention_front(
-        tokens, square_all, tall_all, cosine, sine, members
+    gains = jnp.pad(jnp.stack([attn_gain, moe_gain], axis=1), ((0, 0), (0, HD - 2)))
+    small = gather_small(
+        q_weight,
+        o_weight,
+        k_weight,
+        v_weight,
+        gains,
+        cotangent,
+        expert_ids,
+        route_weights,
+        gate_weight,
+        up_weight,
+        down_weight,
+        members,
+        devices,
     )
-
-    sums = jnp.zeros((rows, 2 * width), f32)
+    square_all, tall_all, grad_all = small[:3]
+    rank_cols, routes, packed = (small[3 + calls * i : 3 + calls * (i + 1)] for i in range(3))
+    near = [tuple(small[3 + 3 * calls :])]
+    cosine, sine = doubled_tables(rows)
+    normed_one, queries, kv_all, mixed, hidden, rows_all, sums, *landed = attention_front(
+        tokens, square_all, tall_all, cosine, sine, packed[1:-1], near[0], members
+    )
+    far = [(landed[1], landed[0])]
+    near += [tuple(landed[2 * i : 2 * i + 2]) for i in range(1, calls - 1)]
+    cut = CALL_PAIRS // 2
     chunks, moved = [], []
     for call in range(calls):
-        some = slice(2 * CALL_PAIRS * call, 2 * CALL_PAIRS * (call + 1))
-        columns = slice(2 * CALL_PAIRS * call, 2 * CALL_PAIRS * call + HD)
+        if call == 0:
+            to_x = [from_y[cut:] for _, from_y in near[1:]] + [packed[-1]]
+            to_y = [from_x[:cut] for from_x, _ in near[1:]] + [packed[-1]]
+            got = flip(jnp.concatenate(to_x), 2), flip(jnp.concatenate(to_y), 4)
+        elif call == 1:
+            far += [tuple(side[cut * i : cut * (i + 1)] for side in got) for i in range(calls - 2)]
+            near.append(tuple(side[cut * (calls - 2) :] for side in got))
+            far.append((flip(near[-1][1][cut:], 2), flip(near[-1][0][:cut], 4)))
+        (from_x, from_y), (second, first) = near[call], far[call]
+        own = packed[call]
         grads, sums = expert_call(
-            rank_cols[:, columns],
-            after(rank_rows[some], moved[call - 2] if call >= 2 else ()),
-            weight_rows[some],
+            rank_cols[call],
+            after(routes[call], moved[call - 2] if call >= 2 else ()),
             rows_all,
             grad_all,
-            gathered[call],
+            [
+                [(own, 0), (from_x, 0), (from_y, 0), (first, 0)],
+                [(own, cut), (from_x, cut), (from_y, cut), (second, 0)],
+            ],
             sums,
             True,
         )
         chunks.append(grads)
-        moved.append(scatter_step(grads, before_of(chunks, moved, call)))
-    moved.append(scatter_step(None, before_of(chunks, moved, calls)))
-
-    output, tokens_grad, parts = attention_back(
-        sums.astype(bf16),
+        if call + 1 < calls:
+            moved.append(scatter_step(grads, before_of(chunks, moved, call)))
+
+    blocks, via_x, via_y = before_of(chunks, moved, calls - 1)
+    to_x = jnp.concatenate([blocks[1, :cut], add(blocks[1, cut:], via_y)])
+    to_y = jnp.concatenate([add(blocks[2, :cut], via_x), blocks[2, cut:]])
+    tokens_grad, parts, x_before, y_before, x_last, y_last = attention_back(
+        sums,
         cotangent,
         hidden,
         tokens,
@@ -1353,15 +1550,18 @@
         square_all,
         tall_all,
         cosine,
-        after(sine, moved[calls - 2]),
+        sine,
+        chunks[-1],
+        to_x,
+        to_y,
         members,
     )
-    square_grad, tall_grad = reduce_small(parts, members, devices)
-    shares = []
-    for call in range(calls):
-        from_x, from_y = (got[:CALL_PAIRS].astype(f32) for got in moved[call + 1])
-        shares.append(unpack(chunks[call][0].astype(f32) + from_x + from_y))
-    gate_out, up_out, down_out = (jnp.concatenate(blocks, axis=1) for blocks in zip(*shares))
+    output, square_grad, tall_grad = reduce_small(parts, sums, hidden, members, devices)
+    gate_out, up_out, down_out = unpack_all(
+        chunks,
+        [got[0] for got in moved[1:]] + [x_before, x_last],
+        [got[1] for got in moved[1:]] + [y_before, y_last],
+    )
     part = width // members
     return (
         output,
@@ -1378,6 +1578,14 @@
     )
 
 
+def doubled_tables(rows):
+    half = HD // 2
+    frequency = np.float32(rope_base) ** -(np.arange(half, dtype=np.float32) * np.float32(2.0 / HD))
+    angles = (np.arange(rows) % SEQ).astype(np.float32)[:, None] * frequency
+    cosine, sine = np.cos(angles), np.sin(angles)
+    return jnp.asarray(np.concatenate([cosine, cosine], axis=1)), jnp.asarray(np.concatenate([-sine, sine], axis=1))
+
+
 def solution(mesh):
     rows = P(("dp", "tensor"), None)
     experts = P("dp", None, "tensor")

time: 1030 us -> 814 us (0.79)
  local copies, waits for them, and re-layouts: 138 us -> 36.7 us
  waiting for transfers between devices: 74.2 us -> 20.4 us
  other arithmetic: 56.2 us -> 22.9 us
  Pallas kernels: 730 us -> 716 us
  starting transfers between devices: 20.8 us -> 10.2 us
    slice x74 -> x8, local copies, waits for them, and re-layouts: 69.3 us -> 14.2 us  [the longest x2 6.02 us: body_by_chips(): near.append(tuple((side[cut * (calls - 2):] for side in got)))]
    ppermute x18 -> x10, waiting for transfers between devices: 74.2 us -> 20.4 us  [flip(): return lax.ppermute(value, 'dp', [(i, i ^ bit) for i in range(count)])]
    unnamed x109 -> x40, local copies, waits for them, and re-layouts: 34.7 us -> 6.78 us
    pallas_call x4 -> x5, Pallas kernels: 456 us -> 442 us  [the longest x1 115 us: attention_back(): pl.pallas_call(kernel, in_specs=[anywhere] + in_vmem(11) + [anywhere] * 3...]
    concatenate x13 -> x2, other arithmetic: 16.6 us -> 5.6 us  [the longest x1 3.36 us: body_by_chips(): got = (flip(jnp.concatenate(to_x), 2), flip(jnp.concatenate(to_y), 4))]
    ppermute x18 -> x10, starting transfers between devices: 20.8 us -> 10.2 us  [flip(): return lax.ppermute(value, 'dp', [(i, i ^ bit) for i in range(count)])]
    add x4 -> x0, other arithmetic: 10.3 us -> none  [body_by_chips(): shares.append(unpack(chunks[call][0].astype(f32) + from_x + from_y))]
  transfers between devices with their start and end apart: 18 -> 10, of which waited for: 3 -> 2; matrix products, arithmetic and copies ran while one was open for 12% -> 3% of each run, Pallas kernels for 48% -> 25%
where the time goes in v4:
time: 814 us; the launch traced here: 807 us
  Pallas kernels  716 us (88%)
  local copies, waits for them, and re-layouts  36.7 us (5%)
  other arithmetic  22.9 us (3%)
  waiting for transfers between devices  20.4 us (3%)
  starting transfers between devices  10.2 us (1%)
    pallas_call x4, Pallas kernels, expert_call(): pl.pallas_call(kernel, grid=(pairs + blocks,), in_specs=[pl.BlockSpec((ro...  274 us
    pallas_call x1, Pallas kernels, attention_back(): pl.pallas_call(kernel, in_specs=[anywhere] + in_vmem(11) + [anywhere] * 3...  115 us
    pallas_call x1, Pallas kernels, gather_small(): pl.pallas_call(kernel, in_specs=in_vmem(11), out_specs=in_vmem(3 + 3 * ca...  110 us
    pallas_call x1, Pallas kernels, attention_front(): pl.pallas_call(kernel, in_specs=in_vmem(5) + [anywhere] * count, out_spec...  104 us
    pallas_call x1, Pallas kernels, reduce_small(): pl.pallas_call(kernel, in_specs=[pl.BlockSpec(memory_space=pl.ANY)] * 2 +...  99.3 us
    ppermute x10, waiting for transfers between devices, flip(): return lax.ppermute(value, 'dp', [(i, i ^ bit) for i in range(count)])  20.4 us
  transfers between devices with their start and end apart: 10, of which 2 were waited for; matrix products, arithmetic and copies ran while one was open for 3% of the time, Pallas kernels for 25%

profile of v4, /device:TPU:0, one launch (start us, length us, event | category | flops | bytes accessed | tf_op | source)
XLA Modules:
  0.0 807.3 jit_solution(11869331055565829559)
XLA Ops:
  2.1 1.7 copy.35.refs_6_
  3.9 1.7 copy.36.refs_7_
  6.2 110.1 %gather_small.1 = (bf16[4,1536,768]{2,1,0:T(8,128)(2,1)}, bf16[1536,640]{1,0:T(8,128)(2,1)}, bf16[1024,1536]{1,0:T(8,128)(2,1)}, bf16[1024,128]{1,0:T(8,128)(2,1...) custom-call(bf16[192,384]{1,0:T(8,128)(2,1)} %refs_0_.1, ...), custom_call_target="tpu_custom_call" | custom-call | flops 80000000000 | bytes 10000000 | tf_op jit(solution)/shard_map/gather_small/pallas_call | solution.py:747
  116.4 104.4 %attention_front.1 = (bf16[256,1536]{1,0:T(8,128)(2,1)}, bf16[256,1536]{1,0:T(8,128)(2,1)}, bf16[1024,512]{1,0:T(8,128)(2,1)}, bf16[256,1536]{1,0:T(8,128)(2,1)}...) custom-call(bf16[256,1536]{1,0:T(8,128)(2,1)} %x_ref.3, ...), custom_call_target="tpu_custom_call" | custom-call | flops 99999997952 | bytes 10000000 | tf_op jit(solution)/shard_map/attention_front/pallas_call | solution.py:867
  224.1 3.4 pad_maximum_fusion
  229.5 68.5 %experts.4 = (bf16[4,4,192,1152]{3,2,1,0:T(8,128)(2,1)}, f32[1024,3072]{1,0:T(8,128)}) custom-call(bf16[1024,128]{1,0:T(8,128)(2,1)} %get-tuple-element.63.rank_c, f32[8,2,1024]{2,1,0:T(2,128)} %get-tuple-element.64.routes_ref, bf16[1024,1536]{1,0:T(8,128)(2,1)} %get-tuple-element.71.x_ref, bf16[1024,1536]{1,0:T(8,128)(2,1)} %get-tuple-element.72.gy_ref, ...), custom_call_target="tpu_custom_call" | custom-call | flops 73282879488 | bytes 37748736 | tf_op jit(solution)/shard_map/experts/pallas_call | solution.py:391
  298.0 3.5 slice_bitcast_fusion.8
  303.6 20.0 %collective-permute-done.4.refs_1_ = bf16[2,192,1152]{2,1,0:T(8,128)(2,1)} collective-permute-done((bf16[2,192,1152]{2,1,0:T(8,128)(2,1)S(1)}, bf16[2,192,1152]{2,1,0:T(8,128)(2,1)}, u32[]{:S(2)}, u32[]{:S(2)}) %collective-permute-start.4) | collective-permute-done | bytes 884768 | tf_op jit(solution)/shard_map/ppermute | solution.py:1287
  324.0 3.6 fusion.4
  327.6 1.6 fusion.7
  329.2 3.7 fusion.6
  332.9 68.2 %experts.5 = (bf16[4,4,192,1152]{3,2,1,0:T(8,128)(2,1)}, f32[1024,3072]{1,0:T(8,128)}) custom-call(bf16[1024,128]{1,0:T(8,128)(2,1)} %get-tuple-element.78.rank_c, f32[8,2,1024]{2,1,0:T(2,128)} %get-tuple-element.79.routes_ref, bf16[1024,1536]{1,0:T(8,128)(2,1)} %get-tuple-element.71.x_ref, bf16[1024,1536]{1,0:T(8,128)(2,1)} %get-tuple-element.72.gy_ref, ...), custom_call_target="tpu_custom_call" | custom-call | flops 73282879488 | bytes 37748736 | tf_op jit(solution)/shard_map/experts/pallas_call | solution.py:391
  401.2 3.3 slice_bitcast_fusion.2
  404.5 1.9 pad_maximum_fusion.2
  406.3 1.4 collective-permute-start.3
  407.7 1.9 pad_maximum_fusion.3
  412.3 68.5 %experts.6 = (bf16[4,4,192,1152]{3,2,1,0:T(8,128)(2,1)}, f32[1024,3072]{1,0:T(8,128)}) custom-call(bf16[1024,128]{1,0:T(8,128)(2,1)} %get-tuple-element.87.rank_c, f32[8,2,1024]{2,1,0:T(2,128)} %after.3.routes_ref, bf16[1024,1536]{1,0:T(8,128)(2,1)} %get-tuple-element.71.x_ref, bf16[1024,1536]{1,0:T(8,128)(2,1)} %get-tuple-element.72.gy_ref, ...), custom_call_target="tpu_custom_call" | custom-call | flops 73282879488 | bytes 37748736 | tf_op jit(solution)/shard_map/experts/pallas_call | solution.py:391
  480.7 3.0 slice.164.rest_1_
  483.7 3.0 slice.165.rest_2_
  488.0 3.1 fusion
  491.1 1.9 pad_maximum_fusion.5
  493.0 1.4 collective-permute-start.9
  494.4 1.9 pad_maximum_fusion.4
  496.9 68.3 %experts.7 = (bf16[4,4,192,1152]{3,2,1,0:T(8,128)(2,1)}, f32[1024,3072]{1,0:T(8,128)}) custom-call(bf16[1024,128]{1,0:T(8,128)(2,1)} %get-tuple-element.61.rank_c, f32[8,2,1024]{2,1,0:T(2,128)} %after.2.routes_ref, bf16[1024,1536]{1,0:T(8,128)(2,1)} %get-tuple-element.71.x_ref, bf16[1024,1536]{1,0:T(8,128)(2,1)} %get-tuple-element.72.gy_ref, ...), custom_call_target="tpu_custom_call" | custom-call | flops 73282879488 | bytes 37748736 | tf_op jit(solution)/shard_map/experts/pallas_call | solution.py:391
  565.2 3.1 fusion.1
  568.4 2.2 pad_maximum_fusion.6
  570.6 115.1 %attention_back.1 = (f32[256,1536]{1,0:T(8,128)}, bf16[1536,3712]{1,0:T(8,128)(2,1)}, bf16[4,192,1152]{2,1,0:T(8,128)(2,1)}, bf16[4,192,1152]{2,1,0:T(8,128)(2,1...) custom-call(f32[1024,3072]{1,0:T(8,128)} %get-tuple-element.91.sums_ref, f32[256,1536]{1,0:T(8,128)} %cot_ref.1, ...), custom_call_target="tpu_custom_call" | custom-call | flops 99999997952 | bytes 10000000 | tf_op jit(solution)/shard_map/attention_back/pallas_call | solution.py:1031
  685.8 99.3 %reduce_small.1 = (bf16[256,1536]{1,0:T(8,128)(2,1)}, f32[192,768]{1,0:T(8,128)}, f32[192,640]{1,0:T(8,128)}) custom-call(bf16[1536,3712]{1,0:T(8,128)(2,1)} %get-tuple-element.99.parts_ref, f32[1024,3072]{1,0:T(8,128)} %get-tuple-element.91.sums_ref, f32[256,1536]{1,0:T(8,128)} %get-tuple-element.92.hidden_ref), custom_call_target="tpu_custom_call" | custom-call | flops 80000000000 | bytes 10000000 | tf_op jit(solution)/shard_map/reduce_small/pallas_call | solution.py:1179
  785.1 1.9 slice_reduce_fusion
  787.0 1.8 fusion.9
  788.8 1.9 fusion.8
  790.7 13.4 %unpack.1 = (f32[192,32,192]{2,1,0:T(8,128)}, f32[192,32,192]{2,1,0:T(8,128)}, f32[192,32,192]{2,1,0:T(8,128)}) custom-call(bf16[4,4,192,1152]{3,2,1,0:T(8,128)(2,1)} %get-tuple-element.77.refs_0_, bf16[6,192,1152]{2,1,0:T(8,128)(2,1)} %copy-done.4, bf16[6,192,1152]{2,1,0:T(8,128)(2,1)} %collective-permute-done.5.refs_2_, ...), custom_call_target="tpu_custom_call" | custom-call | tf_op jit(solution)/shard_map/unpack/pallas_call | solution.py:1245
  (67 shorter events, 17.3 us)
Async XLA Ops:
  220.7 2.8 copy-start.16
  220.8 2.9 copy-start.17
  222.2 2.0 copy-start.13
  227.5 100.1 %collective-permute-start.1 = (bf16[8,192,1152]{2,1,0:T(8,128)(2,1)}, bf16[8,192,1152]{2,1,0:T(8,128)(2,1)S(1)}, u32[]{:S(2)}, u32[]{:S(2)}) collective-permute-start(bf16[8,192,1152]{2,1,0:T(8,128)(2,1)} %get-tuple-element.138), channel_id=1, source_target_pairs={{0,16},{4,20},{8,24},{12,28},{16,0},{20,4},{24,8},{28,12},{1,17},{... | collective-permute-start | bytes 10616840 | tf_op jit(solution)/shard_map/ppermute | solution.py:1287
  228.1 101.0 %collective-permute-start.2 = (bf16[8,192,1152]{2,1,0:T(8,128)(2,1)}, bf16[8,192,1152]{2,1,0:T(8,128)(2,1)}, u32[]{:S(2)}, u32[]{:S(2)}) collective-permute-start(bf16[8,192,1152]{2,1,0:T(8,128)(2,1)} %get-tuple-element.137), channel_id=1, source_target_pairs={{0,8},{4,12},{8,0},{12,4},{16,24},{20,28},{24,16},{28,20},{1,9},{5... | collective-permute-start | bytes 10616840 | tf_op jit(solution)/shard_map/ppermute | solution.py:1287
  301.6 22.0 %collective-permute-start.4 = (bf16[2,192,1152]{2,1,0:T(8,128)(2,1)S(1)}, bf16[2,192,1152]{2,1,0:T(8,128)(2,1)}, u32[]{:S(2)}, u32[]{:S(2)}) collective-permute-start(bf16[2,192,1152]{2,1,0:T(8,128)(2,1)S(1)} %get-tuple-element.127), channel_id=1, source_target_pairs={{0,8},{4,12},{8,0},{12,4},{16,24},{20,28},{24,16},{28,20},{1,9},{5... | collective-permute-start | bytes 2654216 | tf_op jit(solution)/shard_map/ppermute | solution.py:1287
  302.2 21.7 %collective-permute-start = (bf16[2,192,1152]{2,1,0:T(8,128)(2,1)S(1)}, bf16[2,192,1152]{2,1,0:T(8,128)(2,1)}, u32[]{:S(2)}, u32[]{:S(2)}) collective-permute-start(bf16[2,192,1152]{2,1,0:T(8,128)(2,1)S(1)} %get-tuple-element.129), channel_id=1, source_target_pairs={{0,16},{4,20},{8,24},{12,28},{16,0},{20,4},{24,8},{28,12},{1,17},{... | collective-permute-start | bytes 2654216 | tf_op jit(solution)/shard_map/ppermute | solution.py:1287
  327.6 5.3 copy-start.5
  401.1 3.3 copy-start.10
  401.1 3.3 copy-start.12
  404.4 3.3 copy-start.8
  404.5 3.3 copy-start.11
  406.3 81.7 %collective-permute-start.3 = (bf16[6,192,1152]{2,1,0:T(8,128)(2,1)}, bf16[6,192,1152]{2,1,0:T(8,128)(2,1)S(1)}, u32[]{:S(2)}, u32[]{:S(2)}) collective-permute-start(bf16[6,192,1152]{2,1,0:T(8,128)(2,1)} %pad_maximum_fusion.2), channel_id=1, source_target_pairs={{0,8},{4,12},{8,0},{12,4},{16,24},{20,28},{24,16},{28,20},{1,9},{5... | collective-permute-start | bytes 7962632 | tf_op jit(solution)/shard_map/ppermute | solution.py:1287
  409.6 78.4 %collective-permute-start.5 = (bf16[6,192,1152]{2,1,0:T(8,128)(2,1)}, bf16[6,192,1152]{2,1,0:T(8,128)(2,1)}, u32[]{:S(2)}, u32[]{:S(2)}) collective-permute-start(bf16[6,192,1152]{2,1,0:T(8,128)(2,1)} %pad_maximum_fusion.3), channel_id=1, source_target_pairs={{0,16},{4,20},{8,24},{12,28},{16,0},{20,4},{24,8},{28,12},{1,17},{... | collective-permute-start | bytes 7962632 | tf_op jit(solution)/shard_map/ppermute | solution.py:1287
  410.2 86.7 %collective-permute-start.6 = (bf16[2,192,1152]{2,1,0:T(8,128)(2,1)}, bf16[2,192,1152]{2,1,0:T(8,128)(2,1)}, u32[]{:S(2)}, u32[]{:S(2)}) collective-permute-start(bf16[2,192,1152]{2,1,0:T(8,128)(2,1)} %get-tuple-element.132), channel_id=1, source_target_pairs={{0,16},{4,20},{8,24},{12,28},{16,0},{20,4},{24,8},{28,12},{1,17},{... | collective-permute-start | bytes 2654216 | tf_op jit(solution)/shard_map/ppermute | solution.py:1287
  411.6 85.3 %collective-permute-start.7 = (bf16[2,192,1152]{2,1,0:T(8,128)(2,1)}, bf16[2,192,1152]{2,1,0:T(8,128)(2,1)}, u32[]{:S(2)}, u32[]{:S(2)}) collective-permute-start(bf16[2,192,1152]{2,1,0:T(8,128)(2,1)} %get-tuple-element.135), channel_id=1, source_target_pairs={{0,8},{4,12},{8,0},{12,4},{16,24},{20,28},{24,16},{28,20},{1,9},{5... | collective-permute-start | bytes 2654216 | tf_op jit(solution)/shard_map/ppermute | solution.py:1287
  480.7 6.0 copy-start.3
  488.0 3.1 copy-start.9
  488.0 3.1 copy-start.4
  493.0 72.2 %collective-permute-start.9 = (bf16[6,192,1152]{2,1,0:T(8,128)(2,1)}, bf16[6,192,1152]{2,1,0:T(8,128)(2,1)S(1)}, u32[]{:S(2)}, u32[]{:S(2)}) collective-permute-start(bf16[6,192,1152]{2,1,0:T(8,128)(2,1)} %pad_maximum_fusion.5), channel_id=1, source_target_pairs={{0,8},{4,12},{8,0},{12,4},{16,24},{20,28},{24,16},{28,20},{1,9},{5... | collective-permute-start | bytes 7962632 | tf_op jit(solution)/shard_map/ppermute | solution.py:1287
  496.3 69.0 %collective-permute-start.8 = (bf16[6,192,1152]{2,1,0:T(8,128)(2,1)}, bf16[6,192,1152]{2,1,0:T(8,128)(2,1)}, u32[]{:S(2)}, u32[]{:S(2)}) collective-permute-start(bf16[6,192,1152]{2,1,0:T(8,128)(2,1)} %pad_maximum_fusion.4), channel_id=1, source_target_pairs={{0,16},{4,20},{8,24},{12,28},{16,0},{20,4},{24,8},{28,12},{1,17},{... | collective-permute-start | bytes 7962632 | tf_op jit(solution)/shard_map/ppermute | solution.py:1287
  565.2 3.2 copy-start.7
  565.2 3.1 copy-start.6
  685.7 104.9 %copy-start.1 = (bf16[4,192,1152]{2,1,0:T(8,128)(2,1)S(1)}, bf16[4,192,1152]{2,1,0:T(8,128)(2,1)}, u32[]{:S(2)}) copy-start(bf16[4,192,1152]{2,1,0:T(8,128)(2,1)} %get-tuple-element.105.refs_8_) | copy-start | bytes 5308420
  685.7 104.9 %copy-start.2 = (bf16[4,192,1152]{2,1,0:T(8,128)(2,1)S(1)}, bf16[4,192,1152]{2,1,0:T(8,128)(2,1)}, u32[]{:S(2)}) copy-start(bf16[4,192,1152]{2,1,0:T(8,128)(2,1)} %get-tuple-element.106.refs_10_) | copy-start | bytes 5308420
  785.1 5.6 copy-start
  790.7 13.4 %copy-start.15 = (bf16[256,1536]{1,0:T(8,128)(2,1)S(1)}, bf16[256,1536]{1,0:T(8,128)(2,1)}, u32[]{:S(2)}) copy-start(bf16[256,1536]{1,0:T(8,128)(2,1)} %get-tuple-element.156) | copy-start | bytes 2359300
  804.1 1.7 copy-start.14

commit v5 on v4

--- a/solution.py
+++ b/solution.py
@@ -153,209 +153,89 @@
     )(first_row, q, k, v, do)
 
 
-def after(value, waits):
-    if not waits:
-        return value
-
-    def kernel(*refs):
-        del refs
-
-    anywhere = pl.BlockSpec(memory_space=pl.ANY)
-    return pl.pallas_call(
-        kernel,
-        in_specs=[anywhere] * (1 + len(waits)),
-        out_specs=anywhere,
-        out_shape=jax.ShapeDtypeStruct(value.shape, value.dtype),
-        input_output_aliases={0: 0},
-        name="after",
-    )(value, *waits)
-
-
 def sibling():
     me = lax.axis_index("dp")
     return me + 1 - 2 * lax.rem(me, 2)
 
 
-def expert_call(rank_cols, routes, x, gy, pieces, sums, exchange):
+def pair_of_experts(expert, place, w, rank_c, routes_ref, x_ref, gy_ref, y_buf, pick_buf, put):
+    rows, width = x_ref.shape
+    lanes = w.shape[1]
+    third = lanes // 3
+    low_half = lax.broadcasted_iota(jnp.int32, (CAP, HD), 1) < TAIL
+    slot_of = lax.broadcasted_iota(jnp.int32, (rows, CAP), 1).astype(f32)
+    slot_at = lax.broadcasted_iota(jnp.int32, (CAP, rows), 0).astype(f32)
+    gate_up = [slice(q * third, (q + 1) * third) for q in range(2)]
+    down = [slice(2 * third + q * HD, 2 * third + (q + 2) * HD) for q in range(2)]
+
+    def place_of(q):
+        return pl.ds(pl.multiple_of((place + q) * CAP, CAP), CAP)
+
+    def rows_of(q):
+        hit = slot_at == routes_ref[q, 0:1]
+        weight = jnp.sum(jnp.where(hit, routes_ref[q, 1:2], 0.0), axis=1, keepdims=True)
+        pick = hit.astype(bf16)
+        return nn(pick, x_ref[...]).astype(bf16), (nn(pick, gy_ref[...]) * weight).astype(bf16), weight
+
+    def picked(q):
+        column = (lax.broadcasted_iota(jnp.int32, (HD, CAP), 0) == expert + q).astype(bf16)
+        pick_buf[:, place_of(q)] = (nn(rank_c[...], column) == slot_of).astype(bf16)
+
+    def unit(gate, up, dact):
+        sig = jax.nn.sigmoid(gate)
+        silu = gate * sig
+        return silu * up, dact * up * sig * (1.0 + gate * (1.0 - sig)), dact * silu
+
+    def middle(q, gu, dact):
+        tail = gu[:, 2 * HD :]
+        if q == 0:
+            d0, d1 = dact[:, :HD], dact[:, HD:]
+        else:
+            d0, d1 = dact[:, HD:], pltpu.roll(dact[:, :HD], TAIL, 1)
+        a0, dg0, du0 = unit(gu[:, :HD], gu[:, HD : 2 * HD], d0)
+        a1, dg1, du1 = unit(tail, pltpu.roll(tail, TAIL, 1), d1)
+        a1 = jnp.where(low_half, a1, 0.0)
+        dgu1 = jnp.where(low_half, dg1, pltpu.roll(du1, TAIL, 1))
+        act = [a0, a1] if q == 0 else [pltpu.roll(a1, TAIL, 1), a0]
+        act = jnp.concatenate([part.astype(bf16) for part in act], axis=1)
+        return act, jnp.concatenate([part.astype(bf16) for part in (dg0, du0, dgu1)], axis=1)
+
+    def ends(q, xe, deo, weight, act, dgu):
+        y_buf[place_of(q), :width] = (nt(act, w[:, down[q]]) * weight).astype(bf16)
+        y_buf[place_of(q), width:] = nt(dgu, w[:, gate_up[q]]).astype(bf16)
+        put(q * third, tn(xe, dgu))
+        grad = tn(deo, act)
+        put(2 * third + 2 * q * HD, grad[:, :HD] if q == 0 else grad[:, HD:])
+        return grad[:, HD:] if q == 0 else grad[:, :HD]
+
+    xe0, deo0, weight0 = rows_of(0)
+    first = nn(xe0, w[:, gate_up[0]]), nn(deo0, w[:, down[0]])
+    xe1, deo1, weight1 = rows_of(1)
+    act0, dgu0 = middle(0, *first)
+    second = nn(xe1, w[:, gate_up[1]]), nn(deo1, w[:, down[1]])
+    picked(0)
+    tail0 = ends(0, xe0, deo0, weight0, act0, dgu0)
+    act1, dgu1 = middle(1, *second)
+    picked(1)
+    tail1 = ends(1, xe1, deo1, weight1, act1, dgu1)
+    put(2 * third + HD, tail0 + tail1)
+
+
+def expert_call(rank_cols, routes, x, gy, weights, sums):
     rows, width = x.shape
-    subs, count = len(pieces), len(pieces[0])
-    height, lanes = pieces[0][0][0].shape[1:]
-    pairs = routes.shape[0] // 2
-    sub_pairs = pairs // subs
-    blocks = 12
+    pairs, _, lanes = weights.shape
+    blocks = 6
     tile = 2 * width // blocks
-    flat = []
-    place = []
-    for sub in pieces:
-        place.append([])
-        for array, begin in sub:
-            known = [i for i, other in enumerate(flat) if other is array]
-            if not known:
-                flat.append(array)
-            place[-1].append((known[0] if known else len(flat) - 1, begin))
-    third = lanes // 3
-    stride = 2 if exchange else 1
-
-    def kernel(rank_c, routes_ref, x_ref, gy_ref, *rest):
-        w_hbm = rest[: len(flat)]
-        rest = rest[len(flat) :]
-        sums_in, rest = rest[0], rest[1:]
-        grad_out, sums_out, w_buf, y_buf, pick_buf, local_sem = rest[:6]
+
+    def kernel(rank_c, routes_ref, x_ref, gy_ref, w_ref, sums_in, grad_out, sums_out, y_buf, pick_buf):
         step = pl.program_id(0)
-        if exchange:
-            kept, leaving, arriving, push_sem, pull_sem, send_sem, recv_sem, w_free, g_free = rest[6:]
-            other = {"dp": sibling()}
-
-        def weights(pair, slot, sub):
-            found = []
-            for k in range(count):
-                array, begin = place[sub][k]
-                source = w_hbm[array].at[pair - sub * sub_pairs + begin]
-                target = w_buf.at[slot, pl.ds(stride * k * height, height)]
-                found.append(pltpu.make_async_copy(source, target, local_sem.at[slot, k]))
-                if exchange:
-                    target = w_buf.at[slot, pl.ds((stride * k + 1) * height, height)]
-                    found.append(
-                        pltpu.make_async_remote_copy(
-                            src_ref=source,
-                            dst_ref=target,
-                            send_sem=push_sem.at[slot, k],
-                            recv_sem=pull_sem.at[slot, k],
-                            device_id=other,
-                            device_id_type=pl.DeviceIdType.MESH,
-                        )
-                    )
-            return found
-
-        def start(pair):
-            slot = lax.rem(pair, 2)
-            for sub in range(subs):
-
-                @pl.when((pair >= sub * sub_pairs) & (pair < (sub + 1) * sub_pairs))
-                def _():
-                    for copy in weights(pair, slot, sub):
-                        copy.start()
-
-        def leave(slot):
-            return pltpu.make_async_remote_copy(
-                src_ref=leaving.at[slot],
-                dst_ref=arriving.at[slot],
-                send_sem=send_sem.at[slot],
-                recv_sem=recv_sem.at[slot],
-                device_id=other,
-                device_id_type=pl.DeviceIdType.MESH,
-            )
-
-        def put(at, value, slot):
-            for k in range(count):
-                for parity in range(stride):
-                    row = (stride * k + parity) * height
-                    part = value[row : row + height].astype(bf16)
-                    span = slice(at, at + value.shape[1])
-                    if not exchange:
-                        grad_out[k, 0, :, span] = part
-                    elif parity == 0:
-                        kept[slot, k, :, span] = part
-                    else:
-                        leaving[slot, k, :, span] = part
-
-        def signal(sem):
-            pl.semaphore_signal(sem, inc=1, device_id=other, device_id_type=pl.DeviceIdType.MESH)
-
-        def finish(pair):
-            slot = lax.rem(pair, 2)
-            leave(slot).wait()
-            for k in range(count):
-                both = kept[slot, k].astype(f32) + arriving[slot, k].astype(f32)
-                grad_out[k, 0] = both.astype(bf16)
-
-        @pl.when(step == 0)
-        def _():
-            if exchange:
-                barrier = pltpu.get_barrier_semaphore()
-                signal(barrier)
-                pl.semaphore_wait(barrier, 1)
-            start(step)
-
-        if exchange:
-
-            @pl.when((step >= 1) & (step + 1 < pairs))
-            def _():
-                signal(w_free)
-                pl.semaphore_wait(w_free, 1)
-
-        @pl.when(step + 1 < pairs)
-        def _():
-            start(step + 1)
+
+        def put(at, value):
+            grad_out[0, :, at : at + value.shape[1]] = value.astype(bf16)
 
         @pl.when(step < pairs)
         def _():
-            slot = lax.rem(step, 2)
-            for copy in weights(0, slot, 0):
-                copy.wait()
-            w = w_buf.at[slot]
-            low_half = lax.broadcasted_iota(jnp.int32, (CAP, HD), 1) < TAIL
-            tails = []
-            for q in range(2):
-                e = 2 * step + q
-                column = (lax.broadcasted_iota(jnp.int32, (HD, CAP), 0) == e).astype(bf16)
-                rank = nn(rank_c[...], column)
-                slot_of = lax.broadcasted_iota(jnp.int32, (rows, CAP), 1).astype(f32)
-                at = pl.ds(pl.multiple_of(e * CAP, CAP), CAP)
-                pick_buf[:, at] = (rank == slot_of).astype(bf16)
-                hit = lax.broadcasted_iota(jnp.int32, (CAP, rows), 0).astype(f32) == routes_ref[q, 0:1]
-                pick = hit.astype(bf16)
-                weight = jnp.sum(jnp.where(hit, routes_ref[q, 1:2], 0.0), axis=1, keepdims=True)
-                xe = nn(pick, x_ref[...]).astype(bf16)
-                deo = (nn(pick, gy_ref[...]) * weight).astype(bf16)
-                gate_up = slice(q * third, (q + 1) * third)
-                down = slice(2 * third + q * HD, 2 * third + (q + 1) * HD)
-                down_tail = slice(2 * third + 2 * HD, lanes)
-                gu = nn(xe, w[:, gate_up])
-                d0 = nn(deo, w[:, down])
-                d1 = nn(deo, w[:, down_tail])
-                if q == 1:
-                    d1 = pltpu.roll(d1, TAIL, 1)
-                tail = gu[:, 2 * HD :]
-
-                def unit(gate, up, dact):
-                    sig = jax.nn.sigmoid(gate)
-                    silu = gate * sig
-                    return silu * up, dact * up * sig * (1.0 + gate * (1.0 - sig)), dact * silu
-
-                a0, dg0, du0 = unit(gu[:, :HD], gu[:, HD : 2 * HD], d0)
-                a1, dg1, du1 = unit(tail, pltpu.roll(tail, TAIL, 1), d1)
-                a1 = jnp.where(low_half, a1, 0.0)
-                if q == 1:
-                    a1 = pltpu.roll(a1, TAIL, 1)
-                dgu1 = jnp.where(low_half, dg1, pltpu.roll(du1, TAIL, 1))
-                a0, a1 = a0.astype(bf16), a1.astype(bf16)
-                dgu = jnp.concatenate([dg0.astype(bf16), du0.astype(bf16), dgu1.astype(bf16)], axis=1)
-                eo = nt(a0, w[:, down]) + nt(a1, w[:, down_tail])
-                y_buf[at, :width] = (eo * weight).astype(bf16)
-                y_buf[at, width:] = nt(dgu, w[:, gate_up]).astype(bf16)
-                put(q * third, tn(xe, dgu), slot)
-                put(2 * third + q * HD, tn(deo, a0), slot)
-                tails.append((deo, a1))
-            put(2 * third + 2 * HD, tn(*tails[0]) + tn(*tails[1]), slot)
-
-        if exchange:
-
-            @pl.when((step >= 1) & (step <= pairs))
-            def _():
-                finish(step - 1)
-
-            @pl.when((step >= 1) & (step + 1 < pairs))
-            def _():
-                signal(g_free)
-
-            @pl.when((step >= 2) & (step < pairs))
-            def _():
-                pl.semaphore_wait(g_free, 1)
-
-            @pl.when(step < pairs)
-            def _():
-                leave(lax.rem(step, 2)).start()
+            pair_of_experts(2 * step, 2 * step, w_ref.at[0], rank_c, routes_ref, x_ref, gy_ref, y_buf, pick_buf, put)
 
         @pl.when(step >= pairs)
         def _():
@@ -365,58 +245,352 @@
     def held(step):
         return jnp.minimum(step, pairs - 1)
 
-    def behind(step):
-        return jnp.clip(step - 1, 0, pairs - 1) if exchange else held(step)
-
     def block(step):
         return (0, jnp.maximum(step - pairs, 0))
 
     once = pl.Buffered(1)
     whole = pl.BlockSpec((rows, width), lambda s: (0, 0), pipeline_mode=once)
-    of_pair = pl.BlockSpec((2, 2, rows), lambda s: (held(s), 0, 0))
-    anywhere = pl.BlockSpec(memory_space=pl.ANY)
-    dma = pltpu.SemaphoreType.DMA
-    traded = [
-        pltpu.VMEM((2, count, height, lanes), bf16),
-        pltpu.VMEM((2, count, height, lanes), bf16),
-        pltpu.VMEM((2, count, height, lanes), bf16),
-        dma((2, count)),
-        dma((2, count)),
-        dma((2,)),
-        dma((2,)),
-        pltpu.SemaphoreType.REGULAR,
-        pltpu.SemaphoreType.REGULAR,
-    ]
-    remote = dict(collective_id=1, has_side_effects=True) if exchange else {}
+    of_pair = pl.BlockSpec((1, width, lanes), lambda s: (held(s), 0, 0))
     return pl.pallas_call(
         kernel,
         grid=(pairs + blocks,),
-        in_specs=[pl.BlockSpec((rows, HD), lambda s: (0, 0), pipeline_mode=once), of_pair, whole, whole]
-        + [anywhere] * len(flat)
-        + [pl.BlockSpec((rows, tile), block)],
-        out_specs=[
-            pl.BlockSpec((count, 1, height, lanes), lambda s: (0, behind(s), 0, 0)),
+        in_specs=[
+            pl.BlockSpec((rows, HD), lambda s: (0, 0), pipeline_mode=once),
+            pl.BlockSpec((2, 2, rows), lambda s: (held(s), 0, 0)),
+            whole,
+            whole,
+            of_pair,
             pl.BlockSpec((rows, tile), block),
         ],
+        out_specs=[of_pair, pl.BlockSpec((rows, tile), block)],
+        scratch_shapes=[pltpu.VMEM((2 * pairs * CAP, 2 * width), bf16), pltpu.VMEM((rows, 2 * pairs * CAP), bf16)],
+        out_shape=[
+            jax.ShapeDtypeStruct((pairs, width, lanes), bf16),
+            jax.ShapeDtypeStruct((rows, 2 * width), f32),
+        ],
+        compiler_params=pltpu.CompilerParams(vmem_limit_bytes=62 * 10**6),
+        name="experts",
+    )(rank_cols, routes, x, gy, weights, sums)
+
+
+def expert_pass(rank_cols, routes, x, gy, packed, near, far, members):
+    rows, width = x.shape
+    calls = len(packed)
+    size, height, lanes = packed[0].shape
+    half = size // 2
+    pairs = calls * size
+    blocks = 6
+    tile = 2 * width // blocks
+    period = size + blocks
+    early = calls - 1
+    dma = pltpu.SemaphoreType.DMA
+    n_in = 4 + calls + 2 * early + 2
+
+    def kernel(*refs):
+        rank_c, routes_ref, x_ref, gy_ref = refs[:4]
+        own = refs[4 : 4 + calls]
+        near_in = refs[4 + calls : 4 + calls + 2 * early]
+        far_in = refs[n_in - 2 : n_in]
+        outs = refs[n_in:]
+        sums_out, grads, x_last, y_last = outs[:4]
+        far_out = outs[4 : 4 + 2 * early]
+        plain_x, plain_y, added_x, added_y, via_x, via_y = outs[4 + 2 * early : 10 + 2 * early]
+        scratch = outs[10 + 2 * early :]
+        w_buf, y_buf, pick_buf, total, kept, leaving, arriving, load_buf, add_buf = scratch[:9]
+        local_sem, push_sem, pull_sem, send_sem, recv_sem, keep_sem, load_sem, add_sem = scratch[9:17]
+        chip_send, chip_recv, cross_send, cross_recv, straight_send, straight_recv, w_free, g_free = scratch[17:]
+        step = pl.program_id(0)
+        call, phase = step // period, lax.rem(step, period)
+        pair = call * size + phase
+        x_side, y_side = chip_neighbours()
+        other = {"dp": sibling()}
+        near_x = [near_in[2 * i] for i in range(early)] + [x_last]
+        near_y = [near_in[2 * i + 1] for i in range(early)] + [y_last]
+        far_all = [far_in, *(far_out[2 * i : 2 * i + 2] for i in range(early))]
+
+        def chip(index, source, target, device):
+            return remote(source, target, chip_send.at[index], chip_recv.at[index], {"dp": device})
+
+        forward = []
+        for i in range(early):
+            forward.append(chip(2 * i, near_x[i + 1].at[:half], far_out[2 * i], y_side))
+            forward.append(chip(2 * i + 1, near_y[i + 1].at[half:], far_out[2 * i + 1], x_side))
+        fresh = [
+            chip(2 * early, own[-1], x_last, x_side),
+            chip(2 * early + 1, own[-1], y_last, y_side),
+        ]
+
+        def weights(now, slot, sub):
+            chunk, side = sub // 2, sub % 2
+            sources = [own[chunk], near_x[chunk], near_y[chunk], far_all[chunk][side]]
+            begins = [chunk * size] * 3 + [chunk * size + side * half]
+            found = []
+            for k, (source, begin) in enumerate(zip(sources, begins)):
+                source = source.at[now - begin]
+                mine = w_buf.at[slot, pl.ds(2 * k * height, height)]
+                found.append(pltpu.make_async_copy(source, mine, local_sem.at[slot, k]))
+                theirs = w_buf.at[slot, pl.ds((2 * k + 1) * height, height)]
+                found.append(remote(source, theirs, push_sem.at[slot, k], pull_sem.at[slot, k], other))
+            return found
+
+        def start(now):
+            slot = lax.rem(now, 2)
+            for sub in range(2 * calls):
+
+                @pl.when((now >= sub * half) & (now < (sub + 1) * half))
+                def _():
+                    if sub >= 2:
+
+                        @pl.when(now == sub * half)
+                        def _():
+                            forward[sub - 2].wait_recv()
+
+                    for copy in weights(now, slot, sub):
+                        copy.start()
+
+        def leave(slot):
+            return remote(leaving.at[slot], arriving.at[slot], send_sem.at[slot], recv_sem.at[slot], other)
+
+        def keep(now):
+            slot = lax.rem(now, 2)
+            return pltpu.make_async_copy(kept.at[slot], grads.at[:, now], keep_sem.at[slot])
+
+        def crossing(now, first):
+            at = now // size * half + lax.rem(now, size) - (0 if first else half)
+            sems = cross_send.at[now], cross_recv.at[now]
+            if first:
+                return remote(grads.at[3, now], via_x.at[at], *sems, {"dp": x_side})
+            return remote(grads.at[3, now], via_y.at[at], *sems, {"dp": y_side})
+
+        def straight(now, first):
+            at = now // size * half + lax.rem(now, size) - (0 if first else half)
+            sems = straight_send.at[now], straight_recv.at[now]
+            if first:
+                return remote(grads.at[1, now], plain_x.at[at], *sems, {"dp": x_side})
+            return remote(grads.at[2, now], plain_y.at[at], *sems, {"dp": y_side})
+
+        def by_half(now, do):
+            for first in (True, False):
+
+                @pl.when((lax.rem(now, size) < half) if first else (lax.rem(now, size) >= half))
+                def _():
+                    do(first)
+
+        def scatter(now):
+            def both(first):
+                crossing(now, first).start()
+                straight(now, first).start()
+
+            by_half(now, both)
+
+        def finish(now):
+            slot = lax.rem(now, 2)
+            leave(slot).wait()
+            for k in range(4):
+                kept[slot, k] = (kept[slot, k].astype(f32) + arriving[slot, k].astype(f32)).astype(bf16)
+            keep(now).start()
+
+        def signal(sem):
+            pl.semaphore_signal(sem, inc=1, device_id=other, device_id_type=pl.DeviceIdType.MESH)
+
+        def put(at, value):
+            slot = lax.rem(pair, 2)
+            for k in range(4):
+                for parity, target in enumerate((kept, leaving)):
+                    row = (2 * k + parity) * height
+                    target[slot, k, :, at : at + value.shape[1]] = value[row : row + height].astype(bf16)
+
+        def loads(now):
+            at = now // size * half + lax.rem(now, half)
+
+            def copies(first):
+                via, block = (via_x, 2) if first else (via_y, 1)
+                return (
+                    pltpu.make_async_copy(via.at[at], load_buf.at[0], load_sem.at[0]),
+                    pltpu.make_async_copy(grads.at[block, now], load_buf.at[1], load_sem.at[1]),
+                )
+
+            return copies
+
+        def stores(now, first):
+            at = now // size * half + lax.rem(now, half)
+            return pltpu.make_async_copy(add_buf, (added_y if first else added_x).at[at], add_sem)
+
+        @pl.when(step == 0)
+        def _():
+            barrier = pltpu.get_barrier_semaphore()
+            for device in (x_side, y_side, sibling()):
+                pl.semaphore_signal(barrier, inc=1, device_id={"dp": device}, device_id_type=pl.DeviceIdType.MESH)
+            pl.semaphore_wait(barrier, 3)
+            start(step)
+            for copy in (*forward[:2], *fresh, *forward[2 : 2 * early - 2]):
+                copy.start()
+
+        @pl.when(phase < size)
+        def _():
+            @pl.when((pair >= 1) & (pair + 1 < pairs))
+            def _():
+                signal(w_free)
+                pl.semaphore_wait(w_free, 1)
+
+            @pl.when(pair == size + 1)
+            def _():
+                for copy in fresh:
+                    copy.wait_recv()
+                for copy in forward[2 * early - 2 :]:
+                    copy.start()
+
+            @pl.when(pair + 1 < pairs)
+            def _():
+                start(pair + 1)
+
+            @pl.when(pair >= 2)
+            def _():
+                keep(pair - 2).wait()
+
+            @pl.when((pair >= 2) & (pair - 2 < early * size))
+            def _():
+                scatter(pair - 2)
+
+            slot = lax.rem(pair, 2)
+            for copy in weights(0, slot, 0):
+                copy.wait()
+            pair_of_experts(
+                2 * pair, 2 * phase, w_buf.at[slot], rank_c, routes_ref, x_ref, gy_ref, y_buf, pick_buf, put
+            )
+
+        @pl.when((phase >= 1) & (phase <= size))
+        def _():
+            finish(pair - 1)
+
+            @pl.when(pair + 1 < pairs)
+            def _():
+                signal(g_free)
+
+        @pl.when(phase < size)
+        def _():
+            @pl.when(pair >= 2)
+            def _():
+                pl.semaphore_wait(g_free, 1)
+
+            leave(lax.rem(pair, 2)).start()
+
+        @pl.when(phase >= size)
+        def _():
+            block = phase - size
+            at = pl.ds(pl.multiple_of(block * tile, tile), tile)
+            made = nn(pick_buf[...], y_buf[:, at])
+
+            @pl.when(call == 0)
+            def _():
+                total[:, at] = made.astype(bf16)
+
+            @pl.when((call > 0) & (call < calls - 1))
+            def _():
+                total[:, at] = (made + total[:, at].astype(f32)).astype(bf16)
+
+            @pl.when(call == calls - 1)
+            def _():
+                sums_out[...] = (made + total[:, at].astype(f32)).astype(bf16)
+
+            before = (call - 1) * size + block
+
+            @pl.when((call > 0) & (block >= 2) & (block < size + 2))
+            def _():
+                by_half(before - 2, lambda first: stores(before - 2, first).wait())
+
+            @pl.when((call > 0) & (block >= 1) & (block < size + 1))
+            def _():
+                def add_to(first):
+                    for copy in loads(before - 1)(first):
+                        copy.wait()
+                    add_buf[...] = (load_buf[0].astype(f32) + load_buf[1].astype(f32)).astype(bf16)
+                    stores(before - 1, first).start()
+
+                by_half(before - 1, add_to)
+
+            @pl.when((call > 0) & (block < size))
+            def _():
+                def load(first):
+                    crossing(before, first).wait_recv()
+                    for copy in loads(before)(first):
+                        copy.start()
+
+                by_half(before, load)
+
+        @pl.when(step == calls * period - 1)
+        def _():
+            for now in (pairs - 2, pairs - 1):
+                keep(now).wait()
+            for copy in (*forward, *fresh):
+                copy.wait_send()
+            for now in range(early * size):
+                first = now % size < half
+                crossing(now, first).wait_send()
+                straight(now, first).wait()
+
+    def held(step):
+        return step // period * size + jnp.minimum(lax.rem(step, period), size - 1)
+
+    def block(step):
+        return (0, jnp.where(step >= (calls - 1) * period + size, step - (calls - 1) * period - size, 0))
+
+    once = pl.Buffered(1)
+    whole = pl.BlockSpec((rows, width), lambda s: (0, 0), pipeline_mode=once)
+    anywhere = pl.BlockSpec(memory_space=pl.ANY)
+    some = jax.ShapeDtypeStruct((early * half, height, lanes), bf16)
+    regular = pltpu.SemaphoreType.REGULAR
+    return pl.pallas_call(
+        kernel,
+        grid=(calls * period,),
+        in_specs=[
+            pl.BlockSpec((rows, HD), lambda s: (0, 0), pipeline_mode=once),
+            pl.BlockSpec((2, 2, rows), lambda s: (held(s), 0, 0)),
+            whole,
+            whole,
+        ]
+        + [anywhere] * (n_in - 4),
+        out_specs=[pl.BlockSpec((rows, tile), block)] + [anywhere] * (9 + 2 * early),
+        out_shape=[
+            jax.ShapeDtypeStruct((rows, 2 * width), bf16),
+            jax.ShapeDtypeStruct((4, pairs, height, lanes), bf16),
+        ]
+        + [jax.ShapeDtypeStruct((size, height, lanes), bf16)] * 2
+        + [jax.ShapeDtypeStruct((half, height, lanes), bf16)] * (2 * early)
+        + [some] * 6,
         scratch_shapes=[
             pltpu.VMEM((2, width, lanes), bf16),
-            pltpu.VMEM((2 * pairs * CAP, 2 * width), bf16),
-            pltpu.VMEM((rows, 2 * pairs * CAP), bf16),
-            dma((2, count)),
-        ]
-        + (traded if exchange else []),
-        out_shape=[
-            jax.ShapeDtypeStruct((count, pairs, height, lanes), bf16),
-            jax.ShapeDtypeStruct((rows, 2 * width), f32),
+            pltpu.VMEM((2 * size * CAP, 2 * width), bf16),
+            pltpu.VMEM((rows, 2 * size * CAP), bf16),
+            pltpu.VMEM((rows, 2 * width), bf16),
+            pltpu.VMEM((2, 4, height, lanes), bf16),
+            pltpu.VMEM((2, 4, height, lanes), bf16),
+            pltpu.VMEM((2, 4, height, lanes), bf16),
+            pltpu.VMEM((2, height, lanes), bf16),
+            pltpu.VMEM((height, lanes), bf16),
+            dma((2, 4)),
+            dma((2, 4)),
+            dma((2, 4)),
+            dma((2,)),
+            dma((2,)),
+            dma((2,)),
+            dma((2,)),
+            dma,
+            dma((2 * early + 2,)),
+            dma((2 * early + 2,)),
+            dma((early * size,)),
+            dma((early * size,)),
+            dma((early * size,)),
+            dma((early * size,)),
+            regular,
+            regular,
         ],
-        compiler_params=pltpu.CompilerParams(vmem_limit_bytes=62 * 10**6, **remote),
-        cost_estimate=pl.CostEstimate(
-            flops=pairs * 4 * CAP * width * (4 * rows * 2 + 18 * lanes // 6),
-            bytes_accessed=8 * rows * width * 3,
-            transcendentals=0,
+        compiler_params=pltpu.CompilerParams(
+            vmem_limit_bytes=62 * 10**6, collective_id=1, has_side_effects=True
         ),
+        cost_estimate=pl.CostEstimate(flops=2 * 10**11, bytes_accessed=10**8, transcendentals=0),
         name="experts",
-    )(rank_cols, routes, x, gy, *flat, sums)
+    )(rank_cols, routes, x, gy, *packed, *(side for both in near for side in both), *far)
 
 
 def remote(source, target, send_sem, recv_sem, device):
@@ -591,9 +765,13 @@
     def pair(a, b):
         return [a[:, :HD], b[:, :HD], jnp.concatenate([a[:, HD:], b[:, HD:]], axis=1)]
 
+    def inner(a, b):
+        a, b, tails = pair(a, b)
+        return [a, tails, b]
+
     return [
         jnp.concatenate(
-            pair(gate[e], up[e]) + pair(gate[e + 1], up[e + 1]) + pair(down[e], down[e + 1]), axis=1
+            pair(gate[e], up[e]) + pair(gate[e + 1], up[e + 1]) + inner(down[e], down[e + 1]), axis=1
         )
         for e in range(0, 2 * CALL_PAIRS, 2)
     ]
@@ -615,9 +793,10 @@
     def kernel(*refs):
         q_ref, o_ref, k_ref, v_ref, gains_ref, cot_ref, ids_ref, weights_ref, gate_ref, up_ref, down_ref = refs[:11]
         square_all, tall_all, grad_all = refs[11:14]
-        rank_cols, routes, packed = (refs[14 + calls * i : 14 + calls * (i + 1)] for i in range(3))
-        from_x, from_y = refs[14 + 3 * calls : 16 + 3 * calls]
-        sems = refs[16 + 3 * calls :]
+        rank_cols, routes = refs[14:16]
+        packed = refs[16 : 16 + calls]
+        from_x, from_y = refs[16 + calls : 18 + calls]
+        sems = refs[18 + calls :]
         line_send, line_recv, grad_send, grad_recv, chip_send, chip_recv, core_send, core_recv = sems
         me, z = lax.axis_index("dp"), lax.axis_index("tensor")
         x_side, y_side = chip_neighbours()
@@ -687,24 +866,20 @@
         for copy in trades[2:]:
             copy.start()
 
-        lane = lax.broadcasted_iota(jnp.int32, (rows, HD), 1)
-        weight = jnp.zeros((rows, HD), f32)
-        named = jnp.zeros((rows, HD), f32)
-        for route in range(ids_ref.shape[1]):
-            here = ids_ref[:, route : route + 1] == lane
+        expert = lax.broadcasted_iota(jnp.int32, (HD, rows), 0)
+        weight = jnp.zeros((HD, rows), f32)
+        named = jnp.zeros((HD, rows), f32)
+        for route in range(ids_ref.shape[0]):
+            here = ids_ref[route : route + 1, :] == expert
             named = jnp.where(here, 1.0, named)
-            weight = jnp.where(here, weights_ref[:, route : route + 1], weight)
+            weight = jnp.where(here, weights_ref[route : route + 1, :], weight)
         row = lax.broadcasted_iota(jnp.int32, (rows, rows), 0)
-        earlier = (row > lax.broadcasted_iota(jnp.int32, (rows, rows), 1)).astype(bf16)
-        rank = jnp.where(named > 0.0, nn(earlier, named.astype(bf16)), -1.0)
-        by_rank, by_weight = jnp.transpose(rank), jnp.transpose(weight)
-        for call in range(calls):
-            turned = rank if call == 0 else pltpu.roll(rank, HD - 2 * CALL_PAIRS * call, 1)
-            rank_cols[call][...] = turned.astype(bf16)
-            for e in range(2 * CALL_PAIRS):
-                at = 2 * CALL_PAIRS * call + e
-                routes[call][e, 0:1, :] = by_rank[at : at + 1]
-                routes[call][e, 1:2, :] = by_weight[at : at + 1]
+        later = (row < lax.broadcasted_iota(jnp.int32, (rows, rows), 1)).astype(bf16)
+        rank = jnp.where(named > 0.0, nn(named.astype(bf16), later), -1.0)
+        rank_cols[...] = jnp.transpose(rank).astype(bf16)
+        for e in range(EXPERTS):
+            routes[e, 0:1, :] = rank[e : e + 1]
+            routes[e, 1:2, :] = weight[e : e + 1]
         for call in range(1, calls):
             pack(call)
 
@@ -747,14 +922,13 @@
     return pl.pallas_call(
         kernel,
         in_specs=in_vmem(11),
-        out_specs=in_vmem(3 + 3 * calls) + [pl.BlockSpec(memory_space=pl.ANY)] * 2,
+        out_specs=in_vmem(5 + calls) + [pl.BlockSpec(memory_space=pl.ANY)] * 2,
         out_shape=[
             jax.ShapeDtypeStruct((members, devices * height, 2 * part), bf16),
             jax.ShapeDtypeStruct((devices * height, tall), bf16),
             jax.ShapeDtypeStruct((rows, width), bf16),
         ]
-        + [jax.ShapeDtypeStruct((rows, HD), bf16)] * calls
-        + [jax.ShapeDtypeStruct((2 * CALL_PAIRS, 2, rows), f32)] * calls
+        + [jax.ShapeDtypeStruct((rows, HD), bf16), jax.ShapeDtypeStruct((EXPERTS, 2, rows), f32)]
         + [chunk_shape] * (calls + 2),
         scratch_shapes=[dma((2, members - 1))] * 4 + [dma((9,))] * 2 + [dma((8,))] * 2,
         compiler_params=pltpu.CompilerParams(collective_id=2, has_side_effects=True, vmem_limit_bytes=56 * 2**20),
@@ -782,9 +956,9 @@
 
     def kernel(x_ref, square_ref, tall_ref, cos_ref, sin_ref, *rest):
         chunks, rest = rest[:count], rest[count:]
-        normed_ref, q_ref, kv_all, mixed_ref, hidden_ref, rows_all, sums_ref = rest[:7]
-        landed, rest = rest[7 : 5 + 2 * count], rest[5 + 2 * count :]
-        blank, kv_send, kv_recv, row_send, row_recv, chip_send, chip_recv, blank_sem = rest
+        normed_ref, q_ref, kv_all, mixed_ref, hidden_ref, rows_all = rest[:6]
+        landed, rest = rest[6 : 4 + 2 * count], rest[4 + 2 * count :]
+        kv_send, kv_recv, row_send, row_recv, chip_send, chip_recv = rest
         z = lax.axis_index("tensor")
         x_side, y_side = chip_neighbours()
         meet(members, False)
@@ -799,15 +973,6 @@
         ]
         for copy in moves:
             copy.start()
-        blank[...] = jnp.zeros_like(blank)
-        fills = [
-            pltpu.make_async_copy(blank, sums_ref.at[b * own_rows : (b + 1) * own_rows, s * width : (s + 1) * width], blank_sem.at[b, s])
-            for b in range(members)
-            for s in range(2)
-        ]
-        for copy in fills:
-            copy.start()
-
         def block_of(ref):
             return lambda block: ref.at[pl.ds(pl.multiple_of(block * own_rows, 16), own_rows)]
 
@@ -858,8 +1023,6 @@
         row_line.close()
         for copy in moves:
             copy.wait()
-        for copy in fills:
-            copy.wait()
 
     count = 2 + len(packed)
     anywhere = pl.BlockSpec(memory_space=pl.ANY)
@@ -867,7 +1030,7 @@
     return pl.pallas_call(
         kernel,
         in_specs=in_vmem(5) + [anywhere] * count,
-        out_specs=in_vmem(6) + [anywhere] * (1 + 2 + 2 * len(packed)),
+        out_specs=in_vmem(6) + [anywhere] * (2 + 2 * len(packed)),
         out_shape=[
             jax.ShapeDtypeStruct((own_rows, width), bf16),
             jax.ShapeDtypeStruct((own_rows, width), bf16),
@@ -875,14 +1038,10 @@
             jax.ShapeDtypeStruct((own_rows, width), bf16),
             jax.ShapeDtypeStruct((own_rows, width), f32),
             jax.ShapeDtypeStruct((rows, width), bf16),
-            jax.ShapeDtypeStruct((rows, 2 * width), f32),
         ]
         + [jax.ShapeDtypeStruct((size // 2, height, lanes), bf16)] * 2
         + [jax.ShapeDtypeStruct((size, height, lanes), bf16)] * (2 * len(packed)),
-        scratch_shapes=[pltpu.VMEM((own_rows, width), f32)]
-        + [dma((2, members - 1))] * 4
-        + [dma((2 + 2 * len(packed),))] * 2
-        + [dma((members, 2))],
+        scratch_shapes=[dma((2, members - 1))] * 4 + [dma((2 + 2 * len(packed),))] * 2,
         compiler_params=pltpu.CompilerParams(collective_id=3, has_side_effects=True, vmem_limit_bytes=56 * 2**20),
         cost_estimate=pl.CostEstimate(flops=10**11, bytes_accessed=10**7, transcendentals=0),
         name="attention_front",
@@ -890,7 +1049,7 @@
 
 
 def attention_back(
-    sums, cotangent, hidden, tokens, normed, q, kv_all, mixed, square, tall, cosine, sine, last_chunk, to_x, to_y, members
+    sums, cotangent, hidden, tokens, normed, q, kv_all, mixed, square, tall, cosine, sine, grads, to_x, to_y, members
 ):
     own_rows, width = tokens.shape
     rows = own_rows * members
@@ -901,7 +1060,7 @@
     dma = pltpu.SemaphoreType.DMA
 
     def kernel(sums_ref, cot_ref, hidden_ref, x_ref, normed_ref, q_ref, kv_ref, mixed_ref, square_ref, tall_ref, *rest):
-        cos_ref, sin_ref, chunk, to_x_ref, to_y_ref = rest[:5]
+        cos_ref, sin_ref, grads_ref, to_x_ref, to_y_ref = rest[:5]
         grad_ref, parts, x_before, y_before, x_last, y_last = rest[5:11]
         do_ref, dq_ref, dkv_ref, total, kv_total, stage, tall_part, back_part = rest[11:19]
         back_leave, back_arrive, kv_leave, kv_arrive = rest[19:23]
@@ -911,6 +1070,10 @@
         x_side, y_side = chip_neighbours()
         first, second = slice(0, size // 2), slice(size // 2, size)
 
+        def chunk(block, span):
+            return grads_ref.at[block, pairs_before + span.start : pairs_before + span.stop]
+
+
         def chip(index, source, target, device):
             return remote(source, target, chip_send.at[index], chip_recv.at[index], {"dp": device})
 
@@ -920,19 +1083,19 @@
             )
             for b in range(members)
         ] + [
-            pltpu.make_async_copy(chunk.at[1, second], added.at[0], added_sem.at[0]),
-            pltpu.make_async_copy(chunk.at[2, first], added.at[1], added_sem.at[1]),
+            pltpu.make_async_copy(chunk(1, second), added.at[0], added_sem.at[0]),
+            pltpu.make_async_copy(chunk(2, first), added.at[1], added_sem.at[1]),
         ]
         for copy in loads:
             copy.start()
         meet(members, False)
         moves = [
-            chip(0, chunk.at[3, first], through.at[0], x_side),
-            chip(1, chunk.at[3, second], through.at[1], y_side),
+            chip(0, chunk(3, first), through.at[0], x_side),
+            chip(1, chunk(3, second), through.at[1], y_side),
             chip(2, to_x_ref, x_before, x_side),
             chip(3, to_y_ref, y_before, y_side),
-            chip(4, chunk.at[1, first], x_last.at[first], x_side),
-            chip(5, chunk.at[2, second], y_last.at[second], y_side),
+            chip(4, chunk(1, first), x_last.at[first], x_side),
+            chip(5, chunk(2, second), y_last.at[second], y_side),
             chip(6, added.at[0], x_last.at[second], x_side),
             chip(7, added.at[1], y_last.at[first], y_side),
         ]
@@ -1026,7 +1189,9 @@
 
     hops = (2, members - 1)
     anywhere = pl.BlockSpec(memory_space=pl.ANY)
-    size, height, lanes = to_x.shape
+    _, height, lanes = to_x.shape
+    size = CALL_PAIRS
+    pairs_before = grads.shape[1] - size
     halves = (2, size // 2, height, lanes)
     return pl.pallas_call(
         kernel,
@@ -1036,7 +1201,8 @@
             jax.ShapeDtypeStruct((own_rows, width), f32),
             jax.ShapeDtypeStruct((width, 2 * width + tall.shape[1]), bf16),
         ]
-        + [jax.ShapeDtypeStruct((size, height, lanes), bf16)] * 4,
+        + [jax.ShapeDtypeStruct(to_x.shape, bf16)] * 2
+        + [jax.ShapeDtypeStruct((size, height, lanes), bf16)] * 2,
         scratch_shapes=[
             pltpu.VMEM((own_rows, width), bf16),
             pltpu.VMEM((own_rows, width), bf16),
@@ -1045,7 +1211,7 @@
             pltpu.VMEM((own_rows, kv), f32),
             pltpu.VMEM((2, width, part), bf16),
             pltpu.VMEM(tall.shape, bf16),
-            pltpu.VMEM((members, own_rows, width), f32),
+            pltpu.VMEM((members, own_rows, width), bf16),
             pltpu.VMEM((2, own_rows, width), bf16),
             pltpu.VMEM((*hops, own_rows, width), bf16),
             pltpu.VMEM((2, own_rows, kv), bf16),
@@ -1057,7 +1223,7 @@
         cost_estimate=pl.CostEstimate(flops=10**11, bytes_accessed=10**7, transcendentals=0),
         name="attention_back",
     )(
-        sums, cotangent, hidden, tokens, normed, q, kv_all, mixed, square, tall, cosine, sine, last_chunk, to_x, to_y
+        sums, cotangent, hidden, tokens, normed, q, kv_all, mixed, square, tall, cosine, sine, grads, to_x, to_y
     )
 
 
@@ -1194,7 +1360,7 @@
             pltpu.VMEM((2, height, 2 * part), bf16),
             pltpu.VMEM((*hops, height, 2 * part), bf16),
             pltpu.VMEM((members, height, tall), bf16),
-            pltpu.VMEM((members, own_rows, width), f32),
+            pltpu.VMEM((members, own_rows, width), bf16),
             pltpu.VMEM((2, own_rows, width), bf16),
             pltpu.VMEM((*hops, own_rows, width), bf16),
             pltpu.VMEM((own_rows, width), f32),
@@ -1212,45 +1378,51 @@
     )(parts, sums, hidden)
 
 
-def unpack_all(chunks, from_x, from_y):
-    calls = len(chunks)
-    _, pairs, height, lanes = chunks[0].shape
+def unpack_all(grads, plain, added, last):
+    _, pairs, height, lanes = grads.shape
+    half = CALL_PAIRS // 2
     units = lanes // 6
     tail = units - HD
     step = 48 if height % 48 == 0 else height
-
-    def kernel(*refs):
-        gate, up, down = refs[3 * calls :]
-        for call in range(calls):
-            own, by_x, by_y = refs[3 * call : 3 * call + 3]
+    others = (*plain, *added, *last)
+
+    def kernel(own, plain_x, plain_y, added_x, added_y, last_x, last_y, gate, up, down):
+        for call in range(pairs // CALL_PAIRS):
             found = [[], [], []]
-            for pair in range(pairs):
-                value = own[0, pair].astype(f32) + by_x[pair].astype(f32) + by_y[pair].astype(f32)
+            for turn in range(CALL_PAIRS):
+                pair = call * CALL_PAIRS + turn
+                at = call * half + turn % half
+                if pair >= pairs - CALL_PAIRS:
+                    by_x, by_y = last_x[turn], last_y[turn]
+                elif turn < half:
+                    by_x, by_y = plain_x[at], added_y[at]
+                else:
+                    by_x, by_y = added_x[at], plain_y[at]
+                value = own[0, pair].astype(f32) + by_x.astype(f32) + by_y.astype(f32)
                 tiles = [value[:, i * HD : (i + 1) * HD] for i in range(9)]
-                for i, (a, b) in enumerate(((0, 1), (3, 4), (6, 7))):
-                    ends = tiles[a - a % 3 + 2]
-                    left = jnp.concatenate([tiles[a], ends[:, :tail]], axis=1)
-                    right = jnp.concatenate([tiles[b], ends[:, tail:]], axis=1)
+                for i, (a, b, both) in enumerate(((0, 1, 2), (3, 4, 5), (6, 8, 7))):
+                    left = jnp.concatenate([tiles[a], tiles[both][:, :tail]], axis=1)
+                    right = jnp.concatenate([tiles[b], tiles[both][:, tail:]], axis=1)
                     if i < 2:
                         found[0].append(left)
                         found[1].append(right)
                     else:
                         found[2] += [left, right]
+            span = slice(2 * CALL_PAIRS * call, 2 * CALL_PAIRS * (call + 1))
             for out, values in zip((gate, up, down), found):
-                out[:, 2 * pairs * call : 2 * pairs * (call + 1), :] = jnp.swapaxes(jnp.stack(values), 0, 1)
-
-    chunk = pl.BlockSpec((1, pairs, step, lanes), lambda i: (0, 0, i, 0))
-    other = pl.BlockSpec((pairs, step, lanes), lambda i: (0, i, 0))
-    shape = (height, 2 * pairs * calls, units)
+                out[:, span, :] = jnp.swapaxes(jnp.stack(values), 0, 1)
+
+    shape = (height, 2 * pairs, units)
     return pl.pallas_call(
         kernel,
         grid=(height // step,),
-        in_specs=[chunk, other, other] * calls,
+        in_specs=[pl.BlockSpec((1, pairs, step, lanes), lambda i: (0, 0, i, 0))]
+        + [pl.BlockSpec((other.shape[0], step, lanes), lambda i: (0, i, 0)) for other in others],
         out_specs=[pl.BlockSpec((step, *shape[1:]), lambda i: (i, 0, 0))] * 3,
         out_shape=[jax.ShapeDtypeStruct(shape, f32)] * 3,
         compiler_params=pltpu.CompilerParams(vmem_limit_bytes=48 * 2**20),
         name="unpack",
-    )(*(array for call in zip(chunks, from_x, from_y) for array in call))
+    )(grads, *others)
 
 
 def pack(gate, up, down):
@@ -1259,7 +1431,9 @@
 
     gate, up, down = (jnp.transpose(w, (1, 0, 2)) for w in (gate, up, down))
     gate_up = pair(gate, up)
-    return jnp.concatenate([gate_up[0::2], gate_up[1::2], pair(down[0::2], down[1::2])], axis=-1)
+    a, b = down[0::2], down[1::2]
+    inner = jnp.concatenate([a[..., :HD], a[..., HD:], b[..., HD:], b[..., :HD]], axis=-1)
+    return jnp.concatenate([gate_up[0::2], gate_up[1::2], inner], axis=-1)
 
 
 def unpack(packed):
@@ -1278,43 +1452,10 @@
 
     gate0, up0 = halves(packed[..., :third])
     gate1, up1 = halves(packed[..., third : 2 * third])
-    down0, down1 = halves(packed[..., 2 * third :])
+    down0, down1 = packed[..., 2 * third : 2 * third + third // 2], packed[..., 2 * third + third // 2 :]
+    tail = third // 2 - HD
+    down1 = jnp.concatenate([down1[..., tail:], down1[..., :tail]], axis=-1)
     return experts(gate0, gate1), experts(up0, up1), experts(down0, down1)
-
-
-def flip(value, bit):
-    count = lax.axis_size("dp")
-    return lax.ppermute(value, "dp", [(i, i ^ bit) for i in range(count)])
-
-
-def half_of(chunk):
-    cut = chunk.shape[0] // 2
-    return slice(0, cut), slice(cut, None)
-
-
-def scatter_step(chunk, before):
-    to_x, to_y = [], []
-    if before is not None:
-        blocks, via_x, via_y = before
-        first, second = half_of(blocks[0])
-        to_x += [blocks[1, first], add(blocks[1, second], via_y)]
-        to_y += [add(blocks[2, first], via_x), blocks[2, second]]
-    if chunk is not None:
-        first, second = half_of(chunk[0])
-        to_x.append(chunk[3, first])
-        to_y.append(chunk[3, second])
-    return flip(jnp.concatenate(to_x), 2), flip(jnp.concatenate(to_y), 4)
-
-
-def before_of(chunks, moved, call):
-    if call == 0:
-        return None
-    cut = CALL_PAIRS // 2
-    return chunks[call - 1], moved[call - 1][0][-cut:], moved[call - 1][1][-cut:]
-
-
-def add(a, b):
-    return (a.astype(f32) + b.astype(f32)).astype(bf16)
 
 
 def routes_of(expert_ids, route_weights):
@@ -1355,7 +1496,7 @@
         pack(*(w[:, 2 * CALL_PAIRS * i : 2 * CALL_PAIRS * (i + 1)] for w in (gate_weight, up_weight, down_weight)))
         for i in range(calls)
     ]
-    gathered = [[[(lax.all_gather(own, "dp", axis=1, tiled=True), 0)]] for own in packed]
+    gathered = [lax.all_gather(own, "dp", axis=1, tiled=True) for own in packed]
 
     gain_one = lax.all_gather(attn_gain, "dp", axis=0, tiled=True).astype(f32)
     gain_two = lax.all_gather(moe_gain, "dp", axis=0, tiled=True).astype(f32)
@@ -1402,11 +1543,10 @@
             grad_all,
             gathered[call],
             sums,
-            False,
         )
         chunks.append(grads)
     shares = [
-        unpack(lax.psum_scatter(grads[0], "dp", scatter_dimension=1, tiled=True).astype(f32)) for grads in chunks
+        unpack(lax.psum_scatter(grads, "dp", scatter_dimension=1, tiled=True).astype(f32)) for grads in chunks
     ]
     gate_out, up_out, down_out = (jnp.concatenate(parts, axis=1) for parts in zip(*shares))
 
@@ -1489,56 +1629,26 @@
         v_weight,
         gains,
         cotangent,
-        expert_ids,
-        route_weights,
+        expert_ids.T,
+        route_weights.T,
         gate_weight,
         up_weight,
         down_weight,
         members,
         devices,
     )
-    square_all, tall_all, grad_all = small[:3]
-    rank_cols, routes, packed = (small[3 + calls * i : 3 + calls * (i + 1)] for i in range(3))
-    near = [tuple(small[3 + 3 * calls :])]
+    square_all, tall_all, grad_all, rank_cols, routes = small[:5]
+    packed, near = small[5 : 5 + calls], [tuple(small[5 + calls :])]
     cosine, sine = doubled_tables(rows)
-    normed_one, queries, kv_all, mixed, hidden, rows_all, sums, *landed = attention_front(
+    normed_one, queries, kv_all, mixed, hidden, rows_all, *landed = attention_front(
         tokens, square_all, tall_all, cosine, sine, packed[1:-1], near[0], members
     )
-    far = [(landed[1], landed[0])]
     near += [tuple(landed[2 * i : 2 * i + 2]) for i in range(1, calls - 1)]
-    cut = CALL_PAIRS // 2
-    chunks, moved = [], []
-    for call in range(calls):
-        if call == 0:
-            to_x = [from_y[cut:] for _, from_y in near[1:]] + [packed[-1]]
-            to_y = [from_x[:cut] for from_x, _ in near[1:]] + [packed[-1]]
-            got = flip(jnp.concatenate(to_x), 2), flip(jnp.concatenate(to_y), 4)
-        elif call == 1:
-            far += [tuple(side[cut * i : cut * (i + 1)] for side in got) for i in range(calls - 2)]
-            near.append(tuple(side[cut * (calls - 2) :] for side in got))
-            far.append((flip(near[-1][1][cut:], 2), flip(near[-1][0][:cut], 4)))
-        (from_x, from_y), (second, first) = near[call], far[call]
-        own = packed[call]
-        grads, sums = expert_call(
-            rank_cols[call],
-            after(routes[call], moved[call - 2] if call >= 2 else ()),
-            rows_all,
-            grad_all,
-            [
-                [(own, 0), (from_x, 0), (from_y, 0), (first, 0)],
-                [(own, cut), (from_x, cut), (from_y, cut), (second, 0)],
-            ],
-            sums,
-            True,
-        )
-        chunks.append(grads)
-        if call + 1 < calls:
-            moved.append(scatter_step(grads, before_of(chunks, moved, call)))
-
-    blocks, via_x, via_y = before_of(chunks, moved, calls - 1)
-    to_x = jnp.concatenate([blocks[1, :cut], add(blocks[1, cut:], via_y)])
-    to_y = jnp.concatenate([add(blocks[2, :cut], via_x), blocks[2, cut:]])
-    tokens_grad, parts, x_before, y_before, x_last, y_last = attention_back(
+    sums, grads, *others = expert_pass(
+        rank_cols, routes, rows_all, grad_all, packed, near, landed[:2], members
+    )
+    plain, added = others[-6:-4], others[-4:-2]
+    tokens_grad, parts, *moved = attention_back(
         sums,
         cotangent,
         hidden,
@@ -1551,17 +1661,12 @@
         tall_all,
         cosine,
         sine,
-        chunks[-1],
-        to_x,
-        to_y,
+        grads,
+        *added,
         members,
     )
     output, square_grad, tall_grad = reduce_small(parts, sums, hidden, members, devices)
-    gate_out, up_out, down_out = unpack_all(
-        chunks,
-        [got[0] for got in moved[1:]] + [x_before, x_last],
-        [got[1] for got in moved[1:]] + [y_before, y_last],
-    )
+    gate_out, up_out, down_out = unpack_all(grads, plain, moved[:2], moved[2:])
     part = width // members
     return (
         output,

time: 814 us -> 724 us (0.89)
  local copies, waits for them, and re-layouts: 36.7 us -> 13.8 us
  other arithmetic: 22.9 us -> 0.01 us
  waiting for transfers between devices: 20.4 us -> 0 us
  Pallas kernels: 716 us -> 701 us
  starting transfers between devices: 10.2 us -> 0 us
    pallas_call x8 -> x3, Pallas kernels: 397 us -> 372 us  [the longest x1 249 us: expert_pass(): pl.pallas_call(kernel, grid=(calls * period,), in_specs=[pl.BlockSpec((ro...]
    ppermute x10 -> x0, waiting for transfers between devices: 20.4 us -> none  [flip(): return lax.ppermute(value, 'dp', [(i, i ^ bit) for i in range(count)])]
    slice x8 -> x0, local copies, waits for them, and re-layouts: 14.2 us -> none  [the longest x2 6.02 us: body_by_chips(): near.append(tuple((side[cut * (calls - 2):] for side in got)))]
    concatenate x6 -> x0, other arithmetic: 13 us -> none  [the longest x4 7.45 us: scatter_step(): return (flip(jnp.concatenate(to_x), 2), flip(jnp.concatenate(to_y), 4))]
    ppermute x10 -> x0, starting transfers between devices: 10.2 us -> none  [flip(): return lax.ppermute(value, 'dp', [(i, i ^ bit) for i in range(count)])]
    pallas_call x1, Pallas kernels: 115 us -> 125 us  [attention_back(): pl.pallas_call(kernel, in_specs=[anywhere] + in_vmem(11) + [anywhere] * 3...]
    convert_element_type x3 -> x0, other arithmetic: 9.81 us -> none  [add(): return (a.astype(f32) + b.astype(f32)).astype(bf16)]
  transfers between devices with their start and end apart: 10 -> 0, of which waited for: 2 -> 0; matrix products, arithmetic and copies ran while one was open for 3% -> 0% of each run, Pallas kernels for 25% -> 0%
where the time goes in v5:
time: 724 us; the launch traced here: 716 us
  Pallas kernels  701 us (97%)
  local copies, waits for them, and re-layouts  13.8 us (2%)
    pallas_call x1, Pallas kernels, expert_pass(): pl.pallas_call(kernel, grid=(calls * period,), in_specs=[pl.BlockSpec((ro...  249 us
    pallas_call x1, Pallas kernels, attention_back(): pl.pallas_call(kernel, in_specs=[anywhere] + in_vmem(11) + [anywhere] * 3...  125 us
    pallas_call x1, Pallas kernels, gather_small(): pl.pallas_call(kernel, in_specs=in_vmem(11), out_specs=in_vmem(5 + calls)...  109 us
    pallas_call x1, Pallas kernels, attention_front(): pl.pallas_call(kernel, in_specs=in_vmem(5) + [anywhere] * count, out_spec...  104 us
    pallas_call x1, Pallas kernels, reduce_small(): pl.pallas_call(kernel, in_specs=[pl.BlockSpec(memory_space=pl.ANY)] * 2 +...  99.4 us

profile of v5, /device:TPU:0, one launch (start us, length us, event | category | flops | bytes accessed | tf_op | source)
XLA Modules:
  0.0 716.1 jit_solution(12051514012077105178)
XLA Ops:
  0.6 0.7 stack.9
  1.3 0.7 stack.10
  2.0 0.1 copy.28
  2.1 0.6 pad.4.refs_4_
  2.8 109.4 %gather_small.1 = (bf16[4,1536,768]{2,1,0:T(8,128)(2,1)}, bf16[1536,640]{1,0:T(8,128)(2,1)}, bf16[1024,1536]{1,0:T(8,128)(2,1)}, bf16[1024,128]{1,0:T(8,128)(2,1...) custom-call(bf16[192,384]{1,0:T(8,128)(2,1)} %refs_0_.1, ...), custom_call_target="tpu_custom_call" | custom-call | flops 80000000000 | bytes 10000000 | tf_op jit(solution)/shard_map/gather_small/pallas_call | solution.py:922
  112.2 104.3 %attention_front.1 = (bf16[256,1536]{1,0:T(8,128)(2,1)}, bf16[256,1536]{1,0:T(8,128)(2,1)}, bf16[1024,512]{1,0:T(8,128)(2,1)}, bf16[256,1536]{1,0:T(8,128)(2,1)}...) custom-call(bf16[256,1536]{1,0:T(8,128)(2,1)} %x_ref.3, ...), custom_call_target="tpu_custom_call" | custom-call | flops 99999997952 | bytes 10000000 | tf_op jit(solution)/shard_map/attention_front/pallas_call | solution.py:1030
  216.5 249.4 %experts.1 = (bf16[1024,3072]{1,0:T(8,128)(2,1)}, bf16[4,16,192,1152]{3,2,1,0:T(8,128)(2,1)}, bf16[4,192,1152]{2,1,0:T(8,128)(2,1)}, bf16[4,192,1152]{2,1,0:T(8,...) custom-call(bf16[1024,128]{1,0:T(8,128)(2,1)} %get-tuple-element.52., ...), custom_call_target="tpu_custom_call" | custom-call | flops 199999995904 | bytes 100000000 | tf_op jit(solution)/shard_map/experts/pallas_call | solution.py:543
  465.9 0.0 copy-start
  465.9 125.2 %attention_back.1 = (f32[256,1536]{1,0:T(8,128)}, bf16[1536,3712]{1,0:T(8,128)(2,1)}, bf16[6,192,1152]{2,1,0:T(8,128)(2,1)}, bf16[6,192,1152]{2,1,0:T(8,128)(2,1...) custom-call(bf16[1024,3072]{1,0:T(8,128)(2,1)} %get-tuple-element.70.sums_ref, f32[256,1536]{1,0:T(8,128)} %cot_ref.1, ...), custom_call_target="tpu_custom_call" | custom-call | flops 99999997952 | bytes 10000000 | tf_op jit(solution)/shard_map/attention_back/pallas_call | solution.py:1196
  591.1 0.0 copy-done
  591.1 0.0 copy-start.1
  591.1 1.5 copy-done.1
  592.6 0.0 copy-start.2
  592.6 1.5 copy-done.2
  594.1 13.3 %unpack.1 = (f32[192,32,192]{2,1,0:T(8,128)}, f32[192,32,192]{2,1,0:T(8,128)}, f32[192,32,192]{2,1,0:T(8,128)}) custom-call(bf16[4,16,192,1152]{3,2,1,0:T(8,128)(2,1)} %get-tuple-element.76.rest_2_.own, bf16[6,192,1152]{2,1,0:T(8,128)(2,1)S(1)} %copy-done, bf16[6,192,1152]{2,1,0:T(8,128)(2,1)} %get-tuple-element.85.plain_y, ...), custom_call_target="tpu_custom_call" | custom-call | tf_op jit(solution)/shard_map/unpack/pallas_call | solution.py:1416
  607.4 99.4 %reduce_small.1 = (bf16[256,1536]{1,0:T(8,128)(2,1)}, f32[192,768]{1,0:T(8,128)}, f32[192,640]{1,0:T(8,128)}) custom-call(bf16[1536,3712]{1,0:T(8,128)(2,1)} %get-tuple-element.79.parts_ref, bf16[1024,3072]{1,0:T(8,128)(2,1)} %get-tuple-element.70.sums_ref, f32[256,1536]{1,0:T(8,128)} %get-tuple-element.71.hidden_ref), custom_call_target="tpu_custom_call" | custom-call | flops 80000000000 | bytes 10000000 | tf_op jit(solution)/shard_map/reduce_small/pallas_call | solution.py:1345
  706.9 0.0 copy-start.3
  706.9 1.8 slice_reduce_fusion
  708.7 1.8 fusion.1
  710.5 1.9 fusion
  712.4 2.1 copy.31
  714.5 0.0 copy-done.3
  714.5 1.1 copy.32
  (1 shorter events, 0.0 us)
Async XLA Ops:
  465.9 125.2 %copy-start = (bf16[6,192,1152]{2,1,0:T(8,128)(2,1)S(1)}, bf16[6,192,1152]{2,1,0:T(8,128)(2,1)}, u32[]{:S(2)}) copy-start(bf16[6,192,1152]{2,1,0:T(8,128)(2,1)} %get-tuple-element.84.plain_x) | copy-start | bytes 7962628
  591.1 1.5 copy-start.1
  592.6 1.5 copy-start.2
  706.9 7.6 %copy-start.3 = (f32[256,1536]{1,0:T(8,128)S(1)}, f32[256,1536]{1,0:T(8,128)}, u32[]{:S(2)}) copy-start(f32[256,1536]{1,0:T(8,128)} %get-tuple-element.111) | copy-start | bytes 4718596

commit v6 on v5

--- a/solution.py
+++ b/solution.py
@@ -284,18 +284,21 @@
     period = size + blocks
     early = calls - 1
     dma = pltpu.SemaphoreType.DMA
-    n_in = 4 + calls + 2 * early + 2
+    known = len(near)
+    unknown = calls - known
+    n_in = 4 + calls + 2 * known + 2
 
     def kernel(*refs):
         rank_c, routes_ref, x_ref, gy_ref = refs[:4]
         own = refs[4 : 4 + calls]
-        near_in = refs[4 + calls : 4 + calls + 2 * early]
+        near_in = refs[4 + calls : n_in - 2]
         far_in = refs[n_in - 2 : n_in]
         outs = refs[n_in:]
-        sums_out, grads, x_last, y_last = outs[:4]
-        far_out = outs[4 : 4 + 2 * early]
-        plain_x, plain_y, added_x, added_y, via_x, via_y = outs[4 + 2 * early : 10 + 2 * early]
-        scratch = outs[10 + 2 * early :]
+        sums_out, grads = outs[:2]
+        near_out, outs = outs[2 : 2 + 2 * unknown], outs[2 + 2 * unknown :]
+        far_out = outs[: 2 * early]
+        plain_x, plain_y, added_x, added_y, via_x, via_y = outs[2 * early : 6 + 2 * early]
+        scratch = outs[6 + 2 * early :]
         w_buf, y_buf, pick_buf, total, kept, leaving, arriving, load_buf, add_buf = scratch[:9]
         local_sem, push_sem, pull_sem, send_sem, recv_sem, keep_sem, load_sem, add_sem = scratch[9:17]
         chip_send, chip_recv, cross_send, cross_recv, straight_send, straight_recv, w_free, g_free = scratch[17:]
@@ -304,8 +307,8 @@
         pair = call * size + phase
         x_side, y_side = chip_neighbours()
         other = {"dp": sibling()}
-        near_x = [near_in[2 * i] for i in range(early)] + [x_last]
-        near_y = [near_in[2 * i + 1] for i in range(early)] + [y_last]
+        near_all = (*near_in, *near_out)
+        near_x, near_y = near_all[0::2], near_all[1::2]
         far_all = [far_in, *(far_out[2 * i : 2 * i + 2] for i in range(early))]
 
         def chip(index, source, target, device):
@@ -315,10 +318,10 @@
         for i in range(early):
             forward.append(chip(2 * i, near_x[i + 1].at[:half], far_out[2 * i], y_side))
             forward.append(chip(2 * i + 1, near_y[i + 1].at[half:], far_out[2 * i + 1], x_side))
-        fresh = [
-            chip(2 * early, own[-1], x_last, x_side),
-            chip(2 * early + 1, own[-1], y_last, y_side),
-        ]
+        fresh = []
+        for i in range(unknown):
+            fresh.append(chip(2 * early + 2 * i, own[known + i], near_out[2 * i], x_side))
+            fresh.append(chip(2 * early + 2 * i + 1, own[known + i], near_out[2 * i + 1], y_side))
 
         def weights(now, slot, sub):
             chunk, side = sub // 2, sub % 2
@@ -423,7 +426,7 @@
                 pl.semaphore_signal(barrier, inc=1, device_id={"dp": device}, device_id_type=pl.DeviceIdType.MESH)
             pl.semaphore_wait(barrier, 3)
             start(step)
-            for copy in (*forward[:2], *fresh, *forward[2 : 2 * early - 2]):
+            for copy in forward[:2]:
                 copy.start()
 
         @pl.when(phase < size)
@@ -433,11 +436,23 @@
                 signal(w_free)
                 pl.semaphore_wait(w_free, 1)
 
-            @pl.when(pair == size + 1)
+            @pl.when(pair == 1)
+            def _():
+                for copy in fresh:
+                    copy.start()
+
+            for i in range(1, known - 1):
+
+                @pl.when(pair == 1 + i)
+                def _():
+                    for copy in forward[2 * i : 2 * i + 2]:
+                        copy.start()
+
+            @pl.when(pair == size + 2)
             def _():
                 for copy in fresh:
                     copy.wait_recv()
-                for copy in forward[2 * early - 2 :]:
+                for copy in forward[2 * known - 2 :]:
                     copy.start()
 
             @pl.when(pair + 1 < pairs)
@@ -550,12 +565,12 @@
             whole,
         ]
         + [anywhere] * (n_in - 4),
-        out_specs=[pl.BlockSpec((rows, tile), block)] + [anywhere] * (9 + 2 * early),
+        out_specs=[pl.BlockSpec((rows, tile), block)] + [anywhere] * (7 + 2 * unknown + 2 * early),
         out_shape=[
             jax.ShapeDtypeStruct((rows, 2 * width), bf16),
             jax.ShapeDtypeStruct((4, pairs, height, lanes), bf16),
         ]
-        + [jax.ShapeDtypeStruct((size, height, lanes), bf16)] * 2
+        + [jax.ShapeDtypeStruct((size, height, lanes), bf16)] * (2 * unknown)
         + [jax.ShapeDtypeStruct((half, height, lanes), bf16)] * (2 * early)
         + [some] * 6,
         scratch_shapes=[
@@ -576,8 +591,8 @@
             dma((2,)),
             dma((2,)),
             dma,
-            dma((2 * early + 2,)),
-            dma((2 * early + 2,)),
+            dma((2 * early + 2 * unknown,)),
+            dma((2 * early + 2 * unknown,)),
             dma((early * size,)),
             dma((early * size,)),
             dma((early * size,)),
@@ -695,8 +710,8 @@
             (1, z + hop <= last, z + hop, z > 0, z + 1, (z > 0) & (z - 1 + hop <= last)),
         )
 
-    def start(self, hop):
-        if hop + 1 < self.members:
+    def start(self, hop, begun=True):
+        if hop + 1 < self.members and begun:
             self.leave(hop + 1)
         for way, present, block, behind, device, _ in self.ways(hop):
 
@@ -777,33 +792,48 @@
     ]
 
 
-def gather_small(
-    q_weight, o_weight, k_weight, v_weight, gains, cotangent, ids, route_weights, gate, up, down, members, devices
+def turn(values, cosine, sine):
+    return values * cosine + pltpu.roll(values, HD // 2, 1) * sine
+
+
+def front(
+    tokens, q_weight, o_weight, k_weight, v_weight, gains, cosine, sine, cotangent, ids, route_weights, gate, up, down, members, devices
 ):
     height, part = q_weight.shape
     own_rows, width = cotangent.shape
     rows = own_rows * members
-    kv = k_weight.shape[1]
-    tall = 2 * kv + HD
+    kv = 2 * KV * HD
+    tall = kv + HD
     lanes = 9 * HD
     calls = EXPERTS // 2 // CALL_PAIRS
+    half = CALL_PAIRS // 2
+    heads = width // HD
+    per_kv = heads // KV
+    last = members - 1
     dma = pltpu.SemaphoreType.DMA
-    cut = part
 
     def kernel(*refs):
-        q_ref, o_ref, k_ref, v_ref, gains_ref, cot_ref, ids_ref, weights_ref, gate_ref, up_ref, down_ref = refs[:11]
-        square_all, tall_all, grad_all = refs[11:14]
-        rank_cols, routes = refs[14:16]
-        packed = refs[16 : 16 + calls]
-        from_x, from_y = refs[16 + calls : 18 + calls]
-        sems = refs[18 + calls :]
-        line_send, line_recv, grad_send, grad_recv, chip_send, chip_recv, core_send, core_recv = sems
+        x_ref, q_weight_ref, o_ref, k_ref, v_ref, gains_ref, cos_ref, sin_ref, cot_ref = refs[:9]
+        ids_ref, weights_ref, gate_ref, up_ref, down_ref = refs[9:14]
+        square_all, tall_all, grad_all, rank_cols, routes = refs[14:19]
+        normed_ref, q_ref, kv_all, mixed_ref, hidden_ref, rows_all = refs[19:25]
+        packed = refs[25 : 25 + calls]
+        from_x, from_y, far_x, far_y, next_x, next_y = refs[25 + calls : 31 + calls]
+        after, rest = refs[31 + calls : 25 + 3 * calls], refs[25 + 3 * calls :]
+        line_send, line_recv, grad_send, grad_recv, kv_send, kv_recv, row_send, row_recv = rest[:8]
+        chip_send, chip_recv, core_send, core_recv = rest[8:]
         me, z = lax.axis_index("dp"), lax.axis_index("tensor")
         x_side, y_side = chip_neighbours()
+        diagonal = x_side + y_side - me
         core = sibling()
 
         def rows_of(device):
             return pl.ds(pl.multiple_of(device * height, 16), height)
+
+        def block_of(ref):
+            return lambda block: ref.at[pl.ds(pl.multiple_of(block * own_rows, 16), own_rows)]
+
+        own = pl.ds(pl.multiple_of(z * own_rows, 16), own_rows)
 
         def pack(call):
             chunk = pack_chunk(gate_ref, up_ref, down_ref, 2 * CALL_PAIRS * call)
@@ -820,51 +850,86 @@
         def tall_at(device):
             return tall_all.at[rows_of(device)]
 
-        def square_at(device, half=None):
-            span = slice(None) if half is None else slice(half * cut, (half + 1) * cut)
+        def square_at(device, side=None):
+            span = slice(None) if side is None else slice(side * part, (side + 1) * part)
             return square_all.at[:, rows_of(device), span]
 
-        square_all[z, rows_of(me), :part] = q_ref[...]
+        trades = []
+
+        def trade(index, source):
+            trades.append(across(index, source))
+            trades[-1].start()
+
+        def there(index, device, of):
+            across(index, of(core if device is None else device + core - me)).wait_recv()
+
+        square_all[z, rows_of(me), :part] = q_weight_ref[...]
         square_all[z, rows_of(me), part:] = o_ref[...]
-        tall_all[rows_of(me), :kv] = k_ref[...]
-        tall_all[rows_of(me), kv : 2 * kv] = v_ref[...]
-        tall_all[rows_of(me), 2 * kv :] = gains_ref[...]
+        tall_all[rows_of(me), : kv // 2] = k_ref[...]
+        tall_all[rows_of(me), kv // 2 : kv] = v_ref[...]
+        tall_all[rows_of(me), kv:] = gains_ref[...]
         line = LineGather(members, lambda block: square_all.at[block, rows_of(me)], line_send, line_recv)
-        group = LineGather(
-            members,
-            lambda block: grad_all.at[pl.ds(pl.multiple_of(block * own_rows, 16), own_rows)],
-            grad_send,
-            grad_recv,
-        )
+        group = LineGather(members, block_of(grad_all), grad_send, grad_recv)
+        kv_line = LineGather(members, block_of(kv_all), kv_send, kv_recv)
+        row_line = LineGather(members, block_of(rows_all), row_send, row_recv)
+        moves = [
+            chip(0, tall_at(me), x_side),
+            chip(1, tall_at(me), y_side),
+            chip(2, packed[0].at[:half], x_side, from_x.at[:half]),
+            chip(3, packed[0].at[:half], y_side, from_y.at[:half]),
+            chip(4, square_at(me), x_side),
+            chip(5, square_at(me), y_side),
+            chip(6, packed[0].at[half:], x_side, from_x.at[half:]),
+            chip(7, packed[0].at[half:], y_side, from_y.at[half:]),
+            chip(8, tall_at(x_side), y_side),
+            chip(9, square_at(x_side, 0), y_side),
+            chip(10, square_at(y_side, 1), x_side),
+            chip(11, from_x.at[:half], y_side, far_x),
+            chip(12, from_y.at[half:], x_side, far_y),
+            chip(13, packed[1], x_side, next_x),
+            chip(14, packed[1], y_side, next_y),
+        ]
+        for i in range(2, calls - 1):
+            moves.append(chip(11 + 2 * i, packed[i], x_side, after[2 * i - 4]))
+            moves.append(chip(12 + 2 * i, packed[i], y_side, after[2 * i - 3]))
         meet(members, True)
         line.start(1)
-        near = [chip(0, tall_at(me), x_side), chip(1, tall_at(me), y_side)]
-        for copy in near:
+        for copy in moves[:2]:
             copy.start()
+        trade(0, tall_at(me))
         pack(0)
-        chunk = [chip(7, packed[0], x_side, from_x), chip(8, packed[0], y_side, from_y)]
-        for copy in chunk:
+        for copy in moves[2:4]:
             copy.start()
-        grad_all[pl.ds(pl.multiple_of(z * own_rows, 16), own_rows), :] = swap_blocks(cot_ref[...]).astype(bf16)
-        for hop in range(1, members):
+        for index, device in ((0, x_side), (1, y_side)):
+            chip(index, tall_at(device), device).wait_recv()
+        moves[8].start()
+        trade(2, tall_at(x_side))
+        trade(3, tall_at(y_side))
+        line.arrive(1)
+        if last > 1:
+            line.start(2)
+        grad_all[own, :] = swap_blocks(cot_ref[...]).astype(bf16)
+        chip(8, tall_at(diagonal), y_side).wait_recv()
+        trade(6, tall_at(diagonal))
+        for hop in range(2, members):
             line.arrive(hop)
-            if hop + 1 < members:
+            if hop < last:
                 line.start(hop + 1)
-        near += [chip(2, square_at(me), x_side), chip(3, square_at(me), y_side)]
-        for copy in near[2:]:
+        for copy in moves[4:6]:
             copy.start()
-        group.start(1)
-        trades = [across(0, tall_at(me)), across(1, square_at(me))]
-        for copy in trades:
-            copy.start()
-        chip(0, tall_at(x_side), x_side).wait_recv()
-        chip(1, tall_at(y_side), y_side).wait_recv()
-        diagonal = x_side + y_side - me
-        far = [chip(4, tall_at(x_side), y_side)]
-        far[0].start()
-        trades += [across(2, tall_at(x_side)), across(3, tall_at(y_side))]
-        for copy in trades[2:]:
-            copy.start()
+        trade(1, square_at(me))
+
+        for index, device in ((0, None), (2, x_side), (3, y_side), (6, diagonal)):
+            there(index, device, tall_at)
+        gain_one, gain_two = (jnp.transpose(tall_all[:, kv:].astype(f32))[i : i + 1] for i in range(2))
+        cosine, sine = cos_ref[own], sin_ref[own]
+        normed_ref[...] = (rms_pieces(x_ref[...].astype(f32))[1] * gain_one).astype(bf16)
+        made = nn(normed_ref[...], tall_all[:, :kv])
+        for head in range(KV):
+            span = slice(head * HD, (head + 1) * HD)
+            kv_all[own, span] = turn(made[:, span], cosine, sine).astype(bf16)
+        kv_all[own, KV * HD :] = made[:, KV * HD :].astype(bf16)
+        kv_line.start(1)
 
         expert = lax.broadcasted_iota(jnp.int32, (HD, rows), 0)
         weight = jnp.zeros((HD, rows), f32)
@@ -881,171 +946,132 @@
             routes[e, 0:1, :] = rank[e : e + 1]
             routes[e, 1:2, :] = weight[e : e + 1]
         for call in range(1, calls):
+            kv_line_hop = call
+            if kv_line_hop < members:
+                kv_line.arrive(kv_line_hop)
+                if kv_line_hop < last:
+                    kv_line.start(kv_line_hop + 1)
             pack(call)
-
+        for hop in range(calls, members):
+            kv_line.arrive(hop)
+            if hop < last:
+                kv_line.start(hop + 1)
+        group.start(1)
+
+        for index, device in ((4, x_side), (5, y_side)):
+            chip(index, square_at(device), device).wait_recv()
+        for copy in moves[9:11]:
+            copy.start()
+        trade(4, square_at(x_side))
+        trade(5, square_at(y_side))
+        chip(9, square_at(diagonal, 0), y_side).wait_recv()
+        chip(10, square_at(diagonal, 1), x_side).wait_recv()
+        trade(7, square_at(diagonal))
+        for copy in moves[2:4]:
+            copy.wait_recv()
+        for copy in (*moves[6:8], moves[11]):
+            copy.start()
         group.arrive(1)
-        if members > 2:
+        if last > 1:
             group.start(2)
-        chip(2, square_at(x_side), x_side).wait_recv()
-        chip(3, square_at(y_side), y_side).wait_recv()
-        far += [chip(5, square_at(x_side, 0), y_side), chip(6, square_at(y_side, 1), x_side)]
-        for copy in far[1:]:
-            copy.start()
-        trades += [across(4, square_at(x_side)), across(5, square_at(y_side))]
-        for copy in trades[4:]:
-            copy.start()
-        chip(4, tall_at(diagonal), y_side).wait_recv()
-        trades.append(across(6, tall_at(diagonal)))
-        trades[-1].start()
-        for hop in range(2, members - 1):
-            group.arrive(hop)
-            group.start(hop + 1)
-        chip(5, square_at(diagonal, 0), y_side).wait_recv()
-        chip(6, square_at(diagonal, 1), x_side).wait_recv()
-        trades.append(across(7, square_at(diagonal)))
-        trades[-1].start()
-        theirs = [core, core, x_side, y_side, x_side, y_side, diagonal, diagonal]
-        for index, device in enumerate(theirs):
-            there = device if index < 2 else device + core - me
-            source = square_at(there) if index in (1, 4, 5, 7) else tall_at(there)
-            across(index, source).wait_recv()
-        if members > 2:
-            group.arrive(members - 1)
-        for copy in chunk:
-            copy.wait()
-        for copy in near + far + trades:
-            copy.wait_send()
-        line.close()
-        group.close()
-
-    chunk_shape = jax.ShapeDtypeStruct((CALL_PAIRS, height, lanes), bf16)
-    return pl.pallas_call(
-        kernel,
-        in_specs=in_vmem(11),
-        out_specs=in_vmem(5 + calls) + [pl.BlockSpec(memory_space=pl.ANY)] * 2,
-        out_shape=[
-            jax.ShapeDtypeStruct((members, devices * height, 2 * part), bf16),
-            jax.ShapeDtypeStruct((devices * height, tall), bf16),
-            jax.ShapeDtypeStruct((rows, width), bf16),
-        ]
-        + [jax.ShapeDtypeStruct((rows, HD), bf16), jax.ShapeDtypeStruct((EXPERTS, 2, rows), f32)]
-        + [chunk_shape] * (calls + 2),
-        scratch_shapes=[dma((2, members - 1))] * 4 + [dma((9,))] * 2 + [dma((8,))] * 2,
-        compiler_params=pltpu.CompilerParams(collective_id=2, has_side_effects=True, vmem_limit_bytes=56 * 2**20),
-        cost_estimate=pl.CostEstimate(flops=8 * 10**10, bytes_accessed=10**7, transcendentals=0),
-        name="gather_small",
-    )(q_weight, o_weight, k_weight, v_weight, gains, cotangent, ids, route_weights, gate, up, down)
-
-
-def turn(values, cosine, sine):
-    return values * cosine + pltpu.roll(values, HD // 2, 1) * sine
-
-
-def gain_rows(tall_ref, kv):
-    return jnp.transpose(tall_ref[:, kv:].astype(f32))
-
-
-def attention_front(tokens, square, tall, cosine, sine, packed, near, members):
-    own_rows, width = tokens.shape
-    rows = own_rows * members
-    kv = 2 * KV * HD
-    heads = width // HD
-    per_kv = heads // KV
-    part = width // members
-    dma = pltpu.SemaphoreType.DMA
-
-    def kernel(x_ref, square_ref, tall_ref, cos_ref, sin_ref, *rest):
-        chunks, rest = rest[:count], rest[count:]
-        normed_ref, q_ref, kv_all, mixed_ref, hidden_ref, rows_all = rest[:6]
-        landed, rest = rest[6 : 4 + 2 * count], rest[4 + 2 * count :]
-        kv_send, kv_recv, row_send, row_recv, chip_send, chip_recv = rest
-        z = lax.axis_index("tensor")
-        x_side, y_side = chip_neighbours()
-        meet(members, False)
-        pairs = chunks[0].shape[0]
-        first, second = slice(0, pairs // 2), slice(pairs // 2, pairs)
-        moves = [(chunks[0].at[first], y_side), (chunks[1].at[second], x_side)]
-        for chunk in chunks[2:]:
-            moves += [(chunk, x_side), (chunk, y_side)]
-        moves = [
-            remote(source, landed[i], chip_send.at[i], chip_recv.at[i], {"dp": device})
-            for i, (source, device) in enumerate(moves)
-        ]
-        for copy in moves:
-            copy.start()
-        def block_of(ref):
-            return lambda block: ref.at[pl.ds(pl.multiple_of(block * own_rows, 16), own_rows)]
-
-        own = pl.ds(pl.multiple_of(z * own_rows, 16), own_rows)
-        kv_line = LineGather(members, block_of(kv_all), kv_send, kv_recv)
-        row_line = LineGather(members, block_of(rows_all), row_send, row_recv)
-        gains = gain_rows(tall_ref, kv)
-        x = x_ref[...].astype(f32)
-        normed_ref[...] = (rms_pieces(x)[1] * gains[0:1]).astype(bf16)
-        cosine, sine = cos_ref[own], sin_ref[own]
-        made = nn(normed_ref[...], tall_ref[:, :kv])
-        for head in range(KV):
-            span = slice(head * HD, (head + 1) * HD)
-            kv_all[own, span] = turn(made[:, span], cosine, sine).astype(bf16)
-        kv_all[own, KV * HD :] = made[:, KV * HD :].astype(bf16)
-        kv_line.start(1)
+        for index, device in ((1, None), (4, x_side), (5, y_side), (7, diagonal)):
+            there(index, device, square_at)
+
         for t in range(members):
-            made = nn(normed_ref[...], square_ref[t, :, :part])
+            made = nn(normed_ref[...], square_all[t, :, :part])
             for head in range(part // HD):
                 span = slice(head * HD, (head + 1) * HD)
                 q_ref[:, t * part + head * HD : t * part + (head + 1) * HD] = turn(
                     made[:, span], cosine, sine
                 ).astype(bf16)
-            if 1 <= t + 1 < members:
-                kv_line.arrive(t + 1)
-                if t + 2 < members:
-                    kv_line.start(t + 2)
-        first_row = z * own_rows
-
-        @pl.loop(0, heads)
-        def _(head):
-            span = pl.ds(pl.multiple_of(head * HD, HD), HD)
-            key_span = pl.ds(pl.multiple_of(head // per_kv * HD, HD), HD)
-            value_span = pl.ds(pl.multiple_of((KV + head // per_kv) * HD, HD), HD)
-            p = probabilities(q_ref[:, span], kv_all[:, key_span], first_row).astype(bf16)
-            mixed_ref[:, span] = nn(p, kv_all[:, value_span]).astype(bf16)
-
+
+        def attend(begin, end):
+            @pl.loop(begin, end)
+            def _(head):
+                span = pl.ds(pl.multiple_of(head * HD, HD), HD)
+                key_span = pl.ds(pl.multiple_of(head // per_kv * HD, HD), HD)
+                value_span = pl.ds(pl.multiple_of((KV + head // per_kv) * HD, HD), HD)
+                p = probabilities(q_ref[:, span], kv_all[:, key_span], z * own_rows).astype(bf16)
+                mixed_ref[:, span] = nn(p, kv_all[:, value_span]).astype(bf16)
+
+        for copy in moves[13:15]:
+            copy.start()
+        attend(0, heads // 2)
+        for hop in range(2, members):
+            group.arrive(hop)
+            if hop < last:
+                group.start(hop + 1)
+            if hop == 2:
+                attend(heads // 2, heads)
+        if members <= 2:
+            attend(heads // 2, heads)
         hidden = x_ref[...].astype(f32)
         for t in range(members):
-            hidden += nt(mixed_ref[:, t * part : (t + 1) * part], square_ref[t, :, part:])
+            hidden += nt(mixed_ref[:, t * part : (t + 1) * part], square_all[t, :, part:])
         hidden_ref[...] = hidden
-        normed = rms_pieces(hidden)[1] * gains[1:2]
-        rows_all[own, :] = swap_blocks(normed).astype(bf16)
+        rows_all[own, :] = swap_blocks(rms_pieces(hidden)[1] * gain_two).astype(bf16)
         for hop in range(1, members):
             row_line.start(hop)
+            if hop == 1:
+                for copy in moves[6:8]:
+                    copy.wait_recv()
+                for copy in (moves[12], *moves[15:]):
+                    copy.start()
             row_line.arrive(hop)
-        kv_line.close()
-        row_line.close()
-        for copy in moves:
-            copy.wait()
-
-    count = 2 + len(packed)
-    anywhere = pl.BlockSpec(memory_space=pl.ANY)
-    size, height, lanes = near[0].shape
+        for copy in moves[11:]:
+            copy.wait_recv()
+        for copy in moves + trades:
+            copy.wait_send()
+        for each in (line, group, kv_line, row_line):
+            each.close()
+
+    chunk_shape = jax.ShapeDtypeStruct((CALL_PAIRS, height, lanes), bf16)
+    half_shape = jax.ShapeDtypeStruct((half, height, lanes), bf16)
+    low_rows = jax.ShapeDtypeStruct((own_rows, width), bf16)
     return pl.pallas_call(
         kernel,
-        in_specs=in_vmem(5) + [anywhere] * count,
-        out_specs=in_vmem(6) + [anywhere] * (2 + 2 * len(packed)),
+        in_specs=in_vmem(14),
+        out_specs=in_vmem(11 + calls) + [pl.BlockSpec(memory_space=pl.ANY)] * (2 * calls),
         out_shape=[
-            jax.ShapeDtypeStruct((own_rows, width), bf16),
-            jax.ShapeDtypeStruct((own_rows, width), bf16),
+            jax.ShapeDtypeStruct((members, devices * height, 2 * part), bf16),
+            jax.ShapeDtypeStruct((devices * height, tall), bf16),
+            jax.ShapeDtypeStruct((rows, width), bf16),
+            jax.ShapeDtypeStruct((rows, HD), bf16),
+            jax.ShapeDtypeStruct((EXPERTS, 2, rows), f32),
+            low_rows,
+            low_rows,
             jax.ShapeDtypeStruct((rows, kv), bf16),
-            jax.ShapeDtypeStruct((own_rows, width), bf16),
+            low_rows,
             jax.ShapeDtypeStruct((own_rows, width), f32),
             jax.ShapeDtypeStruct((rows, width), bf16),
         ]
-        + [jax.ShapeDtypeStruct((size // 2, height, lanes), bf16)] * 2
-        + [jax.ShapeDtypeStruct((size, height, lanes), bf16)] * (2 * len(packed)),
-        scratch_shapes=[dma((2, members - 1))] * 4 + [dma((2 + 2 * len(packed),))] * 2,
-        compiler_params=pltpu.CompilerParams(collective_id=3, has_side_effects=True, vmem_limit_bytes=56 * 2**20),
-        cost_estimate=pl.CostEstimate(flops=10**11, bytes_accessed=10**7, transcendentals=0),
-        name="attention_front",
-    )(tokens, square, tall, cosine, sine, *near, *packed)
+        + [chunk_shape] * (calls + 2)
+        + [half_shape] * 2
+        + [chunk_shape] * (2 * calls - 4),
+        scratch_shapes=[dma((2, members - 1))] * 8 + [dma((9 + 2 * calls,))] * 2 + [dma((8,))] * 2,
+        compiler_params=pltpu.CompilerParams(collective_id=2, has_side_effects=True, vmem_limit_bytes=62 * 10**6),
+        cost_estimate=pl.CostEstimate(flops=2 * 10**11, bytes_accessed=10**7, transcendentals=0),
+        name="front",
+    )(
+        tokens,
+        q_weight,
+        o_weight,
+        k_weight,
+        v_weight,
+        gains,
+        cosine,
+        sine,
+        cotangent,
+        ids,
+        route_weights,
+        gate,
+        up,
+        down,
+    )
+
+
+def gain_rows(tall_ref, kv):
+    return jnp.transpose(tall_ref[:, kv:].astype(f32))
 
 
 def attention_back(
@@ -1061,11 +1087,11 @@
 
     def kernel(sums_ref, cot_ref, hidden_ref, x_ref, normed_ref, q_ref, kv_ref, mixed_ref, square_ref, tall_ref, *rest):
         cos_ref, sin_ref, grads_ref, to_x_ref, to_y_ref = rest[:5]
-        grad_ref, parts, x_before, y_before, x_last, y_last = rest[5:11]
-        do_ref, dq_ref, dkv_ref, total, kv_total, stage, tall_part, back_part = rest[11:19]
-        back_leave, back_arrive, kv_leave, kv_arrive = rest[19:23]
-        back_send, back_recv, kv_send, kv_recv, stage_sem, part_sem = rest[23:29]
-        through, added, added_sem, chip_send, chip_recv = rest[29:]
+        grad_ref, moe_out, parts, x_before, y_before, x_last, y_last = rest[5:12]
+        do_ref, dq_ref, dkv_ref, total, kv_total, stage, tall_part, back_part = rest[12:20]
+        back_leave, back_arrive, moe_leave, moe_arrive, kv_leave, kv_arrive = rest[20:26]
+        back_send, back_recv, moe_send, moe_recv, kv_send, kv_recv, stage_sem, part_sem = rest[26:34]
+        through, added, added_sem, chip_send, chip_recv = rest[34:]
         z = lax.axis_index("tensor")
         x_side, y_side = chip_neighbours()
         first, second = slice(0, size // 2), slice(size // 2, size)
@@ -1077,12 +1103,15 @@
         def chip(index, source, target, device):
             return remote(source, target, chip_send.at[index], chip_recv.at[index], {"dp": device})
 
-        loads = [
-            pltpu.make_async_copy(
-                sums_ref.at[b * own_rows : (b + 1) * own_rows, width:], back_part.at[b], part_sem.at[b]
-            )
-            for b in range(members)
-        ] + [
+        def sums_of(begin):
+            return [
+                pltpu.make_async_copy(
+                    sums_ref.at[b * own_rows : (b + 1) * own_rows, begin : begin + width], back_part.at[b], part_sem.at[b]
+                )
+                for b in range(members)
+            ]
+
+        loads = sums_of(width) + [
             pltpu.make_async_copy(chunk(1, second), added.at[0], added_sem.at[0]),
             pltpu.make_async_copy(chunk(2, first), added.at[1], added_sem.at[1]),
         ]
@@ -1109,6 +1138,7 @@
             return lambda b: ref[pl.ds(pl.multiple_of(b * own_rows, 16), own_rows), span]
 
         back = LineSum(members, lambda b: back_part[b], back_leave, back_arrive, back_send, back_recv)
+        moe = LineSum(members, lambda b: back_part[b], moe_leave, moe_arrive, moe_send, moe_recv)
         pairs = LineSum(members, block(dkv_ref, slice(None)), kv_leave, kv_arrive, kv_send, kv_recv)
         gains = gain_rows(tall_ref, kv)
         cosine, sine = cos_ref[own], sin_ref[own]
@@ -1128,51 +1158,91 @@
             back.start(hop)
             back.arrive(hop)
         back.total(total)
+        loads = sums_of(0)
+        for copy in loads:
+            copy.start()
         normed_grad = swap_blocks(total[...])
         inverse, unit = rms_pieces(hidden_ref[...])
+        for copy in loads:
+            copy.wait()
+        if last > 1:
+            moe.start(last)
         by_hidden, gain_two = rms_backward(normed_grad, unit, inverse, gains[1:2])
         grad_ref[...] = cot_ref[...] + by_hidden
         low = grad_ref[...].astype(bf16)
         for t in range(members):
             span = slice(t * part, (t + 1) * part)
             do_ref[:, span] = nn(low, square_ref[t, :, part:]).astype(bf16)
-            store(tn(low, mixed_ref[:, span]), width + t * part)
+            store(tn(low, mixed_ref[:, span]), t * part)
         dkv_ref[...] = jnp.zeros_like(dkv_ref)
         first_row = z * own_rows
 
-        @pl.loop(0, heads)
-        def _(head):
-            span = pl.ds(pl.multiple_of(head * HD, HD), HD)
-            key_span = pl.ds(pl.multiple_of(head // per_kv * HD, HD), HD)
-            value_span = pl.ds(pl.multiple_of((KV + head // per_kv) * HD, HD), HD)
-            q_now, k_now, do_now = q_ref[:, span], kv_ref[:, key_span], do_ref[:, span]
-            p = probabilities(q_now, k_now, first_row)
-            dp = nt(do_now, kv_ref[:, value_span])
-            ds = (p * (dp - jnp.sum(p * dp, axis=-1, keepdims=True))).astype(bf16)
-            dq_ref[:, span] = turn(nn(ds, k_now) * (HD**-0.5), cosine, -sine).astype(bf16)
-            dkv_ref[:, key_span] += tn(ds, q_now) * (HD**-0.5)
-            dkv_ref[:, value_span] += tn(p.astype(bf16), do_now)
+        def attend(begin, end):
+            @pl.loop(begin, end)
+            def _(head):
+                span = pl.ds(pl.multiple_of(head * HD, HD), HD)
+                key_span = pl.ds(pl.multiple_of(head // per_kv * HD, HD), HD)
+                value_span = pl.ds(pl.multiple_of((KV + head // per_kv) * HD, HD), HD)
+                q_now, k_now, do_now = q_ref[:, span], kv_ref[:, key_span], do_ref[:, span]
+                p = probabilities(q_now, k_now, first_row)
+                dp = nt(do_now, kv_ref[:, value_span])
+                ds = (p * (dp - jnp.sum(p * dp, axis=-1, keepdims=True))).astype(bf16)
+                dq_ref[:, span] = turn(nn(ds, k_now) * (HD**-0.5), cosine, -sine).astype(bf16)
+                dkv_ref[:, key_span] += tn(ds, q_now) * (HD**-0.5)
+                dkv_ref[:, value_span] += tn(p.astype(bf16), do_now)
+
+        attend(0, heads // 3)
+        if last > 1:
+            moe.arrive(last)
+            if last > 2:
+                moe.start(last - 1)
+        attend(heads // 3, heads)
 
         pairs.start(last)
+
+        def query_part(t):
+            store(tn(normed_ref[...], dq_ref[:, t * part : (t + 1) * part]), width + t * part)
+
+        def normed_part(t):
+            made = nt(dq_ref[:, t * part : (t + 1) * part], square_ref[t, :, :part])
+            if t == 0:
+                total[...] = made
+            else:
+                total[...] += made
+
         for i, copy in enumerate(moves[:2]):
             copy.wait()
             added[1 - i] = (added[1 - i].astype(f32) + through[i].astype(f32)).astype(bf16)
             moves[7 - i].start()
-        for t in range(members):
-            span = slice(t * part, (t + 1) * part)
-            store(tn(normed_ref[...], dq_ref[:, span]), t * part)
+        work = [(do, t) for do in (query_part, normed_part) for t in range(members)]
+        share = len(work) // last
         for hop in range(last, 0, -1):
-            if hop < last:
-                pairs.start(hop)
+            for do, t in work[: share if hop > 1 else None]:
+                do(t)
+            work = work[share:]
             pairs.arrive(hop)
+            if hop > 1:
+                pairs.start(hop - 1)
+        for hop in range(last - 1, 1, -1):
+            moe.arrive(hop)
+            if hop > 2:
+                moe.start(hop - 1)
+        for way, present in ((0, (z < last) & (z >= 1)), (1, (z > 0) & (z + 1 <= last))):
+
+            @pl.when(present)
+            def _():
+                moe_out[way] = moe_arrive[way, 1]
+
+            @pl.when(jnp.logical_not(present))
+            def _():
+                moe_out[way] = jnp.zeros((own_rows, width), bf16)
+
         pairs.total(kv_total)
         low_kv = [
             turn(kv_total[:, head * HD : (head + 1) * HD], cosine, -sine).astype(bf16) for head in range(KV)
         ] + [kv_total[:, KV * HD :].astype(bf16)]
         low_kv = jnp.concatenate(low_kv, axis=1)
-        normed_grad = nt(low_kv, tall_ref[:, :kv])
-        for t in range(members):
-            normed_grad += nt(dq_ref[:, t * part : (t + 1) * part], square_ref[t, :, :part])
+        normed_grad = total[...] + nt(low_kv, tall_ref[:, :kv])
         inverse, unit = rms_pieces(x_ref[...].astype(f32))
         by_tokens, gain_one = rms_backward(normed_grad, unit, inverse, gains[0:1])
         grad_ref[...] += by_tokens
@@ -1184,6 +1254,8 @@
         tall_copy.start()
         for line in (back, pairs):
             line.close()
+        if last > 1:
+            moe.leave(2)
         for copy in (*stored[-2:], tall_copy, *moves[2:]):
             copy.wait()
 
@@ -1196,9 +1268,10 @@
     return pl.pallas_call(
         kernel,
         in_specs=[anywhere] + in_vmem(11) + [anywhere] * 3,
-        out_specs=in_vmem(1) + [anywhere] * 5,
+        out_specs=in_vmem(2) + [anywhere] * 5,
         out_shape=[
             jax.ShapeDtypeStruct((own_rows, width), f32),
+            jax.ShapeDtypeStruct((2, own_rows, width), bf16),
             jax.ShapeDtypeStruct((width, 2 * width + tall.shape[1]), bf16),
         ]
         + [jax.ShapeDtypeStruct(to_x.shape, bf16)] * 2
@@ -1214,10 +1287,12 @@
             pltpu.VMEM((members, own_rows, width), bf16),
             pltpu.VMEM((2, own_rows, width), bf16),
             pltpu.VMEM((*hops, own_rows, width), bf16),
+            pltpu.VMEM((2, own_rows, width), bf16),
+            pltpu.VMEM((*hops, own_rows, width), bf16),
             pltpu.VMEM((2, own_rows, kv), bf16),
             pltpu.VMEM((*hops, own_rows, kv), bf16),
         ]
-        + [dma(hops)] * 4
+        + [dma(hops)] * 6
         + [dma((3,)), dma((members,)), pltpu.VMEM(halves, bf16), pltpu.VMEM(halves, bf16), dma((2,)), dma((8,)), dma((8,))],
         compiler_params=pltpu.CompilerParams(collective_id=4, has_side_effects=True, vmem_limit_bytes=62 * 10**6),
         cost_estimate=pl.CostEstimate(flops=10**11, bytes_accessed=10**7, transcendentals=0),
@@ -1227,21 +1302,23 @@
     )
 
 
-def reduce_small(parts, sums, hidden, members, devices):
+def reduce_small(parts, sums, moved, hidden, members, devices):
     own_rows = hidden.shape[0]
     width = parts.shape[0]
     height = width // devices
     lanes = parts.shape[1]
     tall = lanes - 2 * width
+    kv = KV * HD
     part = width // members
     half = height // 2
+    groups = (slice(0, width), slice(width, lanes))
     dma = pltpu.SemaphoreType.DMA
 
-    def kernel(parts_ref, sums_ref, hidden_ref, out_ref, square_out, tall_out, *rest):
-        own, theirs, leave, arrive, blocks, line_leave, line_arrive, tall_all = rest[:8]
-        moe_part, moe_leave, moe_arrive, total_ref = rest[8:12]
-        own_sem, core_send, core_recv, chip_send, chip_recv, line_send, line_recv, tall_send, tall_recv = rest[12:21]
-        moe_send, moe_recv, part_sem = rest[21:]
+    def kernel(parts_ref, sums_ref, moved_ref, hidden_ref, out_ref, q_out, o_out, k_out, v_out, gains_out, *rest):
+        own, theirs, leave, arrive, blocks, line_leave, line_arrive, tall_all, line_total = rest[:9]
+        moe_part, moe_leave, moe_arrive, total_ref = rest[9:13]
+        own_sem, core_send, core_recv, chip_send, chip_recv = rest[13:18]
+        o_send, o_recv, q_send, q_recv, tall_send, tall_recv, moe_send, moe_recv, part_sem = rest[18:]
         me, z = lax.axis_index("dp"), lax.axis_index("tensor")
         x_side, y_side = chip_neighbours()
         core = sibling()
@@ -1254,128 +1331,155 @@
         ]
         for copy in loads:
             copy.start()
+
+        def rows(device, span):
+            return parts_ref.at[pl.ds(pl.multiple_of(device * height, 16), height), span]
+
+        def trade(m, g):
+            target = theirs.at[m, :, groups[g]]
+            source = rows(chips[m] + core - me, groups[g])
+            return remote(source, target, core_send.at[m, g], core_recv.at[m, g], {"dp": core})
+
+        def keep(m, g):
+            return pltpu.make_async_copy(rows(chips[m], groups[g]), own.at[m, :, groups[g]], own_sem.at[m, g])
+
+        order = (3, 2, 1, 0)
+        for g in range(2):
+            for m in order:
+                keep(m, g).start()
         meet(members, True)
+        for g in range(2):
+            for m in order:
+                trade(m, g).start()
         moe = LineSum(members, lambda b: moe_part[b], moe_leave, moe_arrive, moe_send, moe_recv)
-        last = members - 1
-
-        def rows(device):
-            return parts_ref.at[pl.ds(pl.multiple_of(device * height, 16), height)]
-
-        def trade(m):
-            return remote(rows(chips[m] + core - me), theirs.at[m], core_send.at[m], core_recv.at[m], {"dp": core})
-
-        def keep(m):
-            return pltpu.make_async_copy(rows(chips[m]), own.at[m], own_sem.at[m])
-
-        for m in (3, 2, 1, 0):
-            trade(m).start()
-            keep(m).start()
+        if members > 2:
+            for way in range(2):
+                moe_arrive[way, 1] = moved_ref[way]
         for copy in loads:
             copy.wait()
-        moe.start(last)
-
-        def both(m, span):
-            return own[m, span].astype(f32) + theirs[m, span].astype(f32)
-
-        def chip(index, source, target, device):
-            return remote(source, target, chip_send.at[index], chip_recv.at[index], {"dp": device})
+        moe.start(1, False)
+
+        def both(m, rows, lanes):
+            return own[m, rows, lanes].astype(f32) + theirs[m, rows, lanes].astype(f32)
+
+        def chip(index, g, slot, span, device):
+            source, target = leave.at[slot, span, groups[g]], arrive.at[slot, span, groups[g]]
+            return remote(source, target, chip_send.at[index, g], chip_recv.at[index, g], {"dp": device})
 
         first, second = slice(0, half), slice(half, height)
-        far = [
-            chip(0, leave.at[0, first], arrive.at[0, first], x_side),
-            chip(1, leave.at[0, second], arrive.at[0, second], y_side),
-        ]
-        near = [chip(2, leave.at[1], arrive.at[1], x_side), chip(3, leave.at[2], arrive.at[2], y_side)]
-        for m in (3, 2, 1, 0):
-            trade(m).wait()
-            keep(m).wait()
-            if m == 3:
-                for copy, span in zip(far, (first, second)):
-                    leave[0, span] = both(3, span).astype(bf16)
-                    copy.start()
-        for copy in far:
-            copy.wait()
-        moe.arrive(last)
-        if last > 1:
-            moe.start(last - 1)
-        leave[1, first] = both(1, first).astype(bf16)
-        leave[1, second] = (both(1, second) + arrive[0, second].astype(f32)).astype(bf16)
-        near[0].start()
-        leave[2, first] = (both(2, first) + arrive[0, first].astype(f32)).astype(bf16)
-        leave[2, second] = both(2, second).astype(bf16)
-        near[1].start()
-        for hop in range(last - 1, 0, -1):
-            moe.arrive(hop)
-            if hop > 1:
-                moe.start(hop - 1)
+        every = slice(0, height)
+        far = [[chip(0, g, 0, first, x_side), chip(1, g, 0, second, y_side)] for g in range(2)]
+        near = [[chip(2, g, 1, every, x_side), chip(3, g, 2, every, y_side)] for g in range(2)]
+
+        def ready(m, g):
+            trade(m, g).wait()
+            keep(m, g).wait()
+
+        for g, span in enumerate(groups):
+            ready(3, g)
+            for copy, part_of in zip(far[g], (first, second)):
+                leave[0, part_of, span] = both(3, part_of, span).astype(bf16)
+                copy.start()
+            for m in order[1:]:
+                ready(m, g)
+        for g, span in enumerate(groups):
+            leave[1, first, span] = both(1, first, span).astype(bf16)
+            leave[2, second, span] = both(2, second, span).astype(bf16)
+            far[g][1].wait()
+            leave[1, second, span] = (both(1, second, span) + arrive[0, second, span].astype(f32)).astype(bf16)
+            near[g][0].start()
+            far[g][0].wait()
+            leave[2, first, span] = (both(2, first, span) + arrive[0, first, span].astype(f32)).astype(bf16)
+            near[g][1].start()
+        moe.arrive(1)
         moe.total(total_ref)
         out_ref[...] = (hidden_ref[...] + swap_blocks(total_ref[...])).astype(bf16)
-        for copy in near:
+
+        def total(span):
+            return both(0, every, span) + arrive[1, :, span].astype(f32) + arrive[2, :, span].astype(f32)
+
+        lines = [
+            LineSum(members, lambda b, g=g: blocks[g, b], line_leave.at[g], line_arrive.at[g], send, recv)
+            for g, (send, recv) in enumerate(((o_send, o_recv), (q_send, q_recv)))
+        ]
+        group = LineGather(members, lambda b: tall_all.at[b], tall_send, tall_recv)
+
+        def hop_of(line, hop):
+            line.arrive(hop)
+            if hop > 1:
+                line.start(hop - 1)
+
+        last = members - 1
+        for copy in near[0]:
             copy.wait()
-
-        def total(span):
-            return (
-                own[0, :, span].astype(f32)
-                + theirs[0, :, span].astype(f32)
-                + arrive[1, :, span].astype(f32)
-                + arrive[2, :, span].astype(f32)
-            )
-
+        for t in range(members):
+            blocks[0, t] = total(slice(t * part, (t + 1) * part))
+        lines[0].start(last)
+        for copy in near[1]:
+            copy.wait()
         tall_all[z] = total(slice(2 * width, lanes)).astype(bf16)
         for t in range(members):
-            blocks[t, :, :part] = total(slice(t * part, (t + 1) * part))
-            blocks[t, :, part:] = total(slice(width + t * part, width + (t + 1) * part))
-        line = LineSum(members, lambda b: blocks[b], line_leave, line_arrive, line_send, line_recv)
-        group = LineGather(members, lambda b: tall_all.at[b], tall_send, tall_recv)
-        for hop in range(1, members):
-            line.start(members - hop)
-            group.start(hop)
-            line.arrive(members - hop)
-            group.arrive(hop)
-        line.total(square_out)
+            blocks[1, t] = total(slice(width + t * part, width + (t + 1) * part))
+        lines[1].start(last)
+        group.start(1)
+        for hop in range(last, 0, -1):
+            hop_of(lines[0], hop)
+            hop_of(lines[1], hop)
+            group.arrive(members - hop)
+            if hop > 1:
+                group.start(members - hop + 1)
+        lines[0].total(line_total)
+        o_out[...] = line_total[...]
+        lines[1].total(line_total)
+        q_out[...] = line_total[...]
         summed = tall_all[0].astype(f32)
         for t in range(1, members):
             summed += tall_all[t].astype(f32)
-        tall_out[...] = summed
-        line.close()
-        group.close()
-        moe.close()
+        k_out[...] = summed[:, :kv]
+        v_out[...] = summed[:, kv : 2 * kv]
+        gains_out[...] = summed[:, 2 * kv :]
+        for line in (*lines, group, moe):
+            line.close()
 
     hops = (2, members - 1)
     return pl.pallas_call(
         kernel,
-        in_specs=[pl.BlockSpec(memory_space=pl.ANY)] * 2 + in_vmem(1),
-        out_specs=in_vmem(3),
+        in_specs=[pl.BlockSpec(memory_space=pl.ANY)] * 2 + in_vmem(2),
+        out_specs=in_vmem(6),
         out_shape=[
             jax.ShapeDtypeStruct((own_rows, width), bf16),
-            jax.ShapeDtypeStruct((height, 2 * part), f32),
-            jax.ShapeDtypeStruct((height, tall), f32),
+            jax.ShapeDtypeStruct((height, part), f32),
+            jax.ShapeDtypeStruct((height, part), f32),
+            jax.ShapeDtypeStruct((height, kv), f32),
+            jax.ShapeDtypeStruct((height, kv), f32),
+            jax.ShapeDtypeStruct((height, tall - 2 * kv), f32),
         ],
         scratch_shapes=[
             pltpu.VMEM((4, height, lanes), bf16),
             pltpu.VMEM((4, height, lanes), bf16),
             pltpu.VMEM((3, height, lanes), bf16),
             pltpu.VMEM((3, height, lanes), bf16),
-            pltpu.VMEM((members, height, 2 * part), f32),
-            pltpu.VMEM((2, height, 2 * part), bf16),
-            pltpu.VMEM((*hops, height, 2 * part), bf16),
+            pltpu.VMEM((2, members, height, part), f32),
+            pltpu.VMEM((2, 2, height, part), bf16),
+            pltpu.VMEM((2, *hops, height, part), bf16),
             pltpu.VMEM((members, height, tall), bf16),
+            pltpu.VMEM((height, part), f32),
             pltpu.VMEM((members, own_rows, width), bf16),
             pltpu.VMEM((2, own_rows, width), bf16),
             pltpu.VMEM((*hops, own_rows, width), bf16),
             pltpu.VMEM((own_rows, width), f32),
-            dma((4,)),
-            dma((4,)),
-            dma((4,)),
-            dma((4,)),
-            dma((4,)),
+            dma((4, 2)),
+            dma((4, 2)),
+            dma((4, 2)),
+            dma((4, 2)),
+            dma((4, 2)),
         ]
-        + [dma(hops)] * 6
+        + [dma(hops)] * 8
         + [dma((members,))],
         compiler_params=pltpu.CompilerParams(collective_id=5, has_side_effects=True, vmem_limit_bytes=60 * 2**20),
         cost_estimate=pl.CostEstimate(flops=8 * 10**10, bytes_accessed=10**7, transcendentals=0),
         name="reduce_small",
-    )(parts, sums, hidden)
+    )(parts, sums, moved, hidden)
 
 
 def unpack_all(grads, plain, added, last):
@@ -1619,15 +1723,18 @@
     own_rows, width = tokens.shape
     rows = own_rows * members
     calls = EXPERTS // 2 // CALL_PAIRS
-    kv_width = k_weight.shape[1]
 
     gains = jnp.pad(jnp.stack([attn_gain, moe_gain], axis=1), ((0, 0), (0, HD - 2)))
-    small = gather_small(
+    cosine, sine = doubled_tables(rows)
+    square_all, tall_all, grad_all, rank_cols, routes, normed_one, queries, kv_all, mixed, hidden, rows_all, *chunks = front(
+        tokens,
         q_weight,
         o_weight,
         k_weight,
         v_weight,
         gains,
+        cosine,
+        sine,
         cotangent,
         expert_ids.T,
         route_weights.T,
@@ -1637,18 +1744,13 @@
         members,
         devices,
     )
-    square_all, tall_all, grad_all, rank_cols, routes = small[:5]
-    packed, near = small[5 : 5 + calls], [tuple(small[5 + calls :])]
-    cosine, sine = doubled_tables(rows)
-    normed_one, queries, kv_all, mixed, hidden, rows_all, *landed = attention_front(
-        tokens, square_all, tall_all, cosine, sine, packed[1:-1], near[0], members
-    )
-    near += [tuple(landed[2 * i : 2 * i + 2]) for i in range(1, calls - 1)]
+    packed, (from_x, from_y, far_x, far_y, *after) = chunks[:calls], chunks[calls:]
+    near = [(from_x, from_y), *zip(after[0::2], after[1::2])]
     sums, grads, *others = expert_pass(
-        rank_cols, routes, rows_all, grad_all, packed, near, landed[:2], members
+        rank_cols, routes, rows_all, grad_all, packed, near, (far_x, far_y), members
     )
     plain, added = others[-6:-4], others[-4:-2]
-    tokens_grad, parts, *moved = attention_back(
+    tokens_grad, moe_moved, parts, *moved = attention_back(
         sums,
         cotangent,
         hidden,
@@ -1665,18 +1767,17 @@
         *added,
         members,
     )
-    output, square_grad, tall_grad = reduce_small(parts, sums, hidden, members, devices)
+    output, q_grad, o_grad, k_grad, v_grad, gain_grads = reduce_small(parts, sums, moe_moved, hidden, members, devices)
     gate_out, up_out, down_out = unpack_all(grads, plain, moved[:2], moved[2:])
-    part = width // members
     return (
         output,
         tokens_grad,
-        tall_grad[:, 2 * kv_width],
-        square_grad[:, :part],
-        tall_grad[:, :kv_width],
-        tall_grad[:, kv_width : 2 * kv_width],
-        square_grad[:, part:],
-        tall_grad[:, 2 * kv_width + 1],
+        gain_grads[:, 0],
+        q_grad,
+        k_grad,
+        v_grad,
+        o_grad,
+        gain_grads[:, 1],
         gate_out,
         up_out,
         down_out,

time: 724 us -> 696 us (0.961)
  Pallas kernels: 701 us -> 673 us
    pallas_call x1, Pallas kernels: 99.4 us -> 83.7 us  [reduce_small(): pl.pallas_call(kernel, in_specs=[pl.BlockSpec(memory_space=pl.ANY)] * 2 +...]
    pallas_call x1, Pallas kernels: 249 us -> 237 us  [expert_pass(): pl.pallas_call(kernel, grid=(calls * period,), in_specs=[pl.BlockSpec((ro...]
    pallas_call x2 -> x1, Pallas kernels: 214 us -> 211 us  [front(): pl.pallas_call(kernel, in_specs=in_vmem(14), out_specs=in_vmem(11 + calls...]
where the time goes in v6:
time: 696 us; the launch traced here: 688 us
  Pallas kernels  673 us (97%)
  local copies, waits for them, and re-layouts  13 us (2%)
    pallas_call x1, Pallas kernels, expert_pass(): pl.pallas_call(kernel, grid=(calls * period,), in_specs=[pl.BlockSpec((ro...  237 us
    pallas_call x1, Pallas kernels, front(): pl.pallas_call(kernel, in_specs=in_vmem(14), out_specs=in_vmem(11 + calls...  211 us
    pallas_call x1, Pallas kernels, attention_back(): pl.pallas_call(kernel, in_specs=[anywhere] + in_vmem(11) + [anywhere] * 3...  129 us
    pallas_call x1, Pallas kernels, reduce_small(): pl.pallas_call(kernel, in_specs=[pl.BlockSpec(memory_space=pl.ANY)] * 2 +...  83.7 us

profile of v6, /device:TPU:0, one launch (start us, length us, event | category | flops | bytes accessed | tf_op | source)
XLA Modules:
  0.0 687.5 jit_solution(14501576808761633133)
XLA Ops:
  0.6 0.7 stack.9
  1.3 0.7 stack.10
  2.0 0.1 copy.28
  2.1 0.6 pad.4.refs_5_
  2.8 210.6 %front.1 = (bf16[4,1536,768]{2,1,0:T(8,128)(2,1)}, bf16[1536,640]{1,0:T(8,128)(2,1)}, bf16[1024,1536]{1,0:T(8,128)(2,1)}, bf16[1024,128]{1,0:T(8,128)(2,1)}, f32...) custom-call(bf16[256,1536]{1,0:T(8,128)(2,1)} %x_ref.1, ...), custom_call_target="tpu_custom_call" | custom-call | flops 199999995904 | bytes 10000000 | tf_op jit(solution)/shard_map/front/pallas_call | solution.py:1031
  213.3 237.2 %experts.1 = (bf16[1024,3072]{1,0:T(8,128)(2,1)}, bf16[4,16,192,1152]{3,2,1,0:T(8,128)(2,1)}, bf16[4,192,1152]{2,1,0:T(8,128)(2,1)}, bf16[4,192,1152]{2,1,0:T(8,...) custom-call(bf16[1024,128]{1,0:T(8,128)(2,1)} %get-tuple-element.56., ...), custom_call_target="tpu_custom_call" | custom-call | flops 199999995904 | bytes 100000000 | tf_op jit(solution)/shard_map/experts/pallas_call | solution.py:558
  450.5 0.0 copy-start
  450.6 128.5 %attention_back.1 = (f32[256,1536]{1,0:T(8,128)}, bf16[2,256,1536]{2,1,0:T(8,128)(2,1)}, bf16[1536,3712]{1,0:T(8,128)(2,1)}, bf16[6,192,1152]{2,1,0:T(8,128)(2,1...) custom-call(bf16[1024,3072]{1,0:T(8,128)(2,1)} %get-tuple-element.72.sums_ref, ...), custom_call_target="tpu_custom_call" | custom-call | flops 99999997952 | bytes 10000000 | tf_op jit(solution)/shard_map/attention_back/pallas_call | solution.py:1268
  579.1 0.0 copy-done
  579.1 0.0 copy-start.1
  579.1 1.5 copy-done.1
  580.6 0.0 copy-start.2
  580.6 1.5 copy-done.2
  582.1 13.3 %unpack.1 = (f32[192,32,192]{2,1,0:T(8,128)}, f32[192,32,192]{2,1,0:T(8,128)}, f32[192,32,192]{2,1,0:T(8,128)}) custom-call(bf16[4,16,192,1152]{3,2,1,0:T(8,128)(2,1)} %get-tuple-element.80.rest_2_.own, bf16[6,192,1152]{2,1,0:T(8,128)(2,1)S(1)} %copy-done, bf16[6,192,1152]{2,1,0:T(8,128)(2,1)} %get-tuple-element.93.plain_y, ...), custom_call_target="tpu_custom_call" | custom-call | tf_op jit(solution)/shard_map/unpack/pallas_call | solution.py:1520
  595.4 83.7 %reduce_small.1 = (bf16[256,1536]{1,0:T(8,128)(2,1)}, f32[192,384]{1,0:T(8,128)}, f32[192,384]{1,0:T(8,128)}, f32[192,256]{1,0:T(8,128)}, f32[192,256]{1,0:T(8,128)}, /*index=5*/f32[192,128]{1,0:T(8,128)}) custom-call(bf16[1536,3712]{1,0:T(8,128)(2,1)} %get-tuple-element.83.parts_ref, bf16[1024,3072]{1,0:T(8,128)(2,1)} %get-tuple-element.72.sums_ref, ...), custom_call_target="tpu_custom_call" | custom-call | flops 80000000000 | bytes 10000000 | tf_op jit(solution)/shard_map/reduce_small/pallas_call | solution.py:1445
  679.1 0.0 copy-start.3
  679.1 0.0 copy-start.5
  679.1 1.9 slice_reduce_fusion
  681.0 0.0 copy-start.7
  681.0 0.0 copy-start.6
  681.0 2.1 copy.35
  683.1 0.0 copy-done.3
  683.1 0.0 copy-start.4
  683.1 1.1 copy.36
  684.3 0.0 copy-done.5
  684.3 0.7 copy.37
  685.0 0.0 copy-done.7
  685.0 0.7 copy.38
  685.7 0.0 copy-done.6
  685.7 0.7 copy.39
  686.4 0.0 copy-done.4
  686.4 0.7 copy.40
  (1 shorter events, 0.0 us)
Async XLA Ops:
  450.5 128.6 %copy-start = (bf16[6,192,1152]{2,1,0:T(8,128)(2,1)S(1)}, bf16[6,192,1152]{2,1,0:T(8,128)(2,1)}, u32[]{:S(2)}) copy-start(bf16[6,192,1152]{2,1,0:T(8,128)(2,1)} %get-tuple-element.92.plain_x) | copy-start | bytes 7962628
  579.1 1.5 copy-start.1
  580.6 1.5 copy-start.2
  679.1 4.0 copy-start.3
  679.1 5.1 copy-start.5
  681.0 4.0 copy-start.7
  681.0 4.7 copy-start.6
  683.1 3.2 copy-start.4

commit v7 on v6

--- a/solution.py
+++ b/solution.py
@@ -15,6 +15,7 @@
 CAP = 256
 TAIL = 64
 CALL_PAIRS = 4
+STRAIGHT = 2
 
 eps = 1e-06
 rope_base = 1000000.0
@@ -380,11 +381,7 @@
                     do(first)
 
         def scatter(now):
-            def both(first):
-                crossing(now, first).start()
-                straight(now, first).start()
-
-            by_half(now, both)
+            by_half(now, lambda first: crossing(now, first).start())
 
         def finish(now):
             slot = lax.rem(now, 2)
@@ -436,24 +433,26 @@
                 signal(w_free)
                 pl.semaphore_wait(w_free, 1)
 
-            @pl.when(pair == 1)
-            def _():
-                for copy in fresh:
-                    copy.start()
-
-            for i in range(1, known - 1):
-
-                @pl.when(pair == 1 + i)
+            for i in range(unknown):
+
+                @pl.when(pair == (1 if i == 0 else i * size + 2))
                 def _():
-                    for copy in forward[2 * i : 2 * i + 2]:
+                    for copy in fresh[2 * i : 2 * i + 2]:
                         copy.start()
 
-            @pl.when(pair == size + 2)
-            def _():
-                for copy in fresh:
-                    copy.wait_recv()
-                for copy in forward[2 * known - 2 :]:
-                    copy.start()
+                @pl.when(pair == (i + 1) * size + i)
+                def _():
+                    for copy in fresh[2 * i : 2 * i + 2]:
+                        copy.wait_recv()
+                    begin = 2 * (known + i - 1)
+                    for copy in forward[begin : begin + 2]:
+                        copy.start()
+
+            @pl.when(pair >= early * size)
+            def _():
+                for i in range(STRAIGHT):
+                    now = pair - (early - i) * size
+                    by_half(now, lambda first, now=now: straight(now, first).start())
 
             @pl.when(pair + 1 < pairs)
             def _():
@@ -542,7 +541,8 @@
             for now in range(early * size):
                 first = now % size < half
                 crossing(now, first).wait_send()
-                straight(now, first).wait()
+                if now < STRAIGHT * size:
+                    straight(now, first).wait()
 
     def held(step):
         return step // period * size + jnp.minimum(lax.rem(step, period), size - 1)
@@ -572,7 +572,8 @@
         ]
         + [jax.ShapeDtypeStruct((size, height, lanes), bf16)] * (2 * unknown)
         + [jax.ShapeDtypeStruct((half, height, lanes), bf16)] * (2 * early)
-        + [some] * 6,
+        + [jax.ShapeDtypeStruct((STRAIGHT * half, height, lanes), bf16)] * 2
+        + [some] * 4,
         scratch_shapes=[
             pltpu.VMEM((2, width, lanes), bf16),
             pltpu.VMEM((2 * size * CAP, 2 * width), bf16),
@@ -819,7 +820,7 @@
         normed_ref, q_ref, kv_all, mixed_ref, hidden_ref, rows_all = refs[19:25]
         packed = refs[25 : 25 + calls]
         from_x, from_y, far_x, far_y, next_x, next_y = refs[25 + calls : 31 + calls]
-        after, rest = refs[31 + calls : 25 + 3 * calls], refs[25 + 3 * calls :]
+        rest = refs[31 + calls :]
         line_send, line_recv, grad_send, grad_recv, kv_send, kv_recv, row_send, row_recv = rest[:8]
         chip_send, chip_recv, core_send, core_recv = rest[8:]
         me, z = lax.axis_index("dp"), lax.axis_index("tensor")
@@ -889,9 +890,6 @@
             chip(13, packed[1], x_side, next_x),
             chip(14, packed[1], y_side, next_y),
         ]
-        for i in range(2, calls - 1):
-            moves.append(chip(11 + 2 * i, packed[i], x_side, after[2 * i - 4]))
-            moves.append(chip(12 + 2 * i, packed[i], y_side, after[2 * i - 3]))
         meet(members, True)
         line.start(1)
         for copy in moves[:2]:
@@ -1015,8 +1013,7 @@
             if hop == 1:
                 for copy in moves[6:8]:
                     copy.wait_recv()
-                for copy in (moves[12], *moves[15:]):
-                    copy.start()
+                moves[12].start()
             row_line.arrive(hop)
         for copy in moves[11:]:
             copy.wait_recv()
@@ -1031,7 +1028,7 @@
     return pl.pallas_call(
         kernel,
         in_specs=in_vmem(14),
-        out_specs=in_vmem(11 + calls) + [pl.BlockSpec(memory_space=pl.ANY)] * (2 * calls),
+        out_specs=in_vmem(11 + calls) + [pl.BlockSpec(memory_space=pl.ANY)] * 6,
         out_shape=[
             jax.ShapeDtypeStruct((members, devices * height, 2 * part), bf16),
             jax.ShapeDtypeStruct((devices * height, tall), bf16),
@@ -1047,8 +1044,8 @@
         ]
         + [chunk_shape] * (calls + 2)
         + [half_shape] * 2
-        + [chunk_shape] * (2 * calls - 4),
-        scratch_shapes=[dma((2, members - 1))] * 8 + [dma((9 + 2 * calls,))] * 2 + [dma((8,))] * 2,
+        + [chunk_shape] * 2,
+        scratch_shapes=[dma((2, members - 1))] * 8 + [dma((15,))] * 2 + [dma((8,))] * 2,
         compiler_params=pltpu.CompilerParams(collective_id=2, has_side_effects=True, vmem_limit_bytes=62 * 10**6),
         cost_estimate=pl.CostEstimate(flops=2 * 10**11, bytes_accessed=10**7, transcendentals=0),
         name="front",
@@ -1087,11 +1084,11 @@
 
     def kernel(sums_ref, cot_ref, hidden_ref, x_ref, normed_ref, q_ref, kv_ref, mixed_ref, square_ref, tall_ref, *rest):
         cos_ref, sin_ref, grads_ref, to_x_ref, to_y_ref = rest[:5]
-        grad_ref, moe_out, parts, x_before, y_before, x_last, y_last = rest[5:12]
-        do_ref, dq_ref, dkv_ref, total, kv_total, stage, tall_part, back_part = rest[12:20]
-        back_leave, back_arrive, moe_leave, moe_arrive, kv_leave, kv_arrive = rest[20:26]
-        back_send, back_recv, moe_send, moe_recv, kv_send, kv_recv, stage_sem, part_sem = rest[26:34]
-        through, added, added_sem, chip_send, chip_recv = rest[34:]
+        grad_ref, moe_out, parts, x_before, y_before, x_last, y_last, x_late, y_late = rest[5:14]
+        do_ref, dq_ref, dkv_ref, total, kv_total, stage, tall_part, back_part = rest[14:22]
+        back_leave, back_arrive, moe_leave, moe_arrive, kv_leave, kv_arrive = rest[22:28]
+        back_send, back_recv, moe_send, moe_recv, kv_send, kv_recv, stage_sem, part_sem = rest[28:36]
+        through, added, added_sem, chip_send, chip_recv = rest[36:]
         z = lax.axis_index("tensor")
         x_side, y_side = chip_neighbours()
         first, second = slice(0, size // 2), slice(size // 2, size)
@@ -1121,14 +1118,19 @@
         moves = [
             chip(0, chunk(3, first), through.at[0], x_side),
             chip(1, chunk(3, second), through.at[1], y_side),
-            chip(2, to_x_ref, x_before, x_side),
-            chip(3, to_y_ref, y_before, y_side),
+            chip(2, to_x_ref.at[:soon], x_before, x_side),
+            chip(3, to_y_ref.at[:soon], y_before, y_side),
             chip(4, chunk(1, first), x_last.at[first], x_side),
             chip(5, chunk(2, second), y_last.at[second], y_side),
             chip(6, added.at[0], x_last.at[second], x_side),
             chip(7, added.at[1], y_last.at[first], y_side),
         ]
-        for copy in moves[:6]:
+        for i in range(late):
+            begin, here = (i + STRAIGHT) * size, slice(i * size // 2, (i + 1) * size // 2)
+            middle = begin + size // 2
+            moves.append(chip(8 + 2 * i, grads_ref.at[1, begin:middle], x_late.at[here], x_side))
+            moves.append(chip(9 + 2 * i, grads_ref.at[2, middle : begin + size], y_late.at[here], y_side))
+        for copy in (*moves[:6], *moves[8:]):
             copy.start()
         own = pl.ds(pl.multiple_of(z * own_rows, 16), own_rows)
         for copy in loads:
@@ -1264,18 +1266,21 @@
     _, height, lanes = to_x.shape
     size = CALL_PAIRS
     pairs_before = grads.shape[1] - size
+    late = pairs_before // size - STRAIGHT
+    soon = to_x.shape[0] - size // 2
     halves = (2, size // 2, height, lanes)
     return pl.pallas_call(
         kernel,
         in_specs=[anywhere] + in_vmem(11) + [anywhere] * 3,
-        out_specs=in_vmem(2) + [anywhere] * 5,
+        out_specs=in_vmem(2) + [anywhere] * 7,
         out_shape=[
             jax.ShapeDtypeStruct((own_rows, width), f32),
             jax.ShapeDtypeStruct((2, own_rows, width), bf16),
             jax.ShapeDtypeStruct((width, 2 * width + tall.shape[1]), bf16),
         ]
-        + [jax.ShapeDtypeStruct(to_x.shape, bf16)] * 2
-        + [jax.ShapeDtypeStruct((size, height, lanes), bf16)] * 2,
+        + [jax.ShapeDtypeStruct((soon, height, lanes), bf16)] * 2
+        + [jax.ShapeDtypeStruct((size, height, lanes), bf16)] * 2
+        + [jax.ShapeDtypeStruct((late * size // 2, height, lanes), bf16)] * 2,
         scratch_shapes=[
             pltpu.VMEM((own_rows, width), bf16),
             pltpu.VMEM((own_rows, width), bf16),
@@ -1293,7 +1298,7 @@
             pltpu.VMEM((*hops, own_rows, kv), bf16),
         ]
         + [dma(hops)] * 6
-        + [dma((3,)), dma((members,)), pltpu.VMEM(halves, bf16), pltpu.VMEM(halves, bf16), dma((2,)), dma((8,)), dma((8,))],
+        + [dma((3,)), dma((members,)), pltpu.VMEM(halves, bf16), pltpu.VMEM(halves, bf16), dma((2,)), dma((8 + 2 * late,)), dma((8 + 2 * late,))],
         compiler_params=pltpu.CompilerParams(collective_id=4, has_side_effects=True, vmem_limit_bytes=62 * 10**6),
         cost_estimate=pl.CostEstimate(flops=10**11, bytes_accessed=10**7, transcendentals=0),
         name="attention_back",
@@ -1302,7 +1307,7 @@
     )
 
 
-def reduce_small(parts, sums, moved, hidden, members, devices):
+def reduce_small(parts, sums, moved, hidden, to_x, to_y, members, devices):
     own_rows = hidden.shape[0]
     width = parts.shape[0]
     height = width // devices
@@ -1312,13 +1317,16 @@
     part = width // members
     half = height // 2
     groups = (slice(0, width), slice(width, lanes))
+    begun = to_x.shape[0] - CALL_PAIRS // 2
     dma = pltpu.SemaphoreType.DMA
 
-    def kernel(parts_ref, sums_ref, moved_ref, hidden_ref, out_ref, q_out, o_out, k_out, v_out, gains_out, *rest):
+    def kernel(parts_ref, sums_ref, to_x_ref, to_y_ref, moved_ref, hidden_ref, *rest):
+        out_ref, q_out, o_out, k_out, v_out, gains_out, x_end, y_end = rest[:8]
+        rest = rest[8:]
         own, theirs, leave, arrive, blocks, line_leave, line_arrive, tall_all, line_total = rest[:9]
         moe_part, moe_leave, moe_arrive, total_ref = rest[9:13]
         own_sem, core_send, core_recv, chip_send, chip_recv = rest[13:18]
-        o_send, o_recv, q_send, q_recv, tall_send, tall_recv, moe_send, moe_recv, part_sem = rest[18:]
+        o_send, o_recv, q_send, q_recv, tall_send, tall_recv, moe_send, moe_recv, part_sem, end_send, end_recv = rest[18:]
         me, z = lax.axis_index("dp"), lax.axis_index("tensor")
         x_side, y_side = chip_neighbours()
         core = sibling()
@@ -1417,6 +1425,12 @@
         lines[0].start(last)
         for copy in near[1]:
             copy.wait()
+        ends = [
+            remote(source.at[begun:], target, end_send.at[i], end_recv.at[i], {"dp": device})
+            for i, (source, target, device) in enumerate(((to_x_ref, x_end, x_side), (to_y_ref, y_end, y_side)))
+        ]
+        for copy in ends:
+            copy.start()
         tall_all[z] = total(slice(2 * width, lanes)).astype(bf16)
         for t in range(members):
             blocks[1, t] = total(slice(width + t * part, width + (t + 1) * part))
@@ -1440,12 +1454,14 @@
         gains_out[...] = summed[:, 2 * kv :]
         for line in (*lines, group, moe):
             line.close()
+        for copy in ends:
+            copy.wait()
 
     hops = (2, members - 1)
     return pl.pallas_call(
         kernel,
-        in_specs=[pl.BlockSpec(memory_space=pl.ANY)] * 2 + in_vmem(2),
-        out_specs=in_vmem(6),
+        in_specs=[pl.BlockSpec(memory_space=pl.ANY)] * 4 + in_vmem(2),
+        out_specs=in_vmem(6) + [pl.BlockSpec(memory_space=pl.ANY)] * 2,
         out_shape=[
             jax.ShapeDtypeStruct((own_rows, width), bf16),
             jax.ShapeDtypeStruct((height, part), f32),
@@ -1453,7 +1469,8 @@
             jax.ShapeDtypeStruct((height, kv), f32),
             jax.ShapeDtypeStruct((height, kv), f32),
             jax.ShapeDtypeStruct((height, tall - 2 * kv), f32),
-        ],
+        ]
+        + [jax.ShapeDtypeStruct((CALL_PAIRS // 2, *to_x.shape[1:]), bf16)] * 2,
         scratch_shapes=[
             pltpu.VMEM((4, height, lanes), bf16),
             pltpu.VMEM((4, height, lanes), bf16),
@@ -1475,11 +1492,11 @@
             dma((4, 2)),
         ]
         + [dma(hops)] * 8
-        + [dma((members,))],
+        + [dma((members,)), dma((2,)), dma((2,))],
         compiler_params=pltpu.CompilerParams(collective_id=5, has_side_effects=True, vmem_limit_bytes=60 * 2**20),
         cost_estimate=pl.CostEstimate(flops=8 * 10**10, bytes_accessed=10**7, transcendentals=0),
         name="reduce_small",
-    )(parts, sums, moved, hidden)
+    )(parts, sums, to_x, to_y, moved, hidden)
 
 
 def unpack_all(grads, plain, added, last):
@@ -1488,21 +1505,32 @@
     units = lanes // 6
     tail = units - HD
     step = 48 if height % 48 == 0 else height
-    others = (*plain, *added, *last)
-
-    def kernel(own, plain_x, plain_y, added_x, added_y, last_x, last_y, gate, up, down):
+    kinds = (*plain, *added, last[:1], last[1:])
+    others = [array for kind in kinds for array in kind]
+
+    def kernel(own, *refs):
+        gate, up, down = refs[len(others) :]
+        given = iter(refs)
+        plain_x, plain_y, added_x, added_y, last_x, last_y = (
+            [(ref, i) for _, ref in zip(kind, given) for i in range(ref.shape[0])] for kind in kinds
+        )
+
+        def of(kind, at):
+            ref, i = kind[at]
+            return ref[i].astype(f32)
+
         for call in range(pairs // CALL_PAIRS):
             found = [[], [], []]
             for turn in range(CALL_PAIRS):
                 pair = call * CALL_PAIRS + turn
                 at = call * half + turn % half
                 if pair >= pairs - CALL_PAIRS:
-                    by_x, by_y = last_x[turn], last_y[turn]
+                    by_x, by_y = of(last_x, turn), of(last_y, turn)
                 elif turn < half:
-                    by_x, by_y = plain_x[at], added_y[at]
+                    by_x, by_y = of(plain_x, at), of(added_y, at)
                 else:
-                    by_x, by_y = added_x[at], plain_y[at]
-                value = own[0, pair].astype(f32) + by_x.astype(f32) + by_y.astype(f32)
+                    by_x, by_y = of(added_x, at), of(plain_y, at)
+                value = own[0, pair].astype(f32) + by_x + by_y
                 tiles = [value[:, i * HD : (i + 1) * HD] for i in range(9)]
                 for i, (a, b, both) in enumerate(((0, 1, 2), (3, 4, 5), (6, 8, 7))):
                     left = jnp.concatenate([tiles[a], tiles[both][:, :tail]], axis=1)
@@ -1767,8 +1795,16 @@
         *added,
         members,
     )
-    output, q_grad, o_grad, k_grad, v_grad, gain_grads = reduce_small(parts, sums, moe_moved, hidden, members, devices)
-    gate_out, up_out, down_out = unpack_all(grads, plain, moved[:2], moved[2:])
+    output, q_grad, o_grad, k_grad, v_grad, gain_grads, x_end, y_end = reduce_small(
+        parts, sums, moe_moved, hidden, *added, members, devices
+    )
+    x_before, y_before, x_last, y_last, x_late, y_late = moved
+    gate_out, up_out, down_out = unpack_all(
+        grads,
+        [(plain[0], x_late), (plain[1], y_late)],
+        [(x_before, x_end), (y_before, y_end)],
+        (x_last, y_last),
+    )
     return (
         output,
         tokens_grad,

time: 696 us -> 683 us (0.981)
  Pallas kernels: 673 us -> 663 us
    pallas_call x1, Pallas kernels: 211 us -> 178 us  [front(): pl.pallas_call(kernel, in_specs=in_vmem(14), out_specs=in_vmem(11 + calls...]
    pallas_call x1, Pallas kernels: 237 us -> 262 us  [expert_pass(): pl.pallas_call(kernel, grid=(calls * period,), in_specs=[pl.BlockSpec((ro...]
where the time goes in v7:
time: 683 us; the launch traced here: 674 us
  Pallas kernels  663 us (97%)
  local copies, waits for them, and re-layouts  10.1 us (1%)
    pallas_call x1, Pallas kernels, expert_pass(): pl.pallas_call(kernel, grid=(calls * period,), in_specs=[pl.BlockSpec((ro...  262 us
    pallas_call x1, Pallas kernels, front(): pl.pallas_call(kernel, in_specs=in_vmem(14), out_specs=in_vmem(11 + calls...  178 us
    pallas_call x1, Pallas kernels, attention_back(): pl.pallas_call(kernel, in_specs=[anywhere] + in_vmem(11) + [anywhere] * 3...  126 us
    pallas_call x1, Pallas kernels, reduce_small(): pl.pallas_call(kernel, in_specs=[pl.BlockSpec(memory_space=pl.ANY)] * 4 +...  83.4 us
    pallas_call x1, Pallas kernels, unpack_all(): pl.pallas_call(kernel, grid=(height // step,), in_specs=[pl.BlockSpec((1,...  13.7 us

profile of v7, /device:TPU:0, one launch (start us, length us, event | category | flops | bytes accessed | tf_op | source)
XLA Modules:
  0.0 674.5 jit_solution(14583536875065125844)
XLA Ops:
  0.6 0.7 stack.9
  1.3 0.7 stack.10
  2.0 0.1 copy.28
  2.1 0.6 pad.4.refs_5_
  2.8 178.1 %front.1 = (bf16[4,1536,768]{2,1,0:T(8,128)(2,1)}, bf16[1536,640]{1,0:T(8,128)(2,1)}, bf16[1024,1536]{1,0:T(8,128)(2,1)}, bf16[1024,128]{1,0:T(8,128)(2,1)}, f32...) custom-call(bf16[256,1536]{1,0:T(8,128)(2,1)} %x_ref.1, ...), custom_call_target="tpu_custom_call" | custom-call | flops 199999995904 | bytes 10000000 | tf_op jit(solution)/shard_map/front/pallas_call | solution.py:1028
  180.9 261.7 %experts.1 = (bf16[1024,3072]{1,0:T(8,128)(2,1)}, bf16[4,16,192,1152]{3,2,1,0:T(8,128)(2,1)}, bf16[4,192,1152]{2,1,0:T(8,128)(2,1)}, bf16[4,192,1152]{2,1,0:T(8,...) custom-call(bf16[1024,128]{1,0:T(8,128)(2,1)} %get-tuple-element.58., ...), custom_call_target="tpu_custom_call" | custom-call | flops 199999995904 | bytes 100000000 | tf_op jit(solution)/shard_map/experts/pallas_call | solution.py:558
  442.6 126.3 %attention_back.1 = (f32[256,1536]{1,0:T(8,128)}, bf16[2,256,1536]{2,1,0:T(8,128)(2,1)}, bf16[1536,3712]{1,0:T(8,128)(2,1)}, bf16[4,192,1152]{2,1,0:T(8,128)(2,1...) custom-call(bf16[1024,3072]{1,0:T(8,128)(2,1)} %get-tuple-element.72, ...), custom_call_target="tpu_custom_call" | custom-call | flops 99999997952 | bytes 10000000 | tf_op jit(solution)/shard_map/attention_back/pallas_call | solution.py:1272
  568.9 0.0 copy-start
  568.9 0.0 copy-start.1
  568.9 0.0 copy-start.2
  568.9 83.4 %reduce_small.1 = (bf16[256,1536]{1,0:T(8,128)(2,1)}, f32[192,384]{1,0:T(8,128)}, f32[192,384]{1,0:T(8,128)}, f32[192,256]{1,0:T(8,128)}, f32[192,256]{1,0:T(8,1...) custom-call(bf16[1536,3712]{1,0:T(8,128)(2,1)} %get-tuple-element.83.parts_ref, ...), custom_call_target="tpu_custom_call" | custom-call | flops 80000000000 | bytes 10000000 | tf_op jit(solution)/shard_map/reduce_small/pallas_call | solution.py:1461
  652.3 0.0 copy-done
  652.3 0.0 copy-done.1
  652.4 0.0 copy-done.2
  652.4 0.0 copy-start.3
  652.4 1.2 copy-done.3
  653.5 1.2 copy-done.4
  654.7 13.7 %unpack.1 = (f32[192,32,192]{2,1,0:T(8,128)}, f32[192,32,192]{2,1,0:T(8,128)}, f32[192,32,192]{2,1,0:T(8,128)}) custom-call(bf16[4,16,192,1152]{3,2,1,0:T(8,128)(2,1)} %get-tuple-element.80.rest_2_.own, bf16[4,192,1152]{2,1,0:T(8,128)(2,1)S(1)} %copy-done, bf16[2,192,1152]{2,1,0:T(8,128)(2,1)S(1)} %copy-done.1, ...), custom_call_target="tpu_custom_call" | custom-call | tf_op jit(solution)/shard_map/unpack/pallas_call | solution.py:1548
  668.4 0.0 copy-done.7
  668.4 0.8 slice_reduce_fusion
  669.2 0.0 copy-done.6
  669.2 0.9 copy.35
  670.1 0.0 copy-done.5
  670.1 0.0 copy-start.8
  670.1 1.1 copy.36
  671.2 0.0 copy-done.9
  671.3 0.7 copy.37
  672.0 0.0 copy-done.11
  672.0 0.7 copy.38
  672.6 0.0 copy-done.10
  672.6 0.7 copy.39
  673.3 0.7 copy.40
  (9 shorter events, 0.0 us)
Async XLA Ops:
  568.9 83.5 %copy-start = (bf16[4,192,1152]{2,1,0:T(8,128)(2,1)S(1)}, bf16[4,192,1152]{2,1,0:T(8,128)(2,1)}, u32[]{:S(2)}) copy-start(bf16[4,192,1152]{2,1,0:T(8,128)(2,1)} %get-tuple-element.92.refs_0_) | copy-start | bytes 5308420
  568.9 83.5 %copy-start.1 = (bf16[2,192,1152]{2,1,0:T(8,128)(2,1)S(1)}, bf16[2,192,1152]{2,1,0:T(8,128)(2,1)}, u32[]{:S(2)}) copy-start(bf16[2,192,1152]{2,1,0:T(8,128)(2,1)} %get-tuple-element.93.refs_1_) | copy-start | bytes 2654212
  568.9 83.5 %copy-start.2 = (bf16[2,192,1152]{2,1,0:T(8,128)(2,1)S(1)}, bf16[2,192,1152]{2,1,0:T(8,128)(2,1)}, u32[]{:S(2)}) copy-start(bf16[2,192,1152]{2,1,0:T(8,128)(2,1)} %get-tuple-element.95.refs_3_) | copy-start | bytes 2654212
  652.4 1.2 copy-start.3
  653.5 1.2 copy-start.4
  654.7 13.7 %copy-start.7 = (f32[192,128]{1,0:T(8,128)S(1)}, f32[192,128]{1,0:T(8,128)}, u32[]{:S(2)}) copy-start(f32[192,128]{1,0:T(8,128)} %get-tuple-element.87) | copy-start | bytes 294916
  654.7 14.5 %copy-start.6 = (bf16[256,1536]{1,0:T(8,128)(2,1)S(1)}, bf16[256,1536]{1,0:T(8,128)(2,1)}, u32[]{:S(2)}) copy-start(bf16[256,1536]{1,0:T(8,128)(2,1)} %get-tuple-element.118) | copy-start | bytes 2359300
  668.4 1.7 copy-start.5
  670.1 1.2 copy-start.9
  670.1 1.9 copy-start.11
  670.1 2.6 copy-start.10
  670.1 3.2 copy-start.8

commit v8 on v7

--- a/solution.py
+++ b/solution.py
@@ -462,7 +462,12 @@
             def _():
                 keep(pair - 2).wait()
 
-            @pl.when((pair >= 2) & (pair - 2 < early * size))
+            @pl.when(pair == size + 1)
+            def _():
+                for now in range(size - 1):
+                    crossing(now, now < half).start()
+
+            @pl.when((pair > size) & (pair - 2 < early * size))
             def _():
                 scatter(pair - 2)
 
@@ -896,8 +901,6 @@
             copy.start()
         trade(0, tall_at(me))
         pack(0)
-        for copy in moves[2:4]:
-            copy.start()
         for index, device in ((0, x_side), (1, y_side)):
             chip(index, tall_at(device), device).wait_recv()
         moves[8].start()
@@ -965,9 +968,7 @@
         chip(9, square_at(diagonal, 0), y_side).wait_recv()
         chip(10, square_at(diagonal, 1), x_side).wait_recv()
         trade(7, square_at(diagonal))
-        for copy in moves[2:4]:
-            copy.wait_recv()
-        for copy in (*moves[6:8], moves[11]):
+        for copy in (*moves[2:4], *moves[6:8]):
             copy.start()
         group.arrive(1)
         if last > 1:
@@ -1011,9 +1012,10 @@
         for hop in range(1, members):
             row_line.start(hop)
             if hop == 1:
-                for copy in moves[6:8]:
+                for copy in (*moves[2:4], *moves[6:8]):
                     copy.wait_recv()
-                moves[12].start()
+                for copy in moves[11:13]:
+                    copy.start()
             row_line.arrive(hop)
         for copy in moves[11:]:
             copy.wait_recv()

time: 683 us -> 679 us (level)
  no operation moved by 1% of the time
where the time goes in v8:
time: 679 us; the launch traced here: 671 us
  Pallas kernels  660 us (97%)
  local copies, waits for them, and re-layouts  10.1 us (1%)
    pallas_call x1, Pallas kernels, expert_pass(): pl.pallas_call(kernel, grid=(calls * period,), in_specs=[pl.BlockSpec((ro...  260 us
    pallas_call x1, Pallas kernels, front(): pl.pallas_call(kernel, in_specs=in_vmem(14), out_specs=in_vmem(11 + calls...  177 us
    pallas_call x1, Pallas kernels, attention_back(): pl.pallas_call(kernel, in_specs=[anywhere] + in_vmem(11) + [anywhere] * 3...  126 us
    pallas_call x1, Pallas kernels, reduce_small(): pl.pallas_call(kernel, in_specs=[pl.BlockSpec(memory_space=pl.ANY)] * 4 +...  83.1 us
    pallas_call x1, Pallas kernels, unpack_all(): pl.pallas_call(kernel, grid=(height // step,), in_specs=[pl.BlockSpec((1,...  13.7 us

profile of v8, /device:TPU:0, one launch (start us, length us, event | category | flops | bytes accessed | tf_op | source)
XLA Modules:
  0.0 671.0 jit_solution(1641374975086224757)
XLA Ops:
  0.6 0.7 stack.9
  1.3 0.7 stack.10
  2.0 0.1 copy.28
  2.1 0.6 pad.4.refs_5_
  2.8 176.9 %front.1 = (bf16[4,1536,768]{2,1,0:T(8,128)(2,1)}, bf16[1536,640]{1,0:T(8,128)(2,1)}, bf16[1024,1536]{1,0:T(8,128)(2,1)}, bf16[1024,128]{1,0:T(8,128)(2,1)}, f32...) custom-call(bf16[256,1536]{1,0:T(8,128)(2,1)} %x_ref.1, ...), custom_call_target="tpu_custom_call" | custom-call | flops 199999995904 | bytes 10000000 | tf_op jit(solution)/shard_map/front/pallas_call | solution.py:1030
  179.7 259.8 %experts.1 = (bf16[1024,3072]{1,0:T(8,128)(2,1)}, bf16[4,16,192,1152]{3,2,1,0:T(8,128)(2,1)}, bf16[4,192,1152]{2,1,0:T(8,128)(2,1)}, bf16[4,192,1152]{2,1,0:T(8,...) custom-call(bf16[1024,128]{1,0:T(8,128)(2,1)} %get-tuple-element.58., ...), custom_call_target="tpu_custom_call" | custom-call | flops 199999995904 | bytes 100000000 | tf_op jit(solution)/shard_map/experts/pallas_call | solution.py:563
  439.5 126.3 %attention_back.1 = (f32[256,1536]{1,0:T(8,128)}, bf16[2,256,1536]{2,1,0:T(8,128)(2,1)}, bf16[1536,3712]{1,0:T(8,128)(2,1)}, bf16[4,192,1152]{2,1,0:T(8,128)(2,1...) custom-call(bf16[1024,3072]{1,0:T(8,128)(2,1)} %get-tuple-element.72, ...), custom_call_target="tpu_custom_call" | custom-call | flops 99999997952 | bytes 10000000 | tf_op jit(solution)/shard_map/attention_back/pallas_call | solution.py:1274
  565.8 0.0 copy-start
  565.8 0.0 copy-start.1
  565.8 0.0 copy-start.2
  565.8 83.1 %reduce_small.1 = (bf16[256,1536]{1,0:T(8,128)(2,1)}, f32[192,384]{1,0:T(8,128)}, f32[192,384]{1,0:T(8,128)}, f32[192,256]{1,0:T(8,128)}, f32[192,256]{1,0:T(8,1...) custom-call(bf16[1536,3712]{1,0:T(8,128)(2,1)} %get-tuple-element.83.parts_ref, ...), custom_call_target="tpu_custom_call" | custom-call | flops 80000000000 | bytes 10000000 | tf_op jit(solution)/shard_map/reduce_small/pallas_call | solution.py:1463
  648.9 0.0 copy-done
  648.9 0.0 copy-done.1
  648.9 0.0 copy-done.2
  648.9 0.0 copy-start.3
  648.9 1.2 copy-done.3
  650.1 1.2 copy-done.4
  651.3 13.7 %unpack.1 = (f32[192,32,192]{2,1,0:T(8,128)}, f32[192,32,192]{2,1,0:T(8,128)}, f32[192,32,192]{2,1,0:T(8,128)}) custom-call(bf16[4,16,192,1152]{3,2,1,0:T(8,128)(2,1)} %get-tuple-element.80.rest_2_.own, bf16[4,192,1152]{2,1,0:T(8,128)(2,1)S(1)} %copy-done, bf16[2,192,1152]{2,1,0:T(8,128)(2,1)S(1)} %copy-done.1, ...), custom_call_target="tpu_custom_call" | custom-call | tf_op jit(solution)/shard_map/unpack/pallas_call | solution.py:1550
  665.0 0.0 copy-done.7
  665.0 0.8 slice_reduce_fusion
  665.8 0.0 copy-done.6
  665.8 0.9 copy.35
  666.6 0.0 copy-done.5
  666.6 0.0 copy-start.8
  666.7 1.1 copy.36
  667.8 0.0 copy-done.9
  667.8 0.7 copy.37
  668.5 0.0 copy-done.11
  668.5 0.7 copy.38
  669.2 0.0 copy-done.10
  669.2 0.7 copy.39
  669.9 0.7 copy.40
  (9 shorter events, 0.0 us)
Async XLA Ops:
  565.8 83.1 %copy-start = (bf16[4,192,1152]{2,1,0:T(8,128)(2,1)S(1)}, bf16[4,192,1152]{2,1,0:T(8,128)(2,1)}, u32[]{:S(2)}) copy-start(bf16[4,192,1152]{2,1,0:T(8,128)(2,1)} %get-tuple-element.92.refs_0_) | copy-start | bytes 5308420
  565.8 83.1 %copy-start.1 = (bf16[2,192,1152]{2,1,0:T(8,128)(2,1)S(1)}, bf16[2,192,1152]{2,1,0:T(8,128)(2,1)}, u32[]{:S(2)}) copy-start(bf16[2,192,1152]{2,1,0:T(8,128)(2,1)} %get-tuple-element.93.refs_1_) | copy-start | bytes 2654212
  565.8 83.1 %copy-start.2 = (bf16[2,192,1152]{2,1,0:T(8,128)(2,1)S(1)}, bf16[2,192,1152]{2,1,0:T(8,128)(2,1)}, u32[]{:S(2)}) copy-start(bf16[2,192,1152]{2,1,0:T(8,128)(2,1)} %get-tuple-element.95.refs_3_) | copy-start | bytes 2654212
  648.9 1.2 copy-start.3
  650.1 1.2 copy-start.4
  651.3 13.7 %copy-start.7 = (f32[192,128]{1,0:T(8,128)S(1)}, f32[192,128]{1,0:T(8,128)}, u32[]{:S(2)}) copy-start(f32[192,128]{1,0:T(8,128)} %get-tuple-element.87) | copy-start | bytes 294916
  651.3 14.5 %copy-start.6 = (bf16[256,1536]{1,0:T(8,128)(2,1)S(1)}, bf16[256,1536]{1,0:T(8,128)(2,1)}, u32[]{:S(2)}) copy-start(bf16[256,1536]{1,0:T(8,128)(2,1)} %get-tuple-element.118) | copy-start | bytes 2359300
  665.0 1.7 copy-start.5
  666.6 1.2 copy-start.9
  666.6 1.9 copy-start.11
  666.6 2.6 copy-start.10
  666.6 3.2 copy-start.8

commit v9 on v8

--- a/solution.py
+++ b/solution.py
@@ -1506,7 +1506,7 @@
     half = CALL_PAIRS // 2
     units = lanes // 6
     tail = units - HD
-    step = 48 if height % 48 == 0 else height
+    step = 96 if height % 96 == 0 else height
     kinds = (*plain, *added, last[:1], last[1:])
     others = [array for kind in kinds for array in kind]
 
@@ -1554,7 +1554,7 @@
         + [pl.BlockSpec((other.shape[0], step, lanes), lambda i: (0, i, 0)) for other in others],
         out_specs=[pl.BlockSpec((step, *shape[1:]), lambda i: (i, 0, 0))] * 3,
         out_shape=[jax.ShapeDtypeStruct(shape, f32)] * 3,
-        compiler_params=pltpu.CompilerParams(vmem_limit_bytes=48 * 2**20),
+        compiler_params=pltpu.CompilerParams(vmem_limit_bytes=62 * 10**6),
         name="unpack",
     )(grads, *others)
 

time: 679 us -> 677 us (level)
  no operation moved by 1% of the time
where the time goes in v9:
time: 677 us; the launch traced here: 669 us
  Pallas kernels  660 us (97%)
  local copies, waits for them, and re-layouts  7.72 us (1%)
    pallas_call x1, Pallas kernels, expert_pass(): pl.pallas_call(kernel, grid=(calls * period,), in_specs=[pl.BlockSpec((ro...  260 us
    pallas_call x1, Pallas kernels, front(): pl.pallas_call(kernel, in_specs=in_vmem(14), out_specs=in_vmem(11 + calls...  177 us
    pallas_call x1, Pallas kernels, attention_back(): pl.pallas_call(kernel, in_specs=[anywhere] + in_vmem(11) + [anywhere] * 3...  126 us
    pallas_call x1, Pallas kernels, reduce_small(): pl.pallas_call(kernel, in_specs=[pl.BlockSpec(memory_space=pl.ANY)] * 4 +...  83.1 us
    pallas_call x1, Pallas kernels, unpack_all(): pl.pallas_call(kernel, grid=(height // step,), in_specs=[pl.BlockSpec((1,...  13.7 us

profile of v9, /device:TPU:0, one launch (start us, length us, event | category | flops | bytes accessed | tf_op | source)
XLA Modules:
  0.0 668.8 jit_solution(14498969875018415248)
XLA Ops:
  0.6 0.7 stack.9
  1.3 0.7 stack.10
  2.0 0.1 copy.28
  2.1 0.6 pad.4.refs_5_
  2.8 176.8 %front.1 = (bf16[4,1536,768]{2,1,0:T(8,128)(2,1)}, bf16[1536,640]{1,0:T(8,128)(2,1)}, bf16[1024,1536]{1,0:T(8,128)(2,1)}, bf16[1024,128]{1,0:T(8,128)(2,1)}, f32...) custom-call(bf16[256,1536]{1,0:T(8,128)(2,1)} %x_ref.1, ...), custom_call_target="tpu_custom_call" | custom-call | flops 199999995904 | bytes 10000000 | tf_op jit(solution)/shard_map/front/pallas_call | solution.py:1030
  179.6 259.8 %experts.1 = (bf16[1024,3072]{1,0:T(8,128)(2,1)}, bf16[4,16,192,1152]{3,2,1,0:T(8,128)(2,1)}, bf16[4,192,1152]{2,1,0:T(8,128)(2,1)}, bf16[4,192,1152]{2,1,0:T(8,...) custom-call(bf16[1024,128]{1,0:T(8,128)(2,1)} %get-tuple-element.58., ...), custom_call_target="tpu_custom_call" | custom-call | flops 199999995904 | bytes 100000000 | tf_op jit(solution)/shard_map/experts/pallas_call | solution.py:563
  439.5 126.3 %attention_back.1 = (f32[256,1536]{1,0:T(8,128)}, bf16[2,256,1536]{2,1,0:T(8,128)(2,1)}, bf16[1536,3712]{1,0:T(8,128)(2,1)}, bf16[4,192,1152]{2,1,0:T(8,128)(2,1...) custom-call(bf16[1024,3072]{1,0:T(8,128)(2,1)} %get-tuple-element.72, ...), custom_call_target="tpu_custom_call" | custom-call | flops 99999997952 | bytes 10000000 | tf_op jit(solution)/shard_map/attention_back/pallas_call | solution.py:1274
  565.8 83.1 %reduce_small.1 = (bf16[256,1536]{1,0:T(8,128)(2,1)}, f32[192,384]{1,0:T(8,128)}, f32[192,384]{1,0:T(8,128)}, f32[192,256]{1,0:T(8,128)}, f32[192,256]{1,0:T(8,1...) custom-call(bf16[1536,3712]{1,0:T(8,128)(2,1)} %get-tuple-element.83.parts_ref, ...), custom_call_target="tpu_custom_call" | custom-call | flops 80000000000 | bytes 10000000 | tf_op jit(solution)/shard_map/reduce_small/pallas_call | solution.py:1463
  648.9 0.0 copy-start.2
  648.9 0.0 copy-start.1
  648.9 13.7 %unpack.1 = (f32[192,32,192]{2,1,0:T(8,128)}, f32[192,32,192]{2,1,0:T(8,128)}, f32[192,32,192]{2,1,0:T(8,128)}) custom-call(bf16[4,16,192,1152]{3,2,1,0:T(8,128)(2,1)} %get-tuple-element.80.rest_2_.own, bf16[4,192,1152]{2,1,0:T(8,128)(2,1)} %get-tuple-element.92.refs_0_, bf16[2,192,1152]{2,1,0:T(8,128)(2,1)} %get-tuple-element.93.refs_1_, ...), custom_call_target="tpu_custom_call" | custom-call | tf_op jit(solution)/shard_map/unpack/pallas_call | solution.py:1550
  662.7 0.0 copy-start
  662.7 0.0 copy-done.2
  662.7 0.8 slice_reduce_fusion
  663.5 0.0 copy-done.1
  663.5 0.9 copy.35
  664.3 0.0 copy-done
  664.3 0.0 copy-start.4
  664.3 0.0 copy-start.6
  664.3 0.0 copy-start.5
  664.3 0.0 copy-start.3
  664.4 1.1 copy.36
  665.5 0.0 copy-done.4
  665.5 0.7 copy.37
  666.2 0.0 copy-done.6
  666.2 0.7 copy.38
  666.9 0.0 copy-done.5
  666.9 0.7 copy.39
  667.6 0.0 copy-done.3
  667.6 0.7 copy.40
  (1 shorter events, 0.0 us)
Async XLA Ops:
  648.9 13.7 %copy-start.2 = (f32[192,128]{1,0:T(8,128)S(1)}, f32[192,128]{1,0:T(8,128)}, u32[]{:S(2)}) copy-start(f32[192,128]{1,0:T(8,128)} %get-tuple-element.87) | copy-start | bytes 294916
  648.9 14.5 %copy-start.1 = (bf16[256,1536]{1,0:T(8,128)(2,1)S(1)}, bf16[256,1536]{1,0:T(8,128)(2,1)}, u32[]{:S(2)}) copy-start(bf16[256,1536]{1,0:T(8,128)(2,1)} %get-tuple-element.118) | copy-start | bytes 2359300
  662.7 1.7 copy-start
  664.3 1.2 copy-start.4
  664.3 1.9 copy-start.6
  664.3 2.6 copy-start.5
  664.3 3.2 copy-start.3
